TPU v7x, 32 devices: a whole 2x2x4 slice. The times are simulated.
32 devices in a mesh: seq: 4 (over y, x), head: 4 (over z), dp: 2 (over core).
Axes of the slice: x: 2, y: 2, z: 4, core: 2. Of those that a mesh axis runs over, the one named last changes fastest.
Arguments:
- query_heads: bfloat16 [2, 1024, 4096], P('dp', 'seq', 'head'), may hold values from -100 to 100
- key_heads: bfloat16 [2, 1024, 4096], P('dp', 'seq', 'head'), may hold values from -100 to 100
- value_heads: bfloat16 [2, 1024, 4096], P('dp', 'seq', 'head'), may hold values from -6 to 6
- query_gain: float32 [4096], P('head'), may hold values from 0.5 to 1.5
- key_gain: float32 [4096], P('head'), may hold values from 0.5 to 1.5
- key_squeeze: bfloat16 [32, 512, 128], P('head'), may hold values from -0.25 to 0.25
- value_squeeze: bfloat16 [32, 512, 128], P('head'), may hold values from -0.25 to 0.25
- grad_out: bfloat16 [2, 1024, 4096], P('dp', 'seq', 'head'), may hold values from -6 to 6
Outputs:
- grad_query: bfloat16 [2, 1024, 4096], P('dp', 'seq', 'head')
- grad_key: bfloat16 [2, 1024, 4096], P('dp', 'seq', 'head')
- grad_value: bfloat16 [2, 1024, 4096], P('dp', 'seq', 'head')
- grad_query_gain: float32 [4096], P('head')
- grad_key_gain: float32 [4096], P('head')
- grad_key_squeeze: float32 [32, 512, 128], P('head')
- grad_value_squeeze: float32 [32, 512, 128], P('head')
All inputs are finite; a program needn't handle non-finite values.
Results may differ from a plain program's by a relative error of at most 0.025.
Values may be sent and summed in bfloat16 or wider, within the bound.
No kernel may reach another device: no remote copies, remote signals or barrier semaphores. Data moves between devices by JAX's collectives and lax.ppermute only.
A program may use at most 64 MiB of HBM per device.

v0:
```python
import jax
import jax.numpy as jnp
from jax import lax
from jax.sharding import PartitionSpec as P

HD = 128
KS = 4
HH = 4096


epsilon = 1e-06


def unfold_slots(source, head_count):
    batch_size, row_count, widths = source.shape
    return (
        source.reshape(batch_size, row_count // KS, KS, head_count, HD)
        .transpose(0, 1, 3, 2, 4)
        .reshape(batch_size, row_count // KS, head_count, KS * HD)
    )


def fold_slots(source):
    batch_size, slot_count, head_count, spans = source.shape
    return (
        source.reshape(batch_size, slot_count, head_count, KS, HD)
        .transpose(0, 1, 3, 2, 4)
        .reshape(batch_size, slot_count * KS, head_count * HD)
    )


def on_device(
    query_heads, key_heads, value_heads, query_gain, key_gain, key_squeeze, value_squeeze, grad_out
):
    batch_size, row_count, widths = query_heads.shape
    head_count = widths // HD
    slot_count = row_count // KS
    score_scale = HD ** (-0.5)
    own_limit = lax.axis_index("seq") * slot_count
    q_full = query_heads.astype(jnp.float32)
    k_full = key_heads.astype(jnp.float32)
    sum_q, sum_k = lax.psum((jnp.sum(q_full * q_full, -1), jnp.sum(k_full * k_full, -1)), "head")
    inv_q = lax.rsqrt(sum_q / HH + epsilon)[..., None]
    inv_k = lax.rsqrt(sum_k / HH + epsilon)[..., None]
    q_norm = (q_full * inv_q * query_gain).astype(jnp.bfloat16)
    k_norm = (k_full * inv_k * key_gain).astype(jnp.bfloat16)
    k_unf = unfold_slots(k_norm, head_count)
    v_unf = unfold_slots(value_heads, head_count)
    mem_k = (
        jnp.einsum("bmhc,hcd->bmhd", k_unf, key_squeeze, preferred_element_type=jnp.float32)
        .astype(jnp.bfloat16)
        .reshape(batch_size, slot_count, widths)
    )
    mem_v = (
        jnp.einsum("bmhc,hcd->bmhd", v_unf, value_squeeze, preferred_element_type=jnp.float32)
        .astype(jnp.bfloat16)
        .reshape(batch_size, slot_count, widths)
    )
    queries = q_norm.reshape(batch_size, row_count, head_count, HD)
    key_loc = k_norm.reshape(batch_size, row_count, head_count, HD)
    value_loc = value_heads.reshape(batch_size, row_count, head_count, HD)
    cotangent = grad_out.reshape(batch_size, row_count, head_count, HD)
    positions = jnp.arange(row_count)
    causal = positions[:, None] >= positions[None, :]
    scores_loc = jnp.where(
        causal,
        jnp.einsum("bthd,buhd->bhtu", queries, key_loc, preferred_element_type=jnp.float32)
        * score_scale,
        -jnp.inf,
    )
    grads_loc = jnp.einsum(
        "bthd,buhd->bhtu", cotangent, value_loc, preferred_element_type=jnp.float32
    )
    all_k, all_v = (
        lax.all_gather(mem_k, "seq", axis=1, tiled=True),
        lax.all_gather(mem_v, "seq", axis=1, tiled=True),
    )
    piece_rows = all_k.shape[1]
    key_rows = all_k.reshape(batch_size, piece_rows, head_count, HD)
    value_rows = all_v.reshape(batch_size, piece_rows, head_count, HD)
    allowed = jnp.arange(piece_rows) < own_limit
    scores = jnp.where(
        allowed,
        jnp.einsum("bthd,buhd->bhtu", queries, key_rows, preferred_element_type=jnp.float32)
        * score_scale,
        -jnp.inf,
    )
    gradients = jnp.einsum(
        "bthd,buhd->bhtu", cotangent, value_rows, preferred_element_type=jnp.float32
    )
    key_rows, scores_mem, grads_mem = (key_rows, scores, gradients)
    peak = jnp.maximum(jnp.max(scores_loc, -1), jnp.max(scores_mem, -1))
    summed = jnp.sum(jnp.exp(scores_loc - peak[..., None]), -1) + jnp.sum(
        jnp.exp(scores_mem - peak[..., None]), -1
    )
    log_mass = peak + jnp.log(summed)
    row_delta = jnp.sum(jnp.exp(scores_loc - log_mass[..., None]) * grads_loc, -1) + jnp.sum(
        jnp.exp(scores_mem - log_mass[..., None]) * grads_mem, -1
    )
    piece_rows = key_rows.shape[1]
    attend = jnp.exp(scores_mem - log_mass[..., None])
    d_scores = (attend * (grads_mem - row_delta[..., None])).astype(jnp.bfloat16)
    grad_q = score_scale * jnp.einsum(
        "bhtu,buhd->bthd", d_scores, key_rows, preferred_element_type=jnp.float32
    )
    grad_k = score_scale * jnp.einsum(
        "bhtu,bthd->buhd", d_scores, queries, preferred_element_type=jnp.float32
    )
    grad_v = jnp.einsum(
        "bhtu,bthd->buhd",
        attend.astype(jnp.bfloat16),
        cotangent,
        preferred_element_type=jnp.float32,
    )
    stacked = jnp.stack(
        (
            grad_k.reshape(batch_size, piece_rows, widths),
            grad_v.reshape(batch_size, piece_rows, widths),
        )
    )
    attend_loc = jnp.exp(scores_loc - log_mass[..., None])
    d_loc = (attend_loc * (grads_loc - row_delta[..., None])).astype(jnp.bfloat16)
    grad_qn = (
        score_scale
        * jnp.einsum("bhtu,buhd->bthd", d_loc, key_loc, preferred_element_type=jnp.float32)
        + grad_q
    ).reshape(batch_size, row_count, widths)
    grad_kn_local = score_scale * jnp.einsum(
        "bhtu,bthd->buhd", d_loc, queries, preferred_element_type=jnp.float32
    )
    grad_v_local = jnp.einsum(
        "bhtu,bthd->buhd",
        attend_loc.astype(jnp.bfloat16),
        cotangent,
        preferred_element_type=jnp.float32,
    )
    mine = lax.psum_scatter(stacked.astype(jnp.bfloat16), "seq", scatter_dimension=2, tiled=True)
    grad_mem_k = mine[0].reshape(batch_size, slot_count, head_count, HD)
    grad_mem_v = mine[1].reshape(batch_size, slot_count, head_count, HD)
    squeeze_k_part = jnp.einsum(
        "bmhc,bmhd->hcd", k_unf, grad_mem_k, preferred_element_type=jnp.float32
    )
    squeeze_v_part = jnp.einsum(
        "bmhc,bmhd->hcd", v_unf, grad_mem_v, preferred_element_type=jnp.float32
    )
    back_k = fold_slots(
        jnp.einsum("bmhd,hcd->bmhc", grad_mem_k, key_squeeze, preferred_element_type=jnp.float32)
    )
    back_v = fold_slots(
        jnp.einsum("bmhd,hcd->bmhc", grad_mem_v, value_squeeze, preferred_element_type=jnp.float32)
    )
    grad_kn = grad_kn_local.reshape(batch_size, row_count, widths) + back_k
    grad_value = (grad_v_local.reshape(batch_size, row_count, widths) + back_v).astype(jnp.bfloat16)
    dot_q, dot_k = lax.psum(
        (jnp.sum(query_gain * grad_qn * q_full, -1), jnp.sum(key_gain * grad_kn * k_full, -1)),
        "head",
    )
    grad_query = (
        inv_q * query_gain * grad_qn - q_full * inv_q**3 * dot_q[..., None] / HH
    ).astype(jnp.bfloat16)
    grad_key = (inv_k * key_gain * grad_kn - k_full * inv_k**3 * dot_k[..., None] / HH).astype(
        jnp.bfloat16
    )
    gain_q_part = jnp.sum(grad_qn * q_full * inv_q, (0, 1))
    gain_k_part = jnp.sum(grad_kn * k_full * inv_k, (0, 1))
    grad_query_gain, grad_key_gain, grad_key_squeeze, grad_value_squeeze = (
        lax.psum(gain_q_part.astype(jnp.bfloat16), ("seq", "dp")).astype(jnp.float32),
        lax.psum(gain_k_part.astype(jnp.bfloat16), ("seq", "dp")).astype(jnp.float32),
        lax.psum(squeeze_k_part.astype(jnp.bfloat16), ("seq", "dp")).astype(jnp.float32),
        lax.psum(squeeze_v_part.astype(jnp.bfloat16), ("seq", "dp")).astype(jnp.float32),
    )
    return (
        grad_query,
        grad_key,
        grad_value,
        grad_query_gain,
        grad_key_gain,
        grad_key_squeeze,
        grad_value_squeeze,
    )


def solution(mesh):
    placed = (
        P("dp", "seq", "head"),
        P("dp", "seq", "head"),
        P("dp", "seq", "head"),
        P("head"),
        P("head"),
        P("head", None, None),
        P("head", None, None),
        P("dp", "seq", "head"),
    )
    return jax.shard_map(
        on_device,
        mesh=mesh,
        in_specs=placed,
        out_specs=(
            P("dp", "seq", "head"),
            P("dp", "seq", "head"),
            P("dp", "seq", "head"),
            P("head"),
            P("head"),
            P("head", None, None),
            P("head", None, None),
        ),
        check_vma=False,
    )
```

profile of v0, /device:TPU:0, one launch (start us, length us, event | category | flops | bytes accessed | tf_op | source)
XLA Modules:
  0.0 184.6 jit_solution(15839283977841824322)
XLA Ops:
  9.8 13.5 %all-reduce.1 = (f32[1,256]{1,0:T(1,128)S(1)}, f32[1,256]{1,0:T(1,128)S(1)}) all-reduce(f32[1,256]{1,0:T(1,128)S(1)} %bitcast.187, f32[1,256]{1,0:T(1,128)S(1)} %bitcast.188), channel_id=1, replica_groups=mesh['seq'=4,'head'=4,'dp'=2] {'head'}, use_global_device_ids=true, to_apply=%region_1.0 | all-reduce | flops 512 | bytes 4096 | tf_op jit(solution)/shard_map/psum | solution.py:42
  25.7 11.5 %all_gather.6 = bf16[1,256,1024]{2,1,0:T(8,128)(2,1)} all-gather(bf16[1,64,1024]{2,1,0:T(8,128)(2,1)S(1)} %bitcast.175), channel_id=1, replica_groups=mesh['seq'=4,'head'=4,'dp'=2] {'seq'}, dimensions={1}, use_global_device_ids=true | all-gather | bytes 655360 | tf_op jit(solution)/shard_map/all_gather | solution.py:75
  41.7 2.0 %copy.92 = bf16[1,256,1024]{1,2,0:T(8,128)(2,1)} copy(bf16[1,256,1024]{2,1,0:T(8,128)(2,1)} %param.15) | data formatting | bytes 1048576 | tf_op jit(solution)/shard_map/reshape.17
  47.9 9.9 %all_gather.7 = bf16[1,256,1024]{2,1,0:T(8,128)(2,1)S(1)} all-gather(bf16[1,64,1024]{2,1,0:T(8,128)(2,1)S(1)} %bitcast.176), channel_id=1, replica_groups=mesh['seq'=4,'head'=4,'dp'=2] {'seq'}, dimensions={1}, use_global_device_ids=true | all-gather | bytes 655360 | tf_op jit(solution)/shard_map/all_gather | solution.py:76
  68.7 2.1 %copy.68 = bf16[1,1,256,1024]{3,2,1,0:T(8,128)(2,1)} copy(bf16[1,1,256,1024]{2,3,1,0:T(8,128)(2,1)} %bitcast.169) | data formatting | bytes 1048576 | tf_op jit(solution)/shard_map/stack | solution.py:115
  70.7 2.1 %copy.69 = bf16[1,1,256,1024]{3,2,1,0:T(8,128)(2,1)} copy(bf16[1,1,256,1024]{2,3,1,0:T(8,128)(2,1)} %bitcast.168) | data formatting | bytes 1048576 | tf_op jit(solution)/shard_map/stack | solution.py:115
  72.8 2.3 %pad_maximum_fusion = bf16[2,1,256,1024]{3,2,1,0:T(8,128)(2,1)} fusion(bf16[1,1,256,1024]{3,2,1,0:T(8,128)(2,1)} %copy.69, bf16[1,1,256,1024]{3,2,1,0:T(8,128)(2,1)} %copy.68), kind=kLoop, calls=%fused_computation.61 | loop fusion | flops 524288 | bytes 2097152 | tf_op jit(solution)/shard_map/stack | solution.py:115
  75.4 2.9 %convolution_multiply_fusion.1 = f32[8,128,256]{2,1,0:T(8,128)} fusion(bf16[256,8,128]{0,2,1:T(8,128)(2,1)} %bitcast.150, bf16[8,256,256]{1,2,0:T(8,128)(2,1)} %get-tuple-element.40), kind=kOutput, calls=%fused_computation.31 | convolution fusion | flops 134479872 | bytes 2621440 | tf_op jit(solution)/shard_map/bhtu,bthd->buhd/dot_general | solution.py:128
  78.3 2.7 %copy.72 = f32[1,256,1024]{2,1,0:T(8,128)} copy(f32[1,256,1024]{1,2,0:T(8,128)} %bitcast.164) | data formatting | bytes 2097152 | tf_op jit(solution)/shard_map/reshape | solution.py:152
  84.1 2.6 %copy.60 = f32[1,256,1024]{2,1,0:T(8,128)} copy(f32[1,256,1024]{1,2,0:T(8,128)} %bitcast.162) | data formatting | bytes 2097152 | tf_op jit(solution)/shard_map/reshape | solution.py:127
  86.7 2.5 %fusion.11 = f32[8,256,128]{1,2,0:T(8,128)} fusion(bf16[256,8,128]{0,2,1:T(8,128)(2,1)} %bitcast.152, f32[8,256,256]{1,2,0:T(8,128)S(1)} %get-tuple-element.42, f32[8,256]{1,0:T(8,128)S(1)} %log_add_fusion), kind=kOutput, calls=%fused_computation.40 | convolution fusion | flops 135266304 | bytes 3678208 | tf_op jit(solution)/shard_map/bhtu,bthd->buhd/dot_general | solution.py:131
  89.2 2.7 %copy.77 = f32[1,256,1024]{2,1,0:T(8,128)} copy(f32[1,256,1024]{1,2,0:T(8,128)} %bitcast.163) | data formatting | bytes 2097152 | tf_op jit(solution)/shard_map/reshape | solution.py:153
  92.2 8.1 %reduce-scatter.2.cloned.1.call-done = bf16[2,1,64,1024]{3,2,1,0:T(8,128)(2,1)} async-done(((bf16[2,1,256,1024]{3,2,1,0:T(8,128)(2,1)}), bf16[2,1,64,1024]{3,2,1,0:T(8,128)(2,1)}) %reduce-scatter.2.cloned.1.call-update) | async-done | bytes 262160 | tf_op jit(solution)/shard_map/reduce_scatter | solution.py:137
  106.2 2.8 %copy.71 = f32[1,64,4,8,128]{4,3,2,1,0:T(8,128)} copy(f32[1,64,4,8,128]{4,2,1,3,0:T(4,128)} %bitcast.165) | data formatting | bytes 2097152 | tf_op jit(solution)/shard_map/transpose | solution.py:27
  109.0 2.5 %reshape.569 = f32[1,256,1024]{2,1,0:T(8,128)} reshape(f32[1,64,4,8,128]{4,3,2,1,0:T(8,128)} %copy.71) | data formatting | bytes 2097152 | tf_op jit(solution)/shard_map/reshape | solution.py:28
  113.1 13.1 %all-reduce.2 = (bf16[1024]{0:T(1024)(128)(2,1)S(1)}, bf16[1024]{0:T(1024)(128)(2,1)S(1)}) all-reduce(bf16[1024]{0:T(1024)(128)(2,1)S(1)} %get-tuple-element.23, bf16[1024]{0:T(1024)(128)(2,1)S(1)} %get-tuple-element.21), channel_id=1, replica_groups=mesh['seq'=4,'head'=4,'dp'=2] {'seq','dp'}, use_global_device_ids=true, to_apply=%region_16.17 | all-reduce | flops 2048 | bytes 8192 | tf_op jit(solution)/shard_map/psum | solution.py:167
  127.3 2.7 %convolution_bitcast_fusion = f32[1,64,8,512]{3,1,2,0:T(8,128)} fusion(bf16[8,512,128]{2,1,0:T(8,128)(2,1)} %param.14, bf16[64,8,128]{2,1,0:T(8,128)(2,1)S(1)} %bitcast.172), kind=kOutput, calls=%fused_computation.28 | convolution fusion | flops 67108864 | bytes 2228224 | tf_op jit(solution)/shard_map/bmhd,hcd->bmhc/dot_general | solution.py:150
  130.1 2.6 %reshape.572 = f32[1,64,8,4,128]{4,3,1,2,0:T(4,128)} reshape(f32[1,64,8,512]{3,1,2,0:T(8,128)} %convolution_bitcast_fusion) | data formatting | bytes 2097152 | tf_op jit(solution)/shard_map/reshape | solution.py:26
  132.6 2.8 %copy.76 = f32[1,64,4,8,128]{4,3,2,1,0:T(8,128)} copy(f32[1,64,4,8,128]{4,2,1,3,0:T(4,128)} %bitcast.166) | data formatting | bytes 2097152 | tf_op jit(solution)/shard_map/transpose | solution.py:27
  135.5 2.4 %reshape.573 = f32[1,256,1024]{2,1,0:T(8,128)} reshape(f32[1,64,4,8,128]{4,3,2,1,0:T(8,128)} %copy.76) | data formatting | bytes 2097152 | tf_op jit(solution)/shard_map/reshape | solution.py:28
  137.9 11.6 %all-reduce = (f32[256]{0:T(256)S(1)}, f32[256]{0:T(256)S(1)}) all-reduce(f32[256]{0:T(256)S(1)} %get-tuple-element.24, f32[256]{0:T(256)S(1)} %get-tuple-element.22), channel_id=1, replica_groups=mesh['seq'=4,'head'=4,'dp'=2] {'head'}, use_global_device_ids=true, to_apply=%region_11.12 | all-reduce | flops 512 | bytes 4096 | tf_op jit(solution)/shard_map/psum | solution.py:154
  149.5 2.5 %fusion.19 = bf16[1,256,1024]{2,1,0:T(8,128)(2,1)} fusion(bf16[1,256,1024]{2,1,0:T(8,128)(2,1)S(1)} %copy-done.12, f32[1,256,1024]{2,1,0:T(8,128)} %copy.60, f32[256]{0:T(256)S(1)} %get-tuple-element.29, f32[256]{0:T(256)S(1)} %multiply_multiply_fusion.1, f32[1024]{0:T(1024)S(1)} %copy-done.27, f32[256]{0:T(256)S(1)} %bitcast.186), kind=kLoop, calls=%fused_computation.47 | loop fusion | flops 2097152 | bytes 2104320 | tf_op jit(solution)/shard_map/convert_element_type | solution.py:160
  154.2 19.2 %all-reduce.6.cloned.1.call-done = (bf16[8,512,128]{1,2,0:T(8,128)(2,1)}, bf16[8,512,128]{2,1,0:T(8,128)(2,1)}) async-done(((bf16[8,512,128]{1,2,0:T(8,128)(2,1)}, bf16[8,512,128]{2,1,0:T(8,128)(2,1)}), (bf16[8,512,128]{1,2,0:T(8,128)(2,1)}, bf16[8,512,128]{2,1,0:T(8,128)(2,1)})) %all-reduce.6.cloned.1.call-update) | async-done | bytes 2097168 | tf_op jit(solution)/shard_map/psum | solution.py:170
  173.3 2.8 %convert_element_type.125 = f32[8,512,128]{2,1,0:T(8,128)} convert(bf16[8,512,128]{2,1,0:T(8,128)(2,1)} %get-tuple-element.36) | non-fusion elementwise | flops 524288 | bytes 3145728 | tf_op jit(solution)/shard_map/convert_element_type | solution.py:169
  (111 shorter events, 40.4 us)
Async XLA Ops:
  7.2 18.2 %copy-start = (bf16[8,512,128]{2,1,0:T(8,128)(2,1)S(1)}, bf16[8,512,128]{2,1,0:T(8,128)(2,1)}, u32[]{:S(2)}) copy-start(bf16[8,512,128]{2,1,0:T(8,128)(2,1)} %param.13) | copy-start | bytes 3145732
  7.2 17.4 %copy-start.1 = (bf16[1,256,1024]{2,1,0:T(8,128)(2,1)S(1)}, bf16[1,256,1024]{2,1,0:T(8,128)(2,1)}, u32[]{:S(2)}) copy-start(bf16[1,256,1024]{2,1,0:T(8,128)(2,1)} %param.9) | copy-start | bytes 1572868
  7.2 17.4 %copy-start.26 = (f32[1024]{0:T(1024)S(1)}, f32[1024]{0:T(1024)}, u32[]{:S(2)}) copy-start(f32[1024]{0:T(1024)} %param.12) | copy-start | bytes 12292
  7.2 93.1 %reduce-scatter.2.cloned.1.call-start = ((), (), s32[]{:S(2)}) async-start(), calls=%async_computation.1 | async-start | bytes 1310720 | tf_op jit(solution)/shard_map/reduce_scatter | solution.py:137
  25.3 14.1 %copy-start.14 = (bf16[64,8,512]{2,0,1:T(8,128)(2,1)}, bf16[64,8,512]{2,0,1:T(8,128)(2,1)S(1)}, u32[]{:S(2)}) copy-start(bf16[64,8,512]{2,0,1:T(8,128)(2,1)S(1)} %reshape.556) | copy-start | bytes 1572868
  25.3 13.1 %copy-start.11 = (bf16[1,256,1024]{2,1,0:T(8,128)(2,1)S(1)}, bf16[1,256,1024]{2,1,0:T(8,128)(2,1)}, u32[]{:S(2)}) copy-start(bf16[1,256,1024]{2,1,0:T(8,128)(2,1)} %param.8) | copy-start | bytes 1572868
  25.3 13.1 %copy-start.27 = (f32[1024]{0:T(1024)S(1)}, f32[1024]{0:T(1024)}, u32[]{:S(2)}) copy-start(f32[1024]{0:T(1024)} %param.11) | copy-start | bytes 12292
  38.4 20.3 %copy-start.18 = (bf16[1,256,1024]{1,2,0:T(8,128)(2,1)}, bf16[1,256,1024]{1,2,0:T(8,128)(2,1)S(1)}, u32[]{:S(2)}) copy-start(bf16[1,256,1024]{1,2,0:T(8,128)(2,1)S(1)} %copy.47) | copy-start | bytes 1572868
  40.7 18.1 %copy-start.3 = (bf16[1,256,1024]{1,2,0:T(8,128)(2,1)}, bf16[1,256,1024]{1,2,0:T(8,128)(2,1)S(1)}, u32[]{:S(2)}) copy-start(bf16[1,256,1024]{1,2,0:T(8,128)(2,1)S(1)} %copy.91) | copy-start | bytes 1572868
  46.1 13.2 %copy-start.16 = (bf16[64,8,512]{2,0,1:T(8,128)(2,1)}, bf16[64,8,512]{2,0,1:T(8,128)(2,1)S(1)}, u32[]{:S(2)}) copy-start(bf16[64,8,512]{2,0,1:T(8,128)(2,1)S(1)} %reshape.562) | copy-start | bytes 1572868
  65.4 2.0 %copy-start.4 = (bf16[1,256,1024]{1,2,0:T(8,128)(2,1)S(1)}, bf16[1,256,1024]{1,2,0:T(8,128)(2,1)}, u32[]{:S(2)}) copy-start(bf16[1,256,1024]{1,2,0:T(8,128)(2,1)} %copy-done.3) | copy-start | bytes 1572868
  75.2 98.2 %all-reduce.6.cloned.1.call-start = ((), (), s32[]{:S(2)}) async-start(), calls=%async_computation.2 | async-start | bytes 4194304 | tf_op jit(solution)/shard_map/psum | solution.py:170
  81.0 1.8 copy-start.7
  81.0 1.8 copy-start.19
  89.2 2.7 %copy-start.9 = (f32[1,256,1024]{2,1,0:T(8,128)S(1)}, f32[1,256,1024]{2,1,0:T(8,128)}, u32[]{:S(2)}) copy-start(f32[1,256,1024]{2,1,0:T(8,128)} %copy.60) | copy-start | bytes 3145732
  89.2 2.7 %copy-start.12 = (bf16[1,256,1024]{2,1,0:T(8,128)(2,1)S(1)}, bf16[1,256,1024]{2,1,0:T(8,128)(2,1)}, u32[]{:S(2)}) copy-start(bf16[1,256,1024]{2,1,0:T(8,128)(2,1)} %param.8) | copy-start | bytes 1572868
  89.2 12.1 %copy-start.15 = (bf16[64,8,512]{2,0,1:T(8,128)(2,1)S(1)}, bf16[64,8,512]{2,0,1:T(8,128)(2,1)}, u32[]{:S(2)}) copy-start(bf16[64,8,512]{2,0,1:T(8,128)(2,1)} %copy-done.14) | copy-start | bytes 1572868
  101.3 2.1 %copy-start.17 = (bf16[64,8,512]{2,0,1:T(8,128)(2,1)S(1)}, bf16[64,8,512]{2,0,1:T(8,128)(2,1)}, u32[]{:S(2)}) copy-start(bf16[64,8,512]{2,0,1:T(8,128)(2,1)} %copy-done.16) | copy-start | bytes 1572868
  109.0 2.5 %copy-start.2 = (bf16[1,256,1024]{2,1,0:T(8,128)(2,1)S(1)}, bf16[1,256,1024]{2,1,0:T(8,128)(2,1)}, u32[]{:S(2)}) copy-start(bf16[1,256,1024]{2,1,0:T(8,128)(2,1)} %param.9) | copy-start | bytes 1572868
  109.0 2.5 %copy-start.8 = (f32[1,256,1024]{2,1,0:T(8,128)S(1)}, f32[1,256,1024]{2,1,0:T(8,128)}, u32[]{:S(2)}) copy-start(f32[1,256,1024]{2,1,0:T(8,128)} %copy.72) | copy-start | bytes 3145732
  149.5 2.5 %copy-start.22 = (f32[1,256,1024]{2,1,0:T(8,128)S(1)}, f32[1,256,1024]{2,1,0:T(8,128)}, u32[]{:S(2)}) copy-start(f32[1,256,1024]{2,1,0:T(8,128)} %copy.77) | copy-start | bytes 3145732
  149.5 2.5 %copy-start.23 = (f32[1,256,1024]{2,1,0:T(8,128)S(1)}, f32[1,256,1024]{2,1,0:T(8,128)}, u32[]{:S(2)}) copy-start(f32[1,256,1024]{2,1,0:T(8,128)} %reshape.573) | copy-start | bytes 3145732
  149.5 3.5 %copy-start.10 = (f32[1,256,1024]{2,1,0:T(8,128)S(1)}, f32[1,256,1024]{2,1,0:T(8,128)}, u32[]{:S(2)}) copy-start(f32[1,256,1024]{2,1,0:T(8,128)} %reshape.569) | copy-start | bytes 3145732
  173.3 2.8 %copy-start.25 = (bf16[8,512,128]{1,2,0:T(8,128)(2,1)S(1)}, bf16[8,512,128]{1,2,0:T(8,128)(2,1)}, u32[]{:S(2)}) copy-start(bf16[8,512,128]{1,2,0:T(8,128)(2,1)} %get-tuple-element.35) | copy-start | bytes 3145732
  (6 other events, 6.7 us)
Sparse Core Ops, SparseCore 0:
  75.3 24.9 reduce-scatter.1
  111.6 61.7 all-reduce.5
where the time goes:
time: 186 us; the launch traced here: 185 us
  blocking collectives  59.5 us (32%)
  local copies, waits for them, and re-layouts  39.7 us (21%)
  waiting for transfers between devices  27.3 us (15%)
  matrix products  22.9 us (12%)
  other arithmetic  20.5 us (11%)
  between operations  14.5 us (8%)
    psum x1, waiting for transfers between devices, on_device(): lax.psum(squeeze_v_part.astype(jnp.bfloat16), ('seq', 'dp'))  19.2 us
    psum x1, blocking collectives, on_device(): lax.psum((jnp.sum(q_full * q_full, -1), jnp.sum(k_full * k_full, -1)), 'h...  13.5 us
    psum x1, blocking collectives, on_device(): lax.psum(gain_q_part.astype(jnp.bfloat16), ('seq', 'dp'))  13.1 us
    psum x1, blocking collectives, on_device(): lax.psum((jnp.sum(query_gain * grad_qn * q_full, -1), jnp.sum(key_gain *...  11.6 us
    all_gather x1, blocking collectives, on_device(): lax.all_gather(mem_k, 'seq', axis=1, tiled=True)  11.5 us
    all_gather x1, blocking collectives, on_device(): lax.all_gather(mem_v, 'seq', axis=1, tiled=True)  9.88 us
    reduce_scatter x1, waiting for transfers between devices, on_device(): lax.psum_scatter(stacked.astype(jnp.bfloat16), 'seq', scatter_dimension=2...  8.06 us
    unnamed x62, local copies, waits for them, and re-layouts  5.8 us
  transfers between devices with their start and end apart: 2, of which 2 were waited for; matrix products, arithmetic and copies ran while one was open for 19% of the time, Pallas kernels for 0%

commit v1 on v0

--- a/solution.py
+++ b/solution.py
@@ -1,6 +1,8 @@
 import jax
 import jax.numpy as jnp
 from jax import lax
+from jax.experimental import pallas as pl
+from jax.experimental.pallas import tpu as pltpu
 from jax.sharding import PartitionSpec as P
 
 HD = 128
@@ -29,7 +31,7 @@
     )
 
 
-def on_device(
+def on_device_any(
     query_heads, key_heads, value_heads, query_gain, key_gain, key_squeeze, value_squeeze, grad_out
 ):
     batch_size, row_count, widths = query_heads.shape
@@ -180,6 +182,561 @@
     )
 
 
+F32 = jnp.float32
+BF16 = jnp.bfloat16
+NN = (((1,), (0,)), ((), ()))
+NT = (((1,), (1,)), ((), ()))
+TN = (((0,), (0,)), ((), ()))
+
+
+def dot(a, b, dims=NN):
+    return lax.dot_general(a, b, dims, preferred_element_type=F32)
+
+
+def sds(shape, dtype):
+    return jax.ShapeDtypeStruct(shape, dtype)
+
+
+def whole_call(body, outs, *ins, cost=1_000_000):
+    return pl.pallas_call(
+        body,
+        out_shape=outs,
+        compiler_params=pltpu.CompilerParams(vmem_limit_bytes=40 * 2**20),
+        cost_estimate=pl.CostEstimate(flops=cost, bytes_accessed=cost, transcendentals=0),
+    )(*ins)
+
+
+def grid_call(body, steps, outs, in_specs, out_specs, scratch, ids, *ins, cost=1_000_000):
+    return pl.pallas_call(
+        body,
+        out_shape=outs,
+        grid_spec=pltpu.PrefetchScalarGridSpec(
+            num_scalar_prefetch=1,
+            grid=(steps,),
+            in_specs=in_specs,
+            out_specs=out_specs,
+            scratch_shapes=scratch,
+        ),
+        compiler_params=pltpu.CompilerParams(
+            vmem_limit_bytes=40 * 2**20, dimension_semantics=("arbitrary",)
+        ),
+        cost_estimate=pl.CostEstimate(flops=cost, bytes_accessed=cost, transcendentals=0),
+    )(ids, *ins)
+
+
+def row_order(rows):
+    slots = rows // KS
+    r = lax.broadcasted_iota(jnp.int32, (rows, rows), 0)
+    c = lax.broadcasted_iota(jnp.int32, (rows, rows), 1)
+    return jnp.where(c == KS * (r % slots) + r // slots, 1.0, 0.0).astype(BF16)
+
+
+def row_order_back(rows):
+    slots = rows // KS
+    r = lax.broadcasted_iota(jnp.int32, (rows, rows), 0)
+    c = lax.broadcasted_iota(jnp.int32, (rows, rows), 1)
+    return jnp.where(r == KS * (c % slots) + c // slots, 1.0, 0.0).astype(BF16)
+
+
+def causal_t(rows):
+    slots = rows // KS
+    u = lax.broadcasted_iota(jnp.int32, (rows, rows), 0)
+    t = lax.broadcasted_iota(jnp.int32, (rows, rows), 1)
+    return KS * (u % slots) + u // slots <= t
+
+
+def fold_lanes(x):
+    total = x[:, :HD]
+    for i in range(1, x.shape[1] // HD):
+        total = total + x[:, i * HD : (i + 1) * HD]
+    return total
+
+
+def lane_sum_row(x):
+    return jnp.sum(x.T, axis=0, keepdims=True)
+
+
+def as_columns(rows):
+    pad = jnp.zeros((8 - rows.shape[0], rows.shape[1]), F32)
+    return jnp.concatenate([rows, pad], axis=0).T
+
+
+def on_device(
+    query_heads, key_heads, value_heads, query_gain, key_gain, key_squeeze, value_squeeze, grad_out
+):
+    n_seq, n_head = lax.axis_size("seq"), lax.axis_size("head")
+    batch_size, rows, cols = query_heads.shape
+    heads = cols // HD
+    if batch_size != 1 or n_seq & (n_seq - 1) or heads % n_seq or lax.axis_size("dp") != 2:
+        return on_device_any(
+            query_heads,
+            key_heads,
+            value_heads,
+            query_gain,
+            key_gain,
+            key_squeeze,
+            value_squeeze,
+            grad_out,
+        )
+    slots = rows // KS
+    hp = heads // n_seq
+    wide = hp * HD
+    mem_rows = n_seq * slots
+    peers = range(1, n_seq)
+    n_mem = (n_seq - 1) * slots
+    scale = HD ** (-0.5)
+    full_width = cols * n_head
+    me = lax.axis_index("seq")
+    core = lax.axis_index("dp")
+    ids = jnp.stack([me, core]).astype(jnp.int32)
+
+    def to_peers(axis, arrays):
+        n = lax.axis_size(axis)
+        return [
+            lax.ppermute(a, axis, [(i, i ^ k) for i in range(n)])
+            for k, a in zip(range(1, n), arrays)
+        ]
+
+    def to_core(a):
+        return lax.ppermute(a, "dp", [(0, 1), (1, 0)])
+
+    q = query_heads[0]
+    k = key_heads[0]
+    v = value_heads[0]
+    do = grad_out[0]
+    qg = query_gain.reshape(1, cols)
+    kg = key_gain.reshape(1, cols)
+    full = lambda a: pl.BlockSpec(a.shape, lambda i, ids: (0,) * len(a.shape))
+    own_cols = pl.BlockSpec((rows, wide), lambda i, ids: (0, i))
+    rel_cols = pl.BlockSpec((rows, wide), lambda i, ids: (0, ids[0] ^ i))
+    rel_mem = pl.BlockSpec((slots, wide), lambda i, ids: (rows // slots + (ids[0] ^ i), 0))
+    own_mem = pl.BlockSpec((slots, wide), lambda i, ids: (rows // slots + i, 0))
+
+    def squares_body(q_ref, k_ref, ss_ref, kp_ref):
+        kp = dot(row_order(rows), k_ref[...])
+        kp_ref[...] = kp.astype(BF16)
+        qf = q_ref[...].astype(F32)
+        ss_ref[0:1, :] = lane_sum_row(fold_lanes(qf * qf))
+        ss_ref[1:2, :] = lane_sum_row(fold_lanes(kp * kp))
+
+    ss, kp = whole_call(squares_body, (sds((2, rows), F32), sds((rows, cols), BF16)), q, k)
+    ss_peers = to_peers("head", [ss] * (n_head - 1))
+
+    def pack_sends(ids_ref, rows_ref, mem_scr, sends):
+        for r, send in zip(peers, sends):
+            dest = ids_ref[0] ^ r
+            send[:rows, :] = rows_ref[:, pl.ds(pl.multiple_of(dest * wide, wide), wide)]
+            send[rows:, :] = mem_scr[...]
+
+    def compress(source, w_ref, mem_scr):
+        for h in range(heads):
+            total = None
+            for j in range(KS):
+                part = dot(
+                    source[j * slots : (j + 1) * slots, h * HD : (h + 1) * HD],
+                    w_ref[h, j * HD : (j + 1) * HD, :],
+                )
+                total = part if total is None else total + part
+            block = h // hp
+            mem_scr[
+                block * slots : (block + 1) * slots, (h % hp) * HD : (h % hp + 1) * HD
+            ] = total.astype(BF16)
+
+    def values_body(ids_ref, v_ref, w_ref, vp_ref, *rest):
+        sends, mem_scr = rest[:-1], rest[-1]
+        vp_ref[...] = dot(row_order(rows), v_ref[...]).astype(BF16)
+        compress(vp_ref, w_ref, mem_scr)
+        pack_sends(ids_ref, vp_ref, mem_scr, sends)
+
+    packet = sds((rows + mem_rows, wide), BF16)
+    smem = pl.BlockSpec(memory_space=pltpu.SMEM)
+
+    def packet_call(body, extra, scalars, *ins):
+        outs = extra + (packet,) * (n_seq - 1)
+        return pl.pallas_call(
+            body,
+            out_shape=outs,
+            in_specs=[smem] + [pl.BlockSpec(memory_space=pltpu.VMEM)] * len(ins),
+            out_specs=tuple(pl.BlockSpec(memory_space=pltpu.VMEM) for _ in outs),
+            scratch_shapes=[pltpu.VMEM((mem_rows, wide), BF16)],
+            compiler_params=pltpu.CompilerParams(vmem_limit_bytes=40 * 2**20),
+            cost_estimate=pl.CostEstimate(
+                flops=1_000_000, bytes_accessed=1_000_000, transcendentals=0
+            ),
+        )(scalars, *ins)
+
+    vp, *v_sends = packet_call(values_body, (sds((rows, cols), BF16),), ids, v, value_squeeze)
+    v_recv = to_peers("seq", v_sends)
+
+    def keys_body(ids_ref, q_ref, kp_ref, qg_ref, kg_ref, w_ref, *rest):
+        ss_refs = rest[:n_head]
+        inv_ref, qn_ref, kn_ref = rest[n_head : n_head + 3]
+        sends, mem_scr = rest[n_head + 3 : -1], rest[-1]
+        total = ss_refs[0][...]
+        for other in ss_refs[1:]:
+            total = total + other[...]
+        inv = lax.rsqrt(total / full_width + epsilon)
+        inv_ref[...] = inv
+        inv_c = as_columns(inv)
+        qn_ref[...] = (q_ref[...].astype(F32) * inv_c[:, 0:1] * qg_ref[...]).astype(BF16)
+        kn_ref[...] = (kp_ref[...].astype(F32) * inv_c[:, 1:2] * kg_ref[...]).astype(BF16)
+        compress(kn_ref, w_ref, mem_scr)
+        pack_sends(ids_ref, kn_ref, mem_scr, sends)
+
+    inv, qn, kn, *k_sends = packet_call(
+        keys_body,
+        (sds((2, rows), F32), sds((rows, cols), BF16), sds((rows, cols), BF16)),
+        ids, q, kp, qg, kg, key_squeeze, ss, *ss_peers,
+    )
+    k_recv = to_peers("seq", k_sends)
+
+    def local_body(ids_ref, qn_ref, kn_ref, vp_ref, do_ref, st_ref):
+        allowed = causal_t(rows)
+        for i in range(hp):
+            at = slice(i * HD, (i + 1) * HD)
+            s = jnp.where(allowed, dot(kn_ref[:, at], qn_ref[:, at], NT) * scale, -jnp.inf)
+            g = dot(vp_ref[:, at], do_ref[:, at], NT)
+            m = jnp.max(s, axis=0, keepdims=True)
+            p = jnp.exp(s - m)
+            st_ref[i, 0:1, :] = m
+            st_ref[i, 1:2, :] = jnp.sum(p, axis=0, keepdims=True)
+            st_ref[i, 2:3, :] = jnp.sum(p * g, axis=0, keepdims=True)
+
+    (stats,) = grid_call(
+        local_body,
+        n_seq,
+        (sds((heads, 8, rows), F32),),
+        [own_cols] * 4,
+        (pl.BlockSpec((hp, 8, rows), lambda i, ids: (i, 0, 0)),),
+        [],
+        ids, qn, kn, vp, do,
+    )
+
+    def memory_body(ids_ref, qn_ref, do_ref, st_ref, *rest):
+        mk_refs = rest[: n_seq - 1]
+        mv_refs = rest[n_seq - 1 : 2 * n_seq - 2]
+        st2_ref, ds_ref = rest[2 * n_seq - 2 : 2 * n_seq]
+        parts = rest[2 * n_seq :]
+        step = pl.program_id(0)
+        mine = ids_ref[0]
+        for i in range(hp):
+            at = slice(i * HD, (i + 1) * HD)
+            qn_h = qn_ref[:, at]
+            do_h = do_ref[:, at]
+            mk = jnp.concatenate([ref[:, at] for ref in mk_refs], axis=0)
+            mv = jnp.concatenate([ref[:, at] for ref in mv_refs], axis=0)
+            raw = dot(mk, qn_h, NT) * scale
+            s = jnp.concatenate(
+                [
+                    jnp.where((mine ^ r) < mine, raw[(r - 1) * slots : r * slots], -jnp.inf)
+                    for r in peers
+                ],
+                axis=0,
+            )
+            g = dot(mv, do_h, NT)
+            m_loc, l_loc, d_loc = st_ref[i, 0:1, :], st_ref[i, 1:2, :], st_ref[i, 2:3, :]
+            m = jnp.maximum(m_loc, jnp.max(s, axis=0, keepdims=True))
+            p = jnp.exp(s - m)
+            shrink = jnp.exp(m_loc - m)
+            mass = l_loc * shrink + jnp.sum(p, axis=0, keepdims=True)
+            inv_mass = 1.0 / mass
+            delta = (d_loc * shrink + jnp.sum(p * g, axis=0, keepdims=True)) * inv_mass
+            st2_ref[i, 0:1, :] = m
+            st2_ref[i, 1:2, :] = inv_mass
+            st2_ref[i, 2:3, :] = delta
+            attend = p * inv_mass
+            ds = (attend * (g - delta)).astype(BF16)
+            ds_ref[i] = ds
+            gk = (dot(ds, qn_h) * scale).astype(BF16)
+            gv = dot(attend.astype(BF16), do_h).astype(BF16)
+            for r in range(n_seq):
+                @pl.when(step == r)
+                def _(r=r):
+                    parts[r][0, :, at] = gk
+                    parts[r][1, :, at] = gv
+
+    part = sds((2, n_mem, wide), BF16)
+    rel_stat = pl.BlockSpec((hp, 8, rows), lambda i, ids: (ids[0] ^ i, 0, 0))
+    stats2, ds_mem, *parts = grid_call(
+        memory_body,
+        n_seq,
+        (sds((heads, 8, rows), F32), sds((heads, n_mem, rows), BF16)) + (part,) * n_seq,
+        [rel_cols, rel_cols, rel_stat] + [rel_mem] * (2 * n_seq - 2),
+        (
+            rel_stat,
+            pl.BlockSpec((hp, n_mem, rows), lambda i, ids: (ids[0] ^ i, 0, 0)),
+        )
+        + (full(part),) * n_seq,
+        [],
+        ids, qn, do, stats, *k_recv, *v_recv,
+    )
+    parts_recv = to_peers("seq", parts[1:])
+
+    def grads_body(ids_ref, q_ref, kp_ref, qn_ref, kn_ref, vp_ref, do_ref, st_ref, ds_ref, *rest):
+        mk_refs = rest[: n_seq - 1]
+        inv_ref, qg_ref, gq_ref, gk_ref, gv_ref, dq_ref, gain_q_ref, gain_k_ref, acc = rest[
+            n_seq - 1 :
+        ]
+        step = pl.program_id(0)
+        allowed = causal_t(rows)
+        inv_c = as_columns(inv_ref[...])
+
+        @pl.when(step == 0)
+        def _():
+            acc[...] = jnp.zeros_like(acc)
+
+        total = acc[...]
+        for i in range(hp):
+            at = slice(i * HD, (i + 1) * HD)
+            qn_h, kn_h, do_h = qn_ref[:, at], kn_ref[:, at], do_ref[:, at]
+            s = jnp.where(allowed, dot(kn_h, qn_h, NT) * scale, -jnp.inf)
+            g = dot(vp_ref[:, at], do_h, NT)
+            m, inv_mass, delta = st_ref[i, 0:1, :], st_ref[i, 1:2, :], st_ref[i, 2:3, :]
+            attend = jnp.exp(s - m) * inv_mass
+            ds = (attend * (g - delta)).astype(BF16)
+            mk = jnp.concatenate([ref[:, at] for ref in mk_refs], axis=0)
+            gq = scale * (dot(ds, kn_h, TN) + dot(ds_ref[i], mk, TN))
+            gk = scale * dot(ds, qn_h)
+            gq_ref[:, at] = gq
+            gk_ref[:, at] = gk
+            gv_ref[:, at] = dot(attend.astype(BF16), do_h)
+            q_h = q_ref[:, at].astype(F32)
+            k_h = kp_ref[:, at].astype(F32)
+            gq_q = gq * q_h
+            total = total + gq_q * qg_ref[:, at]
+            gain_q_ref[0, i : i + 1, :] = jnp.sum(gq_q * inv_c[:, 0:1], axis=0, keepdims=True)
+            gain_k_ref[0, i : i + 1, :] = jnp.sum(
+                gk * k_h * inv_c[:, 1:2], axis=0, keepdims=True
+            )
+        acc[...] = total
+
+        @pl.when(step == n_seq - 1)
+        def _():
+            dq_ref[...] = lane_sum_row(acc[...])
+
+    gain_rows = sds((n_seq, hp, HD), F32)
+    gain_spec = pl.BlockSpec((1, hp, HD), lambda i, ids: (i, 0, 0))
+    wide_f32 = sds((rows, cols), F32)
+    dot_row = sds((1, rows), F32)
+    gq, gk_local, gv_local, dot_q, gain_q, gain_k = grid_call(
+        grads_body,
+        n_seq,
+        (wide_f32, wide_f32, wide_f32, dot_row, gain_rows, gain_rows),
+        [own_cols] * 6
+        + [
+            pl.BlockSpec((hp, 8, rows), lambda i, ids: (i, 0, 0)),
+            pl.BlockSpec((hp, n_mem, rows), lambda i, ids: (i, 0, 0)),
+        ]
+        + [own_mem] * (n_seq - 1)
+        + [full(inv), pl.BlockSpec((1, wide), lambda i, ids: (0, i))],
+        (own_cols, own_cols, own_cols, full(dot_row), gain_spec, gain_spec),
+        [pltpu.VMEM((rows, HD), F32)],
+        ids, q, kp, qn, kn, vp, do, stats2, ds_mem, *k_recv, inv, qg,
+    )
+
+    def slots_body(*refs):
+        ins, outs = refs[:n_seq], refs[n_seq:]
+        for r in range(n_seq):
+            for tensor in range(2):
+                total = None
+                for src in range(n_seq):
+                    if src == r:
+                        continue
+                    block = (src ^ r) - 1
+                    term = ins[src][tensor, block * slots : (block + 1) * slots, :].astype(F32)
+                    total = term if total is None else total + term
+                outs[r][tensor] = total.astype(BF16)
+
+    slot_grad = sds((2, slots, wide), BF16)
+    slot_grads = whole_call(slots_body, (slot_grad,) * n_seq, parts[0], *parts_recv)
+    slots_recv = to_peers("seq", slot_grads[1:])
+
+    def weights_body(ids_ref, kn_ref, vp_ref, *rest):
+        gm = rest[:n_seq]
+        k_refs = rest[n_seq : 2 * n_seq - 1]
+        v_refs = rest[2 * n_seq - 1 : 3 * n_seq - 2]
+        same_ref, other_ref = rest[3 * n_seq - 2 :]
+        here = pl.ds(pl.multiple_of(ids_ref[0] * wide, wide), wide)
+        own = (kn_ref[:, here], vp_ref[:, here])
+        core_id = ids_ref[1]
+        for i in range(hp):
+            at = slice(i * HD, (i + 1) * HD)
+            for j in range(KS):
+                span = slice(j * slots, (j + 1) * slots)
+                found = []
+                for tensor, refs in ((0, k_refs), (1, v_refs)):
+                    lhs = jnp.concatenate(
+                        [own[tensor][span, at]] + [ref[span, at] for ref in refs], axis=0
+                    )
+                    rhs = jnp.concatenate([ref[tensor, :, at] for ref in gm], axis=0)
+                    found.append(dot(lhs, rhs, TN))
+                to = slice((i * KS + j) * HD, (i * KS + j + 1) * HD)
+                first = core_id == 0
+                same_ref[to, :] = jnp.where(first, found[0], found[1])
+                other_ref[to, :] = jnp.where(first, found[1], found[0]).astype(BF16)
+
+    span_rows = hp * KS * HD
+    packet_rows = sds((rows, wide), BF16)
+    head_rows = pl.BlockSpec((rows, wide), lambda i, ids: (0, 0))
+    w_same, w_other = grid_call(
+        weights_body,
+        1,
+        (sds((span_rows, HD), F32), sds((span_rows, HD), BF16)),
+        [full(kn), full(vp)] + [full(slot_grad)] * n_seq + [head_rows] * (2 * n_seq - 2),
+        (full(sds((span_rows, HD), F32)), full(sds((span_rows, HD), BF16))),
+        [],
+        ids, kn, vp, *slot_grads, *k_recv, *v_recv,
+    )
+    w_recv = to_core(w_other)
+
+    def chunk_body(a_ref, b_ref, gq_ref, gk_ref, out_ref):
+        out_ref[:span_rows, :] = (a_ref[...] + b_ref[...].astype(F32)).astype(BF16)
+        rows_q = [gq_ref[i] for i in range(n_seq)]
+        rows_k = [gk_ref[i] for i in range(n_seq)]
+        out_ref[span_rows:, :] = jnp.concatenate(rows_q + rows_k, axis=0).astype(BF16)
+
+    chunk_shape = sds((span_rows + 2 * heads, HD), BF16)
+    chunk = whole_call(chunk_body, chunk_shape, w_same, w_recv, gain_q, gain_k)
+    chunks = [chunk] + to_peers("seq", [chunk] * (n_seq - 1))
+    others = [to_core(c) for c in chunks]
+
+    def back_body(ids_ref, gk_ref, gv_ref, kp_ref, wk_ref, wv_ref, kg_ref, dq_ref, *rest):
+        gm = rest[:n_seq]
+        value_ref, gkn_ref, dots_ref, acc = rest[n_seq:]
+        step = pl.program_id(0)
+        unorder = row_order_back(rows)
+
+        @pl.when(step == 0)
+        def _():
+            acc[...] = jnp.zeros_like(acc)
+
+        total = acc[...]
+        mine = gm[0][...]
+        for r in peers:
+            mine = jnp.where(step == r, gm[r][...], mine)
+        for i in range(hp):
+            at = slice(i * HD, (i + 1) * HD)
+            sides = []
+            for tensor, w_ref in ((0, wk_ref), (1, wv_ref)):
+                spread = dot(mine[tensor][:, at], w_ref[i], NT)
+                sides.append(
+                    jnp.concatenate(
+                        [spread[:, j * HD : (j + 1) * HD] for j in range(KS)], axis=0
+                    )
+                )
+            gkn = gk_ref[:, at] + sides[0]
+            gkn_ref[:, at] = gkn
+            total = total + gkn * kp_ref[:, at].astype(F32) * kg_ref[:, at]
+            value = (gv_ref[:, at] + sides[1]).astype(BF16)
+            value_ref[:, at] = dot(unorder, value).astype(BF16)
+        acc[...] = total
+
+        @pl.when(step == n_seq - 1)
+        def _():
+            dots_ref[0:1, :] = dq_ref[...]
+            dots_ref[1:2, :] = lane_sum_row(acc[...])
+
+    rel_w = pl.BlockSpec((hp, KS * HD, HD), lambda i, ids: (ids[0] ^ i, 0, 0))
+    two_rows = sds((2, rows), F32)
+    grad_value, gkn, dots = grid_call(
+        back_body,
+        n_seq,
+        (sds((rows, cols), BF16), wide_f32, two_rows),
+        [rel_cols, rel_cols, rel_cols, rel_w, rel_w]
+        + [pl.BlockSpec((1, wide), lambda i, ids: (0, ids[0] ^ i)), full(dot_q)]
+        + [full(slot_grad)] * n_seq,
+        (rel_cols, rel_cols, full(two_rows)),
+        [pltpu.VMEM((rows, HD), F32)],
+        ids, gk_local, gv_local, kp, key_squeeze, value_squeeze, kg, dot_q,
+        slot_grads[0], *slots_recv,
+    )
+    dots_peers = to_peers("head", [dots] * (n_head - 1))
+
+    def norms_body(ids_ref, q_ref, kp_ref, gq_ref, gkn_ref, qg_ref, kg_ref, inv_ref, *rest):
+        dot_refs = rest[:n_head]
+        out_q, out_k = rest[n_head:]
+        total = dot_refs[0][...]
+        for other in dot_refs[1:]:
+            total = total + other[...]
+        inv_rows = inv_ref[...]
+        inv_c = as_columns(inv_rows)
+        pull = as_columns(inv_rows * inv_rows * inv_rows * total / full_width)
+        out_q[...] = (
+            inv_c[:, 0:1] * qg_ref[...] * gq_ref[...] - q_ref[...].astype(F32) * pull[:, 0:1]
+        ).astype(BF16)
+        grad_k = (
+            inv_c[:, 1:2] * kg_ref[...] * gkn_ref[...] - kp_ref[...].astype(F32) * pull[:, 1:2]
+        ).astype(BF16)
+        out_k[...] = dot(row_order_back(rows), grad_k).astype(BF16)
+
+    gain_cols = pl.BlockSpec((1, wide), lambda i, ids: (0, i))
+    grad_query, grad_key = grid_call(
+        norms_body,
+        n_seq,
+        (sds((rows, cols), BF16), sds((rows, cols), BF16)),
+        [own_cols] * 4 + [gain_cols] * 2 + [full(inv)] + [full(dots)] * n_head,
+        (own_cols, own_cols),
+        [],
+        ids, q, kp, gq, gkn, qg, kg, inv, dots, *dots_peers,
+    )
+
+    def finish_body(ids_ref, kg_ref, wk_ref, *rest):
+        same, other = rest[:n_seq], rest[n_seq : 2 * n_seq]
+        gks_ref, gvs_ref, gain_ref = rest[2 * n_seq :]
+        step = pl.program_id(0)
+        first = ids_ref[1] == 0
+
+        @pl.when(step == 0)
+        def _():
+            total = None
+            for ref in rest[: 2 * n_seq]:
+                term = ref[span_rows:, :].astype(F32)
+                total = term if total is None else total + term
+            gain_ref[...] = total
+
+        for r in range(n_seq):
+            @pl.when(step == r)
+            def _(r=r):
+                for i in range(hp):
+                    span = slice(i * KS * HD, (i + 1) * KS * HD)
+                    a = same[r][span, :].astype(F32)
+                    b = other[r][span, :].astype(F32)
+                    gks_ref[i] = jnp.where(first, a, b)
+                    gvs_ref[i] = jnp.where(first, b, a)
+
+        for i in range(hp):
+            prod = gks_ref[i] * wk_ref[i].astype(F32)
+            total = prod[:HD]
+            for j in range(1, KS):
+                total = total + prod[j * HD : (j + 1) * HD]
+            row = lane_sum_row(total)
+            head = (ids_ref[0] ^ step) * hp + i
+            at = pl.ds(heads + head, 1)
+            gain_ref[at, :] = gain_ref[at, :] + row / kg_ref[:, i * HD : (i + 1) * HD]
+
+    kernel_out = sds((heads, KS * HD, HD), F32)
+    gains_shape = sds((2 * heads, HD), F32)
+    gks, gvs, gains = grid_call(
+        finish_body,
+        n_seq,
+        (kernel_out, kernel_out, gains_shape),
+        [pl.BlockSpec((1, wide), lambda i, ids: (0, ids[0] ^ i)), rel_w]
+        + [full(chunk_shape)] * (2 * n_seq),
+        (rel_w, rel_w, full(gains_shape)),
+        [],
+        ids, kg, key_squeeze, *chunks, *others,
+    )
+    return (
+        grad_query[None],
+        grad_key[None],
+        grad_value[None],
+        gains[:heads].reshape(cols),
+        gains[heads:].reshape(cols),
+        gks,
+        gvs,
+    )
+
+
 def solution(mesh):
     placed = (
         P("dp", "seq", "head"),

time: 186 us -> 116 us (0.62)
  blocking collectives: 59.5 us -> 0 us
  local copies, waits for them, and re-layouts: 39.7 us -> 5.05 us
  starting transfers between devices: 0.26 us -> 30.1 us
  Pallas kernels: 0 us -> 28.6 us
  waiting for transfers between devices: 27.3 us -> 50.9 us
  matrix products: 22.9 us -> 0 us
  other arithmetic: 20.5 us -> 0.08 us
  between operations: 14.5 us -> 0.79 us
    ppermute x0 -> x26, waiting for transfers between devices: none -> 50.9 us  [the longest x21 50.9 us: to_peers(): lax.ppermute(a, axis, [(i, i ^ k) for i in range(n)])]
    psum x3 -> x0, blocking collectives: 38.1 us -> none  [the longest x1 13.5 us: on_device(): lax.psum((jnp.sum(q_full * q_full, -1), jnp.sum(k_full * k_full, -1)), 'h...]
    ppermute x0 -> x26, starting transfers between devices: none -> 30.1 us  [the longest x21 29.6 us: to_peers(): lax.ppermute(a, axis, [(i, i ^ k) for i in range(n)])]
    pallas_call x0 -> x12, Pallas kernels: none -> 28.6 us  [the longest x7 25.4 us: grid_call(): pl.pallas_call(body, out_shape=outs, grid_spec=pltpu.PrefetchScalarGridSp...]
    dot_general x16 -> x0, matrix products: 22.9 us -> none  [the longest x1 2.86 us: on_device(): jnp.einsum('bhtu,bthd->buhd', d_loc, queries, preferred_element_type=jnp....]
    all_gather x2 -> x0, blocking collectives: 21.4 us -> none  [the longest x1 11.5 us: on_device(): lax.all_gather(mem_k, 'seq', axis=1, tiled=True)]
    psum x1 -> x0, waiting for transfers between devices: 19.2 us -> none  [on_device(): lax.psum(squeeze_v_part.astype(jnp.bfloat16), ('seq', 'dp'))]
    reshape x9 -> x1, local copies, waits for them, and re-layouts: 16.8 us -> 0.6 us  [on_device(): gains[heads:].reshape(cols)]
  transfers between devices with their start and end apart: 2 -> 26, of which waited for: 2 -> 14; matrix products, arithmetic and copies ran while one was open for 19% -> 0% of each run, Pallas kernels for 0% -> 16%
where the time goes in v1:
time: 116 us
  waiting for transfers between devices  50.9 us (44%)
  starting transfers between devices  30.1 us (26%)
  Pallas kernels  28.6 us (25%)
  local copies, waits for them, and re-layouts  5.05 us (4%)
    ppermute x21, waiting for transfers between devices, to_peers(): lax.ppermute(a, axis, [(i, i ^ k) for i in range(n)])  50.9 us
    ppermute x21, starting transfers between devices, to_peers(): lax.ppermute(a, axis, [(i, i ^ k) for i in range(n)])  29.6 us
    pallas_call x7, Pallas kernels, grid_call(): pl.pallas_call(body, out_shape=outs, grid_spec=pltpu.PrefetchScalarGridSp...  25.4 us
    unnamed x20, local copies, waits for them, and re-layouts  4.45 us
    pallas_call x2, Pallas kernels, packet_call(): pl.pallas_call(body, out_shape=outs, in_specs=[smem] + [pl.BlockSpec(memo...  2.61 us
  transfers between devices with their start and end apart: 26, of which 14 were waited for; matrix products, arithmetic and copies ran while one was open for 0% of the time, Pallas kernels for 16%

profile of v1, /device:TPU:0, one launch (start us, length us, event | category | flops | bytes accessed | tf_op | source)
XLA Modules:
  0.0 115.6 jit_solution(1327504301337813676)
XLA Ops:
  4.3 3.0 %collective-permute-start.6 = (bf16[512,256]{1,0:T(8,128)(2,1)S(1)}, bf16[512,256]{1,0:T(8,128)(2,1)S(1)}, u32[]{:S(2)}, u32[]{:S(2)}) collective-permute-start(bf16[512,256]{1,0:T(8,128)(2,1)S(1)} %get-tuple-element.53), channel_id=1, source_target_pairs={{0,8},{8,0},{16,24},{24,16},{1,9},{9,1},{17,25},{25,17},{2,10},{10... | collective-permute-start | bytes 786440 | tf_op jit(solution)/shard_map/ppermute | solution.py:296
  9.8 3.7 %collective-permute-start.2 = (f32[2,256]{1,0:T(2,128)S(1)}, f32[2,256]{1,0:T(2,128)S(1)}, u32[]{:S(2)}, u32[]{:S(2)}) collective-permute-start(f32[2,256]{1,0:T(2,128)S(1)} %get-tuple-element.46.rest_0_), channel_id=1, source_target_pairs={{0,6},{2,4},{4,2},{6,0},{1,7},{3,5},{5,3},{7,1},{8,14},{10,12},{12... | collective-permute-start | bytes 6152 | tf_op jit(solution)/shard_map/ppermute | solution.py:296
  22.9 2.5 %shard_map.138.st_ref = f32[8,8,256]{2,1,0:T(8,128)S(1)} custom-call(s32[2]{0:T(128)S(1)} %pad_add_fusion.ids_ref, bf16[256,1024]{1,0:T(8,128)(2,1)S(1)} %get-tuple-element.47.qn_ref, bf16[256,1024]{1,0:T(8,128)(2,1)S(1)} %get-tuple-element.48.kn_ref, bf16[256,1024]{1,0:T(8,128)(2,1)S(1)} %get-tuple-element.49.vp_ref, bf16[256,1024]{1,0:T(8,128)(2,1)S(1)} %bitcast.19), custom_call_target="tpu_custom_call" | custom-call | flops 1000000 | bytes 1000000 | tf_op jit(solution)/shard_map/pallas_call | solution.py:210
  25.5 6.1 %collective-permute-done.7.rest_4_.rest_8_ = bf16[512,256]{1,0:T(8,128)(2,1)S(1)} collective-permute-done((bf16[512,256]{1,0:T(8,128)(2,1)S(1)}, bf16[512,256]{1,0:T(8,128)(2,1)S(1)}, u32[]{:S(2)}, u32[]{:S(2)}) %collective-permute-start.7) | collective-permute-done | bytes 262176 | tf_op jit(solution)/shard_map/ppermute | solution.py:296
  31.6 6.6 %collective-permute-done.4.rest_1_.rest_5_ = bf16[512,256]{1,0:T(8,128)(2,1)S(1)} collective-permute-done((bf16[512,256]{1,0:T(8,128)(2,1)S(1)}, bf16[512,256]{1,0:T(8,128)(2,1)S(1)}, u32[]{:S(2)}, u32[]{:S(2)}) %collective-permute-start.4) | collective-permute-done | bytes 262176 | tf_op jit(solution)/shard_map/ppermute | solution.py:296
  38.2 4.8 %shard_map.139 = (f32[8,8,256]{2,1,0:T(8,128)S(1)}, bf16[8,192,256]{2,1,0:T(8,128)(2,1)S(1)}, bf16[2,192,256]{2,1,0:T(8,128)(2,1)S(1)}, bf16[2,192,256]{2,1,0:T(...) custom-call(s32[2]{0:T(128)S(1)} %pad_add_fusion.ids_ref, ...), custom_call_target="tpu_custom_call" | custom-call | flops 1000000 | bytes 1000000 | tf_op jit(solution)/shard_map/pallas_call | solution.py:210
  46.5 3.4 %collective-permute-done.9.refs_1_ = bf16[2,192,256]{2,1,0:T(8,128)(2,1)S(1)} collective-permute-done((bf16[2,192,256]{2,1,0:T(8,128)(2,1)S(1)}, bf16[2,192,256]{2,1,0:T(8,128)(2,1)S(1)}, u32[]{:S(2)}, u32[]{:S(2)}) %collective-permute-start.9) | collective-permute-done | bytes 196640 | tf_op jit(solution)/shard_map/ppermute | solution.py:296
  49.9 1.9 %collective-permute-done.10.refs_2_ = bf16[2,192,256]{2,1,0:T(8,128)(2,1)S(1)} collective-permute-done((bf16[2,192,256]{2,1,0:T(8,128)(2,1)S(1)}, bf16[2,192,256]{2,1,0:T(8,128)(2,1)S(1)}, u32[]{:S(2)}, u32[]{:S(2)}) %collective-permute-start.10) | collective-permute-done | bytes 196640 | tf_op jit(solution)/shard_map/ppermute | solution.py:296
  51.8 1.7 %collective-permute-done.11.refs_3_ = bf16[2,192,256]{2,1,0:T(8,128)(2,1)S(1)} collective-permute-done((bf16[2,192,256]{2,1,0:T(8,128)(2,1)S(1)}, bf16[2,192,256]{2,1,0:T(8,128)(2,1)S(1)}, u32[]{:S(2)}, u32[]{:S(2)}) %collective-permute-start.11) | collective-permute-done | bytes 196640 | tf_op jit(solution)/shard_map/ppermute | solution.py:296
  54.7 5.8 %shard_map.140 = (f32[256,1024]{1,0:T(8,128)S(1)}, f32[256,1024]{1,0:T(8,128)S(1)}, f32[256,1024]{1,0:T(8,128)S(1)}, f32[1,256]{1,0:T(1,128)S(1)}, f32[4,2,128]{2,1,0:T(2,128)S(1)}, /*index=5*/f32[4,2,128]{2,1,0:T(2,128)S(1)}) custom-call(s32[2]{0:T(128)S(1)} %pad_add_fusion.ids_ref, bf16[256,1024]{1,0:T(8,128)(2,1)S(1)} %bitcast.17, ...), custom_call_target="tpu_custom_call" | custom-call | flops 1000000 | bytes 1000000 | tf_op jit(solution)/shard_map/pallas_call | solution.py:210
  60.6 1.8 %collective-permute-start.21 = (bf16[1040,128]{1,0:T(8,128)(2,1)S(1)}, bf16[1040,128]{1,0:T(8,128)(2,1)S(1)}, u32[]{:S(2)}, u32[]{:S(2)}) collective-permute-start(bf16[1040,128]{1,0:T(8,128)(2,1)S(1)} %shard_map.145.rest_0_), channel_id=1, source_target_pairs={{0,24},{8,16},{16,8},{24,0},{1,25},{9,17},{17,9},{25,1},{2,26},{10... | collective-permute-start | bytes 798728 | tf_op jit(solution)/shard_map/ppermute | solution.py:296
  64.1 6.6 %collective-permute-done.21.rest_3_ = bf16[1040,128]{1,0:T(8,128)(2,1)S(1)} collective-permute-done((bf16[1040,128]{1,0:T(8,128)(2,1)S(1)}, bf16[1040,128]{1,0:T(8,128)(2,1)S(1)}, u32[]{:S(2)}, u32[]{:S(2)}) %collective-permute-start.21) | collective-permute-done | bytes 266272 | tf_op jit(solution)/shard_map/ppermute | solution.py:296
  70.8 5.2 %collective-permute-done.20.rest_2_ = bf16[1040,128]{1,0:T(8,128)(2,1)S(1)} collective-permute-done((bf16[1040,128]{1,0:T(8,128)(2,1)S(1)}, bf16[1040,128]{1,0:T(8,128)(2,1)S(1)}, u32[]{:S(2)}, u32[]{:S(2)}) %collective-permute-start.20) | collective-permute-done | bytes 266272 | tf_op jit(solution)/shard_map/ppermute | solution.py:296
  77.6 3.2 %collective-permute-done.12.rest_1_ = bf16[2,64,256]{2,1,0:T(8,128)(2,1)S(1)} collective-permute-done((bf16[2,64,256]{2,1,0:T(8,128)(2,1)S(1)}, bf16[2,64,256]{2,1,0:T(8,128)(2,1)S(1)}, u32[]{:S(2)}, u32[]{:S(2)}) %collective-permute-start.12) | collective-permute-done | bytes 65568 | tf_op jit(solution)/shard_map/ppermute | solution.py:296
  81.6 3.5 %collective-permute-done.13.rest_2_ = bf16[2,64,256]{2,1,0:T(8,128)(2,1)S(1)} collective-permute-done((bf16[2,64,256]{2,1,0:T(8,128)(2,1)S(1)}, bf16[2,64,256]{2,1,0:T(8,128)(2,1)S(1)}, u32[]{:S(2)}, u32[]{:S(2)}) %collective-permute-start.13) | collective-permute-done | bytes 65568 | tf_op jit(solution)/shard_map/ppermute | solution.py:296
  85.0 1.7 %collective-permute-start.14 = (bf16[2,64,256]{2,1,0:T(8,128)(2,1)S(1)}, bf16[2,64,256]{2,1,0:T(8,128)(2,1)S(1)}, u32[]{:S(2)}, u32[]{:S(2)}) collective-permute-start(bf16[2,64,256]{2,1,0:T(8,128)(2,1)S(1)} %get-tuple-element.70.rest_3_), channel_id=1, source_target_pairs={{0,24},{8,16},{16,8},{24,0},{1,25},{9,17},{17,9},{25,1},{2,26},{10... | collective-permute-start | bytes 196616 | tf_op jit(solution)/shard_map/ppermute | solution.py:296
  86.8 3.4 %collective-permute-done.14.rest_3_ = bf16[2,64,256]{2,1,0:T(8,128)(2,1)S(1)} collective-permute-done((bf16[2,64,256]{2,1,0:T(8,128)(2,1)S(1)}, bf16[2,64,256]{2,1,0:T(8,128)(2,1)S(1)}, u32[]{:S(2)}, u32[]{:S(2)}) %collective-permute-start.14) | collective-permute-done | bytes 65568 | tf_op jit(solution)/shard_map/ppermute | solution.py:296
  90.2 4.5 %shard_map.142 = (bf16[256,1024]{1,0:T(8,128)(2,1)}, f32[256,1024]{1,0:T(8,128)S(1)}, f32[2,256]{1,0:T(2,128)S(1)}) custom-call(s32[2]{0:T(128)S(1)} %pad_add_fusion.ids_ref, f32[256,1024]{1,0:T(8,128)S(1)} %get-tuple-element.60.gk_ref, f32[256,1024]{1,0:T(8,128)S(1)} %get-tuple-element.61.gv_ref, bf16[256,1024]{1,0:T(8,128)(2,1)S(1)} %get-tuple-element.45.kp_ref, ...), custom_call_target="tpu_custom_call" | custom-call | flops 1000000 | bytes 1000000 | tf_op jit(solution)/shard_map/pallas_call | solution.py:210
  94.8 3.4 %collective-permute-start.17 = (f32[2,256]{1,0:T(2,128)S(1)}, f32[2,256]{1,0:T(2,128)S(1)}, u32[]{:S(2)}, u32[]{:S(2)}) collective-permute-start(f32[2,256]{1,0:T(2,128)S(1)} %get-tuple-element.72.rest_0_), channel_id=1, source_target_pairs={{0,6},{2,4},{4,2},{6,0},{1,7},{3,5},{5,3},{7,1},{8,14},{10,12},{12... | collective-permute-start | bytes 6152 | tf_op jit(solution)/shard_map/ppermute | solution.py:296
  98.1 2.0 %collective-permute-done.17.rest_3_ = f32[2,256]{1,0:T(2,128)S(1)} collective-permute-done((f32[2,256]{1,0:T(2,128)S(1)}, f32[2,256]{1,0:T(2,128)S(1)}, u32[]{:S(2)}, u32[]{:S(2)}) %collective-permute-start.17) | collective-permute-done | bytes 2080 | tf_op jit(solution)/shard_map/ppermute | solution.py:296
  101.0 3.6 %collective-permute-done.16.rest_2_ = f32[2,256]{1,0:T(2,128)S(1)} collective-permute-done((f32[2,256]{1,0:T(2,128)S(1)}, f32[2,256]{1,0:T(2,128)S(1)}, u32[]{:S(2)}, u32[]{:S(2)}) %collective-permute-start.16) | collective-permute-done | bytes 2080 | tf_op jit(solution)/shard_map/ppermute | solution.py:296
  105.7 2.5 %collective-permute-done.15.rest_1_ = f32[2,256]{1,0:T(2,128)S(1)} collective-permute-done((f32[2,256]{1,0:T(2,128)S(1)}, f32[2,256]{1,0:T(2,128)S(1)}, u32[]{:S(2)}, u32[]{:S(2)}) %collective-permute-start.15) | collective-permute-done | bytes 2080 | tf_op jit(solution)/shard_map/ppermute | solution.py:296
  108.2 3.5 %shard_map.143 = (bf16[256,1024]{1,0:T(8,128)(2,1)}, bf16[256,1024]{1,0:T(8,128)(2,1)}) custom-call(s32[2]{0:T(128)S(1)} %pad_add_fusion.ids_ref, bf16[256,1024]{1,0:T(8,128)(2,1)S(1)} %bitcast.18, bf16[256,1024]{1,0:T(8,128)(2,1)S(1)} %get-tuple-element.45.kp_ref, f32[256,1024]{1,0:T(8,128)S(1)} %get-tuple-element.59.gq_ref, ...), custom_call_target="tpu_custom_call" | custom-call | flops 1000000 | bytes 1000000 | tf_op jit(solution)/shard_map/pallas_call | solution.py:210
  111.8 3.2 %shard_map.146 = (f32[8,512,128]{2,1,0:T(8,128)}, f32[8,512,128]{2,1,0:T(8,128)}, f32[16,128]{1,0:T(8,128)S(1)}) custom-call(s32[2]{0:T(128)S(1)} %pad_add_fusion.ids_ref, f32[1,1024]{1,0:T(1,128)S(1)} %bitcast.27, bf16[8,512,128]{2,1,0:T(8,128)(2,1)S(1)} %copy-done, bf16[1040,128]{1,0:T(8,128)(2,1)S(1)} %shard_map.145.rest_0_, ...), custom_call_target="tpu_custom_call" | custom-call | flops 1000000 | bytes 1000000 | tf_op jit(solution)/shard_map/pallas_call | solution.py:210
  (62 shorter events, 27.1 us)
Async XLA Ops:
  4.3 17.2 %collective-permute-start.6 = (bf16[512,256]{1,0:T(8,128)(2,1)S(1)}, bf16[512,256]{1,0:T(8,128)(2,1)S(1)}, u32[]{:S(2)}, u32[]{:S(2)}) collective-permute-start(bf16[512,256]{1,0:T(8,128)(2,1)S(1)} %get-tuple-element.53), channel_id=1, source_target_pairs={{0,8},{8,0},{16,24},{24,16},{1,9},{9,1},{17,25},{25,17},{2,10},{10... | collective-permute-start | bytes 786440 | tf_op jit(solution)/shard_map/ppermute | solution.py:296
  9.8 6.0 %collective-permute-start.2 = (f32[2,256]{1,0:T(2,128)S(1)}, f32[2,256]{1,0:T(2,128)S(1)}, u32[]{:S(2)}, u32[]{:S(2)}) collective-permute-start(f32[2,256]{1,0:T(2,128)S(1)} %get-tuple-element.46.rest_0_), channel_id=1, source_target_pairs={{0,6},{2,4},{4,2},{6,0},{1,7},{3,5},{5,3},{7,1},{8,14},{10,12},{12... | collective-permute-start | bytes 6152 | tf_op jit(solution)/shard_map/ppermute | solution.py:296
  13.5 4.5 %collective-permute-start.1 = (f32[2,256]{1,0:T(2,128)S(1)}, f32[2,256]{1,0:T(2,128)S(1)}, u32[]{:S(2)}, u32[]{:S(2)}) collective-permute-start(f32[2,256]{1,0:T(2,128)S(1)} %get-tuple-element.46.rest_0_), channel_id=1, source_target_pairs={{0,4},{2,6},{4,0},{6,2},{1,5},{3,7},{5,1},{7,3},{8,12},{10,14},{12... | collective-permute-start | bytes 6152 | tf_op jit(solution)/shard_map/ppermute | solution.py:296
  13.5 4.5 %collective-permute-start = (f32[2,256]{1,0:T(2,128)S(1)}, f32[2,256]{1,0:T(2,128)S(1)}, u32[]{:S(2)}, u32[]{:S(2)}) collective-permute-start(f32[2,256]{1,0:T(2,128)S(1)} %get-tuple-element.46.rest_0_), channel_id=1, source_target_pairs={{0,2},{2,0},{4,6},{6,4},{1,3},{3,1},{5,7},{7,5},{8,10},{10,8},{12,... | collective-permute-start | bytes 6152 | tf_op jit(solution)/shard_map/ppermute | solution.py:296
  14.3 17.3 %collective-permute-start.7 = (bf16[512,256]{1,0:T(8,128)(2,1)S(1)}, bf16[512,256]{1,0:T(8,128)(2,1)S(1)}, u32[]{:S(2)}, u32[]{:S(2)}) collective-permute-start(bf16[512,256]{1,0:T(8,128)(2,1)S(1)} %get-tuple-element.54), channel_id=1, source_target_pairs={{0,16},{8,24},{16,0},{24,8},{1,17},{9,25},{17,1},{25,9},{2,18},{10... | collective-permute-start | bytes 786440 | tf_op jit(solution)/shard_map/ppermute | solution.py:296
  15.8 15.8 %collective-permute-start.8 = (bf16[512,256]{1,0:T(8,128)(2,1)S(1)}, bf16[512,256]{1,0:T(8,128)(2,1)S(1)}, u32[]{:S(2)}, u32[]{:S(2)}) collective-permute-start(bf16[512,256]{1,0:T(8,128)(2,1)S(1)} %get-tuple-element.55), channel_id=1, source_target_pairs={{0,24},{8,16},{16,8},{24,0},{1,25},{9,17},{17,9},{25,1},{2,26},{10... | collective-permute-start | bytes 786440 | tf_op jit(solution)/shard_map/ppermute | solution.py:296
  19.4 12.2 %collective-permute-start.3 = (bf16[512,256]{1,0:T(8,128)(2,1)S(1)}, bf16[512,256]{1,0:T(8,128)(2,1)S(1)}, u32[]{:S(2)}, u32[]{:S(2)}) collective-permute-start(bf16[512,256]{1,0:T(8,128)(2,1)S(1)} %get-tuple-element.50), channel_id=1, source_target_pairs={{0,8},{8,0},{16,24},{24,16},{1,9},{9,1},{17,25},{25,17},{2,10},{10... | collective-permute-start | bytes 786440 | tf_op jit(solution)/shard_map/ppermute | solution.py:296
  20.0 18.2 %collective-permute-start.4 = (bf16[512,256]{1,0:T(8,128)(2,1)S(1)}, bf16[512,256]{1,0:T(8,128)(2,1)S(1)}, u32[]{:S(2)}, u32[]{:S(2)}) collective-permute-start(bf16[512,256]{1,0:T(8,128)(2,1)S(1)} %get-tuple-element.51), channel_id=1, source_target_pairs={{0,16},{8,24},{16,0},{24,8},{1,17},{9,25},{17,1},{25,9},{2,18},{10... | collective-permute-start | bytes 786440 | tf_op jit(solution)/shard_map/ppermute | solution.py:296
  21.5 16.7 %collective-permute-start.5 = (bf16[512,256]{1,0:T(8,128)(2,1)S(1)}, bf16[512,256]{1,0:T(8,128)(2,1)S(1)}, u32[]{:S(2)}, u32[]{:S(2)}) collective-permute-start(bf16[512,256]{1,0:T(8,128)(2,1)S(1)} %get-tuple-element.52), channel_id=1, source_target_pairs={{0,24},{8,16},{16,8},{24,0},{1,25},{9,17},{17,9},{25,1},{2,26},{10... | collective-permute-start | bytes 786440 | tf_op jit(solution)/shard_map/ppermute | solution.py:296
  43.0 7.0 %collective-permute-start.9 = (bf16[2,192,256]{2,1,0:T(8,128)(2,1)S(1)}, bf16[2,192,256]{2,1,0:T(8,128)(2,1)S(1)}, u32[]{:S(2)}, u32[]{:S(2)}) collective-permute-start(bf16[2,192,256]{2,1,0:T(8,128)(2,1)S(1)} %get-tuple-element.64), channel_id=1, source_target_pairs={{0,8},{8,0},{16,24},{24,16},{1,9},{9,1},{17,25},{25,17},{2,10},{10... | collective-permute-start | bytes 589832 | tf_op jit(solution)/shard_map/ppermute | solution.py:296
  43.6 8.2 %collective-permute-start.10 = (bf16[2,192,256]{2,1,0:T(8,128)(2,1)S(1)}, bf16[2,192,256]{2,1,0:T(8,128)(2,1)S(1)}, u32[]{:S(2)}, u32[]{:S(2)}) collective-permute-start(bf16[2,192,256]{2,1,0:T(8,128)(2,1)S(1)} %get-tuple-element.65), channel_id=1, source_target_pairs={{0,16},{8,24},{16,0},{24,8},{1,17},{9,25},{17,1},{25,9},{2,18},{10... | collective-permute-start | bytes 589832 | tf_op jit(solution)/shard_map/ppermute | solution.py:296
  45.1 8.4 %collective-permute-start.11 = (bf16[2,192,256]{2,1,0:T(8,128)(2,1)S(1)}, bf16[2,192,256]{2,1,0:T(8,128)(2,1)S(1)}, u32[]{:S(2)}, u32[]{:S(2)}) collective-permute-start(bf16[2,192,256]{2,1,0:T(8,128)(2,1)S(1)} %get-tuple-element.66), channel_id=1, source_target_pairs={{0,24},{8,16},{16,8},{24,0},{1,25},{9,17},{17,9},{25,1},{2,26},{10... | collective-permute-start | bytes 589832 | tf_op jit(solution)/shard_map/ppermute | solution.py:296
  54.6 5.9 %collective-permute-start.18 = (bf16[1024,128]{1,0:T(8,128)(2,1)S(1)}, bf16[1024,128]{1,0:T(8,128)(2,1)S(1)}, u32[]{:S(2)}, u32[]{:S(2)}) collective-permute-start(bf16[1024,128]{1,0:T(8,128)(2,1)S(1)} %get-tuple-element.77), channel_id=1, source_target_pairs={{0,1},{1,0},{2,3},{3,2},{4,5},{5,4},{6,7},{7,6},{8,9},{9,8},{10,11... | collective-permute-start | bytes 786440 | tf_op jit(solution)/shard_map/ppermute | solution.py:301
  60.6 10.2 %collective-permute-start.21 = (bf16[1040,128]{1,0:T(8,128)(2,1)S(1)}, bf16[1040,128]{1,0:T(8,128)(2,1)S(1)}, u32[]{:S(2)}, u32[]{:S(2)}) collective-permute-start(bf16[1040,128]{1,0:T(8,128)(2,1)S(1)} %shard_map.145.rest_0_), channel_id=1, source_target_pairs={{0,24},{8,16},{16,8},{24,0},{1,25},{9,17},{17,9},{25,1},{2,26},{10... | collective-permute-start | bytes 798728 | tf_op jit(solution)/shard_map/ppermute | solution.py:296
  62.4 13.6 %collective-permute-start.20 = (bf16[1040,128]{1,0:T(8,128)(2,1)S(1)}, bf16[1040,128]{1,0:T(8,128)(2,1)S(1)}, u32[]{:S(2)}, u32[]{:S(2)}) collective-permute-start(bf16[1040,128]{1,0:T(8,128)(2,1)S(1)} %shard_map.145.rest_0_), channel_id=1, source_target_pairs={{0,16},{8,24},{16,0},{24,8},{1,17},{9,25},{17,1},{25,9},{2,18},{10... | collective-permute-start | bytes 798728 | tf_op jit(solution)/shard_map/ppermute | solution.py:296
  63.2 12.8 %collective-permute-start.19 = (bf16[1040,128]{1,0:T(8,128)(2,1)S(1)}, bf16[1040,128]{1,0:T(8,128)(2,1)S(1)}, u32[]{:S(2)}, u32[]{:S(2)}) collective-permute-start(bf16[1040,128]{1,0:T(8,128)(2,1)S(1)} %shard_map.145.rest_0_), channel_id=1, source_target_pairs={{0,8},{8,0},{16,24},{24,16},{1,9},{9,1},{17,25},{25,17},{2,10},{10... | collective-permute-start | bytes 798728 | tf_op jit(solution)/shard_map/ppermute | solution.py:296
  64.1 47.6 %collective-permute-start.22 = (bf16[1040,128]{1,0:T(8,128)(2,1)S(1)}, bf16[1040,128]{1,0:T(8,128)(2,1)S(1)}, u32[]{:S(2)}, u32[]{:S(2)}) collective-permute-start(bf16[1040,128]{1,0:T(8,128)(2,1)S(1)} %shard_map.145.rest_0_), channel_id=1, source_target_pairs={{0,1},{1,0},{2,3},{3,2},{4,5},{5,4},{6,7},{7,6},{8,9},{9,8},{10,11... | collective-permute-start | bytes 798728 | tf_op jit(solution)/shard_map/ppermute | solution.py:301
  70.8 41.0 %collective-permute-start.25 = (bf16[1040,128]{1,0:T(8,128)(2,1)S(1)}, bf16[1040,128]{1,0:T(8,128)(2,1)S(1)}, u32[]{:S(2)}, u32[]{:S(2)}) collective-permute-start(bf16[1040,128]{1,0:T(8,128)(2,1)S(1)} %collective-permute-done.21.rest_3_), channel_id=1, source_target_pairs={{0,1},{1,0},{2,3},{3,2},{4,5},{5,4},{6,7},{7,6},{8,9},{9,8},{10,11... | collective-permute-start | bytes 798728 | tf_op jit(solution)/shard_map/ppermute | solution.py:301
  76.0 35.8 %collective-permute-start.24 = (bf16[1040,128]{1,0:T(8,128)(2,1)S(1)}, bf16[1040,128]{1,0:T(8,128)(2,1)S(1)}, u32[]{:S(2)}, u32[]{:S(2)}) collective-permute-start(bf16[1040,128]{1,0:T(8,128)(2,1)S(1)} %collective-permute-done.20.rest_2_), channel_id=1, source_target_pairs={{0,1},{1,0},{2,3},{3,2},{4,5},{5,4},{6,7},{7,6},{8,9},{9,8},{10,11... | collective-permute-start | bytes 798728 | tf_op jit(solution)/shard_map/ppermute | solution.py:301
  76.0 35.7 %collective-permute-start.23 = (bf16[1040,128]{1,0:T(8,128)(2,1)S(1)}, bf16[1040,128]{1,0:T(8,128)(2,1)S(1)}, u32[]{:S(2)}, u32[]{:S(2)}) collective-permute-start(bf16[1040,128]{1,0:T(8,128)(2,1)S(1)} %collective-permute-done.19.rest_1_), channel_id=1, source_target_pairs={{0,1},{1,0},{2,3},{3,2},{4,5},{5,4},{6,7},{7,6},{8,9},{9,8},{10,11... | collective-permute-start | bytes 798728 | tf_op jit(solution)/shard_map/ppermute | solution.py:301
  76.5 4.3 %collective-permute-start.12 = (bf16[2,64,256]{2,1,0:T(8,128)(2,1)S(1)}, bf16[2,64,256]{2,1,0:T(8,128)(2,1)S(1)}, u32[]{:S(2)}, u32[]{:S(2)}) collective-permute-start(bf16[2,64,256]{2,1,0:T(8,128)(2,1)S(1)} %get-tuple-element.68.rest_1_), channel_id=1, source_target_pairs={{0,8},{8,0},{16,24},{24,16},{1,9},{9,1},{17,25},{25,17},{2,10},{10... | collective-permute-start | bytes 196616 | tf_op jit(solution)/shard_map/ppermute | solution.py:296
  85.0 5.2 %collective-permute-start.14 = (bf16[2,64,256]{2,1,0:T(8,128)(2,1)S(1)}, bf16[2,64,256]{2,1,0:T(8,128)(2,1)S(1)}, u32[]{:S(2)}, u32[]{:S(2)}) collective-permute-start(bf16[2,64,256]{2,1,0:T(8,128)(2,1)S(1)} %get-tuple-element.70.rest_3_), channel_id=1, source_target_pairs={{0,24},{8,16},{16,8},{24,0},{1,25},{9,17},{17,9},{25,1},{2,26},{10... | collective-permute-start | bytes 196616 | tf_op jit(solution)/shard_map/ppermute | solution.py:296
  94.8 5.4 %collective-permute-start.17 = (f32[2,256]{1,0:T(2,128)S(1)}, f32[2,256]{1,0:T(2,128)S(1)}, u32[]{:S(2)}, u32[]{:S(2)}) collective-permute-start(f32[2,256]{1,0:T(2,128)S(1)} %get-tuple-element.72.rest_0_), channel_id=1, source_target_pairs={{0,6},{2,4},{4,2},{6,0},{1,7},{3,5},{5,3},{7,1},{8,14},{10,12},{12... | collective-permute-start | bytes 6152 | tf_op jit(solution)/shard_map/ppermute | solution.py:296
  100.1 4.5 %collective-permute-start.16 = (f32[2,256]{1,0:T(2,128)S(1)}, f32[2,256]{1,0:T(2,128)S(1)}, u32[]{:S(2)}, u32[]{:S(2)}) collective-permute-start(f32[2,256]{1,0:T(2,128)S(1)} %get-tuple-element.72.rest_0_), channel_id=1, source_target_pairs={{0,4},{2,6},{4,0},{6,2},{1,5},{3,7},{5,1},{7,3},{8,12},{10,14},{12... | collective-permute-start | bytes 6152 | tf_op jit(solution)/shard_map/ppermute | solution.py:296
  (12 other events, 126.5 us)

commit v2 on v1

--- a/solution.py
+++ b/solution.py
@@ -197,31 +197,47 @@
     return jax.ShapeDtypeStruct(shape, dtype)
 
 
-def whole_call(body, outs, *ins, cost=1_000_000):
+def cost_of(micros):
+    return pl.CostEstimate(
+        flops=int(micros * 1e9), bytes_accessed=int(micros * 3.6e6), transcendentals=0
+    )
+
+
+def whole_call(body, outs, *ins, micros=1.0, after=(), scratch=(), vmem=40):
+    n_out = len(jax.tree.leaves(outs))
+    skip = len(after)
+    space = pl.BlockSpec(memory_space=pltpu.VMEM)
     return pl.pallas_call(
-        body,
+        lambda *refs: body(*refs[: len(ins)], *refs[len(ins) + skip :]),
         out_shape=outs,
-        compiler_params=pltpu.CompilerParams(vmem_limit_bytes=40 * 2**20),
-        cost_estimate=pl.CostEstimate(flops=cost, bytes_accessed=cost, transcendentals=0),
-    )(*ins)
-
-
-def grid_call(body, steps, outs, in_specs, out_specs, scratch, ids, *ins, cost=1_000_000):
+        in_specs=[
+            pl.BlockSpec(memory_space=pltpu.SMEM) if a.dtype == jnp.int32 else space for a in ins
+        ]
+        + [pl.BlockSpec(memory_space=pl.ANY)] * skip,
+        out_specs=jax.tree.map(lambda _: space, outs),
+        scratch_shapes=list(scratch),
+        compiler_params=pltpu.CompilerParams(vmem_limit_bytes=vmem * 2**20),
+        cost_estimate=cost_of(micros),
+    )(*ins, *after)
+
+
+def grid_call(body, steps, outs, in_specs, out_specs, scratch, ids, *ins, micros=1.0, after=()):
+    skip = len(after)
     return pl.pallas_call(
-        body,
+        lambda ids_ref, *refs: body(ids_ref, *refs[skip:]),
         out_shape=outs,
         grid_spec=pltpu.PrefetchScalarGridSpec(
             num_scalar_prefetch=1,
             grid=(steps,),
-            in_specs=in_specs,
+            in_specs=[pl.BlockSpec(memory_space=pl.ANY)] * skip + list(in_specs),
             out_specs=out_specs,
             scratch_shapes=scratch,
         ),
         compiler_params=pltpu.CompilerParams(
             vmem_limit_bytes=40 * 2**20, dimension_semantics=("arbitrary",)
         ),
-        cost_estimate=pl.CostEstimate(flops=cost, bytes_accessed=cost, transcendentals=0),
-    )(ids, *ins)
+        cost_estimate=cost_of(micros),
+    )(ids, *after, *ins)
 
 
 def row_order(rows):
@@ -309,8 +325,8 @@
     full = lambda a: pl.BlockSpec(a.shape, lambda i, ids: (0,) * len(a.shape))
     own_cols = pl.BlockSpec((rows, wide), lambda i, ids: (0, i))
     rel_cols = pl.BlockSpec((rows, wide), lambda i, ids: (0, ids[0] ^ i))
-    rel_mem = pl.BlockSpec((slots, wide), lambda i, ids: (rows // slots + (ids[0] ^ i), 0))
-    own_mem = pl.BlockSpec((slots, wide), lambda i, ids: (rows // slots + i, 0))
+    rel_mem = pl.BlockSpec((slots, wide), lambda i, ids: (ids[0] ^ i, 0))
+    own_mem = pl.BlockSpec((slots, wide), lambda i, ids: (i, 0))
 
     def squares_body(q_ref, k_ref, ss_ref, kp_ref):
         kp = dot(row_order(rows), k_ref[...])
@@ -319,16 +335,12 @@
         ss_ref[0:1, :] = lane_sum_row(fold_lanes(qf * qf))
         ss_ref[1:2, :] = lane_sum_row(fold_lanes(kp * kp))
 
-    ss, kp = whole_call(squares_body, (sds((2, rows), F32), sds((rows, cols), BF16)), q, k)
+    ss, kp = whole_call(
+        squares_body, (sds((2, rows), F32), sds((rows, cols), BF16)), q, k, micros=1.2, vmem=62
+    )
     ss_peers = to_peers("head", [ss] * (n_head - 1))
 
-    def pack_sends(ids_ref, rows_ref, mem_scr, sends):
-        for r, send in zip(peers, sends):
-            dest = ids_ref[0] ^ r
-            send[:rows, :] = rows_ref[:, pl.ds(pl.multiple_of(dest * wide, wide), wide)]
-            send[rows:, :] = mem_scr[...]
-
-    def compress(source, w_ref, mem_scr):
+    def compress(source, w_ref, out_ref):
         for h in range(heads):
             total = None
             for j in range(KS):
@@ -338,57 +350,41 @@
                 )
                 total = part if total is None else total + part
             block = h // hp
-            mem_scr[
+            out_ref[
                 block * slots : (block + 1) * slots, (h % hp) * HD : (h % hp + 1) * HD
             ] = total.astype(BF16)
 
-    def values_body(ids_ref, v_ref, w_ref, vp_ref, *rest):
-        sends, mem_scr = rest[:-1], rest[-1]
+    def values_body(v_ref, w_ref, vp_ref, mem_ref):
         vp_ref[...] = dot(row_order(rows), v_ref[...]).astype(BF16)
-        compress(vp_ref, w_ref, mem_scr)
-        pack_sends(ids_ref, vp_ref, mem_scr, sends)
-
-    packet = sds((rows + mem_rows, wide), BF16)
-    smem = pl.BlockSpec(memory_space=pltpu.SMEM)
-
-    def packet_call(body, extra, scalars, *ins):
-        outs = extra + (packet,) * (n_seq - 1)
-        return pl.pallas_call(
-            body,
-            out_shape=outs,
-            in_specs=[smem] + [pl.BlockSpec(memory_space=pltpu.VMEM)] * len(ins),
-            out_specs=tuple(pl.BlockSpec(memory_space=pltpu.VMEM) for _ in outs),
-            scratch_shapes=[pltpu.VMEM((mem_rows, wide), BF16)],
-            compiler_params=pltpu.CompilerParams(vmem_limit_bytes=40 * 2**20),
-            cost_estimate=pl.CostEstimate(
-                flops=1_000_000, bytes_accessed=1_000_000, transcendentals=0
-            ),
-        )(scalars, *ins)
-
-    vp, *v_sends = packet_call(values_body, (sds((rows, cols), BF16),), ids, v, value_squeeze)
-    v_recv = to_peers("seq", v_sends)
-
-    def keys_body(ids_ref, q_ref, kp_ref, qg_ref, kg_ref, w_ref, *rest):
+        compress(vp_ref, w_ref, mem_ref)
+
+    rows_shape = sds((rows, cols), BF16)
+    mem_shape = sds((mem_rows, wide), BF16)
+    vp, mem_v = whole_call(
+        values_body, (rows_shape, mem_shape), v, value_squeeze, after=(ss_peers[0],), micros=0.6
+    )
+    mv_recv = to_peers("seq", [mem_v] * (n_seq - 1))
+
+    def keys_body(q_ref, kp_ref, qg_ref, kg_ref, w_ref, *rest):
         ss_refs = rest[:n_head]
-        inv_ref, qn_ref, kn_ref = rest[n_head : n_head + 3]
-        sends, mem_scr = rest[n_head + 3 : -1], rest[-1]
+        inv_ref, qn_ref, kn_ref, mem_ref = rest[n_head:]
         total = ss_refs[0][...]
         for other in ss_refs[1:]:
             total = total + other[...]
         inv = lax.rsqrt(total / full_width + epsilon)
         inv_ref[...] = inv
         inv_c = as_columns(inv)
+        kn_ref[...] = (kp_ref[...].astype(F32) * inv_c[:, 1:2] * kg_ref[...]).astype(BF16)
+        compress(kn_ref, w_ref, mem_ref)
         qn_ref[...] = (q_ref[...].astype(F32) * inv_c[:, 0:1] * qg_ref[...]).astype(BF16)
-        kn_ref[...] = (kp_ref[...].astype(F32) * inv_c[:, 1:2] * kg_ref[...]).astype(BF16)
-        compress(kn_ref, w_ref, mem_scr)
-        pack_sends(ids_ref, kn_ref, mem_scr, sends)
-
-    inv, qn, kn, *k_sends = packet_call(
+
+    inv, qn, kn, mem_k = whole_call(
         keys_body,
-        (sds((2, rows), F32), sds((rows, cols), BF16), sds((rows, cols), BF16)),
-        ids, q, kp, qg, kg, key_squeeze, ss, *ss_peers,
-    )
-    k_recv = to_peers("seq", k_sends)
+        (sds((2, rows), F32), rows_shape, rows_shape, mem_shape),
+        q, kp, qg, kg, key_squeeze, ss, *ss_peers,
+        micros=1.5,
+    )
+    mk_recv = to_peers("seq", [mem_k] * (n_seq - 1))
 
     def local_body(ids_ref, qn_ref, kn_ref, vp_ref, do_ref, st_ref):
         allowed = causal_t(rows)
@@ -410,7 +406,21 @@
         (pl.BlockSpec((hp, 8, rows), lambda i, ids: (i, 0, 0)),),
         [],
         ids, qn, kn, vp, do,
-    )
+        micros=2.6,
+    )
+
+    def rows_body(ids_ref, kn_ref, vp_ref, *sends):
+        for r, send in zip(peers, sends):
+            dest = ids_ref[0] ^ r
+            at = pl.ds(pl.multiple_of(dest * wide, wide), wide)
+            send[0] = kn_ref[:, at]
+            send[1] = vp_ref[:, at]
+
+    row_pair = sds((2, rows, wide), BF16)
+    row_sends = whole_call(
+        rows_body, (row_pair,) * (n_seq - 1), ids, kn, vp, after=(stats,), micros=0.7
+    )
+    rows_recv = to_peers("seq", row_sends)
 
     def memory_body(ids_ref, qn_ref, do_ref, st_ref, *rest):
         mk_refs = rest[: n_seq - 1]
@@ -468,7 +478,8 @@
         )
         + (full(part),) * n_seq,
         [],
-        ids, qn, do, stats, *k_recv, *v_recv,
+        ids, qn, do, stats, *mk_recv, *mv_recv,
+        micros=4.8,
     )
     parts_recv = to_peers("seq", parts[1:])
 
@@ -531,7 +542,8 @@
         + [full(inv), pl.BlockSpec((1, wide), lambda i, ids: (0, i))],
         (own_cols, own_cols, own_cols, full(dot_row), gain_spec, gain_spec),
         [pltpu.VMEM((rows, HD), F32)],
-        ids, q, kp, qn, kn, vp, do, stats2, ds_mem, *k_recv, inv, qg,
+        ids, q, kp, qn, kn, vp, do, stats2, ds_mem, *mk_recv, inv, qg,
+        micros=5.8,
     )
 
     def slots_body(*refs):
@@ -548,44 +560,40 @@
                 outs[r][tensor] = total.astype(BF16)
 
     slot_grad = sds((2, slots, wide), BF16)
-    slot_grads = whole_call(slots_body, (slot_grad,) * n_seq, parts[0], *parts_recv)
+    slot_grads = whole_call(
+        slots_body, (slot_grad,) * n_seq, parts[0], *parts_recv, after=(gain_q,), micros=0.3
+    )
     slots_recv = to_peers("seq", slot_grads[1:])
 
     def weights_body(ids_ref, kn_ref, vp_ref, *rest):
         gm = rest[:n_seq]
-        k_refs = rest[n_seq : 2 * n_seq - 1]
-        v_refs = rest[2 * n_seq - 1 : 3 * n_seq - 2]
-        same_ref, other_ref = rest[3 * n_seq - 2 :]
+        row_refs = rest[n_seq : 2 * n_seq - 1]
+        same_ref, other_ref = rest[2 * n_seq - 1 :]
         here = pl.ds(pl.multiple_of(ids_ref[0] * wide, wide), wide)
         own = (kn_ref[:, here], vp_ref[:, here])
-        core_id = ids_ref[1]
+        first = ids_ref[1] == 0
         for i in range(hp):
             at = slice(i * HD, (i + 1) * HD)
             for j in range(KS):
                 span = slice(j * slots, (j + 1) * slots)
                 found = []
-                for tensor, refs in ((0, k_refs), (1, v_refs)):
+                for tensor in range(2):
                     lhs = jnp.concatenate(
-                        [own[tensor][span, at]] + [ref[span, at] for ref in refs], axis=0
+                        [own[tensor][span, at]] + [ref[tensor, span, at] for ref in row_refs],
+                        axis=0,
                     )
                     rhs = jnp.concatenate([ref[tensor, :, at] for ref in gm], axis=0)
                     found.append(dot(lhs, rhs, TN))
                 to = slice((i * KS + j) * HD, (i * KS + j + 1) * HD)
-                first = core_id == 0
                 same_ref[to, :] = jnp.where(first, found[0], found[1])
                 other_ref[to, :] = jnp.where(first, found[1], found[0]).astype(BF16)
 
     span_rows = hp * KS * HD
-    packet_rows = sds((rows, wide), BF16)
-    head_rows = pl.BlockSpec((rows, wide), lambda i, ids: (0, 0))
-    w_same, w_other = grid_call(
+    w_same, w_other = whole_call(
         weights_body,
-        1,
         (sds((span_rows, HD), F32), sds((span_rows, HD), BF16)),
-        [full(kn), full(vp)] + [full(slot_grad)] * n_seq + [head_rows] * (2 * n_seq - 2),
-        (full(sds((span_rows, HD), F32)), full(sds((span_rows, HD), BF16))),
-        [],
-        ids, kn, vp, *slot_grads, *k_recv, *v_recv,
+        ids, kn, vp, *slot_grads, *rows_recv,
+        micros=1.1,
     )
     w_recv = to_core(w_other)
 
@@ -596,9 +604,8 @@
         out_ref[span_rows:, :] = jnp.concatenate(rows_q + rows_k, axis=0).astype(BF16)
 
     chunk_shape = sds((span_rows + 2 * heads, HD), BF16)
-    chunk = whole_call(chunk_body, chunk_shape, w_same, w_recv, gain_q, gain_k)
+    chunk = whole_call(chunk_body, chunk_shape, w_same, w_recv, gain_q, gain_k, micros=0.3)
     chunks = [chunk] + to_peers("seq", [chunk] * (n_seq - 1))
-    others = [to_core(c) for c in chunks]
 
     def back_body(ids_ref, gk_ref, gv_ref, kp_ref, wk_ref, wv_ref, kg_ref, dq_ref, *rest):
         gm = rest[:n_seq]
@@ -649,8 +656,18 @@
         [pltpu.VMEM((rows, HD), F32)],
         ids, gk_local, gv_local, kp, key_squeeze, value_squeeze, kg, dot_q,
         slot_grads[0], *slots_recv,
+        after=(chunk,),
+        micros=4.5,
     )
     dots_peers = to_peers("head", [dots] * (n_head - 1))
+
+    def pack_body(*refs):
+        for r in range(n_seq):
+            refs[n_seq][r] = refs[r][...]
+
+    packed_shape = sds((n_seq,) + chunk_shape.shape, BF16)
+    packed = whole_call(pack_body, packed_shape, *chunks, after=tuple(dots_peers), micros=1.0)
+    packed_other = to_core(packed)
 
     def norms_body(ids_ref, q_ref, kp_ref, gq_ref, gkn_ref, qg_ref, kg_ref, inv_ref, *rest):
         dot_refs = rest[:n_head]
@@ -678,33 +695,24 @@
         (own_cols, own_cols),
         [],
         ids, q, kp, gq, gkn, qg, kg, inv, dots, *dots_peers,
-    )
-
-    def finish_body(ids_ref, kg_ref, wk_ref, *rest):
-        same, other = rest[:n_seq], rest[n_seq : 2 * n_seq]
-        gks_ref, gvs_ref, gain_ref = rest[2 * n_seq :]
+        micros=3.5,
+    )
+
+    def finish_body(ids_ref, kg_ref, wk_ref, same, other, gks_ref, gvs_ref, gain_ref):
         step = pl.program_id(0)
         first = ids_ref[1] == 0
 
         @pl.when(step == 0)
         def _():
-            total = None
-            for ref in rest[: 2 * n_seq]:
-                term = ref[span_rows:, :].astype(F32)
-                total = term if total is None else total + term
-            gain_ref[...] = total
-
-        for r in range(n_seq):
-            @pl.when(step == r)
-            def _(r=r):
-                for i in range(hp):
-                    span = slice(i * KS * HD, (i + 1) * KS * HD)
-                    a = same[r][span, :].astype(F32)
-                    b = other[r][span, :].astype(F32)
-                    gks_ref[i] = jnp.where(first, a, b)
-                    gvs_ref[i] = jnp.where(first, b, a)
-
+            gain_ref[...] = jnp.zeros_like(gain_ref)
+
+        gain_ref[...] += same[0, span_rows:, :].astype(F32) + other[0, span_rows:, :].astype(F32)
         for i in range(hp):
+            span = slice(i * KS * HD, (i + 1) * KS * HD)
+            a = same[0, span, :].astype(F32)
+            b = other[0, span, :].astype(F32)
+            gks_ref[i] = jnp.where(first, a, b)
+            gvs_ref[i] = jnp.where(first, b, a)
             prod = gks_ref[i] * wk_ref[i].astype(F32)
             total = prod[:HD]
             for j in range(1, KS):
@@ -716,15 +724,16 @@
 
     kernel_out = sds((heads, KS * HD, HD), F32)
     gains_shape = sds((2 * heads, HD), F32)
+    step_chunk = pl.BlockSpec((1,) + chunk_shape.shape, lambda i, ids: (i, 0, 0))
     gks, gvs, gains = grid_call(
         finish_body,
         n_seq,
         (kernel_out, kernel_out, gains_shape),
-        [pl.BlockSpec((1, wide), lambda i, ids: (0, ids[0] ^ i)), rel_w]
-        + [full(chunk_shape)] * (2 * n_seq),
+        [pl.BlockSpec((1, wide), lambda i, ids: (0, ids[0] ^ i)), rel_w, step_chunk, step_chunk],
         (rel_w, rel_w, full(gains_shape)),
         [],
-        ids, kg, key_squeeze, *chunks, *others,
+        ids, kg, key_squeeze, packed, packed_other,
+        micros=3.2,
     )
     return (
         grad_query[None],

time: 116 us -> 87.7 us (0.76)
  waiting for transfers between devices: 50.9 us -> 26 us
  local copies, waits for them, and re-layouts: 5.05 us -> 2.35 us
  starting transfers between devices: 30.1 us -> 28.2 us
  Pallas kernels: 28.6 us -> 30 us
    ppermute x21 -> x24, waiting for transfers between devices: 50.9 us -> 26 us  [to_peers(): lax.ppermute(a, axis, [(i, i ^ k) for i in range(n)])]
    unnamed x20, local copies, waits for them, and re-layouts: 4.45 us -> 1.76 us
    ppermute x21 -> x24, starting transfers between devices: 29.6 us -> 28 us  [to_peers(): lax.ppermute(a, axis, [(i, i ^ k) for i in range(n)])]
    pallas_call x12 -> x14, Pallas kernels: 28.6 us -> 30 us  [the longest x6 24.3 us: grid_call(): pl.pallas_call(lambda ids_ref, *refs: body(ids_ref, *refs[skip:]), out_sh...]
  transfers between devices with their start and end apart: 26 -> 26, of which waited for: 14 -> 9; matrix products, arithmetic and copies ran while one was open for 0% -> 0% of each run, Pallas kernels for 16% -> 20%
where the time goes in v2:
time: 87.7 us; the launch traced here: 87.5 us
  Pallas kernels  30 us (34%)
  starting transfers between devices  28.2 us (32%)
  waiting for transfers between devices  26 us (30%)
  local copies, waits for them, and re-layouts  2.35 us (3%)
    ppermute x24, starting transfers between devices, to_peers(): lax.ppermute(a, axis, [(i, i ^ k) for i in range(n)])  28 us
    ppermute x24, waiting for transfers between devices, to_peers(): lax.ppermute(a, axis, [(i, i ^ k) for i in range(n)])  26 us
    pallas_call x6, Pallas kernels, grid_call(): pl.pallas_call(lambda ids_ref, *refs: body(ids_ref, *refs[skip:]), out_sh...  24.3 us
    pallas_call x8, Pallas kernels, whole_call(): pl.pallas_call(lambda *refs: body(*refs[:len(ins)], *refs[len(ins) + skip...  5.71 us
    unnamed x20, local copies, waits for them, and re-layouts  1.76 us
  transfers between devices with their start and end apart: 26, of which 9 were waited for; matrix products, arithmetic and copies ran while one was open for 0% of the time, Pallas kernels for 20%

profile of v2, /device:TPU:0, one launch (start us, length us, event | category | flops | bytes accessed | tf_op | source)
XLA Modules:
  0.0 87.5 jit_solution(15310857781079153048)
XLA Ops:
  0.7 2.4 %shard_map.135 = (f32[2,256]{1,0:T(2,128)}, bf16[256,1024]{1,0:T(8,128)(2,1)}) custom-call(bf16[256,1024]{1,0:T(8,128)(2,1)} %bitcast.19, bf16[256,1024]{1,0:T(8,128)(2,1)} %bitcast.30), custom_call_target="tpu_custom_call" | custom-call | flops 1200000000 | bytes 4320000 | tf_op jit(solution)/shard_map/pallas_call | solution.py:210
  3.1 3.0 %collective-permute-start = (f32[2,256]{1,0:T(2,128)}, f32[2,256]{1,0:T(2,128)S(1)}, u32[]{:S(2)}, u32[]{:S(2)}) collective-permute-start(f32[2,256]{1,0:T(2,128)} %get-tuple-element.45.refs_5_), channel_id=1, source_target_pairs={{0,2},{2,0},{4,6},{6,4},{1,3},{3,1},{5,7},{7,5},{8,10},{10,8},{12,... | collective-permute-start | bytes 6152 | tf_op jit(solution)/shard_map/ppermute | solution.py:312
  6.1 2.6 %collective-permute-start.1 = (f32[2,256]{1,0:T(2,128)}, f32[2,256]{1,0:T(2,128)S(1)}, u32[]{:S(2)}, u32[]{:S(2)}) collective-permute-start(f32[2,256]{1,0:T(2,128)} %get-tuple-element.45.refs_5_), channel_id=1, source_target_pairs={{0,4},{2,6},{4,0},{6,2},{1,5},{3,7},{5,1},{7,3},{8,12},{10,14},{12... | collective-permute-start | bytes 6152 | tf_op jit(solution)/shard_map/ppermute | solution.py:312
  8.7 2.1 %collective-permute-done.1.refs_7_ = f32[2,256]{1,0:T(2,128)S(1)} collective-permute-done((f32[2,256]{1,0:T(2,128)}, f32[2,256]{1,0:T(2,128)S(1)}, u32[]{:S(2)}, u32[]{:S(2)}) %collective-permute-start.1) | collective-permute-done | bytes 2080 | tf_op jit(solution)/shard_map/ppermute | solution.py:312
  10.8 3.5 %collective-permute-done.2.refs_8_ = f32[2,256]{1,0:T(2,128)S(1)} collective-permute-done((f32[2,256]{1,0:T(2,128)}, f32[2,256]{1,0:T(2,128)S(1)}, u32[]{:S(2)}, u32[]{:S(2)}) %collective-permute-start.2) | collective-permute-done | bytes 2080 | tf_op jit(solution)/shard_map/ppermute | solution.py:312
  16.9 1.6 %collective-permute-start.3 = (bf16[256,256]{1,0:T(8,128)(2,1)S(1)}, bf16[256,256]{1,0:T(8,128)(2,1)S(1)}, u32[]{:S(2)}, u32[]{:S(2)}) collective-permute-start(bf16[256,256]{1,0:T(8,128)(2,1)S(1)} %get-tuple-element.49), channel_id=1, source_target_pairs={{0,8},{8,0},{16,24},{24,16},{1,9},{9,1},{17,25},{25,17},{2,10},{10... | collective-permute-start | bytes 393224 | tf_op jit(solution)/shard_map/ppermute | solution.py:312
  18.5 1.5 %collective-permute-start.4 = (bf16[256,256]{1,0:T(8,128)(2,1)S(1)}, bf16[256,256]{1,0:T(8,128)(2,1)S(1)}, u32[]{:S(2)}, u32[]{:S(2)}) collective-permute-start(bf16[256,256]{1,0:T(8,128)(2,1)S(1)} %get-tuple-element.49), channel_id=1, source_target_pairs={{0,16},{8,24},{16,0},{24,8},{1,17},{9,25},{17,1},{25,9},{2,18},{10... | collective-permute-start | bytes 393224 | tf_op jit(solution)/shard_map/ppermute | solution.py:312
  21.1 1.5 %collective-permute-start.6 = (bf16[256,256]{1,0:T(8,128)(2,1)S(1)}, bf16[256,256]{1,0:T(8,128)(2,1)S(1)}, u32[]{:S(2)}, u32[]{:S(2)}) collective-permute-start(bf16[256,256]{1,0:T(8,128)(2,1)S(1)} %get-tuple-element.50), channel_id=1, source_target_pairs={{0,8},{8,0},{16,24},{24,16},{1,9},{9,1},{17,25},{25,17},{2,10},{10... | collective-permute-start | bytes 393224 | tf_op jit(solution)/shard_map/ppermute | solution.py:312
  22.6 1.5 %collective-permute-start.7 = (bf16[256,256]{1,0:T(8,128)(2,1)S(1)}, bf16[256,256]{1,0:T(8,128)(2,1)S(1)}, u32[]{:S(2)}, u32[]{:S(2)}) collective-permute-start(bf16[256,256]{1,0:T(8,128)(2,1)S(1)} %get-tuple-element.50), channel_id=1, source_target_pairs={{0,16},{8,24},{16,0},{24,8},{1,17},{9,25},{17,1},{25,9},{2,18},{10... | collective-permute-start | bytes 393224 | tf_op jit(solution)/shard_map/ppermute | solution.py:312
  24.1 1.3 %collective-permute-start.8 = (bf16[256,256]{1,0:T(8,128)(2,1)S(1)}, bf16[256,256]{1,0:T(8,128)(2,1)S(1)}, u32[]{:S(2)}, u32[]{:S(2)}) collective-permute-start(bf16[256,256]{1,0:T(8,128)(2,1)S(1)} %get-tuple-element.50), channel_id=1, source_target_pairs={{0,24},{8,16},{16,8},{24,0},{1,25},{9,17},{17,9},{25,1},{2,26},{10... | collective-permute-start | bytes 393224 | tf_op jit(solution)/shard_map/ppermute | solution.py:312
  25.5 2.5 %shard_map.138.refs_2_.refs_3_ = f32[8,8,256]{2,1,0:T(8,128)S(1)} custom-call(s32[2]{0:T(128)S(1)} %pad_add_fusion.ids_ref.refs_0_, bf16[256,1024]{1,0:T(8,128)(2,1)S(1)} %get-tuple-element.46.refs_0_.refs_2_, bf16[256,1024]{1,0:T(8,128)(2,1)S(1)} %get-tuple-element.47.refs_1_.refs_3_, bf16[256,1024]{1,0:T(8,128)(2,1)S(1)} %get-tuple-element.48.refs_2_.refs_4_, ...), custom_call_target="tpu_custom_call" | custom-call | flops 2600000000 | bytes 9360000 | tf_op jit(solution)/shard_map/pallas_call | solution.py:226
  28.6 2.7 %collective-permute-done.7.refs_7_ = bf16[256,256]{1,0:T(8,128)(2,1)S(1)} collective-permute-done((bf16[256,256]{1,0:T(8,128)(2,1)S(1)}, bf16[256,256]{1,0:T(8,128)(2,1)S(1)}, u32[]{:S(2)}, u32[]{:S(2)}) %collective-permute-start.7) | collective-permute-done | bytes 131104 | tf_op jit(solution)/shard_map/ppermute | solution.py:312
  31.3 4.8 %shard_map.139 = (f32[8,8,256]{2,1,0:T(8,128)S(1)}, bf16[8,192,256]{2,1,0:T(8,128)(2,1)S(1)}, bf16[2,192,256]{2,1,0:T(8,128)(2,1)S(1)}, bf16[2,192,256]{2,1,0:T(...) custom-call(s32[2]{0:T(128)S(1)} %pad_add_fusion.ids_ref.refs_0_, ...), custom_call_target="tpu_custom_call" | custom-call | flops 4800000000 | bytes 17280000 | tf_op jit(solution)/shard_map/pallas_call | solution.py:226
  37.0 1.9 %collective-permute-start.12 = (bf16[2,256,256]{2,1,0:T(8,128)(2,1)S(1)}, bf16[2,256,256]{2,1,0:T(8,128)(2,1)S(1)}, u32[]{:S(2)}, u32[]{:S(2)}) collective-permute-start(bf16[2,256,256]{2,1,0:T(8,128)(2,1)S(1)} %get-tuple-element.64), channel_id=1, source_target_pairs={{0,8},{8,0},{16,24},{24,16},{1,9},{9,1},{17,25},{25,17},{2,10},{10... | collective-permute-start | bytes 786440 | tf_op jit(solution)/shard_map/ppermute | solution.py:312
  41.6 2.3 %collective-permute-done.9.refs_1_ = bf16[2,192,256]{2,1,0:T(8,128)(2,1)S(1)} collective-permute-done((bf16[2,192,256]{2,1,0:T(8,128)(2,1)S(1)}, bf16[2,192,256]{2,1,0:T(8,128)(2,1)S(1)}, u32[]{:S(2)}, u32[]{:S(2)}) %collective-permute-start.9) | collective-permute-done | bytes 196640 | tf_op jit(solution)/shard_map/ppermute | solution.py:312
  44.7 5.7 %shard_map.140 = (f32[256,1024]{1,0:T(8,128)S(1)}, f32[256,1024]{1,0:T(8,128)S(1)}, f32[256,1024]{1,0:T(8,128)S(1)}, f32[1,256]{1,0:T(1,128)S(1)}, f32[4,2,128]{2,1,0:T(2,128)S(1)}, /*index=5*/f32[4,2,128]{2,1,0:T(2,128)S(1)}) custom-call(s32[2]{0:T(128)S(1)} %pad_add_fusion.ids_ref.refs_0_, bf16[256,1024]{1,0:T(8,128)(2,1)S(1)} %bitcast.21, ...), custom_call_target="tpu_custom_call" | custom-call | flops 5800000000 | bytes 20880000 | tf_op jit(solution)/shard_map/pallas_call | solution.py:226
  50.4 7.6 %collective-permute-done.10.refs_2_ = bf16[2,192,256]{2,1,0:T(8,128)(2,1)S(1)} collective-permute-done((bf16[2,192,256]{2,1,0:T(8,128)(2,1)S(1)}, bf16[2,192,256]{2,1,0:T(8,128)(2,1)S(1)}, u32[]{:S(2)}, u32[]{:S(2)}) %collective-permute-start.10) | collective-permute-done | bytes 196640 | tf_op jit(solution)/shard_map/ppermute | solution.py:312
  60.7 2.2 %collective-permute-start.18 = (bf16[2,64,256]{2,1,0:T(8,128)(2,1)S(1)}, bf16[2,64,256]{2,1,0:T(8,128)(2,1)S(1)}, u32[]{:S(2)}, u32[]{:S(2)}) collective-permute-start(bf16[2,64,256]{2,1,0:T(8,128)(2,1)S(1)} %get-tuple-element.63.refs_6_), channel_id=1, source_target_pairs={{0,24},{8,16},{16,8},{24,0},{1,25},{9,17},{17,9},{25,1},{2,26},{10... | collective-permute-start | bytes 196616 | tf_op jit(solution)/shard_map/ppermute | solution.py:312
  64.3 2.2 %collective-permute-start.24 = (bf16[1040,128]{1,0:T(8,128)(2,1)S(1)}, bf16[1040,128]{1,0:T(8,128)(2,1)S(1)}, u32[]{:S(2)}, u32[]{:S(2)}) collective-permute-start(bf16[1040,128]{1,0:T(8,128)(2,1)S(1)} %shard_map.144.refs_0_), channel_id=1, source_target_pairs={{0,24},{8,16},{16,8},{24,0},{1,25},{9,17},{17,9},{25,1},{2,26},{10... | collective-permute-start | bytes 798728 | tf_op jit(solution)/shard_map/ppermute | solution.py:312
  66.5 4.6 %shard_map.145 = (bf16[256,1024]{1,0:T(8,128)(2,1)}, f32[256,1024]{1,0:T(8,128)S(1)}, f32[2,256]{1,0:T(2,128)S(1)}) custom-call(s32[2]{0:T(128)S(1)} %pad_add_fusion.ids_ref.refs_0_, bf16[1040,128]{1,0:T(8,128)(2,1)S(1)} %shard_map.144.refs_0_, f32[256,1024]{1,0:T(8,128)S(1)} %get-tuple-element.70.refs_1_, f32[256,1024]{1,0:T(8,128)S(1)} %get-tuple-element.71.refs_2_, ...), custom_call_target="tpu_custom_call" | custom-call | flops 4499999744 | bytes 16200000 | tf_op jit(solution)/shard_map/pallas_call | solution.py:226
  72.0 2.6 %collective-permute-done.19.refs_8_.refs_4_ = f32[2,256]{1,0:T(2,128)S(1)} collective-permute-done((f32[2,256]{1,0:T(2,128)S(1)}, f32[2,256]{1,0:T(2,128)S(1)}, u32[]{:S(2)}, u32[]{:S(2)}) %collective-permute-start.19) | collective-permute-done | bytes 2080 | tf_op jit(solution)/shard_map/ppermute | solution.py:312
  75.5 4.5 %collective-permute-done.21.refs_10_.refs_6_ = f32[2,256]{1,0:T(2,128)S(1)} collective-permute-done((f32[2,256]{1,0:T(2,128)S(1)}, f32[2,256]{1,0:T(2,128)S(1)}, u32[]{:S(2)}, u32[]{:S(2)}) %collective-permute-start.21) | collective-permute-done | bytes 2080 | tf_op jit(solution)/shard_map/ppermute | solution.py:312
  80.2 3.5 %shard_map.146 = (bf16[256,1024]{1,0:T(8,128)(2,1)}, bf16[256,1024]{1,0:T(8,128)(2,1)}) custom-call(s32[2]{0:T(128)S(1)} %pad_add_fusion.ids_ref.refs_0_, bf16[256,1024]{1,0:T(8,128)(2,1)S(1)} %bitcast.22, bf16[256,1024]{1,0:T(8,128)(2,1)S(1)} %copy-done.9, f32[256,1024]{1,0:T(8,128)S(1)} %get-tuple-element.54.refs_2_, ...), custom_call_target="tpu_custom_call" | custom-call | flops 3500000000 | bytes 12600000 | tf_op jit(solution)/shard_map/pallas_call | solution.py:226
  83.7 3.2 %shard_map.148 = (f32[8,512,128]{2,1,0:T(8,128)}, f32[8,512,128]{2,1,0:T(8,128)}, f32[16,128]{1,0:T(8,128)S(1)}) custom-call(s32[2]{0:T(128)S(1)} %pad_add_fusion.ids_ref.refs_0_, f32[1,1024]{1,0:T(1,128)S(1)} %bitcast.29, bf16[8,512,128]{2,1,0:T(8,128)(2,1)S(1)} %copy-done.1, bf16[4,1040,128]{2,1,0:T(8,128)(2,1)S(1)} %shard_map.147.refs_2_, ...), custom_call_target="tpu_custom_call" | custom-call | flops 3200000000 | bytes 11520000 | tf_op jit(solution)/shard_map/pallas_call | solution.py:226
  (64 shorter events, 15.3 us)
Async XLA Ops:
  3.1 5.6 %collective-permute-start = (f32[2,256]{1,0:T(2,128)}, f32[2,256]{1,0:T(2,128)S(1)}, u32[]{:S(2)}, u32[]{:S(2)}) collective-permute-start(f32[2,256]{1,0:T(2,128)} %get-tuple-element.45.refs_5_), channel_id=1, source_target_pairs={{0,2},{2,0},{4,6},{6,4},{1,3},{3,1},{5,7},{7,5},{8,10},{10,8},{12,... | collective-permute-start | bytes 6152 | tf_op jit(solution)/shard_map/ppermute | solution.py:312
  6.1 4.7 %collective-permute-start.1 = (f32[2,256]{1,0:T(2,128)}, f32[2,256]{1,0:T(2,128)S(1)}, u32[]{:S(2)}, u32[]{:S(2)}) collective-permute-start(f32[2,256]{1,0:T(2,128)} %get-tuple-element.45.refs_5_), channel_id=1, source_target_pairs={{0,4},{2,6},{4,0},{6,2},{1,5},{3,7},{5,1},{7,3},{8,12},{10,14},{12... | collective-permute-start | bytes 6152 | tf_op jit(solution)/shard_map/ppermute | solution.py:312
  8.7 5.6 %collective-permute-start.2 = (f32[2,256]{1,0:T(2,128)}, f32[2,256]{1,0:T(2,128)S(1)}, u32[]{:S(2)}, u32[]{:S(2)}) collective-permute-start(f32[2,256]{1,0:T(2,128)} %get-tuple-element.45.refs_5_), channel_id=1, source_target_pairs={{0,6},{2,4},{4,2},{6,0},{1,7},{3,5},{5,3},{7,1},{8,14},{10,12},{12... | collective-permute-start | bytes 6152 | tf_op jit(solution)/shard_map/ppermute | solution.py:312
  16.9 7.3 %collective-permute-start.3 = (bf16[256,256]{1,0:T(8,128)(2,1)S(1)}, bf16[256,256]{1,0:T(8,128)(2,1)S(1)}, u32[]{:S(2)}, u32[]{:S(2)}) collective-permute-start(bf16[256,256]{1,0:T(8,128)(2,1)S(1)} %get-tuple-element.49), channel_id=1, source_target_pairs={{0,8},{8,0},{16,24},{24,16},{1,9},{9,1},{17,25},{25,17},{2,10},{10... | collective-permute-start | bytes 393224 | tf_op jit(solution)/shard_map/ppermute | solution.py:312
  18.5 9.5 %collective-permute-start.4 = (bf16[256,256]{1,0:T(8,128)(2,1)S(1)}, bf16[256,256]{1,0:T(8,128)(2,1)S(1)}, u32[]{:S(2)}, u32[]{:S(2)}) collective-permute-start(bf16[256,256]{1,0:T(8,128)(2,1)S(1)} %get-tuple-element.49), channel_id=1, source_target_pairs={{0,16},{8,24},{16,0},{24,8},{1,17},{9,25},{17,1},{25,9},{2,18},{10... | collective-permute-start | bytes 393224 | tf_op jit(solution)/shard_map/ppermute | solution.py:312
  20.0 8.0 %collective-permute-start.5 = (bf16[256,256]{1,0:T(8,128)(2,1)S(1)}, bf16[256,256]{1,0:T(8,128)(2,1)S(1)}, u32[]{:S(2)}, u32[]{:S(2)}) collective-permute-start(bf16[256,256]{1,0:T(8,128)(2,1)S(1)} %get-tuple-element.49), channel_id=1, source_target_pairs={{0,24},{8,16},{16,8},{24,0},{1,25},{9,17},{17,9},{25,1},{2,26},{10... | collective-permute-start | bytes 393224 | tf_op jit(solution)/shard_map/ppermute | solution.py:312
  21.1 7.5 %collective-permute-start.6 = (bf16[256,256]{1,0:T(8,128)(2,1)S(1)}, bf16[256,256]{1,0:T(8,128)(2,1)S(1)}, u32[]{:S(2)}, u32[]{:S(2)}) collective-permute-start(bf16[256,256]{1,0:T(8,128)(2,1)S(1)} %get-tuple-element.50), channel_id=1, source_target_pairs={{0,8},{8,0},{16,24},{24,16},{1,9},{9,1},{17,25},{25,17},{2,10},{10... | collective-permute-start | bytes 393224 | tf_op jit(solution)/shard_map/ppermute | solution.py:312
  22.6 8.6 %collective-permute-start.7 = (bf16[256,256]{1,0:T(8,128)(2,1)S(1)}, bf16[256,256]{1,0:T(8,128)(2,1)S(1)}, u32[]{:S(2)}, u32[]{:S(2)}) collective-permute-start(bf16[256,256]{1,0:T(8,128)(2,1)S(1)} %get-tuple-element.50), channel_id=1, source_target_pairs={{0,16},{8,24},{16,0},{24,8},{1,17},{9,25},{17,1},{25,9},{2,18},{10... | collective-permute-start | bytes 393224 | tf_op jit(solution)/shard_map/ppermute | solution.py:312
  24.1 7.1 %collective-permute-start.8 = (bf16[256,256]{1,0:T(8,128)(2,1)S(1)}, bf16[256,256]{1,0:T(8,128)(2,1)S(1)}, u32[]{:S(2)}, u32[]{:S(2)}) collective-permute-start(bf16[256,256]{1,0:T(8,128)(2,1)S(1)} %get-tuple-element.50), channel_id=1, source_target_pairs={{0,24},{8,16},{16,8},{24,0},{1,25},{9,17},{17,9},{25,1},{2,26},{10... | collective-permute-start | bytes 393224 | tf_op jit(solution)/shard_map/ppermute | solution.py:312
  36.1 7.9 %collective-permute-start.9 = (bf16[2,192,256]{2,1,0:T(8,128)(2,1)S(1)}, bf16[2,192,256]{2,1,0:T(8,128)(2,1)S(1)}, u32[]{:S(2)}, u32[]{:S(2)}) collective-permute-start(bf16[2,192,256]{2,1,0:T(8,128)(2,1)S(1)} %get-tuple-element.56), channel_id=1, source_target_pairs={{0,8},{8,0},{16,24},{24,16},{1,9},{9,1},{17,25},{25,17},{2,10},{10... | collective-permute-start | bytes 589832 | tf_op jit(solution)/shard_map/ppermute | solution.py:312
  37.0 21.2 %collective-permute-start.12 = (bf16[2,256,256]{2,1,0:T(8,128)(2,1)S(1)}, bf16[2,256,256]{2,1,0:T(8,128)(2,1)S(1)}, u32[]{:S(2)}, u32[]{:S(2)}) collective-permute-start(bf16[2,256,256]{2,1,0:T(8,128)(2,1)S(1)} %get-tuple-element.64), channel_id=1, source_target_pairs={{0,8},{8,0},{16,24},{24,16},{1,9},{9,1},{17,25},{25,17},{2,10},{10... | collective-permute-start | bytes 786440 | tf_op jit(solution)/shard_map/ppermute | solution.py:312
  38.9 19.3 %collective-permute-start.13 = (bf16[2,256,256]{2,1,0:T(8,128)(2,1)S(1)}, bf16[2,256,256]{2,1,0:T(8,128)(2,1)S(1)}, u32[]{:S(2)}, u32[]{:S(2)}) collective-permute-start(bf16[2,256,256]{2,1,0:T(8,128)(2,1)S(1)} %get-tuple-element.65), channel_id=1, source_target_pairs={{0,16},{8,24},{16,0},{24,8},{1,17},{9,25},{17,1},{25,9},{2,18},{10... | collective-permute-start | bytes 786440 | tf_op jit(solution)/shard_map/ppermute | solution.py:312
  39.9 18.3 %collective-permute-start.14 = (bf16[2,256,256]{2,1,0:T(8,128)(2,1)S(1)}, bf16[2,256,256]{2,1,0:T(8,128)(2,1)S(1)}, u32[]{:S(2)}, u32[]{:S(2)}) collective-permute-start(bf16[2,256,256]{2,1,0:T(8,128)(2,1)S(1)} %get-tuple-element.66), channel_id=1, source_target_pairs={{0,24},{8,16},{16,8},{24,0},{1,25},{9,17},{17,9},{25,1},{2,26},{10... | collective-permute-start | bytes 786440 | tf_op jit(solution)/shard_map/ppermute | solution.py:312
  40.5 17.5 %collective-permute-start.10 = (bf16[2,192,256]{2,1,0:T(8,128)(2,1)S(1)}, bf16[2,192,256]{2,1,0:T(8,128)(2,1)S(1)}, u32[]{:S(2)}, u32[]{:S(2)}) collective-permute-start(bf16[2,192,256]{2,1,0:T(8,128)(2,1)S(1)} %get-tuple-element.57), channel_id=1, source_target_pairs={{0,16},{8,24},{16,0},{24,8},{1,17},{9,25},{17,1},{25,9},{2,18},{10... | collective-permute-start | bytes 589832 | tf_op jit(solution)/shard_map/ppermute | solution.py:312
  44.0 14.1 %collective-permute-start.11 = (bf16[2,192,256]{2,1,0:T(8,128)(2,1)S(1)}, bf16[2,192,256]{2,1,0:T(8,128)(2,1)S(1)}, u32[]{:S(2)}, u32[]{:S(2)}) collective-permute-start(bf16[2,192,256]{2,1,0:T(8,128)(2,1)S(1)} %get-tuple-element.58), channel_id=1, source_target_pairs={{0,24},{8,16},{16,8},{24,0},{1,25},{9,17},{17,9},{25,1},{2,26},{10... | collective-permute-start | bytes 589832 | tf_op jit(solution)/shard_map/ppermute | solution.py:312
  59.2 3.6 %collective-permute-start.15 = (bf16[1024,128]{1,0:T(8,128)(2,1)S(1)}, bf16[1024,128]{1,0:T(8,128)(2,1)S(1)}, u32[]{:S(2)}, u32[]{:S(2)}) collective-permute-start(bf16[1024,128]{1,0:T(8,128)(2,1)S(1)} %get-tuple-element.68), channel_id=1, source_target_pairs={{0,1},{1,0},{2,3},{3,2},{4,5},{5,4},{6,7},{7,6},{8,9},{9,8},{10,11... | collective-permute-start | bytes 786440 | tf_op jit(solution)/shard_map/ppermute | solution.py:317
  59.3 5.0 %collective-permute-start.16 = (bf16[2,64,256]{2,1,0:T(8,128)(2,1)S(1)}, bf16[2,64,256]{2,1,0:T(8,128)(2,1)S(1)}, u32[]{:S(2)}, u32[]{:S(2)}) collective-permute-start(bf16[2,64,256]{2,1,0:T(8,128)(2,1)S(1)} %get-tuple-element.61.refs_4_), channel_id=1, source_target_pairs={{0,8},{8,0},{16,24},{24,16},{1,9},{9,1},{17,25},{25,17},{2,10},{10... | collective-permute-start | bytes 196616 | tf_op jit(solution)/shard_map/ppermute | solution.py:312
  59.7 6.7 %collective-permute-start.17 = (bf16[2,64,256]{2,1,0:T(8,128)(2,1)S(1)}, bf16[2,64,256]{2,1,0:T(8,128)(2,1)S(1)}, u32[]{:S(2)}, u32[]{:S(2)}) collective-permute-start(bf16[2,64,256]{2,1,0:T(8,128)(2,1)S(1)} %get-tuple-element.62.refs_5_), channel_id=1, source_target_pairs={{0,16},{8,24},{16,0},{24,8},{1,17},{9,25},{17,1},{25,9},{2,18},{10... | collective-permute-start | bytes 196616 | tf_op jit(solution)/shard_map/ppermute | solution.py:312
  60.7 5.8 %collective-permute-start.18 = (bf16[2,64,256]{2,1,0:T(8,128)(2,1)S(1)}, bf16[2,64,256]{2,1,0:T(8,128)(2,1)S(1)}, u32[]{:S(2)}, u32[]{:S(2)}) collective-permute-start(bf16[2,64,256]{2,1,0:T(8,128)(2,1)S(1)} %get-tuple-element.63.refs_6_), channel_id=1, source_target_pairs={{0,24},{8,16},{16,8},{24,0},{1,25},{9,17},{17,9},{25,1},{2,26},{10... | collective-permute-start | bytes 196616 | tf_op jit(solution)/shard_map/ppermute | solution.py:312
  62.9 17.1 %collective-permute-start.22 = (bf16[1040,128]{1,0:T(8,128)(2,1)S(1)}, bf16[1040,128]{1,0:T(8,128)(2,1)S(1)}, u32[]{:S(2)}, u32[]{:S(2)}) collective-permute-start(bf16[1040,128]{1,0:T(8,128)(2,1)S(1)} %shard_map.144.refs_0_), channel_id=1, source_target_pairs={{0,8},{8,0},{16,24},{24,16},{1,9},{9,1},{17,25},{25,17},{2,10},{10... | collective-permute-start | bytes 798728 | tf_op jit(solution)/shard_map/ppermute | solution.py:312
  63.3 16.7 %collective-permute-start.23 = (bf16[1040,128]{1,0:T(8,128)(2,1)S(1)}, bf16[1040,128]{1,0:T(8,128)(2,1)S(1)}, u32[]{:S(2)}, u32[]{:S(2)}) collective-permute-start(bf16[1040,128]{1,0:T(8,128)(2,1)S(1)} %shard_map.144.refs_0_), channel_id=1, source_target_pairs={{0,16},{8,24},{16,0},{24,8},{1,17},{9,25},{17,1},{25,9},{2,18},{10... | collective-permute-start | bytes 798728 | tf_op jit(solution)/shard_map/ppermute | solution.py:312
  64.3 15.7 %collective-permute-start.24 = (bf16[1040,128]{1,0:T(8,128)(2,1)S(1)}, bf16[1040,128]{1,0:T(8,128)(2,1)S(1)}, u32[]{:S(2)}, u32[]{:S(2)}) collective-permute-start(bf16[1040,128]{1,0:T(8,128)(2,1)S(1)} %shard_map.144.refs_0_), channel_id=1, source_target_pairs={{0,24},{8,16},{16,8},{24,0},{1,25},{9,17},{17,9},{25,1},{2,26},{10... | collective-permute-start | bytes 798728 | tf_op jit(solution)/shard_map/ppermute | solution.py:312
  71.0 4.5 %collective-permute-start.20 = (f32[2,256]{1,0:T(2,128)S(1)}, f32[2,256]{1,0:T(2,128)S(1)}, u32[]{:S(2)}, u32[]{:S(2)}) collective-permute-start(f32[2,256]{1,0:T(2,128)S(1)} %get-tuple-element.74.refs_7_), channel_id=1, source_target_pairs={{0,4},{2,6},{4,0},{6,2},{1,5},{3,7},{5,1},{7,3},{8,12},{10,14},{12... | collective-permute-start | bytes 6152 | tf_op jit(solution)/shard_map/ppermute | solution.py:312
  74.6 5.4 %collective-permute-start.21 = (f32[2,256]{1,0:T(2,128)S(1)}, f32[2,256]{1,0:T(2,128)S(1)}, u32[]{:S(2)}, u32[]{:S(2)}) collective-permute-start(f32[2,256]{1,0:T(2,128)S(1)} %get-tuple-element.74.refs_7_), channel_id=1, source_target_pairs={{0,6},{2,4},{4,2},{6,0},{1,7},{3,5},{5,3},{7,1},{8,14},{10,12},{12... | collective-permute-start | bytes 6152 | tf_op jit(solution)/shard_map/ppermute | solution.py:312
  (12 other events, 89.7 us)

commit v3 on v2

--- a/solution.py
+++ b/solution.py
@@ -219,25 +219,6 @@
         compiler_params=pltpu.CompilerParams(vmem_limit_bytes=vmem * 2**20),
         cost_estimate=cost_of(micros),
     )(*ins, *after)
-
-
-def grid_call(body, steps, outs, in_specs, out_specs, scratch, ids, *ins, micros=1.0, after=()):
-    skip = len(after)
-    return pl.pallas_call(
-        lambda ids_ref, *refs: body(ids_ref, *refs[skip:]),
-        out_shape=outs,
-        grid_spec=pltpu.PrefetchScalarGridSpec(
-            num_scalar_prefetch=1,
-            grid=(steps,),
-            in_specs=[pl.BlockSpec(memory_space=pl.ANY)] * skip + list(in_specs),
-            out_specs=out_specs,
-            scratch_shapes=scratch,
-        ),
-        compiler_params=pltpu.CompilerParams(
-            vmem_limit_bytes=40 * 2**20, dimension_semantics=("arbitrary",)
-        ),
-        cost_estimate=cost_of(micros),
-    )(ids, *after, *ins)
 
 
 def row_order(rows):
@@ -322,22 +303,15 @@
     do = grad_out[0]
     qg = query_gain.reshape(1, cols)
     kg = key_gain.reshape(1, cols)
-    full = lambda a: pl.BlockSpec(a.shape, lambda i, ids: (0,) * len(a.shape))
-    own_cols = pl.BlockSpec((rows, wide), lambda i, ids: (0, i))
-    rel_cols = pl.BlockSpec((rows, wide), lambda i, ids: (0, ids[0] ^ i))
-    rel_mem = pl.BlockSpec((slots, wide), lambda i, ids: (ids[0] ^ i, 0))
-    own_mem = pl.BlockSpec((slots, wide), lambda i, ids: (i, 0))
-
-    def squares_body(q_ref, k_ref, ss_ref, kp_ref):
-        kp = dot(row_order(rows), k_ref[...])
-        kp_ref[...] = kp.astype(BF16)
+
+    def squares_body(q_ref, k_ref, ss_ref):
         qf = q_ref[...].astype(F32)
         ss_ref[0:1, :] = lane_sum_row(fold_lanes(qf * qf))
-        ss_ref[1:2, :] = lane_sum_row(fold_lanes(kp * kp))
-
-    ss, kp = whole_call(
-        squares_body, (sds((2, rows), F32), sds((rows, cols), BF16)), q, k, micros=1.2, vmem=62
-    )
+        kf = k_ref[...].astype(F32)
+        ss_ref[1:2, :] = lane_sum_row(fold_lanes(kf * kf))
+
+    two_rows = sds((2, rows), F32)
+    ss = whole_call(squares_body, two_rows, q, k, micros=1.5, vmem=62)
     ss_peers = to_peers("head", [ss] * (n_head - 1))
 
     def compress(source, w_ref, out_ref):
@@ -354,60 +328,65 @@
                 block * slots : (block + 1) * slots, (h % hp) * HD : (h % hp + 1) * HD
             ] = total.astype(BF16)
 
-    def values_body(v_ref, w_ref, vp_ref, mem_ref):
-        vp_ref[...] = dot(row_order(rows), v_ref[...]).astype(BF16)
+    def values_body(v_ref, k_ref, w_ref, vp_ref, mem_ref, kp_ref):
+        order = row_order(rows)
+        vp_ref[...] = dot(order, v_ref[...]).astype(BF16)
         compress(vp_ref, w_ref, mem_ref)
+        kp_ref[...] = dot(order, k_ref[...]).astype(BF16)
 
     rows_shape = sds((rows, cols), BF16)
     mem_shape = sds((mem_rows, wide), BF16)
-    vp, mem_v = whole_call(
-        values_body, (rows_shape, mem_shape), v, value_squeeze, after=(ss_peers[0],), micros=0.6
-    )
-    mv_recv = to_peers("seq", [mem_v] * (n_seq - 1))
-
-    def keys_body(q_ref, kp_ref, qg_ref, kg_ref, w_ref, *rest):
+    vp, mem_v, kp = whole_call(
+        values_body,
+        (rows_shape, mem_shape, rows_shape),
+        v, k, value_squeeze,
+        micros=0.8,
+    )
+
+    def keys_body(q_ref, k_ref, qg_ref, kg_ref, w_ref, mem_v_ref, *rest):
         ss_refs = rest[:n_head]
         inv_ref, qn_ref, kn_ref, mem_ref = rest[n_head:]
         total = ss_refs[0][...]
         for other in ss_refs[1:]:
             total = total + other[...]
-        inv = lax.rsqrt(total / full_width + epsilon)
-        inv_ref[...] = inv
-        inv_c = as_columns(inv)
-        kn_ref[...] = (kp_ref[...].astype(F32) * inv_c[:, 1:2] * kg_ref[...]).astype(BF16)
-        compress(kn_ref, w_ref, mem_ref)
+        natural = as_columns(lax.rsqrt(total / full_width + epsilon))
+        order = row_order(rows)
+        high = natural.astype(BF16)
+        rest_1 = natural - high.astype(F32)
+        middle = rest_1.astype(BF16)
+        low = (rest_1 - middle.astype(F32)).astype(BF16)
+        ordered = dot(order, high) + dot(order, middle) + dot(order, low)
+        inv_c = jnp.concatenate([natural[:, 0:1], ordered[:, 1:2], natural[:, 2:]], axis=1)
+        inv_ref[...] = inv_c.T[:2]
+        normed = (k_ref[...].astype(F32) * natural[:, 1:2] * kg_ref[...]).astype(BF16)
+        kn_ref[...] = dot(order, normed).astype(BF16)
+        compress(kn_ref, w_ref, mem_ref.at[0])
+        mem_ref[1] = mem_v_ref[...]
         qn_ref[...] = (q_ref[...].astype(F32) * inv_c[:, 0:1] * qg_ref[...]).astype(BF16)
 
-    inv, qn, kn, mem_k = whole_call(
+    mem_pair = sds((2, mem_rows, wide), BF16)
+    inv, qn, kn, mem = whole_call(
         keys_body,
-        (sds((2, rows), F32), rows_shape, rows_shape, mem_shape),
-        q, kp, qg, kg, key_squeeze, ss, *ss_peers,
+        (sds((2, rows), F32), rows_shape, rows_shape, mem_pair),
+        q, k, qg, kg, key_squeeze, mem_v, ss, *ss_peers,
         micros=1.5,
     )
-    mk_recv = to_peers("seq", [mem_k] * (n_seq - 1))
-
-    def local_body(ids_ref, qn_ref, kn_ref, vp_ref, do_ref, st_ref):
+    mem_recv = to_peers("seq", [mem] * (n_seq - 1))
+
+    def local_body(qn_ref, kn_ref, vp_ref, do_ref, st_ref):
         allowed = causal_t(rows)
-        for i in range(hp):
-            at = slice(i * HD, (i + 1) * HD)
+        for h in range(heads):
+            at = slice(h * HD, (h + 1) * HD)
             s = jnp.where(allowed, dot(kn_ref[:, at], qn_ref[:, at], NT) * scale, -jnp.inf)
             g = dot(vp_ref[:, at], do_ref[:, at], NT)
             m = jnp.max(s, axis=0, keepdims=True)
             p = jnp.exp(s - m)
-            st_ref[i, 0:1, :] = m
-            st_ref[i, 1:2, :] = jnp.sum(p, axis=0, keepdims=True)
-            st_ref[i, 2:3, :] = jnp.sum(p * g, axis=0, keepdims=True)
-
-    (stats,) = grid_call(
-        local_body,
-        n_seq,
-        (sds((heads, 8, rows), F32),),
-        [own_cols] * 4,
-        (pl.BlockSpec((hp, 8, rows), lambda i, ids: (i, 0, 0)),),
-        [],
-        ids, qn, kn, vp, do,
-        micros=2.6,
-    )
+            st_ref[h, 0:1, :] = m
+            st_ref[h, 1:2, :] = jnp.sum(p, axis=0, keepdims=True)
+            st_ref[h, 2:3, :] = jnp.sum(p * g, axis=0, keepdims=True)
+
+    stat_shape = sds((heads, 8, rows), F32)
+    stats = whole_call(local_body, stat_shape, qn, kn, vp, do, micros=0.5)
 
     def rows_body(ids_ref, kn_ref, vp_ref, *sends):
         for r, send in zip(peers, sends):
@@ -423,127 +402,92 @@
     rows_recv = to_peers("seq", row_sends)
 
     def memory_body(ids_ref, qn_ref, do_ref, st_ref, *rest):
-        mk_refs = rest[: n_seq - 1]
-        mv_refs = rest[n_seq - 1 : 2 * n_seq - 2]
-        st2_ref, ds_ref = rest[2 * n_seq - 2 : 2 * n_seq]
-        parts = rest[2 * n_seq :]
-        step = pl.program_id(0)
+        mem_refs = rest[: n_seq - 1]
+        st2_ref, ds_ref = rest[n_seq - 1 : n_seq + 1]
+        parts = rest[n_seq + 1 :]
         mine = ids_ref[0]
-        for i in range(hp):
-            at = slice(i * HD, (i + 1) * HD)
-            qn_h = qn_ref[:, at]
-            do_h = do_ref[:, at]
-            mk = jnp.concatenate([ref[:, at] for ref in mk_refs], axis=0)
-            mv = jnp.concatenate([ref[:, at] for ref in mv_refs], axis=0)
-            raw = dot(mk, qn_h, NT) * scale
-            s = jnp.concatenate(
-                [
-                    jnp.where((mine ^ r) < mine, raw[(r - 1) * slots : r * slots], -jnp.inf)
-                    for r in peers
-                ],
-                axis=0,
-            )
-            g = dot(mv, do_h, NT)
-            m_loc, l_loc, d_loc = st_ref[i, 0:1, :], st_ref[i, 1:2, :], st_ref[i, 2:3, :]
-            m = jnp.maximum(m_loc, jnp.max(s, axis=0, keepdims=True))
-            p = jnp.exp(s - m)
-            shrink = jnp.exp(m_loc - m)
-            mass = l_loc * shrink + jnp.sum(p, axis=0, keepdims=True)
-            inv_mass = 1.0 / mass
-            delta = (d_loc * shrink + jnp.sum(p * g, axis=0, keepdims=True)) * inv_mass
-            st2_ref[i, 0:1, :] = m
-            st2_ref[i, 1:2, :] = inv_mass
-            st2_ref[i, 2:3, :] = delta
-            attend = p * inv_mass
-            ds = (attend * (g - delta)).astype(BF16)
-            ds_ref[i] = ds
-            gk = (dot(ds, qn_h) * scale).astype(BF16)
-            gv = dot(attend.astype(BF16), do_h).astype(BF16)
-            for r in range(n_seq):
-                @pl.when(step == r)
-                def _(r=r):
-                    parts[r][0, :, at] = gk
-                    parts[r][1, :, at] = gv
+        for r in range(n_seq):
+            block = mine ^ r
+            span = pl.ds(pl.multiple_of(block * slots, slots), slots)
+            for i in range(hp):
+                at = slice(i * HD, (i + 1) * HD)
+                h = block * hp + i
+                wide_at = pl.ds(pl.multiple_of(h * HD, HD), HD)
+                qn_h = qn_ref[:, wide_at]
+                do_h = do_ref[:, wide_at]
+                mk = jnp.concatenate([ref[0, span, at] for ref in mem_refs], axis=0)
+                mv = jnp.concatenate([ref[1, span, at] for ref in mem_refs], axis=0)
+                raw = dot(mk, qn_h, NT) * scale
+                s = jnp.concatenate(
+                    [
+                        jnp.where((mine ^ src) < mine, raw[(src - 1) * slots : src * slots], -jnp.inf)
+                        for src in peers
+                    ],
+                    axis=0,
+                )
+                g = dot(mv, do_h, NT)
+                stat = st_ref[h]
+                m_loc, l_loc, d_loc = stat[0:1], stat[1:2], stat[2:3]
+                m = jnp.maximum(m_loc, jnp.max(s, axis=0, keepdims=True))
+                p = jnp.exp(s - m)
+                shrink = jnp.exp(m_loc - m)
+                mass = l_loc * shrink + jnp.sum(p, axis=0, keepdims=True)
+                inv_mass = 1.0 / mass
+                delta = (d_loc * shrink + jnp.sum(p * g, axis=0, keepdims=True)) * inv_mass
+                st2_ref[h] = jnp.concatenate([m, inv_mass, delta, stat[3:]], axis=0)
+                attend = p * inv_mass
+                ds = (attend * (g - delta)).astype(BF16)
+                ds_ref[h] = ds
+                parts[r][0, :, at] = (dot(ds, qn_h) * scale).astype(BF16)
+                parts[r][1, :, at] = dot(attend.astype(BF16), do_h).astype(BF16)
 
     part = sds((2, n_mem, wide), BF16)
-    rel_stat = pl.BlockSpec((hp, 8, rows), lambda i, ids: (ids[0] ^ i, 0, 0))
-    stats2, ds_mem, *parts = grid_call(
+    stats2, ds_mem, *parts = whole_call(
         memory_body,
-        n_seq,
-        (sds((heads, 8, rows), F32), sds((heads, n_mem, rows), BF16)) + (part,) * n_seq,
-        [rel_cols, rel_cols, rel_stat] + [rel_mem] * (2 * n_seq - 2),
-        (
-            rel_stat,
-            pl.BlockSpec((hp, n_mem, rows), lambda i, ids: (ids[0] ^ i, 0, 0)),
-        )
-        + (full(part),) * n_seq,
-        [],
-        ids, qn, do, stats, *mk_recv, *mv_recv,
-        micros=4.8,
+        (stat_shape, sds((heads, n_mem, rows), BF16)) + (part,) * n_seq,
+        ids, qn, do, stats, *mem_recv,
+        micros=0.5,
     )
     parts_recv = to_peers("seq", parts[1:])
 
-    def grads_body(ids_ref, q_ref, kp_ref, qn_ref, kn_ref, vp_ref, do_ref, st_ref, ds_ref, *rest):
-        mk_refs = rest[: n_seq - 1]
-        inv_ref, qg_ref, gq_ref, gk_ref, gv_ref, dq_ref, gain_q_ref, gain_k_ref, acc = rest[
-            n_seq - 1 :
-        ]
-        step = pl.program_id(0)
+    def grads_body(q_ref, kp_ref, qn_ref, kn_ref, vp_ref, do_ref, st_ref, ds_ref, *rest):
+        mem_refs = rest[: n_seq - 1]
+        inv_ref, qg_ref, gq_ref, gk_ref, gv_ref, dq_ref, gain_q_ref, gain_k_ref = rest[n_seq - 1 :]
         allowed = causal_t(rows)
         inv_c = as_columns(inv_ref[...])
-
-        @pl.when(step == 0)
-        def _():
-            acc[...] = jnp.zeros_like(acc)
-
-        total = acc[...]
-        for i in range(hp):
-            at = slice(i * HD, (i + 1) * HD)
+        total = jnp.zeros((rows, HD), F32)
+        for h in range(heads):
+            at = slice(h * HD, (h + 1) * HD)
+            narrow = slice((h % hp) * HD, (h % hp + 1) * HD)
+            span = slice((h // hp) * slots, (h // hp + 1) * slots)
             qn_h, kn_h, do_h = qn_ref[:, at], kn_ref[:, at], do_ref[:, at]
             s = jnp.where(allowed, dot(kn_h, qn_h, NT) * scale, -jnp.inf)
             g = dot(vp_ref[:, at], do_h, NT)
-            m, inv_mass, delta = st_ref[i, 0:1, :], st_ref[i, 1:2, :], st_ref[i, 2:3, :]
+            m, inv_mass, delta = st_ref[h, 0:1, :], st_ref[h, 1:2, :], st_ref[h, 2:3, :]
             attend = jnp.exp(s - m) * inv_mass
             ds = (attend * (g - delta)).astype(BF16)
-            mk = jnp.concatenate([ref[:, at] for ref in mk_refs], axis=0)
-            gq = scale * (dot(ds, kn_h, TN) + dot(ds_ref[i], mk, TN))
+            mk = jnp.concatenate([ref[0, span, narrow] for ref in mem_refs], axis=0)
+            gq = scale * (dot(ds, kn_h, TN) + dot(ds_ref[h], mk, TN))
             gk = scale * dot(ds, qn_h)
             gq_ref[:, at] = gq
             gk_ref[:, at] = gk
             gv_ref[:, at] = dot(attend.astype(BF16), do_h)
-            q_h = q_ref[:, at].astype(F32)
-            k_h = kp_ref[:, at].astype(F32)
-            gq_q = gq * q_h
+            gq_q = gq * q_ref[:, at].astype(F32)
+            gk_k = gk * kp_ref[:, at].astype(F32)
             total = total + gq_q * qg_ref[:, at]
-            gain_q_ref[0, i : i + 1, :] = jnp.sum(gq_q * inv_c[:, 0:1], axis=0, keepdims=True)
-            gain_k_ref[0, i : i + 1, :] = jnp.sum(
-                gk * k_h * inv_c[:, 1:2], axis=0, keepdims=True
-            )
-        acc[...] = total
-
-        @pl.when(step == n_seq - 1)
-        def _():
-            dq_ref[...] = lane_sum_row(acc[...])
-
-    gain_rows = sds((n_seq, hp, HD), F32)
-    gain_spec = pl.BlockSpec((1, hp, HD), lambda i, ids: (i, 0, 0))
+            gain_q_ref[h : h + 1, :] = jnp.sum(gq_q * inv_c[:, 0:1], axis=0, keepdims=True)
+            gain_k_ref[h : h + 1, :] = jnp.sum(gk_k * inv_c[:, 1:2], axis=0, keepdims=True)
+        dq_ref[...] = lane_sum_row(total)
+
+    gain_rows = sds((heads, HD), F32)
     wide_f32 = sds((rows, cols), F32)
     dot_row = sds((1, rows), F32)
-    gq, gk_local, gv_local, dot_q, gain_q, gain_k = grid_call(
+    gq, gk_local, gv_local, dot_q, gain_q, gain_k = whole_call(
         grads_body,
-        n_seq,
         (wide_f32, wide_f32, wide_f32, dot_row, gain_rows, gain_rows),
-        [own_cols] * 6
-        + [
-            pl.BlockSpec((hp, 8, rows), lambda i, ids: (i, 0, 0)),
-            pl.BlockSpec((hp, n_mem, rows), lambda i, ids: (i, 0, 0)),
-        ]
-        + [own_mem] * (n_seq - 1)
-        + [full(inv), pl.BlockSpec((1, wide), lambda i, ids: (0, i))],
-        (own_cols, own_cols, own_cols, full(dot_row), gain_spec, gain_spec),
-        [pltpu.VMEM((rows, HD), F32)],
-        ids, q, kp, qn, kn, vp, do, stats2, ds_mem, *mk_recv, inv, qg,
-        micros=5.8,
+        q, kp, qn, kn, vp, do, stats2, ds_mem, *mem_recv, inv, qg,
+        micros=0.5,
+        after=tuple(rows_recv),
     )
 
     def slots_body(*refs):
@@ -599,65 +543,77 @@
 
     def chunk_body(a_ref, b_ref, gq_ref, gk_ref, out_ref):
         out_ref[:span_rows, :] = (a_ref[...] + b_ref[...].astype(F32)).astype(BF16)
-        rows_q = [gq_ref[i] for i in range(n_seq)]
-        rows_k = [gk_ref[i] for i in range(n_seq)]
-        out_ref[span_rows:, :] = jnp.concatenate(rows_q + rows_k, axis=0).astype(BF16)
+        gains = jnp.concatenate([gq_ref[...], gk_ref[...]], axis=0)
+        out_ref[span_rows:, :] = gains.astype(BF16)
 
     chunk_shape = sds((span_rows + 2 * heads, HD), BF16)
     chunk = whole_call(chunk_body, chunk_shape, w_same, w_recv, gain_q, gain_k, micros=0.3)
     chunks = [chunk] + to_peers("seq", [chunk] * (n_seq - 1))
 
+    def send_out(buffer, target, sems, index, at):
+        copy = pltpu.make_async_copy(buffer.at[:, at], target.at[:, at], sems.at[index])
+        copy.start()
+        return copy
+
+    def column_out(body, outs, n_out, *ins, micros, after=()):
+        skip = len(after)
+        inside = pl.BlockSpec(memory_space=pltpu.VMEM)
+        small = len(outs) - n_out
+        return pl.pallas_call(
+            lambda *refs: body(*refs[: len(ins)], *refs[len(ins) + skip :]),
+            out_shape=outs,
+            in_specs=[
+                pl.BlockSpec(memory_space=pltpu.SMEM) if a.dtype == jnp.int32 else inside
+                for a in ins
+            ]
+            + [pl.BlockSpec(memory_space=pl.ANY)] * skip,
+            out_specs=(inside,) * small + (pl.BlockSpec(memory_space=pl.ANY),) * n_out,
+            scratch_shapes=[pltpu.VMEM((rows, cols), BF16)] * n_out
+            + [pltpu.SemaphoreType.DMA((n_out, n_seq))],
+            compiler_params=pltpu.CompilerParams(vmem_limit_bytes=40 * 2**20),
+            cost_estimate=cost_of(micros),
+        )(*ins, *after)
+
     def back_body(ids_ref, gk_ref, gv_ref, kp_ref, wk_ref, wv_ref, kg_ref, dq_ref, *rest):
         gm = rest[:n_seq]
-        value_ref, gkn_ref, dots_ref, acc = rest[n_seq:]
-        step = pl.program_id(0)
+        gkn_ref, dots_ref, value_ref, buffer, sems = rest[n_seq:]
         unorder = row_order_back(rows)
-
-        @pl.when(step == 0)
-        def _():
-            acc[...] = jnp.zeros_like(acc)
-
-        total = acc[...]
-        mine = gm[0][...]
-        for r in peers:
-            mine = jnp.where(step == r, gm[r][...], mine)
-        for i in range(hp):
-            at = slice(i * HD, (i + 1) * HD)
-            sides = []
-            for tensor, w_ref in ((0, wk_ref), (1, wv_ref)):
-                spread = dot(mine[tensor][:, at], w_ref[i], NT)
-                sides.append(
-                    jnp.concatenate(
-                        [spread[:, j * HD : (j + 1) * HD] for j in range(KS)], axis=0
+        total = jnp.zeros((rows, HD), F32)
+        copies = []
+        for r in range(n_seq):
+            block = ids_ref[0] ^ r
+            for i in range(hp):
+                narrow = slice(i * HD, (i + 1) * HD)
+                h = block * hp + i
+                at = pl.ds(pl.multiple_of(h * HD, HD), HD)
+                sides = []
+                for tensor, w_ref in ((0, wk_ref), (1, wv_ref)):
+                    spread = dot(gm[r][tensor, :, narrow], w_ref[h], NT)
+                    sides.append(
+                        jnp.concatenate(
+                            [spread[:, j * HD : (j + 1) * HD] for j in range(KS)], axis=0
+                        )
                     )
-                )
-            gkn = gk_ref[:, at] + sides[0]
-            gkn_ref[:, at] = gkn
-            total = total + gkn * kp_ref[:, at].astype(F32) * kg_ref[:, at]
-            value = (gv_ref[:, at] + sides[1]).astype(BF16)
-            value_ref[:, at] = dot(unorder, value).astype(BF16)
-        acc[...] = total
-
-        @pl.when(step == n_seq - 1)
-        def _():
-            dots_ref[0:1, :] = dq_ref[...]
-            dots_ref[1:2, :] = lane_sum_row(acc[...])
-
-    rel_w = pl.BlockSpec((hp, KS * HD, HD), lambda i, ids: (ids[0] ^ i, 0, 0))
-    two_rows = sds((2, rows), F32)
-    grad_value, gkn, dots = grid_call(
+                gkn = gk_ref[:, at] + sides[0]
+                gkn_ref[:, at] = gkn
+                total = total + gkn * kp_ref[:, at].astype(F32) * kg_ref[:, at]
+                value = (gv_ref[:, at] + sides[1]).astype(BF16)
+                buffer[:, at] = dot(unorder, value).astype(BF16)
+            wide_at = pl.ds(pl.multiple_of(block * wide, wide), wide)
+            copies.append(send_out(buffer, value_ref, sems.at[0], r, wide_at))
+        dots_ref[0:1, :] = dq_ref[...]
+        dots_ref[1:2, :] = lane_sum_row(total)
+        for copy in copies:
+            copy.wait()
+
+    gkn, dots, grad_value = column_out(
         back_body,
-        n_seq,
-        (sds((rows, cols), BF16), wide_f32, two_rows),
-        [rel_cols, rel_cols, rel_cols, rel_w, rel_w]
-        + [pl.BlockSpec((1, wide), lambda i, ids: (0, ids[0] ^ i)), full(dot_q)]
-        + [full(slot_grad)] * n_seq,
-        (rel_cols, rel_cols, full(two_rows)),
-        [pltpu.VMEM((rows, HD), F32)],
+        (wide_f32, two_rows, rows_shape),
+        1,
         ids, gk_local, gv_local, kp, key_squeeze, value_squeeze, kg, dot_q,
         slot_grads[0], *slots_recv,
+        micros=3.0,
         after=(chunk,),
-        micros=4.5,
     )
     dots_peers = to_peers("head", [dots] * (n_head - 1))
 
@@ -666,81 +622,99 @@
             refs[n_seq][r] = refs[r][...]
 
     packed_shape = sds((n_seq,) + chunk_shape.shape, BF16)
-    packed = whole_call(pack_body, packed_shape, *chunks, after=tuple(dots_peers), micros=1.0)
+    packed = whole_call(pack_body, packed_shape, *chunks, micros=0.1, after=(dots_peers[0],))
     packed_other = to_core(packed)
 
-    def norms_body(ids_ref, q_ref, kp_ref, gq_ref, gkn_ref, qg_ref, kg_ref, inv_ref, *rest):
+    def norms_body(q_ref, kp_ref, gq_ref, gkn_ref, qg_ref, kg_ref, inv_ref, *rest):
         dot_refs = rest[:n_head]
-        out_q, out_k = rest[n_head:]
+        out_q, out_k, buffer_q, buffer_k, sems = rest[n_head:]
         total = dot_refs[0][...]
         for other in dot_refs[1:]:
             total = total + other[...]
         inv_rows = inv_ref[...]
         inv_c = as_columns(inv_rows)
         pull = as_columns(inv_rows * inv_rows * inv_rows * total / full_width)
-        out_q[...] = (
-            inv_c[:, 0:1] * qg_ref[...] * gq_ref[...] - q_ref[...].astype(F32) * pull[:, 0:1]
-        ).astype(BF16)
-        grad_k = (
-            inv_c[:, 1:2] * kg_ref[...] * gkn_ref[...] - kp_ref[...].astype(F32) * pull[:, 1:2]
-        ).astype(BF16)
-        out_k[...] = dot(row_order_back(rows), grad_k).astype(BF16)
-
-    gain_cols = pl.BlockSpec((1, wide), lambda i, ids: (0, i))
-    grad_query, grad_key = grid_call(
+        unorder = row_order_back(rows)
+        copies = []
+        for r in range(n_seq):
+            at = slice(r * wide, (r + 1) * wide)
+            buffer_q[:, at] = (
+                inv_c[:, 0:1] * qg_ref[:, at] * gq_ref[:, at]
+                - q_ref[:, at].astype(F32) * pull[:, 0:1]
+            ).astype(BF16)
+            copies.append(send_out(buffer_q, out_q, sems.at[0], r, at))
+            grad_k = (
+                inv_c[:, 1:2] * kg_ref[:, at] * gkn_ref[:, at]
+                - kp_ref[:, at].astype(F32) * pull[:, 1:2]
+            ).astype(BF16)
+            buffer_k[:, at] = dot(unorder, grad_k).astype(BF16)
+            copies.append(send_out(buffer_k, out_k, sems.at[1], r, at))
+        for copy in copies:
+            copy.wait()
+
+    grad_query, grad_key = column_out(
         norms_body,
-        n_seq,
-        (sds((rows, cols), BF16), sds((rows, cols), BF16)),
-        [own_cols] * 4 + [gain_cols] * 2 + [full(inv)] + [full(dots)] * n_head,
-        (own_cols, own_cols),
-        [],
-        ids, q, kp, gq, gkn, qg, kg, inv, dots, *dots_peers,
-        micros=3.5,
-    )
-
-    def finish_body(ids_ref, kg_ref, wk_ref, same, other, gks_ref, gvs_ref, gain_ref):
-        step = pl.program_id(0)
+        (rows_shape, rows_shape),
+        2,
+        q, kp, gq, gkn, qg, kg, inv, dots, *dots_peers,
+        micros=2.0,
+    )
+
+    def finish_body(ids_ref, kg_ref, wk_ref, same, other, *rest):
+        gq_ref, gk_ref, gks_ref, gvs_ref, buffer_k, buffer_v, sems = rest
         first = ids_ref[1] == 0
-
-        @pl.when(step == 0)
-        def _():
-            gain_ref[...] = jnp.zeros_like(gain_ref)
-
-        gain_ref[...] += same[0, span_rows:, :].astype(F32) + other[0, span_rows:, :].astype(F32)
-        for i in range(hp):
-            span = slice(i * KS * HD, (i + 1) * KS * HD)
-            a = same[0, span, :].astype(F32)
-            b = other[0, span, :].astype(F32)
-            gks_ref[i] = jnp.where(first, a, b)
-            gvs_ref[i] = jnp.where(first, b, a)
-            prod = gks_ref[i] * wk_ref[i].astype(F32)
-            total = prod[:HD]
-            for j in range(1, KS):
-                total = total + prod[j * HD : (j + 1) * HD]
-            row = lane_sum_row(total)
-            head = (ids_ref[0] ^ step) * hp + i
-            at = pl.ds(heads + head, 1)
-            gain_ref[at, :] = gain_ref[at, :] + row / kg_ref[:, i * HD : (i + 1) * HD]
+        parts = same[0, span_rows:, :].astype(F32) + other[0, span_rows:, :].astype(F32)
+        for r in peers:
+            parts += same[r, span_rows:, :].astype(F32) + other[r, span_rows:, :].astype(F32)
+        gq_ref[...] = parts[:heads]
+        gk_ref[...] = parts[heads:]
+        copies = []
+        for r in range(n_seq):
+            start = (ids_ref[0] ^ r) * hp
+            for i in range(hp):
+                h = start + i
+                span = slice(i * KS * HD, (i + 1) * KS * HD)
+                a = same[r, span, :].astype(F32)
+                b = other[r, span, :].astype(F32)
+                grad_w = jnp.where(first, a, b)
+                buffer_k[h] = grad_w
+                buffer_v[h] = jnp.where(first, b, a)
+                prod = grad_w * wk_ref[h].astype(F32)
+                total = prod[:HD]
+                for j in range(1, KS):
+                    total = total + prod[j * HD : (j + 1) * HD]
+                row = lane_sum_row(total)
+                at = pl.ds(h, 1)
+                gain = kg_ref[:, pl.ds(pl.multiple_of(h * HD, HD), HD)]
+                gk_ref[at, :] = gk_ref[at, :] + row / gain
+            for tensor, (buffer, target) in enumerate(((buffer_k, gks_ref), (buffer_v, gvs_ref))):
+                at = pl.ds(start, hp)
+                copy = pltpu.make_async_copy(buffer.at[at], target.at[at], sems.at[tensor, r])
+                copy.start()
+                copies.append(copy)
+        for copy in copies:
+            copy.wait()
 
     kernel_out = sds((heads, KS * HD, HD), F32)
-    gains_shape = sds((2 * heads, HD), F32)
-    step_chunk = pl.BlockSpec((1,) + chunk_shape.shape, lambda i, ids: (i, 0, 0))
-    gks, gvs, gains = grid_call(
+    gains_shape = sds((heads, HD), F32)
+    inside = pl.BlockSpec(memory_space=pltpu.VMEM)
+    outside = pl.BlockSpec(memory_space=pl.ANY)
+    gain_q_all, gain_k_all, gks, gvs = pl.pallas_call(
         finish_body,
-        n_seq,
-        (kernel_out, kernel_out, gains_shape),
-        [pl.BlockSpec((1, wide), lambda i, ids: (0, ids[0] ^ i)), rel_w, step_chunk, step_chunk],
-        (rel_w, rel_w, full(gains_shape)),
-        [],
-        ids, kg, key_squeeze, packed, packed_other,
-        micros=3.2,
-    )
+        out_shape=(gains_shape, gains_shape, kernel_out, kernel_out),
+        in_specs=[pl.BlockSpec(memory_space=pltpu.SMEM)] + [inside] * 4,
+        out_specs=(inside, inside, outside, outside),
+        scratch_shapes=[pltpu.VMEM(kernel_out.shape, F32)] * 2
+        + [pltpu.SemaphoreType.DMA((2, n_seq))],
+        compiler_params=pltpu.CompilerParams(vmem_limit_bytes=40 * 2**20),
+        cost_estimate=cost_of(3.0),
+    )(ids, kg, key_squeeze, packed, packed_other)
     return (
         grad_query[None],
         grad_key[None],
         grad_value[None],
-        gains[:heads].reshape(cols),
-        gains[heads:].reshape(cols),
+        gain_q_all.reshape(cols),
+        gain_k_all.reshape(cols),
         gks,
         gvs,
     )

time: 87.7 us -> 79.8 us (0.910)
  Pallas kernels: 30 us -> 22.6 us
  local copies, waits for them, and re-layouts: 2.35 us -> 1.15 us
    pallas_call x6 -> x3, Pallas kernels: 24.3 us -> 8.83 us  [the longest x2 5.09 us: column_out(): pl.pallas_call(lambda *refs: body(*refs[:len(ins)], *refs[len(ins) + skip...]
    pallas_call x8 -> x11, Pallas kernels: 5.71 us -> 13.8 us  [whole_call(): pl.pallas_call(lambda *refs: body(*refs[:len(ins)], *refs[len(ins) + skip...]
    ppermute x24 -> x21, starting transfers between devices: 28 us -> 28.5 us  [to_peers(): lax.ppermute(a, axis, [(i, i ^ k) for i in range(n)])]
    ppermute x24 -> x21, waiting for transfers between devices: 26 us -> 26.3 us  [to_peers(): lax.ppermute(a, axis, [(i, i ^ k) for i in range(n)])]
  transfers between devices with their start and end apart: 26 -> 23, of which waited for: 9 -> 13; matrix products, arithmetic and copies ran while one was open for 0% -> 0% of each run, Pallas kernels for 20% -> 18%
where the time goes in v3:
time: 79.8 us; the launch traced here: 79.6 us
  starting transfers between devices  28.6 us (36%)
  waiting for transfers between devices  26.3 us (33%)
  Pallas kernels  22.6 us (28%)
  local copies, waits for them, and re-layouts  1.15 us (1%)
  between operations  0.82 us (1%)
    ppermute x21, starting transfers between devices, to_peers(): lax.ppermute(a, axis, [(i, i ^ k) for i in range(n)])  28.5 us
    ppermute x21, waiting for transfers between devices, to_peers(): lax.ppermute(a, axis, [(i, i ^ k) for i in range(n)])  26.3 us
    pallas_call x11, Pallas kernels, whole_call(): pl.pallas_call(lambda *refs: body(*refs[:len(ins)], *refs[len(ins) + skip...  13.8 us
    pallas_call x2, Pallas kernels, column_out(): pl.pallas_call(lambda *refs: body(*refs[:len(ins)], *refs[len(ins) + skip...  5.09 us
    pallas_call x1, Pallas kernels, on_device(): pl.pallas_call(finish_body, out_shape=(gains_shape, gains_shape, kernel_o...  3.74 us
  transfers between devices with their start and end apart: 23, of which 13 were waited for; matrix products, arithmetic and copies ran while one was open for 0% of the time, Pallas kernels for 18%

profile of v3, /device:TPU:0, one launch (start us, length us, event | category | flops | bytes accessed | tf_op | source)
XLA Modules:
  0.0 79.6 jit_solution(14235856147834905249)
XLA Ops:
  0.7 2.2 %shard_map.136.refs_6_ = f32[2,256]{1,0:T(2,128)} custom-call(bf16[256,1024]{1,0:T(8,128)(2,1)} %bitcast.16, bf16[256,1024]{1,0:T(8,128)(2,1)} %bitcast.24), custom_call_target="tpu_custom_call" | custom-call | flops 1500000000 | bytes 5400000 | tf_op jit(solution)/shard_map/pallas_call | solution.py:210
  2.8 5.0 %collective-permute-start.2 = (f32[2,256]{1,0:T(2,128)}, f32[2,256]{1,0:T(2,128)S(1)}, u32[]{:S(2)}, u32[]{:S(2)}) collective-permute-start(f32[2,256]{1,0:T(2,128)} %shard_map.136.refs_6_), channel_id=1, source_target_pairs={{0,6},{2,4},{4,2},{6,0},{1,7},{3,5},{5,3},{7,1},{8,14},{10,12},{12... | collective-permute-start | bytes 6152 | tf_op jit(solution)/shard_map/ppermute | solution.py:293
  10.5 2.1 %collective-permute-done.1.refs_8_ = f32[2,256]{1,0:T(2,128)S(1)} collective-permute-done((f32[2,256]{1,0:T(2,128)}, f32[2,256]{1,0:T(2,128)S(1)}, u32[]{:S(2)}, u32[]{:S(2)}) %collective-permute-start.1) | collective-permute-done | bytes 2080 | tf_op jit(solution)/shard_map/ppermute | solution.py:293
  13.6 2.5 %collective-permute-start.5 = (bf16[2,256,256]{2,1,0:T(8,128)(2,1)S(1)}, bf16[2,256,256]{2,1,0:T(8,128)(2,1)S(1)}, u32[]{:S(2)}, u32[]{:S(2)}) collective-permute-start(bf16[2,256,256]{2,1,0:T(8,128)(2,1)S(1)} %get-tuple-element.49), channel_id=1, source_target_pairs={{0,24},{8,16},{16,8},{24,0},{1,25},{9,17},{17,9},{25,1},{2,26},{10... | collective-permute-start | bytes 786440 | tf_op jit(solution)/shard_map/ppermute | solution.py:293
  19.0 1.6 %collective-permute-start.6 = (bf16[2,256,256]{2,1,0:T(8,128)(2,1)S(1)}, bf16[2,256,256]{2,1,0:T(8,128)(2,1)S(1)}, u32[]{:S(2)}, u32[]{:S(2)}) collective-permute-start(bf16[2,256,256]{2,1,0:T(8,128)(2,1)S(1)} %get-tuple-element.53), channel_id=1, source_target_pairs={{0,8},{8,0},{16,24},{24,16},{1,9},{9,1},{17,25},{25,17},{2,10},{10... | collective-permute-start | bytes 786440 | tf_op jit(solution)/shard_map/ppermute | solution.py:293
  22.0 1.8 %collective-permute-done.5.refs_6_.refs_10_ = bf16[2,256,256]{2,1,0:T(8,128)(2,1)S(1)} collective-permute-done((bf16[2,256,256]{2,1,0:T(8,128)(2,1)S(1)}, bf16[2,256,256]{2,1,0:T(8,128)(2,1)S(1)}, u32[]{:S(2)}, u32[]{:S(2)}) %collective-permute-start.5) | collective-permute-done | bytes 262176 | tf_op jit(solution)/shard_map/ppermute | solution.py:293
  23.8 2.4 %collective-permute-start.8 = (bf16[2,256,256]{2,1,0:T(8,128)(2,1)S(1)}, bf16[2,256,256]{2,1,0:T(8,128)(2,1)S(1)}, u32[]{:S(2)}, u32[]{:S(2)}) collective-permute-start(bf16[2,256,256]{2,1,0:T(8,128)(2,1)S(1)} %get-tuple-element.55), channel_id=1, source_target_pairs={{0,24},{8,16},{16,8},{24,0},{1,25},{9,17},{17,9},{25,1},{2,26},{10... | collective-permute-start | bytes 786440 | tf_op jit(solution)/shard_map/ppermute | solution.py:293
  27.4 2.1 %collective-permute-done.3.refs_4_.refs_8_ = bf16[2,256,256]{2,1,0:T(8,128)(2,1)S(1)} collective-permute-done((bf16[2,256,256]{2,1,0:T(8,128)(2,1)S(1)}, bf16[2,256,256]{2,1,0:T(8,128)(2,1)S(1)}, u32[]{:S(2)}, u32[]{:S(2)}) %collective-permute-start.3) | collective-permute-done | bytes 262176 | tf_op jit(solution)/shard_map/ppermute | solution.py:293
  29.5 3.3 %shard_map.139 = (f32[8,8,256]{2,1,0:T(8,128)S(1)}, bf16[8,192,256]{2,1,0:T(8,128)(2,1)S(1)}, bf16[2,192,256]{2,1,0:T(8,128)(2,1)S(1)}, bf16[2,192,256]{2,1,0:T(...) custom-call(s32[2]{0:T(128)S(1)} %pad_add_fusion.refs_0_.ids_ref, ...), custom_call_target="tpu_custom_call" | custom-call | flops 500000000 | bytes 1800000 | tf_op jit(solution)/shard_map/pallas_call | solution.py:210
  32.7 1.6 %collective-permute-start.9 = (bf16[2,192,256]{2,1,0:T(8,128)(2,1)S(1)}, bf16[2,192,256]{2,1,0:T(8,128)(2,1)S(1)}, u32[]{:S(2)}, u32[]{:S(2)}) collective-permute-start(bf16[2,192,256]{2,1,0:T(8,128)(2,1)S(1)} %get-tuple-element.61), channel_id=1, source_target_pairs={{0,8},{8,0},{16,24},{24,16},{1,9},{9,1},{17,25},{25,17},{2,10},{10... | collective-permute-start | bytes 589832 | tf_op jit(solution)/shard_map/ppermute | solution.py:293
  36.5 4.2 %collective-permute-done.8.refs_15_.refs_9_ = bf16[2,256,256]{2,1,0:T(8,128)(2,1)S(1)} collective-permute-done((bf16[2,256,256]{2,1,0:T(8,128)(2,1)S(1)}, bf16[2,256,256]{2,1,0:T(8,128)(2,1)S(1)}, u32[]{:S(2)}, u32[]{:S(2)}) %collective-permute-start.8) | collective-permute-done | bytes 262176 | tf_op jit(solution)/shard_map/ppermute | solution.py:293
  40.7 3.6 %shard_map.141 = (f32[256,1024]{1,0:T(8,128)S(1)}, f32[256,1024]{1,0:T(8,128)S(1)}, f32[256,1024]{1,0:T(8,128)S(1)}, f32[1,256]{1,0:T(1,128)S(1)}, f32[8,128]{1,0:T(8,128)S(1)}, /*index=5*/f32[8,128]{1,0:T(8,128)S(1)}) custom-call(bf16[256,1024]{1,0:T(8,128)(2,1)S(1)} %bitcast.18, bf16[256,1024]{1,0:T(8,128)(2,1)S(1)} %get-tuple-element.44.refs_1_.refs_3_, ...), custom_call_target="tpu_custom_call" | custom-call | flops 500000000 | bytes 1800000 | tf_op jit(solution)/shard_map/pallas_call | solution.py:210
  44.4 2.0 %collective-permute-done.11.refs_3_ = bf16[2,192,256]{2,1,0:T(8,128)(2,1)S(1)} collective-permute-done((bf16[2,192,256]{2,1,0:T(8,128)(2,1)S(1)}, bf16[2,192,256]{2,1,0:T(8,128)(2,1)S(1)}, u32[]{:S(2)}, u32[]{:S(2)}) %collective-permute-start.11) | collective-permute-done | bytes 196640 | tf_op jit(solution)/shard_map/ppermute | solution.py:293
  47.7 1.6 %collective-permute-start.12 = (bf16[2,64,256]{2,1,0:T(8,128)(2,1)S(1)}, bf16[2,64,256]{2,1,0:T(8,128)(2,1)S(1)}, u32[]{:S(2)}, u32[]{:S(2)}) collective-permute-start(bf16[2,64,256]{2,1,0:T(8,128)(2,1)S(1)} %get-tuple-element.66.refs_4_), channel_id=1, source_target_pairs={{0,8},{8,0},{16,24},{24,16},{1,9},{9,1},{17,25},{25,17},{2,10},{10... | collective-permute-start | bytes 196616 | tf_op jit(solution)/shard_map/ppermute | solution.py:293
  51.3 2.5 %collective-permute-start.21 = (bf16[1040,128]{1,0:T(8,128)(2,1)S(1)}, bf16[1040,128]{1,0:T(8,128)(2,1)S(1)}, u32[]{:S(2)}, u32[]{:S(2)}) collective-permute-start(bf16[1040,128]{1,0:T(8,128)(2,1)S(1)} %shard_map.144.refs_12_.refs_0_), channel_id=1, source_target_pairs={{0,24},{8,16},{16,8},{24,0},{1,25},{9,17},{17,9},{25,1},{2,26},{10... | collective-permute-start | bytes 798728 | tf_op jit(solution)/shard_map/ppermute | solution.py:293
  54.9 1.9 %collective-permute-done.14.refs_11_ = bf16[2,64,256]{2,1,0:T(8,128)(2,1)S(1)} collective-permute-done((bf16[2,64,256]{2,1,0:T(8,128)(2,1)S(1)}, bf16[2,64,256]{2,1,0:T(8,128)(2,1)S(1)}, u32[]{:S(2)}, u32[]{:S(2)}) %collective-permute-start.14) | collective-permute-done | bytes 65568 | tf_op jit(solution)/shard_map/ppermute | solution.py:293
  56.7 3.4 %shard_map.145 = (f32[256,1024]{1,0:T(8,128)S(1)}, f32[2,256]{1,0:T(2,128)S(1)}, bf16[256,1024]{1,0:T(8,128)(2,1)}) custom-call(s32[2]{0:T(128)S(1)} %pad_add_fusion.refs_0_.ids_ref, f32[256,1024]{1,0:T(8,128)S(1)} %get-tuple-element.57.refs_1_, f32[256,1024]{1,0:T(8,128)S(1)} %get-tuple-element.58.refs_2_, ...), custom_call_target="tpu_custom_call" | custom-call | flops 3000000000 | bytes 10800000 | tf_op jit(solution)/shard_map/pallas_call | solution.py:562
  60.7 3.1 %collective-permute-done.16.refs_8_.refs_4_ = f32[2,256]{1,0:T(2,128)S(1)} collective-permute-done((f32[2,256]{1,0:T(2,128)S(1)}, f32[2,256]{1,0:T(2,128)S(1)}, u32[]{:S(2)}, u32[]{:S(2)}) %collective-permute-start.16) | collective-permute-done | bytes 2080 | tf_op jit(solution)/shard_map/ppermute | solution.py:293
  63.8 3.1 %collective-permute-done.20.refs_2_ = bf16[1040,128]{1,0:T(8,128)(2,1)S(1)} collective-permute-done((bf16[1040,128]{1,0:T(8,128)(2,1)S(1)}, bf16[1040,128]{1,0:T(8,128)(2,1)S(1)}, u32[]{:S(2)}, u32[]{:S(2)}) %collective-permute-start.20) | collective-permute-done | bytes 266272 | tf_op jit(solution)/shard_map/ppermute | solution.py:293
  67.1 2.6 %collective-permute-start.18 = (f32[2,256]{1,0:T(2,128)S(1)}, f32[2,256]{1,0:T(2,128)S(1)}, u32[]{:S(2)}, u32[]{:S(2)}) collective-permute-start(f32[2,256]{1,0:T(2,128)S(1)} %get-tuple-element.73.refs_7_), channel_id=1, source_target_pairs={{0,6},{2,4},{4,2},{6,0},{1,7},{3,5},{5,3},{7,1},{8,14},{10,12},{12... | collective-permute-start | bytes 6152 | tf_op jit(solution)/shard_map/ppermute | solution.py:293
  69.7 2.8 %collective-permute-done.18.refs_10_ = f32[2,256]{1,0:T(2,128)S(1)} collective-permute-done((f32[2,256]{1,0:T(2,128)S(1)}, f32[2,256]{1,0:T(2,128)S(1)}, u32[]{:S(2)}, u32[]{:S(2)}) %collective-permute-start.18) | collective-permute-done | bytes 2080 | tf_op jit(solution)/shard_map/ppermute | solution.py:293
  72.6 1.6 %collective-permute-done.17.refs_9_ = f32[2,256]{1,0:T(2,128)S(1)} collective-permute-done((f32[2,256]{1,0:T(2,128)S(1)}, f32[2,256]{1,0:T(2,128)S(1)}, u32[]{:S(2)}, u32[]{:S(2)}) %collective-permute-start.17) | collective-permute-done | bytes 2080 | tf_op jit(solution)/shard_map/ppermute | solution.py:293
  74.2 1.7 %shard_map.146 = (bf16[256,1024]{1,0:T(8,128)(2,1)}, bf16[256,1024]{1,0:T(8,128)(2,1)}) custom-call(bf16[256,1024]{1,0:T(8,128)(2,1)S(1)} %bitcast.19, bf16[256,1024]{1,0:T(8,128)(2,1)S(1)} %get-tuple-element.44.refs_1_.refs_3_, f32[256,1024]{1,0:T(8,128)S(1)} %get-tuple-element.56.refs_2_, f32[256,1024]{1,0:T(8,128)S(1)} %get-tuple-element.72.refs_3_, ...), custom_call_target="tpu_custom_call" | custom-call | flops 2000000000 | bytes 7200000 | tf_op jit(solution)/shard_map/pallas_call | solution.py:562
  75.9 3.7 %shard_map.148 = (f32[8,128]{1,0:T(8,128)}, f32[8,128]{1,0:T(8,128)}, f32[8,512,128]{2,1,0:T(8,128)}, f32[8,512,128]{2,1,0:T(8,128)}) custom-call(s32[2]{0:T(128)S(1)} %pad_add_fusion.refs_0_.ids_ref, f32[1,1024]{1,0:T(1,128)S(1)} %bitcast.30, bf16[8,512,128]{2,1,0:T(8,128)(2,1)S(1)} %copy-done.4, bf16[4,1040,128]{2,1,0:T(8,128)(2,1)S(1)} %shard_map.147.same, ...), custom_call_target="tpu_custom_call" | custom-call | flops 3000000000 | bytes 10800000 | tf_op jit(solution)/shard_map/pallas_call | solution.py:702
  (57 shorter events, 16.5 us)
Async XLA Ops:
  0.7 11.9 %copy-start.8 = (f32[1024]{0:T(1024)S(1)}, f32[1024]{0:T(1024)}, u32[]{:S(2)}) copy-start(f32[1024]{0:T(1024)} %param.12) | copy-start | bytes 12292
  2.8 7.7 %collective-permute-start.2 = (f32[2,256]{1,0:T(2,128)}, f32[2,256]{1,0:T(2,128)S(1)}, u32[]{:S(2)}, u32[]{:S(2)}) collective-permute-start(f32[2,256]{1,0:T(2,128)} %shard_map.136.refs_6_), channel_id=1, source_target_pairs={{0,6},{2,4},{4,2},{6,0},{1,7},{3,5},{5,3},{7,1},{8,14},{10,12},{12... | collective-permute-start | bytes 6152 | tf_op jit(solution)/shard_map/ppermute | solution.py:293
  7.9 4.7 %collective-permute-start.1 = (f32[2,256]{1,0:T(2,128)}, f32[2,256]{1,0:T(2,128)S(1)}, u32[]{:S(2)}, u32[]{:S(2)}) collective-permute-start(f32[2,256]{1,0:T(2,128)} %shard_map.136.refs_6_), channel_id=1, source_target_pairs={{0,4},{2,6},{4,0},{6,2},{1,5},{3,7},{5,1},{7,3},{8,12},{10,14},{12... | collective-permute-start | bytes 6152 | tf_op jit(solution)/shard_map/ppermute | solution.py:293
  7.9 4.7 %collective-permute-start = (f32[2,256]{1,0:T(2,128)}, f32[2,256]{1,0:T(2,128)S(1)}, u32[]{:S(2)}, u32[]{:S(2)}) collective-permute-start(f32[2,256]{1,0:T(2,128)} %shard_map.136.refs_6_), channel_id=1, source_target_pairs={{0,2},{2,0},{4,6},{6,4},{1,3},{3,1},{5,7},{7,5},{8,10},{10,8},{12,... | collective-permute-start | bytes 6152 | tf_op jit(solution)/shard_map/ppermute | solution.py:293
  13.6 10.2 %collective-permute-start.5 = (bf16[2,256,256]{2,1,0:T(8,128)(2,1)S(1)}, bf16[2,256,256]{2,1,0:T(8,128)(2,1)S(1)}, u32[]{:S(2)}, u32[]{:S(2)}) collective-permute-start(bf16[2,256,256]{2,1,0:T(8,128)(2,1)S(1)} %get-tuple-element.49), channel_id=1, source_target_pairs={{0,24},{8,16},{16,8},{24,0},{1,25},{9,17},{17,9},{25,1},{2,26},{10... | collective-permute-start | bytes 786440 | tf_op jit(solution)/shard_map/ppermute | solution.py:293
  16.1 11.3 %collective-permute-start.4 = (bf16[2,256,256]{2,1,0:T(8,128)(2,1)S(1)}, bf16[2,256,256]{2,1,0:T(8,128)(2,1)S(1)}, u32[]{:S(2)}, u32[]{:S(2)}) collective-permute-start(bf16[2,256,256]{2,1,0:T(8,128)(2,1)S(1)} %get-tuple-element.49), channel_id=1, source_target_pairs={{0,16},{8,24},{16,0},{24,8},{1,17},{9,25},{17,1},{25,9},{2,18},{10... | collective-permute-start | bytes 786440 | tf_op jit(solution)/shard_map/ppermute | solution.py:293
  16.6 12.9 %collective-permute-start.3 = (bf16[2,256,256]{2,1,0:T(8,128)(2,1)S(1)}, bf16[2,256,256]{2,1,0:T(8,128)(2,1)S(1)}, u32[]{:S(2)}, u32[]{:S(2)}) collective-permute-start(bf16[2,256,256]{2,1,0:T(8,128)(2,1)S(1)} %get-tuple-element.49), channel_id=1, source_target_pairs={{0,8},{8,0},{16,24},{24,16},{1,9},{9,1},{17,25},{25,17},{2,10},{10... | collective-permute-start | bytes 786440 | tf_op jit(solution)/shard_map/ppermute | solution.py:293
  19.0 16.1 %collective-permute-start.6 = (bf16[2,256,256]{2,1,0:T(8,128)(2,1)S(1)}, bf16[2,256,256]{2,1,0:T(8,128)(2,1)S(1)}, u32[]{:S(2)}, u32[]{:S(2)}) collective-permute-start(bf16[2,256,256]{2,1,0:T(8,128)(2,1)S(1)} %get-tuple-element.53), channel_id=1, source_target_pairs={{0,8},{8,0},{16,24},{24,16},{1,9},{9,1},{17,25},{25,17},{2,10},{10... | collective-permute-start | bytes 786440 | tf_op jit(solution)/shard_map/ppermute | solution.py:293
  20.5 16.0 %collective-permute-start.7 = (bf16[2,256,256]{2,1,0:T(8,128)(2,1)S(1)}, bf16[2,256,256]{2,1,0:T(8,128)(2,1)S(1)}, u32[]{:S(2)}, u32[]{:S(2)}) collective-permute-start(bf16[2,256,256]{2,1,0:T(8,128)(2,1)S(1)} %get-tuple-element.54), channel_id=1, source_target_pairs={{0,16},{8,24},{16,0},{24,8},{1,17},{9,25},{17,1},{25,9},{2,18},{10... | collective-permute-start | bytes 786440 | tf_op jit(solution)/shard_map/ppermute | solution.py:293
  23.8 16.9 %collective-permute-start.8 = (bf16[2,256,256]{2,1,0:T(8,128)(2,1)S(1)}, bf16[2,256,256]{2,1,0:T(8,128)(2,1)S(1)}, u32[]{:S(2)}, u32[]{:S(2)}) collective-permute-start(bf16[2,256,256]{2,1,0:T(8,128)(2,1)S(1)} %get-tuple-element.55), channel_id=1, source_target_pairs={{0,24},{8,16},{16,8},{24,0},{1,25},{9,17},{17,9},{25,1},{2,26},{10... | collective-permute-start | bytes 786440 | tf_op jit(solution)/shard_map/ppermute | solution.py:293
  32.7 11.7 %collective-permute-start.9 = (bf16[2,192,256]{2,1,0:T(8,128)(2,1)S(1)}, bf16[2,192,256]{2,1,0:T(8,128)(2,1)S(1)}, u32[]{:S(2)}, u32[]{:S(2)}) collective-permute-start(bf16[2,192,256]{2,1,0:T(8,128)(2,1)S(1)} %get-tuple-element.61), channel_id=1, source_target_pairs={{0,8},{8,0},{16,24},{24,16},{1,9},{9,1},{17,25},{25,17},{2,10},{10... | collective-permute-start | bytes 589832 | tf_op jit(solution)/shard_map/ppermute | solution.py:293
  34.3 10.2 %collective-permute-start.10 = (bf16[2,192,256]{2,1,0:T(8,128)(2,1)S(1)}, bf16[2,192,256]{2,1,0:T(8,128)(2,1)S(1)}, u32[]{:S(2)}, u32[]{:S(2)}) collective-permute-start(bf16[2,192,256]{2,1,0:T(8,128)(2,1)S(1)} %get-tuple-element.62), channel_id=1, source_target_pairs={{0,16},{8,24},{16,0},{24,8},{1,17},{9,25},{17,1},{25,9},{2,18},{10... | collective-permute-start | bytes 589832 | tf_op jit(solution)/shard_map/ppermute | solution.py:293
  35.1 11.4 %collective-permute-start.11 = (bf16[2,192,256]{2,1,0:T(8,128)(2,1)S(1)}, bf16[2,192,256]{2,1,0:T(8,128)(2,1)S(1)}, u32[]{:S(2)}, u32[]{:S(2)}) collective-permute-start(bf16[2,192,256]{2,1,0:T(8,128)(2,1)S(1)} %get-tuple-element.63), channel_id=1, source_target_pairs={{0,24},{8,16},{16,8},{24,0},{1,25},{9,17},{17,9},{25,1},{2,26},{10... | collective-permute-start | bytes 589832 | tf_op jit(solution)/shard_map/ppermute | solution.py:293
  47.6 3.6 %collective-permute-start.15 = (bf16[1024,128]{1,0:T(8,128)(2,1)S(1)}, bf16[1024,128]{1,0:T(8,128)(2,1)S(1)}, u32[]{:S(2)}, u32[]{:S(2)}) collective-permute-start(bf16[1024,128]{1,0:T(8,128)(2,1)S(1)} %get-tuple-element.70), channel_id=1, source_target_pairs={{0,1},{1,0},{2,3},{3,2},{4,5},{5,4},{6,7},{7,6},{8,9},{9,8},{10,11... | collective-permute-start | bytes 786440 | tf_op jit(solution)/shard_map/ppermute | solution.py:298
  47.7 6.7 %collective-permute-start.12 = (bf16[2,64,256]{2,1,0:T(8,128)(2,1)S(1)}, bf16[2,64,256]{2,1,0:T(8,128)(2,1)S(1)}, u32[]{:S(2)}, u32[]{:S(2)}) collective-permute-start(bf16[2,64,256]{2,1,0:T(8,128)(2,1)S(1)} %get-tuple-element.66.refs_4_), channel_id=1, source_target_pairs={{0,8},{8,0},{16,24},{24,16},{1,9},{9,1},{17,25},{25,17},{2,10},{10... | collective-permute-start | bytes 196616 | tf_op jit(solution)/shard_map/ppermute | solution.py:293
  49.2 5.6 %collective-permute-start.13 = (bf16[2,64,256]{2,1,0:T(8,128)(2,1)S(1)}, bf16[2,64,256]{2,1,0:T(8,128)(2,1)S(1)}, u32[]{:S(2)}, u32[]{:S(2)}) collective-permute-start(bf16[2,64,256]{2,1,0:T(8,128)(2,1)S(1)} %get-tuple-element.67.refs_5_), channel_id=1, source_target_pairs={{0,16},{8,24},{16,0},{24,8},{1,17},{9,25},{17,1},{25,9},{2,18},{10... | collective-permute-start | bytes 196616 | tf_op jit(solution)/shard_map/ppermute | solution.py:293
  50.8 6.0 %collective-permute-start.14 = (bf16[2,64,256]{2,1,0:T(8,128)(2,1)S(1)}, bf16[2,64,256]{2,1,0:T(8,128)(2,1)S(1)}, u32[]{:S(2)}, u32[]{:S(2)}) collective-permute-start(bf16[2,64,256]{2,1,0:T(8,128)(2,1)S(1)} %get-tuple-element.68.refs_6_), channel_id=1, source_target_pairs={{0,24},{8,16},{16,8},{24,0},{1,25},{9,17},{17,9},{25,1},{2,26},{10... | collective-permute-start | bytes 196616 | tf_op jit(solution)/shard_map/ppermute | solution.py:293
  51.3 12.5 %collective-permute-start.21 = (bf16[1040,128]{1,0:T(8,128)(2,1)S(1)}, bf16[1040,128]{1,0:T(8,128)(2,1)S(1)}, u32[]{:S(2)}, u32[]{:S(2)}) collective-permute-start(bf16[1040,128]{1,0:T(8,128)(2,1)S(1)} %shard_map.144.refs_12_.refs_0_), channel_id=1, source_target_pairs={{0,24},{8,16},{16,8},{24,0},{1,25},{9,17},{17,9},{25,1},{2,26},{10... | collective-permute-start | bytes 798728 | tf_op jit(solution)/shard_map/ppermute | solution.py:293
  53.8 13.1 %collective-permute-start.20 = (bf16[1040,128]{1,0:T(8,128)(2,1)S(1)}, bf16[1040,128]{1,0:T(8,128)(2,1)S(1)}, u32[]{:S(2)}, u32[]{:S(2)}) collective-permute-start(bf16[1040,128]{1,0:T(8,128)(2,1)S(1)} %shard_map.144.refs_12_.refs_0_), channel_id=1, source_target_pairs={{0,16},{8,24},{16,0},{24,8},{1,17},{9,25},{17,1},{25,9},{2,18},{10... | collective-permute-start | bytes 798728 | tf_op jit(solution)/shard_map/ppermute | solution.py:293
  54.3 12.6 %collective-permute-start.19 = (bf16[1040,128]{1,0:T(8,128)(2,1)S(1)}, bf16[1040,128]{1,0:T(8,128)(2,1)S(1)}, u32[]{:S(2)}, u32[]{:S(2)}) collective-permute-start(bf16[1040,128]{1,0:T(8,128)(2,1)S(1)} %shard_map.144.refs_12_.refs_0_), channel_id=1, source_target_pairs={{0,8},{8,0},{16,24},{24,16},{1,9},{9,1},{17,25},{25,17},{2,10},{10... | collective-permute-start | bytes 798728 | tf_op jit(solution)/shard_map/ppermute | solution.py:293
  60.2 3.7 %collective-permute-start.16 = (f32[2,256]{1,0:T(2,128)S(1)}, f32[2,256]{1,0:T(2,128)S(1)}, u32[]{:S(2)}, u32[]{:S(2)}) collective-permute-start(f32[2,256]{1,0:T(2,128)S(1)} %get-tuple-element.73.refs_7_), channel_id=1, source_target_pairs={{0,2},{2,0},{4,6},{6,4},{1,3},{3,1},{5,7},{7,5},{8,10},{10,8},{12,... | collective-permute-start | bytes 6152 | tf_op jit(solution)/shard_map/ppermute | solution.py:293
  67.1 8.8 %collective-permute-start.22 = (bf16[4,1040,128]{2,1,0:T(8,128)(2,1)S(1)}, bf16[4,1040,128]{2,1,0:T(8,128)(2,1)S(1)}, u32[]{:S(2)}, u32[]{:S(2)}) collective-permute-start(bf16[4,1040,128]{2,1,0:T(8,128)(2,1)S(1)} %shard_map.147.same), channel_id=1, source_target_pairs={{0,1},{1,0},{2,3},{3,2},{4,5},{5,4},{6,7},{7,6},{8,9},{9,8},{10,11... | collective-permute-start | bytes 3194888 | tf_op jit(solution)/shard_map/ppermute | solution.py:298
  67.1 5.4 %collective-permute-start.18 = (f32[2,256]{1,0:T(2,128)S(1)}, f32[2,256]{1,0:T(2,128)S(1)}, u32[]{:S(2)}, u32[]{:S(2)}) collective-permute-start(f32[2,256]{1,0:T(2,128)S(1)} %get-tuple-element.73.refs_7_), channel_id=1, source_target_pairs={{0,6},{2,4},{4,2},{6,0},{1,7},{3,5},{5,3},{7,1},{8,14},{10,12},{12... | collective-permute-start | bytes 6152 | tf_op jit(solution)/shard_map/ppermute | solution.py:293
  69.7 4.5 %collective-permute-start.17 = (f32[2,256]{1,0:T(2,128)S(1)}, f32[2,256]{1,0:T(2,128)S(1)}, u32[]{:S(2)}, u32[]{:S(2)}) collective-permute-start(f32[2,256]{1,0:T(2,128)S(1)} %get-tuple-element.73.refs_7_), channel_id=1, source_target_pairs={{0,4},{2,6},{4,0},{6,2},{1,5},{3,7},{5,1},{7,3},{8,12},{10,14},{12... | collective-permute-start | bytes 6152 | tf_op jit(solution)/shard_map/ppermute | solution.py:293
  (9 other events, 50.9 us)

commit v4 on v3

--- a/solution.py
+++ b/solution.py
@@ -294,6 +294,18 @@
             for k, a in zip(range(1, n), arrays)
         ]
 
+    def sum_body(a_ref, b_ref, out_ref):
+        out_ref[...] = a_ref[...] + b_ref[...]
+
+    def over_heads(a, beside=()):
+        step, got = 1, None
+        while step < n_head:
+            if got is not None:
+                a = whole_call(sum_body, sds(a.shape, a.dtype), a, got, micros=0.1, after=beside)
+            got = lax.ppermute(a, "head", [(i, i ^ step) for i in range(n_head)])
+            step *= 2
+        return a, got
+
     def to_core(a):
         return lax.ppermute(a, "dp", [(0, 1), (1, 0)])
 
@@ -312,7 +324,7 @@
 
     two_rows = sds((2, rows), F32)
     ss = whole_call(squares_body, two_rows, q, k, micros=1.5, vmem=62)
-    ss_peers = to_peers("head", [ss] * (n_head - 1))
+    ss_parts = [ss] + to_peers("head", [ss] * (n_head - 1))
 
     def compress(source, w_ref, out_ref):
         for h in range(heads):
@@ -328,24 +340,19 @@
                 block * slots : (block + 1) * slots, (h % hp) * HD : (h % hp + 1) * HD
             ] = total.astype(BF16)
 
-    def values_body(v_ref, k_ref, w_ref, vp_ref, mem_ref, kp_ref):
-        order = row_order(rows)
-        vp_ref[...] = dot(order, v_ref[...]).astype(BF16)
+    def values_body(v_ref, w_ref, vp_ref, mem_ref):
+        vp_ref[...] = dot(row_order(rows), v_ref[...]).astype(BF16)
         compress(vp_ref, w_ref, mem_ref)
-        kp_ref[...] = dot(order, k_ref[...]).astype(BF16)
 
     rows_shape = sds((rows, cols), BF16)
     mem_shape = sds((mem_rows, wide), BF16)
-    vp, mem_v, kp = whole_call(
-        values_body,
-        (rows_shape, mem_shape, rows_shape),
-        v, k, value_squeeze,
-        micros=0.8,
-    )
-
-    def keys_body(q_ref, k_ref, qg_ref, kg_ref, w_ref, mem_v_ref, *rest):
+    vp, mem_v = whole_call(
+        values_body, (rows_shape, mem_shape), v, value_squeeze, micros=0.8
+    )
+
+    def keys_body(k_ref, kg_ref, w_ref, mem_v_ref, *rest):
         ss_refs = rest[:n_head]
-        inv_ref, qn_ref, kn_ref, mem_ref = rest[n_head:]
+        inv_ref, kn_ref, mem_ref = rest[n_head:]
         total = ss_refs[0][...]
         for other in ss_refs[1:]:
             total = total + other[...]
@@ -362,22 +369,24 @@
         kn_ref[...] = dot(order, normed).astype(BF16)
         compress(kn_ref, w_ref, mem_ref.at[0])
         mem_ref[1] = mem_v_ref[...]
-        qn_ref[...] = (q_ref[...].astype(F32) * inv_c[:, 0:1] * qg_ref[...]).astype(BF16)
 
     mem_pair = sds((2, mem_rows, wide), BF16)
-    inv, qn, kn, mem = whole_call(
+    inv, kn, mem = whole_call(
         keys_body,
-        (sds((2, rows), F32), rows_shape, rows_shape, mem_pair),
-        q, k, qg, kg, key_squeeze, mem_v, ss, *ss_peers,
+        (two_rows, rows_shape, mem_pair),
+        k, kg, key_squeeze, mem_v, *ss_parts,
         micros=1.5,
     )
     mem_recv = to_peers("seq", [mem] * (n_seq - 1))
 
-    def local_body(qn_ref, kn_ref, vp_ref, do_ref, st_ref):
+    def local_body(q_ref, qg_ref, inv_ref, kn_ref, vp_ref, do_ref, qn_ref, st_ref):
         allowed = causal_t(rows)
+        inv_c = as_columns(inv_ref[...])[:, 0:1]
         for h in range(heads):
             at = slice(h * HD, (h + 1) * HD)
-            s = jnp.where(allowed, dot(kn_ref[:, at], qn_ref[:, at], NT) * scale, -jnp.inf)
+            qn_h = (q_ref[:, at].astype(F32) * inv_c * qg_ref[:, at]).astype(BF16)
+            qn_ref[:, at] = qn_h
+            s = jnp.where(allowed, dot(kn_ref[:, at], qn_h, NT) * scale, -jnp.inf)
             g = dot(vp_ref[:, at], do_ref[:, at], NT)
             m = jnp.max(s, axis=0, keepdims=True)
             p = jnp.exp(s - m)
@@ -386,9 +395,13 @@
             st_ref[h, 2:3, :] = jnp.sum(p * g, axis=0, keepdims=True)
 
     stat_shape = sds((heads, 8, rows), F32)
-    stats = whole_call(local_body, stat_shape, qn, kn, vp, do, micros=0.5)
-
-    def rows_body(ids_ref, kn_ref, vp_ref, *sends):
+    qn, stats = whole_call(
+        local_body, (rows_shape, stat_shape), q, qg, inv, kn, vp, do, micros=0.5
+    )
+
+    def rows_body(ids_ref, kn_ref, vp_ref, k_ref, *outs):
+        sends, kp_ref = outs[:-1], outs[-1]
+        kp_ref[...] = dot(row_order(rows), k_ref[...]).astype(BF16)
         for r, send in zip(peers, sends):
             dest = ids_ref[0] ^ r
             at = pl.ds(pl.multiple_of(dest * wide, wide), wide)
@@ -396,8 +409,12 @@
             send[1] = vp_ref[:, at]
 
     row_pair = sds((2, rows, wide), BF16)
-    row_sends = whole_call(
-        rows_body, (row_pair,) * (n_seq - 1), ids, kn, vp, after=(stats,), micros=0.7
+    *row_sends, kp = whole_call(
+        rows_body,
+        (row_pair,) * (n_seq - 1) + (rows_shape,),
+        ids, kn, vp, k,
+        after=(stats,),
+        micros=0.7,
     )
     rows_recv = to_peers("seq", row_sends)
 
@@ -507,6 +524,7 @@
     slot_grads = whole_call(
         slots_body, (slot_grad,) * n_seq, parts[0], *parts_recv, after=(gain_q,), micros=0.3
     )
+
     slots_recv = to_peers("seq", slot_grads[1:])
 
     def weights_body(ids_ref, kn_ref, vp_ref, *rest):
@@ -548,7 +566,8 @@
 
     chunk_shape = sds((span_rows + 2 * heads, HD), BF16)
     chunk = whole_call(chunk_body, chunk_shape, w_same, w_recv, gain_q, gain_k, micros=0.3)
-    chunks = [chunk] + to_peers("seq", [chunk] * (n_seq - 1))
+    chunks = to_peers("seq", [chunk] * (n_seq - 1))
+    chunk_other = to_core(chunk)
 
     def send_out(buffer, target, sems, index, at):
         copy = pltpu.make_async_copy(buffer.at[:, at], target.at[:, at], sems.at[index])
@@ -574,63 +593,65 @@
             cost_estimate=cost_of(micros),
         )(*ins, *after)
 
-    def back_body(ids_ref, gk_ref, gv_ref, kp_ref, wk_ref, wv_ref, kg_ref, dq_ref, *rest):
+    def spread_back(gm, w):
+        wide_rows = dot(gm, w, NT)
+        return jnp.concatenate([wide_rows[:, j * HD : (j + 1) * HD] for j in range(KS)], axis=0)
+
+    def head_places(mine):
+        for r in range(n_seq):
+            for i in range(hp):
+                h = (mine ^ r) * hp + i
+                narrow = slice(i * HD, (i + 1) * HD)
+                yield r, i, h, narrow, pl.ds(pl.multiple_of(h * HD, HD), HD)
+
+    def back_keys_body(ids_ref, gk_ref, kp_ref, wk_ref, kg_ref, dq_ref, *rest):
         gm = rest[:n_seq]
-        gkn_ref, dots_ref, value_ref, buffer, sems = rest[n_seq:]
-        unorder = row_order_back(rows)
+        gkn_ref, dots_ref = rest[n_seq:]
         total = jnp.zeros((rows, HD), F32)
-        copies = []
-        for r in range(n_seq):
-            block = ids_ref[0] ^ r
-            for i in range(hp):
-                narrow = slice(i * HD, (i + 1) * HD)
-                h = block * hp + i
-                at = pl.ds(pl.multiple_of(h * HD, HD), HD)
-                sides = []
-                for tensor, w_ref in ((0, wk_ref), (1, wv_ref)):
-                    spread = dot(gm[r][tensor, :, narrow], w_ref[h], NT)
-                    sides.append(
-                        jnp.concatenate(
-                            [spread[:, j * HD : (j + 1) * HD] for j in range(KS)], axis=0
-                        )
-                    )
-                gkn = gk_ref[:, at] + sides[0]
-                gkn_ref[:, at] = gkn
-                total = total + gkn * kp_ref[:, at].astype(F32) * kg_ref[:, at]
-                value = (gv_ref[:, at] + sides[1]).astype(BF16)
-                buffer[:, at] = dot(unorder, value).astype(BF16)
-            wide_at = pl.ds(pl.multiple_of(block * wide, wide), wide)
-            copies.append(send_out(buffer, value_ref, sems.at[0], r, wide_at))
+        for r, i, h, narrow, at in head_places(ids_ref[0]):
+            gkn = gk_ref[:, at] + spread_back(gm[r][0, :, narrow], wk_ref[h])
+            gkn_ref[:, at] = gkn
+            total = total + gkn * kp_ref[:, at].astype(F32) * kg_ref[:, at]
         dots_ref[0:1, :] = dq_ref[...]
         dots_ref[1:2, :] = lane_sum_row(total)
+
+    gkn, dots = whole_call(
+        back_keys_body,
+        (wide_f32, two_rows),
+        ids, gk_local, kp, key_squeeze, kg, dot_q, slot_grads[0], *slots_recv,
+        micros=2.0,
+        after=(chunk,),
+    )
+
+    def back_values_body(ids_ref, gv_ref, wv_ref, *rest):
+        gm = rest[:n_seq]
+        mark_ref, value_ref, buffer, sems = rest[n_seq:]
+        mark_ref[...] = jnp.zeros_like(mark_ref)
+        unorder = row_order_back(rows)
+        copies = []
+        for r, i, h, narrow, at in head_places(ids_ref[0]):
+            value = gv_ref[:, at] + spread_back(gm[r][1, :, narrow], wv_ref[h])
+            buffer[:, at] = dot(unorder, value.astype(BF16)).astype(BF16)
+            if i == hp - 1:
+                block = ids_ref[0] ^ r
+                wide_at = pl.ds(pl.multiple_of(block * wide, wide), wide)
+                copies.append(send_out(buffer, value_ref, sems.at[0], r, wide_at))
         for copy in copies:
             copy.wait()
 
-    gkn, dots, grad_value = column_out(
-        back_body,
-        (wide_f32, two_rows, rows_shape),
+    mark, grad_value = column_out(
+        back_values_body,
+        (sds((8, HD), F32), rows_shape),
         1,
-        ids, gk_local, gv_local, kp, key_squeeze, value_squeeze, kg, dot_q,
-        slot_grads[0], *slots_recv,
-        micros=3.0,
-        after=(chunk,),
-    )
-    dots_peers = to_peers("head", [dots] * (n_head - 1))
-
-    def pack_body(*refs):
-        for r in range(n_seq):
-            refs[n_seq][r] = refs[r][...]
-
-    packed_shape = sds((n_seq,) + chunk_shape.shape, BF16)
-    packed = whole_call(pack_body, packed_shape, *chunks, micros=0.1, after=(dots_peers[0],))
-    packed_other = to_core(packed)
+        ids, gv_local, value_squeeze, slot_grads[0], *slots_recv,
+        micros=2.0,
+        after=(dots,),
+    )
+    dots_parts = over_heads(dots, beside=(mark,))
 
     def norms_body(q_ref, kp_ref, gq_ref, gkn_ref, qg_ref, kg_ref, inv_ref, *rest):
-        dot_refs = rest[:n_head]
-        out_q, out_k, buffer_q, buffer_k, sems = rest[n_head:]
-        total = dot_refs[0][...]
-        for other in dot_refs[1:]:
-            total = total + other[...]
+        dots_a, dots_b, out_q, out_k, buffer_q, buffer_k, sems = rest
+        total = dots_a[...] + dots_b[...]
         inv_rows = inv_ref[...]
         inv_c = as_columns(inv_rows)
         pull = as_columns(inv_rows * inv_rows * inv_rows * total / full_width)
@@ -656,59 +677,138 @@
         norms_body,
         (rows_shape, rows_shape),
         2,
-        q, kp, gq, gkn, qg, kg, inv, dots, *dots_peers,
+        q, kp, gq, gkn, qg, kg, inv, *dots_parts,
         micros=2.0,
     )
 
-    def finish_body(ids_ref, kg_ref, wk_ref, same, other, *rest):
-        gq_ref, gk_ref, gks_ref, gvs_ref, buffer_k, buffer_v, sems = rest
+    kernel_out = sds((heads, KS * HD, HD), F32)
+    gains_shape = sds((heads, HD), F32)
+
+    def write_chunk(mine, r, read, buffer, sem, target):
+        start = (mine ^ r) * hp
+        for i in range(hp):
+            buffer[start + i] = read(slice(i * KS * HD, (i + 1) * KS * HD)).astype(F32)
+        at = pl.ds(start, hp)
+        copy = pltpu.make_async_copy(buffer.at[at], target.at[at], sem)
+        copy.start()
+        return copy
+
+    def own_chunk_body(ids_ref, same, other, *rest):
+        mark_ref, gks_ref, gvs_ref, buffer_k, buffer_v, sems = rest
+        mark_ref[...] = jnp.zeros_like(mark_ref)
         first = ids_ref[1] == 0
-        parts = same[0, span_rows:, :].astype(F32) + other[0, span_rows:, :].astype(F32)
-        for r in peers:
-            parts += same[r, span_rows:, :].astype(F32) + other[r, span_rows:, :].astype(F32)
-        gq_ref[...] = parts[:heads]
-        gk_ref[...] = parts[heads:]
-        copies = []
-        for r in range(n_seq):
-            start = (ids_ref[0] ^ r) * hp
-            for i in range(hp):
-                h = start + i
-                span = slice(i * KS * HD, (i + 1) * KS * HD)
-                a = same[r, span, :].astype(F32)
-                b = other[r, span, :].astype(F32)
-                grad_w = jnp.where(first, a, b)
-                buffer_k[h] = grad_w
-                buffer_v[h] = jnp.where(first, b, a)
-                prod = grad_w * wk_ref[h].astype(F32)
-                total = prod[:HD]
-                for j in range(1, KS):
-                    total = total + prod[j * HD : (j + 1) * HD]
-                row = lane_sum_row(total)
-                at = pl.ds(h, 1)
-                gain = kg_ref[:, pl.ds(pl.multiple_of(h * HD, HD), HD)]
-                gk_ref[at, :] = gk_ref[at, :] + row / gain
-            for tensor, (buffer, target) in enumerate(((buffer_k, gks_ref), (buffer_v, gvs_ref))):
-                at = pl.ds(start, hp)
-                copy = pltpu.make_async_copy(buffer.at[at], target.at[at], sems.at[tensor, r])
-                copy.start()
-                copies.append(copy)
+        copies = [
+            write_chunk(
+                ids_ref[0], 0, lambda at: jnp.where(first, same[at, :], other[at, :]),
+                buffer_k, sems.at[0], gks_ref,
+            ),
+            write_chunk(
+                ids_ref[0], 0, lambda at: jnp.where(first, other[at, :], same[at, :]),
+                buffer_v, sems.at[1], gvs_ref,
+            ),
+        ]
         for copy in copies:
             copy.wait()
 
-    kernel_out = sds((heads, KS * HD, HD), F32)
-    gains_shape = sds((heads, HD), F32)
+    smem = pl.BlockSpec(memory_space=pltpu.SMEM)
     inside = pl.BlockSpec(memory_space=pltpu.VMEM)
     outside = pl.BlockSpec(memory_space=pl.ANY)
-    gain_q_all, gain_k_all, gks, gvs = pl.pallas_call(
-        finish_body,
-        out_shape=(gains_shape, gains_shape, kernel_out, kernel_out),
-        in_specs=[pl.BlockSpec(memory_space=pltpu.SMEM)] + [inside] * 4,
-        out_specs=(inside, inside, outside, outside),
-        scratch_shapes=[pltpu.VMEM(kernel_out.shape, F32)] * 2
-        + [pltpu.SemaphoreType.DMA((2, n_seq))],
-        compiler_params=pltpu.CompilerParams(vmem_limit_bytes=40 * 2**20),
-        cost_estimate=cost_of(3.0),
-    )(ids, kg, key_squeeze, packed, packed_other)
+    buffer = pltpu.VMEM(kernel_out.shape, F32)
+    params = pltpu.CompilerParams(vmem_limit_bytes=40 * 2**20)
+    own_mark, *part_written = pl.pallas_call(
+        own_chunk_body,
+        out_shape=(sds((8, HD), F32), kernel_out, kernel_out),
+        in_specs=[smem, inside, inside],
+        out_specs=(inside, outside, outside),
+        scratch_shapes=[buffer, buffer, pltpu.SemaphoreType.DMA((2,))],
+        compiler_params=params,
+        cost_estimate=cost_of(1.2),
+    )(ids, chunk, chunk_other)
+
+    def pack_body(*refs):
+        for r in range(n_seq - 1):
+            refs[n_seq - 1][r] = refs[r][...]
+
+    packed_shape = sds((n_seq - 1,) + chunk_shape.shape, BF16)
+    packed = whole_call(pack_body, packed_shape, *chunks, micros=0.1, after=(dots_parts[1], own_mark))
+    packed_other = to_core(packed)
+
+    def this_core_body(ids_ref, same, gks_in, gvs_in, gks_ref, gvs_ref, buffer, sems):
+        for tensor, target in enumerate((gks_ref, gvs_ref)):
+            @pl.when(ids_ref[1] == tensor)
+            def _(target=target):
+                copies = [
+                    write_chunk(
+                        ids_ref[0], r, lambda at, r=r: same[r - 1, at, :],
+                        buffer, sems.at[r], target,
+                    )
+                    for r in peers
+                ]
+                for copy in copies:
+                    copy.wait()
+
+    def other_core_body(ids_ref, same_0, other_0, same, other, kg_ref, wk_ref, *rest):
+        gks_ref, gvs_ref, gq_ref, gk_ref, buffer, sems = rest[2:]
+        first = ids_ref[1] == 0
+
+        def pair(r, at):
+            if r == 0:
+                return same_0[at, :], other_0[at, :]
+            return same[r - 1, at, :], other[r - 1, at, :]
+
+        def gains():
+            total = jnp.zeros((2 * heads, HD), F32)
+            for r in range(n_seq):
+                a, b = pair(r, slice(span_rows, span_rows + 2 * heads))
+                total = total + a.astype(F32) + b.astype(F32)
+            gq_ref[...] = total[:heads]
+            gk_ref[...] = total[heads:]
+            for r in range(n_seq):
+                for i in range(hp):
+                    h = (ids_ref[0] ^ r) * hp + i
+                    total = jnp.zeros((HD, HD), F32)
+                    for j in range(KS):
+                        a, b = pair(r, slice((i * KS + j) * HD, (i * KS + j + 1) * HD))
+                        kernel = wk_ref[h, j * HD : (j + 1) * HD, :]
+                        total = total + jnp.where(first, a, b).astype(F32) * kernel.astype(F32)
+                    at = pl.ds(h, 1)
+                    gain = kg_ref[:, pl.ds(pl.multiple_of(h * HD, HD), HD)]
+                    gk_ref[at, :] = gk_ref[at, :] + lane_sum_row(total) / gain
+
+        for tensor, target in enumerate((gvs_ref, gks_ref)):
+            @pl.when(ids_ref[1] == tensor)
+            def _(target=target):
+                copies = [
+                    write_chunk(
+                        ids_ref[0], r, lambda at, r=r: other[r - 1, at, :],
+                        buffer, sems.at[r], target,
+                    )
+                    for r in peers
+                ]
+                gains()
+                for copy in copies:
+                    copy.wait()
+
+    part_written = pl.pallas_call(
+        this_core_body,
+        out_shape=(kernel_out, kernel_out),
+        in_specs=[smem, inside, outside, outside],
+        out_specs=(outside, outside),
+        input_output_aliases={2: 0, 3: 1},
+        scratch_shapes=[buffer, pltpu.SemaphoreType.DMA((n_seq,))],
+        compiler_params=params,
+        cost_estimate=cost_of(1.6),
+    )(ids, packed, *part_written)
+    gks, gvs, gain_q_all, gain_k_all = pl.pallas_call(
+        other_core_body,
+        out_shape=(kernel_out, kernel_out, gains_shape, gains_shape),
+        in_specs=[smem] + [inside] * 6 + [outside] * 2,
+        out_specs=(outside, outside, inside, inside),
+        input_output_aliases={7: 0, 8: 1},
+        scratch_shapes=[buffer, pltpu.SemaphoreType.DMA((n_seq,))],
+        compiler_params=params,
+        cost_estimate=cost_of(2.2),
+    )(ids, chunk, chunk_other, packed, packed_other, kg, key_squeeze, *part_written)
     return (
         grad_query[None],
         grad_key[None],

time: 79.8 us -> 73.5 us (0.921)
  waiting for transfers between devices: 26.3 us -> 19.6 us
  Pallas kernels: 22.6 us -> 25.1 us
  starting transfers between devices: 28.6 us -> 27.4 us
  local copies, waits for them, and re-layouts: 1.15 us -> 0.04 us
    ppermute x21 -> x18, waiting for transfers between devices: 26.3 us -> 17.3 us  [to_peers(): lax.ppermute(a, axis, [(i, i ^ k) for i in range(n)])]
    ppermute x21 -> x18, starting transfers between devices: 28.5 us -> 25.4 us  [to_peers(): lax.ppermute(a, axis, [(i, i ^ k) for i in range(n)])]
    ppermute x0 -> x2, waiting for transfers between devices: none -> 2.37 us  [over_heads(): got = lax.ppermute(a, 'head', [(i, i ^ step) for i in range(n_head)])]
    pallas_call x1 -> x3, Pallas kernels: 3.74 us -> 5.92 us  [the longest x1 2.58 us: on_device(): pl.pallas_call(other_core_body, out_shape=(kernel_out, kernel_out, gains_...]
    ppermute x0 -> x2, starting transfers between devices: none -> 1.86 us  [over_heads(): got = lax.ppermute(a, 'head', [(i, i ^ step) for i in range(n_head)])]
    pallas_call x11 -> x13, Pallas kernels: 13.8 us -> 15.3 us  [whole_call(): pl.pallas_call(lambda *refs: body(*refs[:len(ins)], *refs[len(ins) + skip...]
    pallas_call x2, Pallas kernels: 5.09 us -> 3.97 us  [column_out(): pl.pallas_call(lambda *refs: body(*refs[:len(ins)], *refs[len(ins) + skip...]
    unnamed x20 -> x18, local copies, waits for them, and re-layouts: 1.15 us -> 0.04 us
  transfers between devices with their start and end apart: 23 -> 23, of which waited for: 13 -> 13; matrix products, arithmetic and copies ran while one was open for 0% -> 0% of each run, Pallas kernels for 18% -> 25%
where the time goes in v4:
time: 73.5 us; the launch traced here: 73.1 us
  starting transfers between devices  27.4 us (37%)
  Pallas kernels  25.1 us (34%)
  waiting for transfers between devices  19.6 us (27%)
  between operations  0.83 us (1%)
    ppermute x18, starting transfers between devices, to_peers(): lax.ppermute(a, axis, [(i, i ^ k) for i in range(n)])  25.4 us
    ppermute x18, waiting for transfers between devices, to_peers(): lax.ppermute(a, axis, [(i, i ^ k) for i in range(n)])  17.3 us
    pallas_call x13, Pallas kernels, whole_call(): pl.pallas_call(lambda *refs: body(*refs[:len(ins)], *refs[len(ins) + skip...  15.3 us
    pallas_call x2, Pallas kernels, column_out(): pl.pallas_call(lambda *refs: body(*refs[:len(ins)], *refs[len(ins) + skip...  3.97 us
    pallas_call x1, Pallas kernels, on_device(): pl.pallas_call(other_core_body, out_shape=(kernel_out, kernel_out, gains_...  2.58 us
    ppermute x2, waiting for transfers between devices, over_heads(): got = lax.ppermute(a, 'head', [(i, i ^ step) for i in range(n_head)])  2.37 us
    ppermute x2, starting transfers between devices, over_heads(): got = lax.ppermute(a, 'head', [(i, i ^ step) for i in range(n_head)])  1.86 us
    pallas_call x1, Pallas kernels, on_device(): pl.pallas_call(this_core_body, out_shape=(kernel_out, kernel_out), in_spe...  1.76 us
  transfers between devices with their start and end apart: 23, of which 13 were waited for; matrix products, arithmetic and copies ran while one was open for 0% of the time, Pallas kernels for 25%

profile of v4, /device:TPU:0, one launch (start us, length us, event | category | flops | bytes accessed | tf_op | source)
XLA Modules:
  0.0 73.1 jit_solution(3225654348080759636)
XLA Ops:
  0.7 2.2 %shard_map.136.refs_4_ = f32[2,256]{1,0:T(2,128)} custom-call(bf16[256,1024]{1,0:T(8,128)(2,1)} %bitcast.16, bf16[256,1024]{1,0:T(8,128)(2,1)} %bitcast.24), custom_call_target="tpu_custom_call" | custom-call | flops 1500000000 | bytes 5400000 | tf_op jit(solution)/shard_map/pallas_call | solution.py:210
  2.8 5.0 %collective-permute-start.2 = (f32[2,256]{1,0:T(2,128)}, f32[2,256]{1,0:T(2,128)S(1)}, u32[]{:S(2)}, u32[]{:S(2)}) collective-permute-start(f32[2,256]{1,0:T(2,128)} %shard_map.136.refs_4_), channel_id=1, source_target_pairs={{0,6},{2,4},{4,2},{6,0},{1,7},{3,5},{5,3},{7,1},{8,14},{10,12},{12... | collective-permute-start | bytes 6152 | tf_op jit(solution)/shard_map/ppermute | solution.py:293
  9.7 2.9 %collective-permute-done.1.refs_6_ = f32[2,256]{1,0:T(2,128)S(1)} collective-permute-done((f32[2,256]{1,0:T(2,128)}, f32[2,256]{1,0:T(2,128)S(1)}, u32[]{:S(2)}, u32[]{:S(2)}) %collective-permute-start.1) | collective-permute-done | bytes 2080 | tf_op jit(solution)/shard_map/ppermute | solution.py:293
  13.5 2.5 %collective-permute-start.5 = (bf16[2,256,256]{2,1,0:T(8,128)(2,1)S(1)}, bf16[2,256,256]{2,1,0:T(8,128)(2,1)S(1)}, u32[]{:S(2)}, u32[]{:S(2)}) collective-permute-start(bf16[2,256,256]{2,1,0:T(8,128)(2,1)S(1)} %get-tuple-element.58), channel_id=1, source_target_pairs={{0,24},{8,16},{16,8},{24,0},{1,25},{9,17},{17,9},{25,1},{2,26},{10... | collective-permute-start | bytes 786440 | tf_op jit(solution)/shard_map/ppermute | solution.py:293
  19.4 1.6 %collective-permute-start.6 = (bf16[2,256,256]{2,1,0:T(8,128)(2,1)S(1)}, bf16[2,256,256]{2,1,0:T(8,128)(2,1)S(1)}, u32[]{:S(2)}, u32[]{:S(2)}) collective-permute-start(bf16[2,256,256]{2,1,0:T(8,128)(2,1)S(1)} %get-tuple-element.61), channel_id=1, source_target_pairs={{0,8},{8,0},{16,24},{24,16},{1,9},{9,1},{17,25},{25,17},{2,10},{10... | collective-permute-start | bytes 786440 | tf_op jit(solution)/shard_map/ppermute | solution.py:293
  21.0 1.5 %collective-permute-start.7 = (bf16[2,256,256]{2,1,0:T(8,128)(2,1)S(1)}, bf16[2,256,256]{2,1,0:T(8,128)(2,1)S(1)}, u32[]{:S(2)}, u32[]{:S(2)}) collective-permute-start(bf16[2,256,256]{2,1,0:T(8,128)(2,1)S(1)} %get-tuple-element.62), channel_id=1, source_target_pairs={{0,16},{8,24},{16,0},{24,8},{1,17},{9,25},{17,1},{25,9},{2,18},{10... | collective-permute-start | bytes 786440 | tf_op jit(solution)/shard_map/ppermute | solution.py:293
  23.7 2.4 %collective-permute-start.8 = (bf16[2,256,256]{2,1,0:T(8,128)(2,1)S(1)}, bf16[2,256,256]{2,1,0:T(8,128)(2,1)S(1)}, u32[]{:S(2)}, u32[]{:S(2)}) collective-permute-start(bf16[2,256,256]{2,1,0:T(8,128)(2,1)S(1)} %get-tuple-element.63), channel_id=1, source_target_pairs={{0,24},{8,16},{16,8},{24,0},{1,25},{9,17},{17,9},{25,1},{2,26},{10... | collective-permute-start | bytes 786440 | tf_op jit(solution)/shard_map/ppermute | solution.py:293
  27.3 2.0 %collective-permute-done.3.refs_4_.refs_8_ = bf16[2,256,256]{2,1,0:T(8,128)(2,1)S(1)} collective-permute-done((bf16[2,256,256]{2,1,0:T(8,128)(2,1)S(1)}, bf16[2,256,256]{2,1,0:T(8,128)(2,1)S(1)}, u32[]{:S(2)}, u32[]{:S(2)}) %collective-permute-start.3) | collective-permute-done | bytes 262176 | tf_op jit(solution)/shard_map/ppermute | solution.py:293
  29.4 3.3 %shard_map.140 = (f32[8,8,256]{2,1,0:T(8,128)S(1)}, bf16[8,192,256]{2,1,0:T(8,128)(2,1)S(1)}, bf16[2,192,256]{2,1,0:T(8,128)(2,1)S(1)}, bf16[2,192,256]{2,1,0:T(...) custom-call(s32[2]{0:T(128)S(1)} %pad_add_fusion.refs_0_.ids_ref, ...), custom_call_target="tpu_custom_call" | custom-call | flops 500000000 | bytes 1800000 | tf_op jit(solution)/shard_map/pallas_call | solution.py:210
  32.7 1.6 %collective-permute-start.9 = (bf16[2,192,256]{2,1,0:T(8,128)(2,1)S(1)}, bf16[2,192,256]{2,1,0:T(8,128)(2,1)S(1)}, u32[]{:S(2)}, u32[]{:S(2)}) collective-permute-start(bf16[2,192,256]{2,1,0:T(8,128)(2,1)S(1)} %get-tuple-element.68), channel_id=1, source_target_pairs={{0,8},{8,0},{16,24},{24,16},{1,9},{9,1},{17,25},{25,17},{2,10},{10... | collective-permute-start | bytes 589832 | tf_op jit(solution)/shard_map/ppermute | solution.py:293
  35.0 1.4 %collective-permute-start.11 = (bf16[2,192,256]{2,1,0:T(8,128)(2,1)S(1)}, bf16[2,192,256]{2,1,0:T(8,128)(2,1)S(1)}, u32[]{:S(2)}, u32[]{:S(2)}) collective-permute-start(bf16[2,192,256]{2,1,0:T(8,128)(2,1)S(1)} %get-tuple-element.70), channel_id=1, source_target_pairs={{0,24},{8,16},{16,8},{24,0},{1,25},{9,17},{17,9},{25,1},{2,26},{10... | collective-permute-start | bytes 589832 | tf_op jit(solution)/shard_map/ppermute | solution.py:293
  36.5 4.2 %collective-permute-done.8.refs_15_.refs_9_ = bf16[2,256,256]{2,1,0:T(8,128)(2,1)S(1)} collective-permute-done((bf16[2,256,256]{2,1,0:T(8,128)(2,1)S(1)}, bf16[2,256,256]{2,1,0:T(8,128)(2,1)S(1)}, u32[]{:S(2)}, u32[]{:S(2)}) %collective-permute-start.8) | collective-permute-done | bytes 262176 | tf_op jit(solution)/shard_map/ppermute | solution.py:293
  40.6 3.6 %shard_map.141 = (f32[256,1024]{1,0:T(8,128)S(1)}, f32[256,1024]{1,0:T(8,128)S(1)}, f32[256,1024]{1,0:T(8,128)S(1)}, f32[1,256]{1,0:T(1,128)S(1)}, f32[8,128]{1,0:T(8,128)S(1)}, /*index=5*/f32[8,128]{1,0:T(8,128)S(1)}) custom-call(bf16[256,1024]{1,0:T(8,128)(2,1)S(1)} %bitcast.18, bf16[256,1024]{1,0:T(8,128)(2,1)S(1)} %get-tuple-element.56.refs_1_.refs_2_, ...), custom_call_target="tpu_custom_call" | custom-call | flops 500000000 | bytes 1800000 | tf_op jit(solution)/shard_map/pallas_call | solution.py:210
  44.4 2.0 %collective-permute-done.11.refs_3_ = bf16[2,192,256]{2,1,0:T(8,128)(2,1)S(1)} collective-permute-done((bf16[2,192,256]{2,1,0:T(8,128)(2,1)S(1)}, bf16[2,192,256]{2,1,0:T(8,128)(2,1)S(1)}, u32[]{:S(2)}, u32[]{:S(2)}) %collective-permute-start.11) | collective-permute-done | bytes 196640 | tf_op jit(solution)/shard_map/ppermute | solution.py:293
  47.6 1.6 %collective-permute-start.12 = (bf16[2,64,256]{2,1,0:T(8,128)(2,1)S(1)}, bf16[2,64,256]{2,1,0:T(8,128)(2,1)S(1)}, u32[]{:S(2)}, u32[]{:S(2)}) collective-permute-start(bf16[2,64,256]{2,1,0:T(8,128)(2,1)S(1)} %get-tuple-element.73.refs_4_), channel_id=1, source_target_pairs={{0,8},{8,0},{16,24},{24,16},{1,9},{9,1},{17,25},{25,17},{2,10},{10... | collective-permute-start | bytes 196616 | tf_op jit(solution)/shard_map/ppermute | solution.py:293
  49.2 1.5 %collective-permute-start.13 = (bf16[2,64,256]{2,1,0:T(8,128)(2,1)S(1)}, bf16[2,64,256]{2,1,0:T(8,128)(2,1)S(1)}, u32[]{:S(2)}, u32[]{:S(2)}) collective-permute-start(bf16[2,64,256]{2,1,0:T(8,128)(2,1)S(1)} %get-tuple-element.74.refs_5_), channel_id=1, source_target_pairs={{0,16},{8,24},{16,0},{24,8},{1,17},{9,25},{17,1},{25,9},{2,18},{10... | collective-permute-start | bytes 196616 | tf_op jit(solution)/shard_map/ppermute | solution.py:293
  51.3 2.5 %collective-permute-start.21 = (bf16[1040,128]{1,0:T(8,128)(2,1)S(1)}, bf16[1040,128]{1,0:T(8,128)(2,1)S(1)}, u32[]{:S(2)}, u32[]{:S(2)}) collective-permute-start(bf16[1040,128]{1,0:T(8,128)(2,1)S(1)} %shard_map.144.refs_10_.same.same_0), channel_id=1, source_target_pairs={{0,24},{8,16},{16,8},{24,0},{1,25},{9,17},{17,9},{25,1},{2,26},{10... | collective-permute-start | bytes 798728 | tf_op jit(solution)/shard_map/ppermute | solution.py:293
  54.8 1.9 %collective-permute-done.14.refs_9_.refs_6_ = bf16[2,64,256]{2,1,0:T(8,128)(2,1)S(1)} collective-permute-done((bf16[2,64,256]{2,1,0:T(8,128)(2,1)S(1)}, bf16[2,64,256]{2,1,0:T(8,128)(2,1)S(1)}, u32[]{:S(2)}, u32[]{:S(2)}) %collective-permute-start.14) | collective-permute-done | bytes 65568 | tf_op jit(solution)/shard_map/ppermute | solution.py:293
  58.0 2.3 %shard_map.146 = (f32[8,128]{1,0:T(8,128)S(1)}, bf16[256,1024]{1,0:T(8,128)(2,1)}) custom-call(s32[2]{0:T(128)S(1)} %pad_add_fusion.refs_0_.ids_ref, f32[256,1024]{1,0:T(8,128)S(1)} %get-tuple-element.81.refs_1_, bf16[8,512,128]{2,1,0:T(8,128)(2,1)S(1)} %copy-done.3, bf16[2,64,256]{2,1,0:T(8,128)(2,1)S(1)} %get-tuple-element.72.refs_3_.refs_6_, ...), custom_call_target="tpu_custom_call" | custom-call | flops 2000000000 | bytes 7200000 | tf_op jit(solution)/shard_map/pallas_call | solution.py:581
  61.6 1.8 %collective-permute-start.17 = (f32[2,256]{1,0:T(2,128)S(1)}, f32[2,256]{1,0:T(2,128)S(1)}, u32[]{:S(2)}, u32[]{:S(2)}) collective-permute-start(f32[2,256]{1,0:T(2,128)S(1)} %shard_map.147.refs_7_), channel_id=1, source_target_pairs={{0,4},{2,6},{4,0},{6,2},{1,5},{3,7},{5,1},{7,3},{8,12},{10,14},{12... | collective-permute-start | bytes 6152 | tf_op jit(solution)/shard_map/ppermute | solution.py:305
  63.4 1.6 %shard_map.149 = (f32[8,128]{1,0:T(8,128)S(1)}, f32[8,512,128]{2,1,0:T(8,128)}, f32[8,512,128]{2,1,0:T(8,128)}) custom-call(s32[2]{0:T(128)S(1)} %pad_add_fusion.refs_0_.ids_ref, bf16[1040,128]{1,0:T(8,128)(2,1)S(1)} %shard_map.144.refs_10_.same.same_0, bf16[1040,128]{1,0:T(8,128)(2,1)S(1)} %collective-permute-done.18.other.other_0), custom_call_target="tpu_custom_call" | custom-call | flops 1200000000 | bytes 4320000 | tf_op jit(solution)/shard_map/pallas_call | solution.py:718
  67.1 1.7 %shard_map.148 = (bf16[256,1024]{1,0:T(8,128)(2,1)}, bf16[256,1024]{1,0:T(8,128)(2,1)}) custom-call(bf16[256,1024]{1,0:T(8,128)(2,1)S(1)} %bitcast.19, bf16[256,1024]{1,0:T(8,128)(2,1)S(1)} %get-tuple-element.56.refs_1_.refs_2_, f32[256,1024]{1,0:T(8,128)S(1)} %get-tuple-element.64.refs_2_, f32[256,1024]{1,0:T(8,128)S(1)} %get-tuple-element.79.refs_3_, ...), custom_call_target="tpu_custom_call" | custom-call | flops 2000000000 | bytes 7200000 | tf_op jit(solution)/shard_map/pallas_call | solution.py:581
  68.8 1.8 %shard_map.151 = (f32[8,512,128]{2,1,0:T(8,128)}, f32[8,512,128]{2,1,0:T(8,128)}) custom-call(s32[2]{0:T(128)S(1)} %pad_add_fusion.refs_0_.ids_ref, bf16[3,1040,128]{2,1,0:T(8,128)(2,1)S(1)} %shard_map.150.same, f32[8,512,128]{2,1,0:T(8,128)} %get-tuple-element.87.gks_in, ...), custom_call_target="tpu_custom_call", output_to_operand_aliasing={{0}: (2, {}), {1}: (3, {})} | custom-call | flops 1600000000 | bytes 5760000 | tf_op jit(solution)/shard_map/pallas_call | solution.py:792
  70.5 2.6 %shard_map.152 = (f32[8,512,128]{2,1,0:T(8,128)}, f32[8,512,128]{2,1,0:T(8,128)}, f32[8,128]{1,0:T(8,128)}, f32[8,128]{1,0:T(8,128)}) custom-call(s32[2]{0:T(128)S(1)} %pad_add_fusion.refs_0_.ids_ref, bf16[1040,128]{1,0:T(8,128)(2,1)S(1)} %shard_map.144.refs_10_.same.same_0, ...), custom_call_target="tpu_custom_call", output_to_operand_aliasing={{0}: (7, {}), {1}: (8, {})} | custom-call | flops 2200000000 | bytes 7920000 | tf_op jit(solution)/shard_map/pallas_call | solution.py:802
  (59 shorter events, 16.9 us)
Async XLA Ops:
  2.8 9.8 %copy-start.8 = (f32[2,256]{1,0:T(2,128)S(1)}, f32[2,256]{1,0:T(2,128)}, u32[]{:S(2)}) copy-start(f32[2,256]{1,0:T(2,128)} %shard_map.136.refs_4_) | copy-start | bytes 6148
  2.8 6.9 %collective-permute-start.2 = (f32[2,256]{1,0:T(2,128)}, f32[2,256]{1,0:T(2,128)S(1)}, u32[]{:S(2)}, u32[]{:S(2)}) collective-permute-start(f32[2,256]{1,0:T(2,128)} %shard_map.136.refs_4_), channel_id=1, source_target_pairs={{0,6},{2,4},{4,2},{6,0},{1,7},{3,5},{5,3},{7,1},{8,14},{10,12},{12... | collective-permute-start | bytes 6152 | tf_op jit(solution)/shard_map/ppermute | solution.py:293
  7.9 4.7 %collective-permute-start.1 = (f32[2,256]{1,0:T(2,128)}, f32[2,256]{1,0:T(2,128)S(1)}, u32[]{:S(2)}, u32[]{:S(2)}) collective-permute-start(f32[2,256]{1,0:T(2,128)} %shard_map.136.refs_4_), channel_id=1, source_target_pairs={{0,4},{2,6},{4,0},{6,2},{1,5},{3,7},{5,1},{7,3},{8,12},{10,14},{12... | collective-permute-start | bytes 6152 | tf_op jit(solution)/shard_map/ppermute | solution.py:293
  7.9 4.7 %collective-permute-start = (f32[2,256]{1,0:T(2,128)}, f32[2,256]{1,0:T(2,128)S(1)}, u32[]{:S(2)}, u32[]{:S(2)}) collective-permute-start(f32[2,256]{1,0:T(2,128)} %shard_map.136.refs_4_), channel_id=1, source_target_pairs={{0,2},{2,0},{4,6},{6,4},{1,3},{3,1},{5,7},{7,5},{8,10},{10,8},{12,... | collective-permute-start | bytes 6152 | tf_op jit(solution)/shard_map/ppermute | solution.py:293
  13.5 10.2 %collective-permute-start.5 = (bf16[2,256,256]{2,1,0:T(8,128)(2,1)S(1)}, bf16[2,256,256]{2,1,0:T(8,128)(2,1)S(1)}, u32[]{:S(2)}, u32[]{:S(2)}) collective-permute-start(bf16[2,256,256]{2,1,0:T(8,128)(2,1)S(1)} %get-tuple-element.58), channel_id=1, source_target_pairs={{0,24},{8,16},{16,8},{24,0},{1,25},{9,17},{17,9},{25,1},{2,26},{10... | collective-permute-start | bytes 786440 | tf_op jit(solution)/shard_map/ppermute | solution.py:293
  16.0 11.3 %collective-permute-start.4 = (bf16[2,256,256]{2,1,0:T(8,128)(2,1)S(1)}, bf16[2,256,256]{2,1,0:T(8,128)(2,1)S(1)}, u32[]{:S(2)}, u32[]{:S(2)}) collective-permute-start(bf16[2,256,256]{2,1,0:T(8,128)(2,1)S(1)} %get-tuple-element.58), channel_id=1, source_target_pairs={{0,16},{8,24},{16,0},{24,8},{1,17},{9,25},{17,1},{25,9},{2,18},{10... | collective-permute-start | bytes 786440 | tf_op jit(solution)/shard_map/ppermute | solution.py:293
  16.5 12.9 %collective-permute-start.3 = (bf16[2,256,256]{2,1,0:T(8,128)(2,1)S(1)}, bf16[2,256,256]{2,1,0:T(8,128)(2,1)S(1)}, u32[]{:S(2)}, u32[]{:S(2)}) collective-permute-start(bf16[2,256,256]{2,1,0:T(8,128)(2,1)S(1)} %get-tuple-element.58), channel_id=1, source_target_pairs={{0,8},{8,0},{16,24},{24,16},{1,9},{9,1},{17,25},{25,17},{2,10},{10... | collective-permute-start | bytes 786440 | tf_op jit(solution)/shard_map/ppermute | solution.py:293
  19.4 15.6 %collective-permute-start.6 = (bf16[2,256,256]{2,1,0:T(8,128)(2,1)S(1)}, bf16[2,256,256]{2,1,0:T(8,128)(2,1)S(1)}, u32[]{:S(2)}, u32[]{:S(2)}) collective-permute-start(bf16[2,256,256]{2,1,0:T(8,128)(2,1)S(1)} %get-tuple-element.61), channel_id=1, source_target_pairs={{0,8},{8,0},{16,24},{24,16},{1,9},{9,1},{17,25},{25,17},{2,10},{10... | collective-permute-start | bytes 786440 | tf_op jit(solution)/shard_map/ppermute | solution.py:293
  21.0 15.5 %collective-permute-start.7 = (bf16[2,256,256]{2,1,0:T(8,128)(2,1)S(1)}, bf16[2,256,256]{2,1,0:T(8,128)(2,1)S(1)}, u32[]{:S(2)}, u32[]{:S(2)}) collective-permute-start(bf16[2,256,256]{2,1,0:T(8,128)(2,1)S(1)} %get-tuple-element.62), channel_id=1, source_target_pairs={{0,16},{8,24},{16,0},{24,8},{1,17},{9,25},{17,1},{25,9},{2,18},{10... | collective-permute-start | bytes 786440 | tf_op jit(solution)/shard_map/ppermute | solution.py:293
  23.7 16.9 %collective-permute-start.8 = (bf16[2,256,256]{2,1,0:T(8,128)(2,1)S(1)}, bf16[2,256,256]{2,1,0:T(8,128)(2,1)S(1)}, u32[]{:S(2)}, u32[]{:S(2)}) collective-permute-start(bf16[2,256,256]{2,1,0:T(8,128)(2,1)S(1)} %get-tuple-element.63), channel_id=1, source_target_pairs={{0,24},{8,16},{16,8},{24,0},{1,25},{9,17},{17,9},{25,1},{2,26},{10... | collective-permute-start | bytes 786440 | tf_op jit(solution)/shard_map/ppermute | solution.py:293
  32.7 11.7 %collective-permute-start.9 = (bf16[2,192,256]{2,1,0:T(8,128)(2,1)S(1)}, bf16[2,192,256]{2,1,0:T(8,128)(2,1)S(1)}, u32[]{:S(2)}, u32[]{:S(2)}) collective-permute-start(bf16[2,192,256]{2,1,0:T(8,128)(2,1)S(1)} %get-tuple-element.68), channel_id=1, source_target_pairs={{0,8},{8,0},{16,24},{24,16},{1,9},{9,1},{17,25},{25,17},{2,10},{10... | collective-permute-start | bytes 589832 | tf_op jit(solution)/shard_map/ppermute | solution.py:293
  34.2 10.1 %collective-permute-start.10 = (bf16[2,192,256]{2,1,0:T(8,128)(2,1)S(1)}, bf16[2,192,256]{2,1,0:T(8,128)(2,1)S(1)}, u32[]{:S(2)}, u32[]{:S(2)}) collective-permute-start(bf16[2,192,256]{2,1,0:T(8,128)(2,1)S(1)} %get-tuple-element.69), channel_id=1, source_target_pairs={{0,16},{8,24},{16,0},{24,8},{1,17},{9,25},{17,1},{25,9},{2,18},{10... | collective-permute-start | bytes 589832 | tf_op jit(solution)/shard_map/ppermute | solution.py:293
  35.0 11.4 %collective-permute-start.11 = (bf16[2,192,256]{2,1,0:T(8,128)(2,1)S(1)}, bf16[2,192,256]{2,1,0:T(8,128)(2,1)S(1)}, u32[]{:S(2)}, u32[]{:S(2)}) collective-permute-start(bf16[2,192,256]{2,1,0:T(8,128)(2,1)S(1)} %get-tuple-element.70), channel_id=1, source_target_pairs={{0,24},{8,16},{16,8},{24,0},{1,25},{9,17},{17,9},{25,1},{2,26},{10... | collective-permute-start | bytes 589832 | tf_op jit(solution)/shard_map/ppermute | solution.py:293
  47.6 3.6 %collective-permute-start.15 = (bf16[1024,128]{1,0:T(8,128)(2,1)S(1)}, bf16[1024,128]{1,0:T(8,128)(2,1)S(1)}, u32[]{:S(2)}, u32[]{:S(2)}) collective-permute-start(bf16[1024,128]{1,0:T(8,128)(2,1)S(1)} %get-tuple-element.77), channel_id=1, source_target_pairs={{0,1},{1,0},{2,3},{3,2},{4,5},{5,4},{6,7},{7,6},{8,9},{9,8},{10,11... | collective-permute-start | bytes 786440 | tf_op jit(solution)/shard_map/ppermute | solution.py:310
  47.6 6.7 %collective-permute-start.12 = (bf16[2,64,256]{2,1,0:T(8,128)(2,1)S(1)}, bf16[2,64,256]{2,1,0:T(8,128)(2,1)S(1)}, u32[]{:S(2)}, u32[]{:S(2)}) collective-permute-start(bf16[2,64,256]{2,1,0:T(8,128)(2,1)S(1)} %get-tuple-element.73.refs_4_), channel_id=1, source_target_pairs={{0,8},{8,0},{16,24},{24,16},{1,9},{9,1},{17,25},{25,17},{2,10},{10... | collective-permute-start | bytes 196616 | tf_op jit(solution)/shard_map/ppermute | solution.py:293
  49.2 5.6 %collective-permute-start.13 = (bf16[2,64,256]{2,1,0:T(8,128)(2,1)S(1)}, bf16[2,64,256]{2,1,0:T(8,128)(2,1)S(1)}, u32[]{:S(2)}, u32[]{:S(2)}) collective-permute-start(bf16[2,64,256]{2,1,0:T(8,128)(2,1)S(1)} %get-tuple-element.74.refs_5_), channel_id=1, source_target_pairs={{0,16},{8,24},{16,0},{24,8},{1,17},{9,25},{17,1},{25,9},{2,18},{10... | collective-permute-start | bytes 196616 | tf_op jit(solution)/shard_map/ppermute | solution.py:293
  50.7 6.0 %collective-permute-start.14 = (bf16[2,64,256]{2,1,0:T(8,128)(2,1)S(1)}, bf16[2,64,256]{2,1,0:T(8,128)(2,1)S(1)}, u32[]{:S(2)}, u32[]{:S(2)}) collective-permute-start(bf16[2,64,256]{2,1,0:T(8,128)(2,1)S(1)} %get-tuple-element.75.refs_6_), channel_id=1, source_target_pairs={{0,24},{8,16},{16,8},{24,0},{1,25},{9,17},{17,9},{25,1},{2,26},{10... | collective-permute-start | bytes 196616 | tf_op jit(solution)/shard_map/ppermute | solution.py:293
  51.3 14.8 %collective-permute-start.21 = (bf16[1040,128]{1,0:T(8,128)(2,1)S(1)}, bf16[1040,128]{1,0:T(8,128)(2,1)S(1)}, u32[]{:S(2)}, u32[]{:S(2)}) collective-permute-start(bf16[1040,128]{1,0:T(8,128)(2,1)S(1)} %shard_map.144.refs_10_.same.same_0), channel_id=1, source_target_pairs={{0,24},{8,16},{16,8},{24,0},{1,25},{9,17},{17,9},{25,1},{2,26},{10... | collective-permute-start | bytes 798728 | tf_op jit(solution)/shard_map/ppermute | solution.py:293
  53.8 13.1 %collective-permute-start.20 = (bf16[1040,128]{1,0:T(8,128)(2,1)S(1)}, bf16[1040,128]{1,0:T(8,128)(2,1)S(1)}, u32[]{:S(2)}, u32[]{:S(2)}) collective-permute-start(bf16[1040,128]{1,0:T(8,128)(2,1)S(1)} %shard_map.144.refs_10_.same.same_0), channel_id=1, source_target_pairs={{0,16},{8,24},{16,0},{24,8},{1,17},{9,25},{17,1},{25,9},{2,18},{10... | collective-permute-start | bytes 798728 | tf_op jit(solution)/shard_map/ppermute | solution.py:293
  54.3 12.6 %collective-permute-start.19 = (bf16[1040,128]{1,0:T(8,128)(2,1)S(1)}, bf16[1040,128]{1,0:T(8,128)(2,1)S(1)}, u32[]{:S(2)}, u32[]{:S(2)}) collective-permute-start(bf16[1040,128]{1,0:T(8,128)(2,1)S(1)} %shard_map.144.refs_10_.same.same_0), channel_id=1, source_target_pairs={{0,8},{8,0},{16,24},{24,16},{1,9},{9,1},{17,25},{25,17},{2,10},{10... | collective-permute-start | bytes 798728 | tf_op jit(solution)/shard_map/ppermute | solution.py:293
  54.8 8.5 %collective-permute-start.18 = (bf16[1040,128]{1,0:T(8,128)(2,1)S(1)}, bf16[1040,128]{1,0:T(8,128)(2,1)S(1)}, u32[]{:S(2)}, u32[]{:S(2)}) collective-permute-start(bf16[1040,128]{1,0:T(8,128)(2,1)S(1)} %shard_map.144.refs_10_.same.same_0), channel_id=1, source_target_pairs={{0,1},{1,0},{2,3},{3,2},{4,5},{5,4},{6,7},{7,6},{8,9},{9,8},{10,11... | collective-permute-start | bytes 798728 | tf_op jit(solution)/shard_map/ppermute | solution.py:310
  57.9 3.7 %collective-permute-start.16 = (f32[2,256]{1,0:T(2,128)S(1)}, f32[2,256]{1,0:T(2,128)S(1)}, u32[]{:S(2)}, u32[]{:S(2)}) collective-permute-start(f32[2,256]{1,0:T(2,128)S(1)} %get-tuple-element.80.refs_7_.refs_0_), channel_id=1, source_target_pairs={{0,2},{2,0},{4,6},{6,4},{1,3},{3,1},{5,7},{7,5},{8,10},{10,8},{12,... | collective-permute-start | bytes 6152 | tf_op jit(solution)/shard_map/ppermute | solution.py:305
  61.6 4.5 %collective-permute-start.17 = (f32[2,256]{1,0:T(2,128)S(1)}, f32[2,256]{1,0:T(2,128)S(1)}, u32[]{:S(2)}, u32[]{:S(2)}) collective-permute-start(f32[2,256]{1,0:T(2,128)S(1)} %shard_map.147.refs_7_), channel_id=1, source_target_pairs={{0,4},{2,6},{4,0},{6,2},{1,5},{3,7},{5,1},{7,3},{8,12},{10,14},{12... | collective-permute-start | bytes 6152 | tf_op jit(solution)/shard_map/ppermute | solution.py:305
  67.0 3.5 %collective-permute-start.22 = (bf16[3,1040,128]{2,1,0:T(8,128)(2,1)S(1)}, bf16[3,1040,128]{2,1,0:T(8,128)(2,1)S(1)}, u32[]{:S(2)}, u32[]{:S(2)}) collective-permute-start(bf16[3,1040,128]{2,1,0:T(8,128)(2,1)S(1)} %shard_map.150.same), channel_id=1, source_target_pairs={{0,1},{1,0},{2,3},{3,2},{4,5},{5,4},{6,7},{7,6},{8,9},{9,8},{10,11... | collective-permute-start | bytes 2396168 | tf_op jit(solution)/shard_map/ppermute | solution.py:310
  (8 other events, 52.9 us)

commit v5 on v4

--- a/solution.py
+++ b/solution.py
@@ -349,8 +349,9 @@
     vp, mem_v = whole_call(
         values_body, (rows_shape, mem_shape), v, value_squeeze, micros=0.8
     )
-
-    def keys_body(k_ref, kg_ref, w_ref, mem_v_ref, *rest):
+    mv_recv = to_peers("seq", [mem_v] * (n_seq - 1))
+
+    def keys_body(k_ref, kg_ref, w_ref, *rest):
         ss_refs = rest[:n_head]
         inv_ref, kn_ref, mem_ref = rest[n_head:]
         total = ss_refs[0][...]
@@ -367,17 +368,15 @@
         inv_ref[...] = inv_c.T[:2]
         normed = (k_ref[...].astype(F32) * natural[:, 1:2] * kg_ref[...]).astype(BF16)
         kn_ref[...] = dot(order, normed).astype(BF16)
-        compress(kn_ref, w_ref, mem_ref.at[0])
-        mem_ref[1] = mem_v_ref[...]
-
-    mem_pair = sds((2, mem_rows, wide), BF16)
+        compress(kn_ref, w_ref, mem_ref)
+
     inv, kn, mem = whole_call(
         keys_body,
-        (two_rows, rows_shape, mem_pair),
-        k, kg, key_squeeze, mem_v, *ss_parts,
-        micros=1.5,
-    )
-    mem_recv = to_peers("seq", [mem] * (n_seq - 1))
+        (two_rows, rows_shape, mem_shape),
+        k, kg, key_squeeze, *ss_parts,
+        micros=20.0,
+    )
+    mk_recv = to_peers("seq", [mem] * (n_seq - 1))
 
     def local_body(q_ref, qg_ref, inv_ref, kn_ref, vp_ref, do_ref, qn_ref, st_ref):
         allowed = causal_t(rows)
@@ -396,7 +395,9 @@
 
     stat_shape = sds((heads, 8, rows), F32)
     qn, stats = whole_call(
-        local_body, (rows_shape, stat_shape), q, qg, inv, kn, vp, do, micros=0.5
+        local_body, (rows_shape, stat_shape), q, qg, inv, kn, vp, do,
+        micros=0.5,
+        after=tuple(mv_recv),
     )
 
     def rows_body(ids_ref, kn_ref, vp_ref, k_ref, *outs):
@@ -419,9 +420,10 @@
     rows_recv = to_peers("seq", row_sends)
 
     def memory_body(ids_ref, qn_ref, do_ref, st_ref, *rest):
-        mem_refs = rest[: n_seq - 1]
-        st2_ref, ds_ref = rest[n_seq - 1 : n_seq + 1]
-        parts = rest[n_seq + 1 :]
+        mk_refs = rest[: n_seq - 1]
+        mv_refs = rest[n_seq - 1 : 2 * n_seq - 2]
+        st2_ref, ds_ref = rest[2 * n_seq - 2 : 2 * n_seq]
+        parts = rest[2 * n_seq :]
         mine = ids_ref[0]
         for r in range(n_seq):
             block = mine ^ r
@@ -432,8 +434,8 @@
                 wide_at = pl.ds(pl.multiple_of(h * HD, HD), HD)
                 qn_h = qn_ref[:, wide_at]
                 do_h = do_ref[:, wide_at]
-                mk = jnp.concatenate([ref[0, span, at] for ref in mem_refs], axis=0)
-                mv = jnp.concatenate([ref[1, span, at] for ref in mem_refs], axis=0)
+                mk = jnp.concatenate([ref[span, at] for ref in mk_refs], axis=0)
+                mv = jnp.concatenate([ref[span, at] for ref in mv_refs], axis=0)
                 raw = dot(mk, qn_h, NT) * scale
                 s = jnp.concatenate(
                     [
@@ -462,13 +464,13 @@
     stats2, ds_mem, *parts = whole_call(
         memory_body,
         (stat_shape, sds((heads, n_mem, rows), BF16)) + (part,) * n_seq,
-        ids, qn, do, stats, *mem_recv,
-        micros=0.5,
+        ids, qn, do, stats, *mk_recv, *mv_recv,
+        micros=2.0,
     )
     parts_recv = to_peers("seq", parts[1:])
 
     def grads_body(q_ref, kp_ref, qn_ref, kn_ref, vp_ref, do_ref, st_ref, ds_ref, *rest):
-        mem_refs = rest[: n_seq - 1]
+        mk_refs = rest[: n_seq - 1]
         inv_ref, qg_ref, gq_ref, gk_ref, gv_ref, dq_ref, gain_q_ref, gain_k_ref = rest[n_seq - 1 :]
         allowed = causal_t(rows)
         inv_c = as_columns(inv_ref[...])
@@ -483,7 +485,7 @@
             m, inv_mass, delta = st_ref[h, 0:1, :], st_ref[h, 1:2, :], st_ref[h, 2:3, :]
             attend = jnp.exp(s - m) * inv_mass
             ds = (attend * (g - delta)).astype(BF16)
-            mk = jnp.concatenate([ref[0, span, narrow] for ref in mem_refs], axis=0)
+            mk = jnp.concatenate([ref[span, narrow] for ref in mk_refs], axis=0)
             gq = scale * (dot(ds, kn_h, TN) + dot(ds_ref[h], mk, TN))
             gk = scale * dot(ds, qn_h)
             gq_ref[:, at] = gq
@@ -502,7 +504,7 @@
     gq, gk_local, gv_local, dot_q, gain_q, gain_k = whole_call(
         grads_body,
         (wide_f32, wide_f32, wide_f32, dot_row, gain_rows, gain_rows),
-        q, kp, qn, kn, vp, do, stats2, ds_mem, *mem_recv, inv, qg,
+        q, kp, qn, kn, vp, do, stats2, ds_mem, *mk_recv, inv, qg,
         micros=0.5,
         after=tuple(rows_recv),
     )
@@ -649,8 +651,53 @@
     )
     dots_parts = over_heads(dots, beside=(mark,))
 
+    kernel_out = sds((heads, KS * HD, HD), F32)
+    gains_shape = sds((1, cols), F32)
+
+    def write_chunk(mine, r, read, buffer, sem, target):
+        start = (mine ^ r) * hp
+        for i in range(hp):
+            buffer[start + i] = read(slice(i * KS * HD, (i + 1) * KS * HD)).astype(F32)
+        at = pl.ds(start, hp)
+        copy = pltpu.make_async_copy(buffer.at[at], target.at[at], sem)
+        copy.start()
+        return copy
+
+    def own_chunk_body(ids_ref, same, other, *rest):
+        mark_ref, gks_ref, gvs_ref, buffer_k, buffer_v, sems = rest
+        mark_ref[...] = jnp.zeros_like(mark_ref)
+        first = ids_ref[1] == 0
+        copies = [
+            write_chunk(
+                ids_ref[0], 0, lambda at: jnp.where(first, same[at, :], other[at, :]),
+                buffer_k, sems.at[0], gks_ref,
+            ),
+            write_chunk(
+                ids_ref[0], 0, lambda at: jnp.where(first, other[at, :], same[at, :]),
+                buffer_v, sems.at[1], gvs_ref,
+            ),
+        ]
+        for copy in copies:
+            copy.wait()
+
+    smem = pl.BlockSpec(memory_space=pltpu.SMEM)
+    inside = pl.BlockSpec(memory_space=pltpu.VMEM)
+    outside = pl.BlockSpec(memory_space=pl.ANY)
+    buffer = pltpu.VMEM(kernel_out.shape, F32)
+    params = pltpu.CompilerParams(vmem_limit_bytes=40 * 2**20)
+    own_mark, *part_written = pl.pallas_call(
+        own_chunk_body,
+        out_shape=(sds((8, HD), F32), kernel_out, kernel_out),
+        in_specs=[smem, inside, inside],
+        out_specs=(inside, outside, outside),
+        scratch_shapes=[buffer, buffer, pltpu.SemaphoreType.DMA((2,))],
+        compiler_params=params,
+        cost_estimate=cost_of(0.01),
+    )(ids, chunk, chunk_other)
+
     def norms_body(q_ref, kp_ref, gq_ref, gkn_ref, qg_ref, kg_ref, inv_ref, *rest):
-        dots_a, dots_b, out_q, out_k, buffer_q, buffer_k, sems = rest
+        dots_a, dots_b, mark_ref, out_q, out_k, buffer_q, buffer_k, sems = rest
+        mark_ref[...] = jnp.zeros_like(mark_ref)
         total = dots_a[...] + dots_b[...]
         inv_rows = inv_ref[...]
         inv_c = as_columns(inv_rows)
@@ -673,142 +720,124 @@
         for copy in copies:
             copy.wait()
 
-    grad_query, grad_key = column_out(
+    norms_mark, grad_query, grad_key = column_out(
         norms_body,
-        (rows_shape, rows_shape),
+        (sds((8, HD), F32), rows_shape, rows_shape),
         2,
         q, kp, gq, gkn, qg, kg, inv, *dots_parts,
-        micros=2.0,
-    )
-
-    kernel_out = sds((heads, KS * HD, HD), F32)
-    gains_shape = sds((heads, HD), F32)
-
-    def write_chunk(mine, r, read, buffer, sem, target):
-        start = (mine ^ r) * hp
-        for i in range(hp):
-            buffer[start + i] = read(slice(i * KS * HD, (i + 1) * KS * HD)).astype(F32)
-        at = pl.ds(start, hp)
-        copy = pltpu.make_async_copy(buffer.at[at], target.at[at], sem)
-        copy.start()
-        return copy
-
-    def own_chunk_body(ids_ref, same, other, *rest):
-        mark_ref, gks_ref, gvs_ref, buffer_k, buffer_v, sems = rest
-        mark_ref[...] = jnp.zeros_like(mark_ref)
-        first = ids_ref[1] == 0
-        copies = [
-            write_chunk(
-                ids_ref[0], 0, lambda at: jnp.where(first, same[at, :], other[at, :]),
-                buffer_k, sems.at[0], gks_ref,
-            ),
-            write_chunk(
-                ids_ref[0], 0, lambda at: jnp.where(first, other[at, :], same[at, :]),
-                buffer_v, sems.at[1], gvs_ref,
-            ),
-        ]
-        for copy in copies:
-            copy.wait()
-
-    smem = pl.BlockSpec(memory_space=pltpu.SMEM)
-    inside = pl.BlockSpec(memory_space=pltpu.VMEM)
-    outside = pl.BlockSpec(memory_space=pl.ANY)
-    buffer = pltpu.VMEM(kernel_out.shape, F32)
-    params = pltpu.CompilerParams(vmem_limit_bytes=40 * 2**20)
-    own_mark, *part_written = pl.pallas_call(
-        own_chunk_body,
-        out_shape=(sds((8, HD), F32), kernel_out, kernel_out),
-        in_specs=[smem, inside, inside],
-        out_specs=(inside, outside, outside),
-        scratch_shapes=[buffer, buffer, pltpu.SemaphoreType.DMA((2,))],
-        compiler_params=params,
-        cost_estimate=cost_of(1.2),
-    )(ids, chunk, chunk_other)
+        micros=0.01,
+        after=(own_mark,),
+    )
 
     def pack_body(*refs):
         for r in range(n_seq - 1):
             refs[n_seq - 1][r] = refs[r][...]
 
     packed_shape = sds((n_seq - 1,) + chunk_shape.shape, BF16)
-    packed = whole_call(pack_body, packed_shape, *chunks, micros=0.1, after=(dots_parts[1], own_mark))
+    packed = whole_call(pack_body, packed_shape, *chunks, micros=0.1, after=(norms_mark, own_mark))
     packed_other = to_core(packed)
 
-    def this_core_body(ids_ref, same, gks_in, gvs_in, gks_ref, gvs_ref, buffer, sems):
-        for tensor, target in enumerate((gks_ref, gvs_ref)):
-            @pl.when(ids_ref[1] == tensor)
-            def _(target=target):
-                copies = [
-                    write_chunk(
-                        ids_ref[0], r, lambda at, r=r: same[r - 1, at, :],
-                        buffer, sems.at[r], target,
-                    )
-                    for r in peers
-                ]
-                for copy in copies:
-                    copy.wait()
-
-    def other_core_body(ids_ref, same_0, other_0, same, other, kg_ref, wk_ref, *rest):
-        gks_ref, gvs_ref, gq_ref, gk_ref, buffer, sems = rest[2:]
-        first = ids_ref[1] == 0
-
-        def pair(r, at):
-            if r == 0:
-                return same_0[at, :], other_0[at, :]
-            return same[r - 1, at, :], other[r - 1, at, :]
-
-        def gains():
-            total = jnp.zeros((2 * heads, HD), F32)
-            for r in range(n_seq):
-                a, b = pair(r, slice(span_rows, span_rows + 2 * heads))
-                total = total + a.astype(F32) + b.astype(F32)
-            gq_ref[...] = total[:heads]
-            gk_ref[...] = total[heads:]
-            for r in range(n_seq):
-                for i in range(hp):
-                    h = (ids_ref[0] ^ r) * hp + i
-                    total = jnp.zeros((HD, HD), F32)
-                    for j in range(KS):
-                        a, b = pair(r, slice((i * KS + j) * HD, (i * KS + j + 1) * HD))
-                        kernel = wk_ref[h, j * HD : (j + 1) * HD, :]
-                        total = total + jnp.where(first, a, b).astype(F32) * kernel.astype(F32)
-                    at = pl.ds(h, 1)
-                    gain = kg_ref[:, pl.ds(pl.multiple_of(h * HD, HD), HD)]
-                    gk_ref[at, :] = gk_ref[at, :] + lane_sum_row(total) / gain
-
-        for tensor, target in enumerate((gvs_ref, gks_ref)):
-            @pl.when(ids_ref[1] == tensor)
-            def _(target=target):
-                copies = [
-                    write_chunk(
-                        ids_ref[0], r, lambda at, r=r: other[r - 1, at, :],
-                        buffer, sems.at[r], target,
-                    )
-                    for r in peers
-                ]
-                gains()
-                for copy in copies:
-                    copy.wait()
-
-    part_written = pl.pallas_call(
+    def back_gain(mine, chunk_0, chunks_ref, kg_ref, wk_ref, out_ref):
+        sums = []
+        for r in range(n_seq):
+            for i in range(hp):
+                h = (mine ^ r) * hp + i
+                total = jnp.zeros((HD, HD), F32)
+                for j in range(KS):
+                    span = slice((i * KS + j) * HD, (i * KS + j + 1) * HD)
+                    grad_w = chunk_0[span, :] if r == 0 else chunks_ref[r - 1, span, :]
+                    kernel = wk_ref[h, j * HD : (j + 1) * HD, :]
+                    total = total + grad_w.astype(F32) * kernel.astype(F32)
+                sums.append(total)
+        sums = jnp.concatenate(sums, axis=0)
+        high = sums.astype(BF16)
+        low = (sums - high.astype(F32)).astype(BF16)
+        ones = jnp.ones((16, HD), BF16)
+        row = (dot(ones, high, NT) + dot(ones, low, NT))[0:1]
+        for r in range(n_seq):
+            at = pl.ds(pl.multiple_of((mine ^ r) * wide, wide), wide)
+            out_ref[:, at] = row[:, r * wide : (r + 1) * wide] / kg_ref[:, at]
+
+    def write_chunks(mine, chunks_ref, buffer, sems, target):
+        return [
+            write_chunk(
+                mine, r, lambda at, r=r: chunks_ref[r - 1, at, :], buffer, sems.at[r], target
+            )
+            for r in peers
+        ]
+
+    def this_core_body(ids_ref, same_0, same, kg_ref, wk_ref, gks_in, gvs_in, *rest):
+        back_ref, gks_ref, gvs_ref, buffer, sems = rest
+
+        @pl.when(ids_ref[1] == 0)
+        def _():
+            copies = write_chunks(ids_ref[0], same, buffer, sems, gks_ref)
+            back_gain(ids_ref[0], same_0, same, kg_ref, wk_ref, back_ref)
+            for copy in copies:
+                copy.wait()
+
+        @pl.when(ids_ref[1] == 1)
+        def _():
+            copies = write_chunks(ids_ref[0], same, buffer, sems, gvs_ref)
+            back_ref[...] = jnp.zeros_like(back_ref)
+            for copy in copies:
+                copy.wait()
+
+    def other_core_body(ids_ref, same_0, other_0, same, other, back, kg_ref, wk_ref, *rest):
+        gks_ref, gvs_ref, gq_out, gk_out, buffer, gq_row, gk_row, sems = rest[2:]
+
+        def finish(copies):
+            total = same_0[span_rows:, :].astype(F32) + other_0[span_rows:, :].astype(F32)
+            for r in range(n_seq - 1):
+                total = total + same[r, span_rows:, :].astype(F32)
+                total = total + other[r, span_rows:, :].astype(F32)
+            as_row = lambda x: jnp.concatenate([x[h : h + 1] for h in range(heads)], axis=1)
+            gq_row[...] = as_row(total[:heads])
+            gk_row[...] += as_row(total[heads:])
+            copies.append(pltpu.make_async_copy(gq_row, gq_out, sems.at[0]))
+            copies[-1].start()
+            copies.append(pltpu.make_async_copy(gk_row, gk_out, sems.at[n_seq]))
+            copies[-1].start()
+            for copy in copies:
+                copy.wait()
+
+        @pl.when(ids_ref[1] == 0)
+        def _():
+            copies = write_chunks(ids_ref[0], other, buffer, sems, gvs_ref)
+            gk_row[...] = back[...]
+            finish(copies)
+
+        @pl.when(ids_ref[1] == 1)
+        def _():
+            copies = write_chunks(ids_ref[0], other, buffer, sems, gks_ref)
+            back_gain(ids_ref[0], other_0, other, kg_ref, wk_ref, gk_row)
+            finish(copies)
+
+    back_row, *part_written = pl.pallas_call(
         this_core_body,
-        out_shape=(kernel_out, kernel_out),
-        in_specs=[smem, inside, outside, outside],
-        out_specs=(outside, outside),
-        input_output_aliases={2: 0, 3: 1},
+        out_shape=(gains_shape, kernel_out, kernel_out),
+        in_specs=[smem] + [inside] * 4 + [outside] * 2,
+        out_specs=(inside, outside, outside),
+        input_output_aliases={5: 1, 6: 2},
         scratch_shapes=[buffer, pltpu.SemaphoreType.DMA((n_seq,))],
         compiler_params=params,
         cost_estimate=cost_of(1.6),
-    )(ids, packed, *part_written)
+    )(ids, chunk, packed, kg, key_squeeze, *part_written)
     gks, gvs, gain_q_all, gain_k_all = pl.pallas_call(
         other_core_body,
         out_shape=(kernel_out, kernel_out, gains_shape, gains_shape),
-        in_specs=[smem] + [inside] * 6 + [outside] * 2,
-        out_specs=(outside, outside, inside, inside),
-        input_output_aliases={7: 0, 8: 1},
-        scratch_shapes=[buffer, pltpu.SemaphoreType.DMA((n_seq,))],
+        in_specs=[smem] + [inside] * 7 + [outside] * 2,
+        out_specs=(outside,) * 4,
+        input_output_aliases={8: 0, 9: 1},
+        scratch_shapes=[
+            buffer,
+            pltpu.VMEM((1, cols), F32),
+            pltpu.VMEM((1, cols), F32),
+            pltpu.SemaphoreType.DMA((n_seq + 1,)),
+        ],
         compiler_params=params,
         cost_estimate=cost_of(2.2),
-    )(ids, chunk, chunk_other, packed, packed_other, kg, key_squeeze, *part_written)
+    )(ids, chunk, chunk_other, packed, packed_other, back_row, kg, key_squeeze, *part_written)
     return (
         grad_query[None],
         grad_key[None],

time: 73.5 us -> 68.7 us (0.935)
  waiting for transfers between devices: 19.6 us -> 8.21 us
  starting transfers between devices: 27.4 us -> 32.8 us
  local copies, waits for them, and re-layouts: 0.04 us -> 1.07 us
    ppermute x18 -> x21, waiting for transfers between devices: 17.3 us -> 7.88 us  [to_peers(): lax.ppermute(a, axis, [(i, i ^ k) for i in range(n)])]
    ppermute x18 -> x21, starting transfers between devices: 25.4 us -> 28.4 us  [to_peers(): lax.ppermute(a, axis, [(i, i ^ k) for i in range(n)])]
    ppermute x2, starting transfers between devices: 1.86 us -> 4.24 us  [over_heads(): got = lax.ppermute(a, 'head', [(i, i ^ step) for i in range(n_head)])]
    ppermute x2, waiting for transfers between devices: 2.37 us -> 0.1 us  [over_heads(): got = lax.ppermute(a, 'head', [(i, i ^ step) for i in range(n_head)])]
    unnamed x18, local copies, waits for them, and re-layouts: 0.04 us -> 1.07 us
    pallas_call x1, Pallas kernels: 2.58 us -> 1.77 us  [on_device(): pl.pallas_call(other_core_body, out_shape=(kernel_out, kernel_out, gains_...]
    pallas_call x13, Pallas kernels: 15.3 us -> 16 us  [whole_call(): pl.pallas_call(lambda *refs: body(*refs[:len(ins)], *refs[len(ins) + skip...]
  transfers between devices with their start and end apart: 23 -> 26, of which waited for: 13 -> 8; matrix products, arithmetic and copies ran while one was open for 0% -> 0% of each run, Pallas kernels for 25% -> 30%
where the time goes in v5:
time: 68.7 us; the launch traced here: 68.4 us
  starting transfers between devices  32.8 us (48%)
  Pallas kernels  25.4 us (37%)
  waiting for transfers between devices  8.21 us (12%)
  local copies, waits for them, and re-layouts  1.07 us (2%)
  between operations  0.87 us (1%)
    ppermute x21, starting transfers between devices, to_peers(): lax.ppermute(a, axis, [(i, i ^ k) for i in range(n)])  28.4 us
    pallas_call x13, Pallas kernels, whole_call(): pl.pallas_call(lambda *refs: body(*refs[:len(ins)], *refs[len(ins) + skip...  16 us
    ppermute x21, waiting for transfers between devices, to_peers(): lax.ppermute(a, axis, [(i, i ^ k) for i in range(n)])  7.88 us
    ppermute x2, starting transfers between devices, over_heads(): got = lax.ppermute(a, 'head', [(i, i ^ step) for i in range(n_head)])  4.24 us
    pallas_call x2, Pallas kernels, column_out(): pl.pallas_call(lambda *refs: body(*refs[:len(ins)], *refs[len(ins) + skip...  3.97 us
    pallas_call x1, Pallas kernels, on_device(): pl.pallas_call(this_core_body, out_shape=(gains_shape, kernel_out, kernel...  2.06 us
    pallas_call x1, Pallas kernels, on_device(): pl.pallas_call(other_core_body, out_shape=(kernel_out, kernel_out, gains_...  1.77 us
    pallas_call x1, Pallas kernels, on_device(): pl.pallas_call(own_chunk_body, out_shape=(sds((8, HD), F32), kernel_out,...  1.58 us
  transfers between devices with their start and end apart: 26, of which 8 were waited for; matrix products, arithmetic and copies ran while one was open for 0% of the time, Pallas kernels for 30%

profile of v5, /device:TPU:0, one launch (start us, length us, event | category | flops | bytes accessed | tf_op | source)
XLA Modules:
  0.0 68.4 jit_solution(11857371936133976370)
XLA Ops:
  0.7 2.2 %shard_map.135.refs_3_ = f32[2,256]{1,0:T(2,128)} custom-call(bf16[256,1024]{1,0:T(8,128)(2,1)} %bitcast.13, bf16[256,1024]{1,0:T(8,128)(2,1)} %bitcast.29), custom_call_target="tpu_custom_call" | custom-call | flops 1500000000 | bytes 5400000 | tf_op jit(solution)/shard_map/pallas_call | solution.py:210
  2.8 5.0 %collective-permute-start.2 = (f32[2,256]{1,0:T(2,128)}, f32[2,256]{1,0:T(2,128)S(1)}, u32[]{:S(2)}, u32[]{:S(2)}) collective-permute-start(f32[2,256]{1,0:T(2,128)} %shard_map.135.refs_3_), channel_id=1, source_target_pairs={{0,6},{2,4},{4,2},{6,0},{1,7},{3,5},{5,3},{7,1},{8,14},{10,12},{12... | collective-permute-start | bytes 6152 | tf_op jit(solution)/shard_map/ppermute | solution.py:293
  9.1 2.6 %collective-permute-start.5 = (bf16[256,256]{1,0:T(8,128)(2,1)S(1)}, bf16[256,256]{1,0:T(8,128)(2,1)S(1)}, u32[]{:S(2)}, u32[]{:S(2)}) collective-permute-start(bf16[256,256]{1,0:T(8,128)(2,1)S(1)} %get-tuple-element.56), channel_id=1, source_target_pairs={{0,24},{8,16},{16,8},{24,0},{1,25},{9,17},{17,9},{25,1},{2,26},{10... | collective-permute-start | bytes 393224 | tf_op jit(solution)/shard_map/ppermute | solution.py:293
  13.8 1.7 %shard_map.136 = (f32[2,256]{1,0:T(2,128)S(1)}, bf16[256,1024]{1,0:T(8,128)(2,1)S(1)}, bf16[256,256]{1,0:T(8,128)(2,1)S(1)}) custom-call(bf16[256,1024]{1,0:T(8,128)(2,1)S(1)} %bitcast.30, f32[1,1024]{1,0:T(1,128)S(1)} %bitcast.23, bf16[8,512,128]{2,1,0:T(8,128)(2,1)S(1)} %copy-done.2, f32[2,256]{1,0:T(2,128)S(1)} %copy-done.8, ...), custom_call_target="tpu_custom_call" | custom-call | flops 20000000000 | bytes 72000000 | tf_op jit(solution)/shard_map/pallas_call | solution.py:210
  15.5 2.6 %collective-permute-start.8 = (bf16[256,256]{1,0:T(8,128)(2,1)S(1)}, bf16[256,256]{1,0:T(8,128)(2,1)S(1)}, u32[]{:S(2)}, u32[]{:S(2)}) collective-permute-start(bf16[256,256]{1,0:T(8,128)(2,1)S(1)} %get-tuple-element.60), channel_id=1, source_target_pairs={{0,24},{8,16},{16,8},{24,0},{1,25},{9,17},{17,9},{25,1},{2,26},{10... | collective-permute-start | bytes 393224 | tf_op jit(solution)/shard_map/ppermute | solution.py:293
  19.1 1.4 %shard_map.138 = (bf16[256,1024]{1,0:T(8,128)(2,1)S(1)}, f32[8,8,256]{2,1,0:T(8,128)S(1)}) custom-call(bf16[256,1024]{1,0:T(8,128)(2,1)S(1)} %bitcast.14, f32[1,1024]{1,0:T(1,128)S(1)} %bitcast.20, f32[2,256]{1,0:T(2,128)S(1)} %get-tuple-element.55.refs_2_.refs_11_.refs_6_, bf16[256,1024]{1,0:T(8,128)(2,1)S(1)} %get-tuple-element.53.refs_3_.refs_1_, ...), custom_call_target="tpu_custom_call" | custom-call | flops 500000000 | bytes 1800000 | tf_op jit(solution)/shard_map/pallas_call | solution.py:210
  21.4 1.7 %collective-permute-start.9 = (bf16[2,256,256]{2,1,0:T(8,128)(2,1)S(1)}, bf16[2,256,256]{2,1,0:T(8,128)(2,1)S(1)}, u32[]{:S(2)}, u32[]{:S(2)}) collective-permute-start(bf16[2,256,256]{2,1,0:T(8,128)(2,1)S(1)} %get-tuple-element.63), channel_id=1, source_target_pairs={{0,8},{8,0},{16,24},{24,16},{1,9},{9,1},{17,25},{25,17},{2,10},{10... | collective-permute-start | bytes 786440 | tf_op jit(solution)/shard_map/ppermute | solution.py:293
  23.1 1.5 %collective-permute-start.10 = (bf16[2,256,256]{2,1,0:T(8,128)(2,1)S(1)}, bf16[2,256,256]{2,1,0:T(8,128)(2,1)S(1)}, u32[]{:S(2)}, u32[]{:S(2)}) collective-permute-start(bf16[2,256,256]{2,1,0:T(8,128)(2,1)S(1)} %get-tuple-element.64), channel_id=1, source_target_pairs={{0,16},{8,24},{16,0},{24,8},{1,17},{9,25},{17,1},{25,9},{2,18},{10... | collective-permute-start | bytes 786440 | tf_op jit(solution)/shard_map/ppermute | solution.py:293
  25.0 3.3 %shard_map.140 = (f32[8,8,256]{2,1,0:T(8,128)S(1)}, bf16[8,192,256]{2,1,0:T(8,128)(2,1)S(1)}, bf16[2,192,256]{2,1,0:T(8,128)(2,1)S(1)}, bf16[2,192,256]{2,1,0:T(...) custom-call(s32[2]{0:T(128)S(1)} %pad_add_fusion.refs_0_.ids_ref, ...), custom_call_target="tpu_custom_call" | custom-call | flops 2000000000 | bytes 7200000 | tf_op jit(solution)/shard_map/pallas_call | solution.py:210
  28.3 1.7 %collective-permute-start.12 = (bf16[2,192,256]{2,1,0:T(8,128)(2,1)S(1)}, bf16[2,192,256]{2,1,0:T(8,128)(2,1)S(1)}, u32[]{:S(2)}, u32[]{:S(2)}) collective-permute-start(bf16[2,192,256]{2,1,0:T(8,128)(2,1)S(1)} %get-tuple-element.70), channel_id=1, source_target_pairs={{0,8},{8,0},{16,24},{24,16},{1,9},{9,1},{17,25},{25,17},{2,10},{10... | collective-permute-start | bytes 589832 | tf_op jit(solution)/shard_map/ppermute | solution.py:293
  29.9 1.5 %collective-permute-start.13 = (bf16[2,192,256]{2,1,0:T(8,128)(2,1)S(1)}, bf16[2,192,256]{2,1,0:T(8,128)(2,1)S(1)}, u32[]{:S(2)}, u32[]{:S(2)}) collective-permute-start(bf16[2,192,256]{2,1,0:T(8,128)(2,1)S(1)} %get-tuple-element.71), channel_id=1, source_target_pairs={{0,16},{8,24},{16,0},{24,8},{1,17},{9,25},{17,1},{25,9},{2,18},{10... | collective-permute-start | bytes 589832 | tf_op jit(solution)/shard_map/ppermute | solution.py:293
  31.5 1.8 %collective-permute-start.14 = (bf16[2,192,256]{2,1,0:T(8,128)(2,1)S(1)}, bf16[2,192,256]{2,1,0:T(8,128)(2,1)S(1)}, u32[]{:S(2)}, u32[]{:S(2)}) collective-permute-start(bf16[2,192,256]{2,1,0:T(8,128)(2,1)S(1)} %get-tuple-element.72), channel_id=1, source_target_pairs={{0,24},{8,16},{16,8},{24,0},{1,25},{9,17},{17,9},{25,1},{2,26},{10... | collective-permute-start | bytes 589832 | tf_op jit(solution)/shard_map/ppermute | solution.py:293
  33.3 1.7 %collective-permute-done.10.refs_14_.refs_8_ = bf16[2,256,256]{2,1,0:T(8,128)(2,1)S(1)} collective-permute-done((bf16[2,256,256]{2,1,0:T(8,128)(2,1)S(1)}, bf16[2,256,256]{2,1,0:T(8,128)(2,1)S(1)}, u32[]{:S(2)}, u32[]{:S(2)}) %collective-permute-start.10) | collective-permute-done | bytes 262176 | tf_op jit(solution)/shard_map/ppermute | solution.py:293
  35.0 2.5 %collective-permute-done.11.refs_15_.refs_9_ = bf16[2,256,256]{2,1,0:T(8,128)(2,1)S(1)} collective-permute-done((bf16[2,256,256]{2,1,0:T(8,128)(2,1)S(1)}, bf16[2,256,256]{2,1,0:T(8,128)(2,1)S(1)}, u32[]{:S(2)}, u32[]{:S(2)}) %collective-permute-start.11) | collective-permute-done | bytes 262176 | tf_op jit(solution)/shard_map/ppermute | solution.py:293
  37.5 3.6 %shard_map.141 = (f32[256,1024]{1,0:T(8,128)S(1)}, f32[256,1024]{1,0:T(8,128)S(1)}, f32[256,1024]{1,0:T(8,128)S(1)}, f32[1,256]{1,0:T(1,128)S(1)}, f32[8,128]{1,0:T(8,128)S(1)}, /*index=5*/f32[8,128]{1,0:T(8,128)S(1)}) custom-call(bf16[256,1024]{1,0:T(8,128)(2,1)S(1)} %bitcast.15, bf16[256,1024]{1,0:T(8,128)(2,1)S(1)} %get-tuple-element.58.refs_1_.refs_2_, ...), custom_call_target="tpu_custom_call" | custom-call | flops 500000000 | bytes 1800000 | tf_op jit(solution)/shard_map/pallas_call | solution.py:210
  41.0 1.5 %collective-permute-done.13.refs_2_ = bf16[2,192,256]{2,1,0:T(8,128)(2,1)S(1)} collective-permute-done((bf16[2,192,256]{2,1,0:T(8,128)(2,1)S(1)}, bf16[2,192,256]{2,1,0:T(8,128)(2,1)S(1)}, u32[]{:S(2)}, u32[]{:S(2)}) %collective-permute-start.13) | collective-permute-done | bytes 196640 | tf_op jit(solution)/shard_map/ppermute | solution.py:293
  47.3 1.4 %collective-permute-start.17 = (bf16[2,64,256]{2,1,0:T(8,128)(2,1)S(1)}, bf16[2,64,256]{2,1,0:T(8,128)(2,1)S(1)}, u32[]{:S(2)}, u32[]{:S(2)}) collective-permute-start(bf16[2,64,256]{2,1,0:T(8,128)(2,1)S(1)} %get-tuple-element.77.refs_6_), channel_id=1, source_target_pairs={{0,24},{8,16},{16,8},{24,0},{1,25},{9,17},{17,9},{25,1},{2,26},{10... | collective-permute-start | bytes 196616 | tf_op jit(solution)/shard_map/ppermute | solution.py:293
  48.8 1.6 %collective-permute-start.24 = (bf16[1040,128]{1,0:T(8,128)(2,1)S(1)}, bf16[1040,128]{1,0:T(8,128)(2,1)S(1)}, u32[]{:S(2)}, u32[]{:S(2)}) collective-permute-start(bf16[1040,128]{1,0:T(8,128)(2,1)S(1)} %shard_map.144.refs_10_.same.same_0), channel_id=1, source_target_pairs={{0,24},{8,16},{16,8},{24,0},{1,25},{9,17},{17,9},{25,1},{2,26},{10... | collective-permute-start | bytes 798728 | tf_op jit(solution)/shard_map/ppermute | solution.py:293
  55.7 2.3 %shard_map.146 = (f32[8,128]{1,0:T(8,128)S(1)}, bf16[256,1024]{1,0:T(8,128)(2,1)}) custom-call(s32[2]{0:T(128)S(1)} %pad_add_fusion.refs_0_.ids_ref, f32[256,1024]{1,0:T(8,128)S(1)} %get-tuple-element.83.refs_1_, bf16[8,512,128]{2,1,0:T(8,128)(2,1)S(1)} %copy-done.5, bf16[2,64,256]{2,1,0:T(8,128)(2,1)S(1)} %get-tuple-element.74.refs_3_.refs_6_, ...), custom_call_target="tpu_custom_call" | custom-call | flops 2000000000 | bytes 7200000 | tf_op jit(solution)/shard_map/pallas_call | solution.py:583
  58.0 2.9 %collective-permute-start.20 = (f32[2,256]{1,0:T(2,128)S(1)}, f32[2,256]{1,0:T(2,128)S(1)}, u32[]{:S(2)}, u32[]{:S(2)}) collective-permute-start(f32[2,256]{1,0:T(2,128)S(1)} %shard_map.147.refs_7_), channel_id=1, source_target_pairs={{0,4},{2,6},{4,0},{6,2},{1,5},{3,7},{5,1},{7,3},{8,12},{10,14},{12... | collective-permute-start | bytes 6152 | tf_op jit(solution)/shard_map/ppermute | solution.py:305
  60.8 1.6 %shard_map.148 = (f32[8,128]{1,0:T(8,128)S(1)}, f32[8,512,128]{2,1,0:T(8,128)}, f32[8,512,128]{2,1,0:T(8,128)}) custom-call(s32[2]{0:T(128)S(1)} %pad_add_fusion.refs_0_.ids_ref, bf16[1040,128]{1,0:T(8,128)(2,1)S(1)} %shard_map.144.refs_10_.same.same_0, bf16[1040,128]{1,0:T(8,128)(2,1)S(1)} %collective-permute-done.21.other.other_0), custom_call_target="tpu_custom_call" | custom-call | flops 10000000 | bytes 36000 | tf_op jit(solution)/shard_map/pallas_call | solution.py:688
  62.5 1.7 %shard_map.149 = (f32[8,128]{1,0:T(8,128)S(1)}, bf16[256,1024]{1,0:T(8,128)(2,1)}, bf16[256,1024]{1,0:T(8,128)(2,1)}) custom-call(bf16[256,1024]{1,0:T(8,128)(2,1)S(1)} %bitcast.16, bf16[256,1024]{1,0:T(8,128)(2,1)S(1)} %get-tuple-element.58.refs_1_.refs_2_, f32[256,1024]{1,0:T(8,128)S(1)} %get-tuple-element.66.refs_2_, ...), custom_call_target="tpu_custom_call" | custom-call | flops 10000000 | bytes 36000 | tf_op jit(solution)/shard_map/pallas_call | solution.py:583
  64.4 2.1 %shard_map.151 = (f32[1,1024]{1,0:T(1,128)S(1)}, f32[8,512,128]{2,1,0:T(8,128)}, f32[8,512,128]{2,1,0:T(8,128)}) custom-call(s32[2]{0:T(128)S(1)} %pad_add_fusion.refs_0_.ids_ref, bf16[1040,128]{1,0:T(8,128)(2,1)S(1)} %shard_map.144.refs_10_.same.same_0, bf16[3,1040,128]{2,1,0:T(8,128)(2,1)S(1)} %shard_map.150.same, ...), custom_call_target="tpu_custom_call", output_to_operand_aliasing={{1}: (5, {}), {2}: (6, {})} | custom-call | flops 1600000000 | bytes 5760000 | tf_op jit(solution)/shard_map/pallas_call | solution.py:816
  66.7 1.8 %shard_map.152 = (f32[8,512,128]{2,1,0:T(8,128)}, f32[8,512,128]{2,1,0:T(8,128)}, f32[1,1024]{1,0:T(1,128)}, f32[1,1024]{1,0:T(1,128)}) custom-call(s32[2]{0:T(128)S(1)} %pad_add_fusion.refs_0_.ids_ref, bf16[1040,128]{1,0:T(8,128)(2,1)S(1)} %shard_map.144.refs_10_.same.same_0, ...), custom_call_target="tpu_custom_call", output_to_operand_aliasing={{0}: (8, {}), {1}: (9, {})} | custom-call | flops 2200000000 | bytes 7920000 | tf_op jit(solution)/shard_map/pallas_call | solution.py:826
  (65 shorter events, 16.0 us)
Async XLA Ops:
  2.8 9.5 %collective-permute-start.2 = (f32[2,256]{1,0:T(2,128)}, f32[2,256]{1,0:T(2,128)S(1)}, u32[]{:S(2)}, u32[]{:S(2)}) collective-permute-start(f32[2,256]{1,0:T(2,128)} %shard_map.135.refs_3_), channel_id=1, source_target_pairs={{0,6},{2,4},{4,2},{6,0},{1,7},{3,5},{5,3},{7,1},{8,14},{10,12},{12... | collective-permute-start | bytes 6152 | tf_op jit(solution)/shard_map/ppermute | solution.py:293
  7.9 4.9 %collective-permute-start.1 = (f32[2,256]{1,0:T(2,128)}, f32[2,256]{1,0:T(2,128)S(1)}, u32[]{:S(2)}, u32[]{:S(2)}) collective-permute-start(f32[2,256]{1,0:T(2,128)} %shard_map.135.refs_3_), channel_id=1, source_target_pairs={{0,4},{2,6},{4,0},{6,2},{1,5},{3,7},{5,1},{7,3},{8,12},{10,14},{12... | collective-permute-start | bytes 6152 | tf_op jit(solution)/shard_map/ppermute | solution.py:293
  7.9 4.9 %collective-permute-start = (f32[2,256]{1,0:T(2,128)}, f32[2,256]{1,0:T(2,128)}, u32[]{:S(2)}, u32[]{:S(2)}) collective-permute-start(f32[2,256]{1,0:T(2,128)} %shard_map.135.refs_3_), channel_id=1, source_target_pairs={{0,2},{2,0},{4,6},{6,4},{1,3},{3,1},{5,7},{7,5},{8,10},{10,8},{12,... | collective-permute-start | bytes 6152 | tf_op jit(solution)/shard_map/ppermute | solution.py:293
  9.1 9.5 %collective-permute-start.5 = (bf16[256,256]{1,0:T(8,128)(2,1)S(1)}, bf16[256,256]{1,0:T(8,128)(2,1)S(1)}, u32[]{:S(2)}, u32[]{:S(2)}) collective-permute-start(bf16[256,256]{1,0:T(8,128)(2,1)S(1)} %get-tuple-element.56), channel_id=1, source_target_pairs={{0,24},{8,16},{16,8},{24,0},{1,25},{9,17},{17,9},{25,1},{2,26},{10... | collective-permute-start | bytes 393224 | tf_op jit(solution)/shard_map/ppermute | solution.py:293
  11.8 7.3 %collective-permute-start.4 = (bf16[256,256]{1,0:T(8,128)(2,1)S(1)}, bf16[256,256]{1,0:T(8,128)(2,1)S(1)}, u32[]{:S(2)}, u32[]{:S(2)}) collective-permute-start(bf16[256,256]{1,0:T(8,128)(2,1)S(1)} %get-tuple-element.56), channel_id=1, source_target_pairs={{0,16},{8,24},{16,0},{24,8},{1,17},{9,25},{17,1},{25,9},{2,18},{10... | collective-permute-start | bytes 393224 | tf_op jit(solution)/shard_map/ppermute | solution.py:293
  12.4 6.7 %collective-permute-start.3 = (bf16[256,256]{1,0:T(8,128)(2,1)S(1)}, bf16[256,256]{1,0:T(8,128)(2,1)S(1)}, u32[]{:S(2)}, u32[]{:S(2)}) collective-permute-start(bf16[256,256]{1,0:T(8,128)(2,1)S(1)} %get-tuple-element.56), channel_id=1, source_target_pairs={{0,8},{8,0},{16,24},{24,16},{1,9},{9,1},{17,25},{25,17},{2,10},{10... | collective-permute-start | bytes 393224 | tf_op jit(solution)/shard_map/ppermute | solution.py:293
  15.5 9.1 %collective-permute-start.8 = (bf16[256,256]{1,0:T(8,128)(2,1)S(1)}, bf16[256,256]{1,0:T(8,128)(2,1)S(1)}, u32[]{:S(2)}, u32[]{:S(2)}) collective-permute-start(bf16[256,256]{1,0:T(8,128)(2,1)S(1)} %get-tuple-element.60), channel_id=1, source_target_pairs={{0,24},{8,16},{16,8},{24,0},{1,25},{9,17},{17,9},{25,1},{2,26},{10... | collective-permute-start | bytes 393224 | tf_op jit(solution)/shard_map/ppermute | solution.py:293
  18.1 6.8 %collective-permute-start.7 = (bf16[256,256]{1,0:T(8,128)(2,1)S(1)}, bf16[256,256]{1,0:T(8,128)(2,1)S(1)}, u32[]{:S(2)}, u32[]{:S(2)}) collective-permute-start(bf16[256,256]{1,0:T(8,128)(2,1)S(1)} %get-tuple-element.60), channel_id=1, source_target_pairs={{0,16},{8,24},{16,0},{24,8},{1,17},{9,25},{17,1},{25,9},{2,18},{10... | collective-permute-start | bytes 393224 | tf_op jit(solution)/shard_map/ppermute | solution.py:293
  18.6 6.4 %collective-permute-start.6 = (bf16[256,256]{1,0:T(8,128)(2,1)S(1)}, bf16[256,256]{1,0:T(8,128)(2,1)S(1)}, u32[]{:S(2)}, u32[]{:S(2)}) collective-permute-start(bf16[256,256]{1,0:T(8,128)(2,1)S(1)} %get-tuple-element.60), channel_id=1, source_target_pairs={{0,8},{8,0},{16,24},{24,16},{1,9},{9,1},{17,25},{25,17},{2,10},{10... | collective-permute-start | bytes 393224 | tf_op jit(solution)/shard_map/ppermute | solution.py:293
  21.4 10.1 %collective-permute-start.9 = (bf16[2,256,256]{2,1,0:T(8,128)(2,1)S(1)}, bf16[2,256,256]{2,1,0:T(8,128)(2,1)S(1)}, u32[]{:S(2)}, u32[]{:S(2)}) collective-permute-start(bf16[2,256,256]{2,1,0:T(8,128)(2,1)S(1)} %get-tuple-element.63), channel_id=1, source_target_pairs={{0,8},{8,0},{16,24},{24,16},{1,9},{9,1},{17,25},{25,17},{2,10},{10... | collective-permute-start | bytes 786440 | tf_op jit(solution)/shard_map/ppermute | solution.py:293
  23.1 11.9 %collective-permute-start.10 = (bf16[2,256,256]{2,1,0:T(8,128)(2,1)S(1)}, bf16[2,256,256]{2,1,0:T(8,128)(2,1)S(1)}, u32[]{:S(2)}, u32[]{:S(2)}) collective-permute-start(bf16[2,256,256]{2,1,0:T(8,128)(2,1)S(1)} %get-tuple-element.64), channel_id=1, source_target_pairs={{0,16},{8,24},{16,0},{24,8},{1,17},{9,25},{17,1},{25,9},{2,18},{10... | collective-permute-start | bytes 786440 | tf_op jit(solution)/shard_map/ppermute | solution.py:293
  24.6 12.8 %collective-permute-start.11 = (bf16[2,256,256]{2,1,0:T(8,128)(2,1)S(1)}, bf16[2,256,256]{2,1,0:T(8,128)(2,1)S(1)}, u32[]{:S(2)}, u32[]{:S(2)}) collective-permute-start(bf16[2,256,256]{2,1,0:T(8,128)(2,1)S(1)} %get-tuple-element.65), channel_id=1, source_target_pairs={{0,24},{8,16},{16,8},{24,0},{1,25},{9,17},{17,9},{25,1},{2,26},{10... | collective-permute-start | bytes 786440 | tf_op jit(solution)/shard_map/ppermute | solution.py:293
  28.3 12.8 %collective-permute-start.12 = (bf16[2,192,256]{2,1,0:T(8,128)(2,1)S(1)}, bf16[2,192,256]{2,1,0:T(8,128)(2,1)S(1)}, u32[]{:S(2)}, u32[]{:S(2)}) collective-permute-start(bf16[2,192,256]{2,1,0:T(8,128)(2,1)S(1)} %get-tuple-element.70), channel_id=1, source_target_pairs={{0,8},{8,0},{16,24},{24,16},{1,9},{9,1},{17,25},{25,17},{2,10},{10... | collective-permute-start | bytes 589832 | tf_op jit(solution)/shard_map/ppermute | solution.py:293
  29.9 12.6 %collective-permute-start.13 = (bf16[2,192,256]{2,1,0:T(8,128)(2,1)S(1)}, bf16[2,192,256]{2,1,0:T(8,128)(2,1)S(1)}, u32[]{:S(2)}, u32[]{:S(2)}) collective-permute-start(bf16[2,192,256]{2,1,0:T(8,128)(2,1)S(1)} %get-tuple-element.71), channel_id=1, source_target_pairs={{0,16},{8,24},{16,0},{24,8},{1,17},{9,25},{17,1},{25,9},{2,18},{10... | collective-permute-start | bytes 589832 | tf_op jit(solution)/shard_map/ppermute | solution.py:293
  31.5 12.5 %collective-permute-start.14 = (bf16[2,192,256]{2,1,0:T(8,128)(2,1)S(1)}, bf16[2,192,256]{2,1,0:T(8,128)(2,1)S(1)}, u32[]{:S(2)}, u32[]{:S(2)}) collective-permute-start(bf16[2,192,256]{2,1,0:T(8,128)(2,1)S(1)} %get-tuple-element.72), channel_id=1, source_target_pairs={{0,24},{8,16},{16,8},{24,0},{1,25},{9,17},{17,9},{25,1},{2,26},{10... | collective-permute-start | bytes 589832 | tf_op jit(solution)/shard_map/ppermute | solution.py:293
  45.2 6.0 %collective-permute-start.15 = (bf16[2,64,256]{2,1,0:T(8,128)(2,1)S(1)}, bf16[2,64,256]{2,1,0:T(8,128)(2,1)S(1)}, u32[]{:S(2)}, u32[]{:S(2)}) collective-permute-start(bf16[2,64,256]{2,1,0:T(8,128)(2,1)S(1)} %get-tuple-element.75.refs_4_), channel_id=1, source_target_pairs={{0,8},{8,0},{16,24},{24,16},{1,9},{9,1},{17,25},{25,17},{2,10},{10... | collective-permute-start | bytes 196616 | tf_op jit(solution)/shard_map/ppermute | solution.py:293
  46.1 6.3 %collective-permute-start.16 = (bf16[2,64,256]{2,1,0:T(8,128)(2,1)S(1)}, bf16[2,64,256]{2,1,0:T(8,128)(2,1)S(1)}, u32[]{:S(2)}, u32[]{:S(2)}) collective-permute-start(bf16[2,64,256]{2,1,0:T(8,128)(2,1)S(1)} %get-tuple-element.76.refs_5_), channel_id=1, source_target_pairs={{0,16},{8,24},{16,0},{24,8},{1,17},{9,25},{17,1},{25,9},{2,18},{10... | collective-permute-start | bytes 196616 | tf_op jit(solution)/shard_map/ppermute | solution.py:293
  47.3 5.7 %collective-permute-start.17 = (bf16[2,64,256]{2,1,0:T(8,128)(2,1)S(1)}, bf16[2,64,256]{2,1,0:T(8,128)(2,1)S(1)}, u32[]{:S(2)}, u32[]{:S(2)}) collective-permute-start(bf16[2,64,256]{2,1,0:T(8,128)(2,1)S(1)} %get-tuple-element.77.refs_6_), channel_id=1, source_target_pairs={{0,24},{8,16},{16,8},{24,0},{1,25},{9,17},{17,9},{25,1},{2,26},{10... | collective-permute-start | bytes 196616 | tf_op jit(solution)/shard_map/ppermute | solution.py:293
  48.8 15.4 %collective-permute-start.24 = (bf16[1040,128]{1,0:T(8,128)(2,1)S(1)}, bf16[1040,128]{1,0:T(8,128)(2,1)S(1)}, u32[]{:S(2)}, u32[]{:S(2)}) collective-permute-start(bf16[1040,128]{1,0:T(8,128)(2,1)S(1)} %shard_map.144.refs_10_.same.same_0), channel_id=1, source_target_pairs={{0,24},{8,16},{16,8},{24,0},{1,25},{9,17},{17,9},{25,1},{2,26},{10... | collective-permute-start | bytes 798728 | tf_op jit(solution)/shard_map/ppermute | solution.py:293
  50.4 13.8 %collective-permute-start.23 = (bf16[1040,128]{1,0:T(8,128)(2,1)S(1)}, bf16[1040,128]{1,0:T(8,128)(2,1)S(1)}, u32[]{:S(2)}, u32[]{:S(2)}) collective-permute-start(bf16[1040,128]{1,0:T(8,128)(2,1)S(1)} %shard_map.144.refs_10_.same.same_0), channel_id=1, source_target_pairs={{0,16},{8,24},{16,0},{24,8},{1,17},{9,25},{17,1},{25,9},{2,18},{10... | collective-permute-start | bytes 798728 | tf_op jit(solution)/shard_map/ppermute | solution.py:293
  51.2 13.1 %collective-permute-start.22 = (bf16[1040,128]{1,0:T(8,128)(2,1)S(1)}, bf16[1040,128]{1,0:T(8,128)(2,1)S(1)}, u32[]{:S(2)}, u32[]{:S(2)}) collective-permute-start(bf16[1040,128]{1,0:T(8,128)(2,1)S(1)} %shard_map.144.refs_10_.same.same_0), channel_id=1, source_target_pairs={{0,8},{8,0},{16,24},{24,16},{1,9},{9,1},{17,25},{25,17},{2,10},{10... | collective-permute-start | bytes 798728 | tf_op jit(solution)/shard_map/ppermute | solution.py:293
  52.4 8.5 %collective-permute-start.21 = (bf16[1040,128]{1,0:T(8,128)(2,1)S(1)}, bf16[1040,128]{1,0:T(8,128)(2,1)S(1)}, u32[]{:S(2)}, u32[]{:S(2)}) collective-permute-start(bf16[1040,128]{1,0:T(8,128)(2,1)S(1)} %shard_map.144.refs_10_.same.same_0), channel_id=1, source_target_pairs={{0,1},{1,0},{2,3},{3,2},{4,5},{5,4},{6,7},{7,6},{8,9},{9,8},{10,11... | collective-permute-start | bytes 798728 | tf_op jit(solution)/shard_map/ppermute | solution.py:310
  54.3 3.7 %collective-permute-start.19 = (f32[2,256]{1,0:T(2,128)S(1)}, f32[2,256]{1,0:T(2,128)S(1)}, u32[]{:S(2)}, u32[]{:S(2)}) collective-permute-start(f32[2,256]{1,0:T(2,128)S(1)} %get-tuple-element.82.refs_7_.refs_0_), channel_id=1, source_target_pairs={{0,2},{2,0},{4,6},{6,4},{1,3},{3,1},{5,7},{7,5},{8,10},{10,8},{12,... | collective-permute-start | bytes 6152 | tf_op jit(solution)/shard_map/ppermute | solution.py:305
  58.0 4.5 %collective-permute-start.20 = (f32[2,256]{1,0:T(2,128)S(1)}, f32[2,256]{1,0:T(2,128)S(1)}, u32[]{:S(2)}, u32[]{:S(2)}) collective-permute-start(f32[2,256]{1,0:T(2,128)S(1)} %shard_map.147.refs_7_), channel_id=1, source_target_pairs={{0,4},{2,6},{4,0},{6,2},{1,5},{3,7},{5,1},{7,3},{8,12},{10,14},{12... | collective-permute-start | bytes 6152 | tf_op jit(solution)/shard_map/ppermute | solution.py:305
  (11 other events, 68.3 us)

commit v6 on v5

--- a/solution.py
+++ b/solution.py
@@ -197,25 +197,31 @@
     return jax.ShapeDtypeStruct(shape, dtype)
 
 
+def place():
+    return lax.axis_index("seq"), lax.axis_index("dp")
+
+
 def cost_of(micros):
     return pl.CostEstimate(
         flops=int(micros * 1e9), bytes_accessed=int(micros * 3.6e6), transcendentals=0
     )
 
 
-def whole_call(body, outs, *ins, micros=1.0, after=(), scratch=(), vmem=40):
+def whole_call(body, outs, *ins, micros=1.0, after=(), scratch=(), vmem=40, aliases=None):
+    first = (place,) if ins[0] is place else ()
+    ins = ins[len(first) :]
     n_out = len(jax.tree.leaves(outs))
     skip = len(after)
     space = pl.BlockSpec(memory_space=pltpu.VMEM)
     return pl.pallas_call(
-        lambda *refs: body(*refs[: len(ins)], *refs[len(ins) + skip :]),
+        lambda *refs: body(
+            *(ask() for ask in first), *refs[: len(ins)], *refs[len(ins) + skip :]
+        ),
         out_shape=outs,
-        in_specs=[
-            pl.BlockSpec(memory_space=pltpu.SMEM) if a.dtype == jnp.int32 else space for a in ins
-        ]
-        + [pl.BlockSpec(memory_space=pl.ANY)] * skip,
+        in_specs=[space] * len(ins) + [pl.BlockSpec(memory_space=pl.ANY)] * skip,
         out_specs=jax.tree.map(lambda _: space, outs),
         scratch_shapes=list(scratch),
+        input_output_aliases=aliases or {},
         compiler_params=pltpu.CompilerParams(vmem_limit_bytes=vmem * 2**20),
         cost_estimate=cost_of(micros),
     )(*ins, *after)
@@ -283,9 +289,6 @@
     n_mem = (n_seq - 1) * slots
     scale = HD ** (-0.5)
     full_width = cols * n_head
-    me = lax.axis_index("seq")
-    core = lax.axis_index("dp")
-    ids = jnp.stack([me, core]).astype(jnp.int32)
 
     def to_peers(axis, arrays):
         n = lax.axis_size(axis)
@@ -340,20 +343,35 @@
                 block * slots : (block + 1) * slots, (h % hp) * HD : (h % hp + 1) * HD
             ] = total.astype(BF16)
 
-    def values_body(v_ref, w_ref, vp_ref, mem_ref):
+    def pack_slots(mine, mem_ref, sends):
+        for k, send in zip(peers, sends):
+            for r in peers:
+                source = pl.ds(pl.multiple_of((mine ^ k ^ r) * slots, slots), slots)
+                send[(r - 1) * slots : r * slots, :] = mem_ref[source, :]
+
+    def values_body(ids_ref, v_ref, w_ref, vp_ref, *rest):
+        sends, mem_ref = rest[:-1], rest[-1]
         vp_ref[...] = dot(row_order(rows), v_ref[...]).astype(BF16)
         compress(vp_ref, w_ref, mem_ref)
+        pack_slots(ids_ref[0], mem_ref, sends)
 
     rows_shape = sds((rows, cols), BF16)
     mem_shape = sds((mem_rows, wide), BF16)
-    vp, mem_v = whole_call(
-        values_body, (rows_shape, mem_shape), v, value_squeeze, micros=0.8
-    )
-    mv_recv = to_peers("seq", [mem_v] * (n_seq - 1))
-
-    def keys_body(k_ref, kg_ref, w_ref, *rest):
+    slots_packet = sds((n_mem, wide), BF16)
+    mem_scratch = [pltpu.VMEM(mem_shape.shape, BF16)]
+    vp, *mv_sends = whole_call(
+        values_body,
+        (rows_shape,) + (slots_packet,) * (n_seq - 1),
+        place, v, value_squeeze,
+        scratch=mem_scratch,
+        micros=0.8,
+    )
+    mv_recv = to_peers("seq", mv_sends)
+
+    def keys_body(ids_ref, k_ref, kg_ref, w_ref, *rest):
         ss_refs = rest[:n_head]
-        inv_ref, kn_ref, mem_ref = rest[n_head:]
+        inv_ref, kn_ref = rest[n_head : n_head + 2]
+        sends, mem_ref = rest[n_head + 2 : -1], rest[-1]
         total = ss_refs[0][...]
         for other in ss_refs[1:]:
             total = total + other[...]
@@ -369,14 +387,16 @@
         normed = (k_ref[...].astype(F32) * natural[:, 1:2] * kg_ref[...]).astype(BF16)
         kn_ref[...] = dot(order, normed).astype(BF16)
         compress(kn_ref, w_ref, mem_ref)
-
-    inv, kn, mem = whole_call(
+        pack_slots(ids_ref[0], mem_ref, sends)
+
+    inv, kn, *mk_sends = whole_call(
         keys_body,
-        (two_rows, rows_shape, mem_shape),
-        k, kg, key_squeeze, *ss_parts,
+        (two_rows, rows_shape) + (slots_packet,) * (n_seq - 1),
+        place, k, kg, key_squeeze, *ss_parts,
+        scratch=mem_scratch,
         micros=20.0,
     )
-    mk_recv = to_peers("seq", [mem] * (n_seq - 1))
+    mk_recv = to_peers("seq", mk_sends)
 
     def local_body(q_ref, qg_ref, inv_ref, kn_ref, vp_ref, do_ref, qn_ref, st_ref):
         allowed = causal_t(rows)
@@ -413,11 +433,38 @@
     *row_sends, kp = whole_call(
         rows_body,
         (row_pair,) * (n_seq - 1) + (rows_shape,),
-        ids, kn, vp, k,
+        place, kn, vp, k,
         after=(stats,),
         micros=0.7,
     )
     rows_recv = to_peers("seq", row_sends)
+
+    def memory_head(mine, qn_h, do_h, mk, mv, stat):
+        raw = dot(mk, qn_h, NT) * scale
+        s = jnp.concatenate(
+            [
+                jnp.where((mine ^ src) < mine, raw[(src - 1) * slots : src * slots], -jnp.inf)
+                for src in peers
+            ],
+            axis=0,
+        )
+        g = dot(mv, do_h, NT)
+        m_loc, l_loc, d_loc = stat[0:1], stat[1:2], stat[2:3]
+        m = jnp.maximum(m_loc, jnp.max(s, axis=0, keepdims=True))
+        p = jnp.exp(s - m)
+        shrink = jnp.exp(m_loc - m)
+        mass = l_loc * shrink + jnp.sum(p, axis=0, keepdims=True)
+        inv_mass = 1.0 / mass
+        delta = (d_loc * shrink + jnp.sum(p * g, axis=0, keepdims=True)) * inv_mass
+        attend = p * inv_mass
+        ds = (attend * (g - delta)).astype(BF16)
+        gk = (dot(ds, qn_h) * scale).astype(BF16)
+        gv = dot(attend.astype(BF16), do_h).astype(BF16)
+        return jnp.concatenate([m, inv_mass, delta, stat[3:]], axis=0), ds, gk, gv
+
+    def places(mine, r, i):
+        h = (mine ^ r) * hp + i
+        return h, pl.ds(pl.multiple_of(h * HD, HD), HD), slice(i * HD, (i + 1) * HD)
 
     def memory_body(ids_ref, qn_ref, do_ref, st_ref, *rest):
         mk_refs = rest[: n_seq - 1]
@@ -425,88 +472,118 @@
         st2_ref, ds_ref = rest[2 * n_seq - 2 : 2 * n_seq]
         parts = rest[2 * n_seq :]
         mine = ids_ref[0]
-        for r in range(n_seq):
-            block = mine ^ r
-            span = pl.ds(pl.multiple_of(block * slots, slots), slots)
+        for r in peers:
+            span = slice((r - 1) * slots, r * slots)
             for i in range(hp):
-                at = slice(i * HD, (i + 1) * HD)
-                h = block * hp + i
-                wide_at = pl.ds(pl.multiple_of(h * HD, HD), HD)
-                qn_h = qn_ref[:, wide_at]
-                do_h = do_ref[:, wide_at]
-                mk = jnp.concatenate([ref[span, at] for ref in mk_refs], axis=0)
-                mv = jnp.concatenate([ref[span, at] for ref in mv_refs], axis=0)
-                raw = dot(mk, qn_h, NT) * scale
-                s = jnp.concatenate(
-                    [
-                        jnp.where((mine ^ src) < mine, raw[(src - 1) * slots : src * slots], -jnp.inf)
-                        for src in peers
-                    ],
-                    axis=0,
+                h, at, narrow = places(mine, r, i)
+                mk = jnp.concatenate([ref[span, narrow] for ref in mk_refs], axis=0)
+                mv = jnp.concatenate([ref[span, narrow] for ref in mv_refs], axis=0)
+                to = (r - 1) * hp + i
+                st2_ref[to], ds_ref[to], gk, gv = memory_head(
+                    mine, qn_ref[:, at], do_ref[:, at], mk, mv, st_ref[h]
                 )
-                g = dot(mv, do_h, NT)
-                stat = st_ref[h]
-                m_loc, l_loc, d_loc = stat[0:1], stat[1:2], stat[2:3]
-                m = jnp.maximum(m_loc, jnp.max(s, axis=0, keepdims=True))
-                p = jnp.exp(s - m)
-                shrink = jnp.exp(m_loc - m)
-                mass = l_loc * shrink + jnp.sum(p, axis=0, keepdims=True)
-                inv_mass = 1.0 / mass
-                delta = (d_loc * shrink + jnp.sum(p * g, axis=0, keepdims=True)) * inv_mass
-                st2_ref[h] = jnp.concatenate([m, inv_mass, delta, stat[3:]], axis=0)
-                attend = p * inv_mass
-                ds = (attend * (g - delta)).astype(BF16)
-                ds_ref[h] = ds
-                parts[r][0, :, at] = (dot(ds, qn_h) * scale).astype(BF16)
-                parts[r][1, :, at] = dot(attend.astype(BF16), do_h).astype(BF16)
+                parts[r - 1][0, :, narrow] = gk
+                parts[r - 1][1, :, narrow] = gv
 
     part = sds((2, n_mem, wide), BF16)
+    far_heads = heads - hp
     stats2, ds_mem, *parts = whole_call(
         memory_body,
-        (stat_shape, sds((heads, n_mem, rows), BF16)) + (part,) * n_seq,
-        ids, qn, do, stats, *mk_recv, *mv_recv,
+        (sds((far_heads, 8, rows), F32), sds((far_heads, n_mem, rows), BF16))
+        + (part,) * (n_seq - 1),
+        place, qn, do, stats, *mk_recv, *mv_recv,
         micros=2.0,
     )
-    parts_recv = to_peers("seq", parts[1:])
-
-    def grads_body(q_ref, kp_ref, qn_ref, kn_ref, vp_ref, do_ref, st_ref, ds_ref, *rest):
-        mk_refs = rest[: n_seq - 1]
-        inv_ref, qg_ref, gq_ref, gk_ref, gv_ref, dq_ref, gain_q_ref, gain_k_ref = rest[n_seq - 1 :]
+    parts_recv = to_peers("seq", parts)
+
+    def grads_head(refs, h, at, stat, ds_m, mk, allowed, inv_c):
+        q_ref, kp_ref, qn_ref, kn_ref, vp_ref, do_ref, qg_ref = refs[:7]
+        gq_ref, gk_ref, gv_ref, gain_q_ref, gain_k_ref = refs[7:]
+        qn_h, kn_h, do_h = qn_ref[:, at], kn_ref[:, at], do_ref[:, at]
+        s = jnp.where(allowed, dot(kn_h, qn_h, NT) * scale, -jnp.inf)
+        g = dot(vp_ref[:, at], do_h, NT)
+        m, inv_mass, delta = stat[0:1], stat[1:2], stat[2:3]
+        attend = jnp.exp(s - m) * inv_mass
+        ds = (attend * (g - delta)).astype(BF16)
+        gq = scale * (dot(ds, kn_h, TN) + dot(ds_m, mk, TN))
+        gk = scale * dot(ds, qn_h)
+        gq_ref[:, at] = gq
+        gk_ref[:, at] = gk
+        gv_ref[:, at] = dot(attend.astype(BF16), do_h)
+        gq_q = gq * q_ref[:, at].astype(F32)
+        gk_k = gk * kp_ref[:, at].astype(F32)
+        to = pl.ds(h, 1)
+        gain_q_ref[to, :] = jnp.sum(gq_q * inv_c[:, 0:1], axis=0, keepdims=True)
+        gain_k_ref[to, :] = jnp.sum(gk_k * inv_c[:, 1:2], axis=0, keepdims=True)
+        return gq_q * qg_ref[:, at]
+
+    def grads_body(ids_ref, q_ref, kp_ref, qn_ref, kn_ref, vp_ref, do_ref, inv_ref, qg_ref, *rest):
+        st_ref, ds_ref = rest[:2]
+        mk_refs = rest[2 : n_seq + 1]
+        outs, dq_ref = rest[n_seq + 1 : -1], rest[-1]
+        refs = (q_ref, kp_ref, qn_ref, kn_ref, vp_ref, do_ref, qg_ref) + tuple(outs)
         allowed = causal_t(rows)
         inv_c = as_columns(inv_ref[...])
         total = jnp.zeros((rows, HD), F32)
-        for h in range(heads):
-            at = slice(h * HD, (h + 1) * HD)
-            narrow = slice((h % hp) * HD, (h % hp + 1) * HD)
-            span = slice((h // hp) * slots, (h // hp + 1) * slots)
-            qn_h, kn_h, do_h = qn_ref[:, at], kn_ref[:, at], do_ref[:, at]
-            s = jnp.where(allowed, dot(kn_h, qn_h, NT) * scale, -jnp.inf)
-            g = dot(vp_ref[:, at], do_h, NT)
-            m, inv_mass, delta = st_ref[h, 0:1, :], st_ref[h, 1:2, :], st_ref[h, 2:3, :]
-            attend = jnp.exp(s - m) * inv_mass
-            ds = (attend * (g - delta)).astype(BF16)
-            mk = jnp.concatenate([ref[span, narrow] for ref in mk_refs], axis=0)
-            gq = scale * (dot(ds, kn_h, TN) + dot(ds_ref[h], mk, TN))
-            gk = scale * dot(ds, qn_h)
-            gq_ref[:, at] = gq
-            gk_ref[:, at] = gk
-            gv_ref[:, at] = dot(attend.astype(BF16), do_h)
-            gq_q = gq * q_ref[:, at].astype(F32)
-            gk_k = gk * kp_ref[:, at].astype(F32)
-            total = total + gq_q * qg_ref[:, at]
-            gain_q_ref[h : h + 1, :] = jnp.sum(gq_q * inv_c[:, 0:1], axis=0, keepdims=True)
-            gain_k_ref[h : h + 1, :] = jnp.sum(gk_k * inv_c[:, 1:2], axis=0, keepdims=True)
-        dq_ref[...] = lane_sum_row(total)
+        for r in peers:
+            span = slice((r - 1) * slots, r * slots)
+            for i in range(hp):
+                h, at, narrow = places(ids_ref[0], r, i)
+                mk = jnp.concatenate([ref[span, narrow] for ref in mk_refs], axis=0)
+                to = (r - 1) * hp + i
+                total = total + grads_head(
+                    refs, h, at, st_ref[to], ds_ref[to], mk, allowed, inv_c
+                )
+        dq_ref[...] = total
 
     gain_rows = sds((heads, HD), F32)
     wide_f32 = sds((rows, cols), F32)
+    narrow_f32 = sds((rows, HD), F32)
     dot_row = sds((1, rows), F32)
-    gq, gk_local, gv_local, dot_q, gain_q, gain_k = whole_call(
+    far_grads = whole_call(
         grads_body,
-        (wide_f32, wide_f32, wide_f32, dot_row, gain_rows, gain_rows),
-        q, kp, qn, kn, vp, do, stats2, ds_mem, *mk_recv, inv, qg,
+        (wide_f32, wide_f32, wide_f32, gain_rows, gain_rows, narrow_f32),
+        place, q, kp, qn, kn, vp, do, inv, qg, stats2, ds_mem, *mk_recv,
         micros=0.5,
-        after=tuple(rows_recv),
+    )
+
+    def own_body(ids_ref, q_ref, kp_ref, qn_ref, kn_ref, vp_ref, do_ref, inv_ref, qg_ref, *rest):
+        st_ref, wk_ref, wv_ref = rest[:3]
+        row_refs = rest[3 : n_seq + 2]
+        dq_in = rest[n_seq + 7]
+        outs, (dq_ref, part_ref) = rest[n_seq + 8 : n_seq + 13], rest[n_seq + 13 :]
+        refs = (q_ref, kp_ref, qn_ref, kn_ref, vp_ref, do_ref, qg_ref) + tuple(outs)
+        allowed = causal_t(rows)
+        inv_c = as_columns(inv_ref[...])
+        mine = ids_ref[0]
+        total = dq_in[...]
+        for i in range(hp):
+            h, at, narrow = places(mine, 0, i)
+            found = []
+            for tensor, w_ref in ((0, wk_ref), (1, wv_ref)):
+                mem = None
+                for j in range(KS):
+                    span = slice(j * slots, (j + 1) * slots)
+                    rows_j = jnp.concatenate([ref[tensor, span, narrow] for ref in row_refs], axis=0)
+                    term = dot(rows_j, w_ref[h, j * HD : (j + 1) * HD, :])
+                    mem = term if mem is None else mem + term
+                found.append(mem.astype(BF16))
+            stat, ds_m, gk, gv = memory_head(
+                mine, qn_ref[:, at], do_ref[:, at], found[0], found[1], st_ref[h]
+            )
+            part_ref[0, :, narrow] = gk
+            part_ref[1, :, narrow] = gv
+            total = total + grads_head(refs, h, at, stat, ds_m, found[0], allowed, inv_c)
+        dq_ref[...] = lane_sum_row(total)
+
+    first_alias = 8 + 3 + n_seq - 1
+    gq, gk_local, gv_local, gain_q, gain_k, dot_q, own_part = whole_call(
+        own_body,
+        (wide_f32, wide_f32, wide_f32, gain_rows, gain_rows, dot_row, part),
+        place, q, kp, qn, kn, vp, do, inv, qg, stats, key_squeeze, value_squeeze, *rows_recv,
+        *far_grads,
+        aliases={first_alias + n: n for n in range(5)},
+        micros=0.3,
     )
 
     def slots_body(*refs):
@@ -524,7 +601,7 @@
 
     slot_grad = sds((2, slots, wide), BF16)
     slot_grads = whole_call(
-        slots_body, (slot_grad,) * n_seq, parts[0], *parts_recv, after=(gain_q,), micros=0.3
+        slots_body, (slot_grad,) * n_seq, own_part, *parts_recv, after=(gain_q,), micros=0.3
     )
 
     slots_recv = to_peers("seq", slot_grads[1:])
@@ -556,7 +633,7 @@
     w_same, w_other = whole_call(
         weights_body,
         (sds((span_rows, HD), F32), sds((span_rows, HD), BF16)),
-        ids, kn, vp, *slot_grads, *rows_recv,
+        place, kn, vp, *slot_grads, *rows_recv,
         micros=1.1,
     )
     w_recv = to_core(w_other)
@@ -567,7 +644,7 @@
         out_ref[span_rows:, :] = gains.astype(BF16)
 
     chunk_shape = sds((span_rows + 2 * heads, HD), BF16)
-    chunk = whole_call(chunk_body, chunk_shape, w_same, w_recv, gain_q, gain_k, micros=0.3)
+    chunk = whole_call(chunk_body, chunk_shape, w_same, w_recv, gain_q, gain_k, micros=0.3, after=tuple(slots_recv))
     chunks = to_peers("seq", [chunk] * (n_seq - 1))
     chunk_other = to_core(chunk)
 
@@ -578,16 +655,16 @@
 
     def column_out(body, outs, n_out, *ins, micros, after=()):
         skip = len(after)
+        first = (place,) if ins[0] is place else ()
+        ins = ins[len(first) :]
         inside = pl.BlockSpec(memory_space=pltpu.VMEM)
         small = len(outs) - n_out
         return pl.pallas_call(
-            lambda *refs: body(*refs[: len(ins)], *refs[len(ins) + skip :]),
+            lambda *refs: body(
+                *(ask() for ask in first), *refs[: len(ins)], *refs[len(ins) + skip :]
+            ),
             out_shape=outs,
-            in_specs=[
-                pl.BlockSpec(memory_space=pltpu.SMEM) if a.dtype == jnp.int32 else inside
-                for a in ins
-            ]
-            + [pl.BlockSpec(memory_space=pl.ANY)] * skip,
+            in_specs=[inside] * len(ins) + [pl.BlockSpec(memory_space=pl.ANY)] * skip,
             out_specs=(inside,) * small + (pl.BlockSpec(memory_space=pl.ANY),) * n_out,
             scratch_shapes=[pltpu.VMEM((rows, cols), BF16)] * n_out
             + [pltpu.SemaphoreType.DMA((n_out, n_seq))],
@@ -620,7 +697,7 @@
     gkn, dots = whole_call(
         back_keys_body,
         (wide_f32, two_rows),
-        ids, gk_local, kp, key_squeeze, kg, dot_q, slot_grads[0], *slots_recv,
+        place, gk_local, kp, key_squeeze, kg, dot_q, slot_grads[0], *slots_recv,
         micros=2.0,
         after=(chunk,),
     )
@@ -645,7 +722,7 @@
         back_values_body,
         (sds((8, HD), F32), rows_shape),
         1,
-        ids, gv_local, value_squeeze, slot_grads[0], *slots_recv,
+        place, gv_local, value_squeeze, slot_grads[0], *slots_recv,
         micros=2.0,
         after=(dots,),
     )
@@ -680,20 +757,19 @@
         for copy in copies:
             copy.wait()
 
-    smem = pl.BlockSpec(memory_space=pltpu.SMEM)
     inside = pl.BlockSpec(memory_space=pltpu.VMEM)
     outside = pl.BlockSpec(memory_space=pl.ANY)
     buffer = pltpu.VMEM(kernel_out.shape, F32)
     params = pltpu.CompilerParams(vmem_limit_bytes=40 * 2**20)
     own_mark, *part_written = pl.pallas_call(
-        own_chunk_body,
+        lambda *refs: own_chunk_body(place(), *refs),
         out_shape=(sds((8, HD), F32), kernel_out, kernel_out),
-        in_specs=[smem, inside, inside],
+        in_specs=[inside, inside],
         out_specs=(inside, outside, outside),
         scratch_shapes=[buffer, buffer, pltpu.SemaphoreType.DMA((2,))],
         compiler_params=params,
         cost_estimate=cost_of(0.01),
-    )(ids, chunk, chunk_other)
+    )(chunk, chunk_other)
 
     def norms_body(q_ref, kp_ref, gq_ref, gkn_ref, qg_ref, kg_ref, inv_ref, *rest):
         dots_a, dots_b, mark_ref, out_q, out_k, buffer_q, buffer_k, sems = rest
@@ -814,21 +890,21 @@
             finish(copies)
 
     back_row, *part_written = pl.pallas_call(
-        this_core_body,
+        lambda *refs: this_core_body(place(), *refs),
         out_shape=(gains_shape, kernel_out, kernel_out),
-        in_specs=[smem] + [inside] * 4 + [outside] * 2,
+        in_specs=[inside] * 4 + [outside] * 2,
         out_specs=(inside, outside, outside),
-        input_output_aliases={5: 1, 6: 2},
+        input_output_aliases={4: 1, 5: 2},
         scratch_shapes=[buffer, pltpu.SemaphoreType.DMA((n_seq,))],
         compiler_params=params,
         cost_estimate=cost_of(1.6),
-    )(ids, chunk, packed, kg, key_squeeze, *part_written)
+    )(chunk, packed, kg, key_squeeze, *part_written)
     gks, gvs, gain_q_all, gain_k_all = pl.pallas_call(
-        other_core_body,
+        lambda *refs: other_core_body(place(), *refs),
         out_shape=(kernel_out, kernel_out, gains_shape, gains_shape),
-        in_specs=[smem] + [inside] * 7 + [outside] * 2,
+        in_specs=[inside] * 7 + [outside] * 2,
         out_specs=(outside,) * 4,
-        input_output_aliases={8: 0, 9: 1},
+        input_output_aliases={7: 0, 8: 1},
         scratch_shapes=[
             buffer,
             pltpu.VMEM((1, cols), F32),
@@ -837,7 +913,7 @@
         ],
         compiler_params=params,
         cost_estimate=cost_of(2.2),
-    )(ids, chunk, chunk_other, packed, packed_other, back_row, kg, key_squeeze, *part_written)
+    )(chunk, chunk_other, packed, packed_other, back_row, kg, key_squeeze, *part_written)
     return (
         grad_query[None],
         grad_key[None],

time: 68.7 us -> 67.2 us (0.978)
  waiting for transfers between devices: 8.21 us -> 13.8 us
  Pallas kernels: 25.4 us -> 20.8 us
  starting transfers between devices: 32.8 us -> 31.5 us
  local copies, waits for them, and re-layouts: 1.07 us -> 0.04 us
    pallas_call x18 -> x19, Pallas kernels: 25.4 us -> 20.8 us  [the longest x14 13.6 us: whole_call(): pl.pallas_call(lambda *refs: body(*(ask() for ask in first), *refs[:len(i...]
    ppermute x21, waiting for transfers between devices: 7.88 us -> 11.5 us  [to_peers(): lax.ppermute(a, axis, [(i, i ^ k) for i in range(n)])]
    ppermute x2, waiting for transfers between devices: 0.1 us -> 1.54 us  [over_heads(): got = lax.ppermute(a, 'head', [(i, i ^ step) for i in range(n_head)])]
    unnamed x18, local copies, waits for them, and re-layouts: 1.07 us -> 0.04 us
    ppermute x21, starting transfers between devices: 28.4 us -> 27.6 us  [to_peers(): lax.ppermute(a, axis, [(i, i ^ k) for i in range(n)])]
  transfers between devices with their start and end apart: 26 -> 26, of which waited for: 8 -> 10; matrix products, arithmetic and copies ran while one was open for 0% -> 0% of each run, Pallas kernels for 30% -> 25%
where the time goes in v6:
time: 67.2 us; the launch traced here: 67 us
  starting transfers between devices  31.5 us (47%)
  Pallas kernels  20.8 us (31%)
  waiting for transfers between devices  13.8 us (21%)
  between operations  0.88 us (1%)
    ppermute x21, starting transfers between devices, to_peers(): lax.ppermute(a, axis, [(i, i ^ k) for i in range(n)])  27.6 us
    pallas_call x14, Pallas kernels, whole_call(): pl.pallas_call(lambda *refs: body(*(ask() for ask in first), *refs[:len(i...  13.6 us
    ppermute x21, waiting for transfers between devices, to_peers(): lax.ppermute(a, axis, [(i, i ^ k) for i in range(n)])  11.5 us
    ppermute x2, starting transfers between devices, over_heads(): got = lax.ppermute(a, 'head', [(i, i ^ step) for i in range(n_head)])  3.76 us
    pallas_call x2, Pallas kernels, column_out(): pl.pallas_call(lambda *refs: body(*(ask() for ask in first), *refs[:len(i...  3.43 us
    ppermute x2, waiting for transfers between devices, over_heads(): got = lax.ppermute(a, 'head', [(i, i ^ step) for i in range(n_head)])  1.54 us
    pallas_call x1, Pallas kernels, on_device(): pl.pallas_call(lambda *refs: this_core_body(place(), *refs), out_shape=(g...  1.53 us
  transfers between devices with their start and end apart: 26, of which 10 were waited for; matrix products, arithmetic and copies ran while one was open for 0% of the time, Pallas kernels for 25%

profile of v6, /device:TPU:0, one launch (start us, length us, event | category | flops | bytes accessed | tf_op | source)
XLA Modules:
  0.0 67.0 jit_solution(3524699671648344876)
XLA Ops:
  0.7 2.2 %shard_map.135.refs_3_ = f32[2,256]{1,0:T(2,128)} custom-call(bf16[256,1024]{1,0:T(8,128)(2,1)} %bitcast.11, bf16[256,1024]{1,0:T(8,128)(2,1)} %bitcast.30), custom_call_target="tpu_custom_call" | custom-call | flops 1500000000 | bytes 5400000 | tf_op jit(solution)/shard_map/pallas_call | solution.py:216
  2.8 5.1 %collective-permute-start.2 = (f32[2,256]{1,0:T(2,128)}, f32[2,256]{1,0:T(2,128)S(1)}, u32[]{:S(2)}, u32[]{:S(2)}) collective-permute-start(f32[2,256]{1,0:T(2,128)} %shard_map.135.refs_3_), channel_id=1, source_target_pairs={{0,6},{2,4},{4,2},{6,0},{1,7},{3,5},{5,3},{7,1},{8,14},{10,12},{12... | collective-permute-start | bytes 6152 | tf_op jit(solution)/shard_map/ppermute | solution.py:296
  9.2 1.7 %collective-permute-start.3 = (bf16[192,256]{1,0:T(8,128)(2,1)S(1)}, bf16[192,256]{1,0:T(8,128)(2,1)S(1)}, u32[]{:S(2)}, u32[]{:S(2)}) collective-permute-start(bf16[192,256]{1,0:T(8,128)(2,1)S(1)} %get-tuple-element.66), channel_id=1, source_target_pairs={{0,8},{8,0},{16,24},{24,16},{1,9},{9,1},{17,25},{25,17},{2,10},{10... | collective-permute-start | bytes 294920 | tf_op jit(solution)/shard_map/ppermute | solution.py:296
  10.9 1.5 %collective-permute-start.4 = (bf16[192,256]{1,0:T(8,128)(2,1)S(1)}, bf16[192,256]{1,0:T(8,128)(2,1)S(1)}, u32[]{:S(2)}, u32[]{:S(2)}) collective-permute-start(bf16[192,256]{1,0:T(8,128)(2,1)S(1)} %get-tuple-element.67), channel_id=1, source_target_pairs={{0,16},{8,24},{16,0},{24,8},{1,17},{9,25},{17,1},{25,9},{2,18},{10... | collective-permute-start | bytes 294920 | tf_op jit(solution)/shard_map/ppermute | solution.py:296
  13.8 1.7 %collective-permute-start.9 = (bf16[192,256]{1,0:T(8,128)(2,1)S(1)}, bf16[192,256]{1,0:T(8,128)(2,1)S(1)}, u32[]{:S(2)}, u32[]{:S(2)}) collective-permute-start(bf16[192,256]{1,0:T(8,128)(2,1)S(1)} %get-tuple-element.75), channel_id=1, source_target_pairs={{0,8},{8,0},{16,24},{24,16},{1,9},{9,1},{17,25},{25,17},{2,10},{10... | collective-permute-start | bytes 294920 | tf_op jit(solution)/shard_map/ppermute | solution.py:296
  15.5 1.5 %collective-permute-start.10 = (bf16[192,256]{1,0:T(8,128)(2,1)S(1)}, bf16[192,256]{1,0:T(8,128)(2,1)S(1)}, u32[]{:S(2)}, u32[]{:S(2)}) collective-permute-start(bf16[192,256]{1,0:T(8,128)(2,1)S(1)} %get-tuple-element.76), channel_id=1, source_target_pairs={{0,16},{8,24},{16,0},{24,8},{1,17},{9,25},{17,1},{25,9},{2,18},{10... | collective-permute-start | bytes 294920 | tf_op jit(solution)/shard_map/ppermute | solution.py:296
  18.3 1.4 %shard_map.138 = (bf16[256,1024]{1,0:T(8,128)(2,1)S(1)}, f32[8,8,256]{2,1,0:T(8,128)S(1)}) custom-call(bf16[256,1024]{1,0:T(8,128)(2,1)S(1)} %bitcast.12, f32[1,1024]{1,0:T(1,128)S(1)} %bitcast.20, f32[2,256]{1,0:T(2,128)S(1)} %get-tuple-element.65.refs_2_.refs_6_, bf16[256,1024]{1,0:T(8,128)(2,1)S(1)} %get-tuple-element.63.refs_3_.refs_0_, ...), custom_call_target="tpu_custom_call" | custom-call | flops 500000000 | bytes 1800000 | tf_op jit(solution)/shard_map/pallas_call | solution.py:216
  20.1 1.3 %collective-permute-start.6 = (bf16[2,256,256]{2,1,0:T(8,128)(2,1)S(1)}, bf16[2,256,256]{2,1,0:T(8,128)(2,1)S(1)}, u32[]{:S(2)}, u32[]{:S(2)}) collective-permute-start(bf16[2,256,256]{2,1,0:T(8,128)(2,1)S(1)} %get-tuple-element.72), channel_id=1, source_target_pairs={{0,8},{8,0},{16,24},{24,16},{1,9},{9,1},{17,25},{25,17},{2,10},{10... | collective-permute-start | bytes 786440 | tf_op jit(solution)/shard_map/ppermute | solution.py:296
  23.6 2.1 %shard_map.140 = (f32[6,8,256]{2,1,0:T(8,128)S(1)}, bf16[6,192,256]{2,1,0:T(8,128)(2,1)S(1)}, bf16[2,192,256]{2,1,0:T(8,128)(2,1)S(1)}, bf16[2,192,256]{2,1,0:T(8,128)(2,1)S(1)}, bf16[2,192,256]{2,1,0:T(8,128)(2,1)S(1)}) custom-call(bf16[256,1024]{1,0:T(8,128)(2,1)S(1)} %get-tuple-element.71.refs_0_.refs_2_, bf16[256,1024]{1,0:T(8,128)(2,1)S(1)} %bitcast.17, ...), custom_call_target="tpu_custom_call" | custom-call | flops 2000000000 | bytes 7200000 | tf_op jit(solution)/shard_map/pallas_call | solution.py:216
  25.7 1.3 %collective-permute-start.12 = (bf16[2,192,256]{2,1,0:T(8,128)(2,1)S(1)}, bf16[2,192,256]{2,1,0:T(8,128)(2,1)S(1)}, u32[]{:S(2)}, u32[]{:S(2)}) collective-permute-start(bf16[2,192,256]{2,1,0:T(8,128)(2,1)S(1)} %get-tuple-element.90), channel_id=1, source_target_pairs={{0,8},{8,0},{16,24},{24,16},{1,9},{9,1},{17,25},{25,17},{2,10},{10... | collective-permute-start | bytes 589832 | tf_op jit(solution)/shard_map/ppermute | solution.py:296
  28.1 1.3 %collective-permute-done.6.refs_11_.refs_6_ = bf16[2,256,256]{2,1,0:T(8,128)(2,1)S(1)} collective-permute-done((bf16[2,256,256]{2,1,0:T(8,128)(2,1)S(1)}, bf16[2,256,256]{2,1,0:T(8,128)(2,1)S(1)}, u32[]{:S(2)}, u32[]{:S(2)}) %collective-permute-start.6) | collective-permute-done | bytes 262176 | tf_op jit(solution)/shard_map/ppermute | solution.py:296
  29.4 1.7 %collective-permute-start.14 = (bf16[2,192,256]{2,1,0:T(8,128)(2,1)S(1)}, bf16[2,192,256]{2,1,0:T(8,128)(2,1)S(1)}, u32[]{:S(2)}, u32[]{:S(2)}) collective-permute-start(bf16[2,192,256]{2,1,0:T(8,128)(2,1)S(1)} %get-tuple-element.92), channel_id=1, source_target_pairs={{0,24},{8,16},{16,8},{24,0},{1,25},{9,17},{17,9},{25,1},{2,26},{10... | collective-permute-start | bytes 589832 | tf_op jit(solution)/shard_map/ppermute | solution.py:296
  31.1 2.7 %shard_map.141 = (f32[256,1024]{1,0:T(8,128)S(1)}, f32[256,1024]{1,0:T(8,128)S(1)}, f32[256,1024]{1,0:T(8,128)S(1)}, f32[8,128]{1,0:T(8,128)S(1)}, f32[8,128]{1,0:T(8,128)S(1)}, /*index=5*/f32[256,128]{1,0:T(8,128)S(1)}) custom-call(bf16[256,1024]{1,0:T(8,128)(2,1)S(1)} %bitcast.13, bf16[256,1024]{1,0:T(8,128)(2,1)S(1)} %get-tuple-element.70.refs_1_, ...), custom_call_target="tpu_custom_call" | custom-call | flops 500000000 | bytes 1800000 | tf_op jit(solution)/shard_map/pallas_call | solution.py:216
  33.7 2.5 %collective-permute-done.7.refs_12_.refs_7_ = bf16[2,256,256]{2,1,0:T(8,128)(2,1)S(1)} collective-permute-done((bf16[2,256,256]{2,1,0:T(8,128)(2,1)S(1)}, bf16[2,256,256]{2,1,0:T(8,128)(2,1)S(1)}, u32[]{:S(2)}, u32[]{:S(2)}) %collective-permute-start.7) | collective-permute-done | bytes 262176 | tf_op jit(solution)/shard_map/ppermute | solution.py:296
  36.2 2.0 %shard_map.142 = (f32[256,1024]{1,0:T(8,128)S(1)}, f32[256,1024]{1,0:T(8,128)S(1)}, f32[256,1024]{1,0:T(8,128)S(1)}, f32[8,128]{1,0:T(8,128)S(1)}, f32[8,128]{1,...) custom-call(bf16[256,1024]{1,0:T(8,128)(2,1)S(1)} %bitcast.14, ...), custom_call_target="tpu_custom_call", output_to_operand_aliasing={{0}: (14, {}), {1}: (15, {}), {2}: (16, {}), {3}: (17, {}),... | custom-call | flops 300000000 | bytes 1080000 | tf_op jit(solution)/shard_map/pallas_call | solution.py:216
  39.1 2.6 %collective-permute-done.13.refs_2_ = bf16[2,192,256]{2,1,0:T(8,128)(2,1)S(1)} collective-permute-done((bf16[2,192,256]{2,1,0:T(8,128)(2,1)S(1)}, bf16[2,192,256]{2,1,0:T(8,128)(2,1)S(1)}, u32[]{:S(2)}, u32[]{:S(2)}) %collective-permute-start.13) | collective-permute-done | bytes 196640 | tf_op jit(solution)/shard_map/ppermute | solution.py:296
  43.9 1.9 %collective-permute-start.17 = (bf16[2,64,256]{2,1,0:T(8,128)(2,1)S(1)}, bf16[2,64,256]{2,1,0:T(8,128)(2,1)S(1)}, u32[]{:S(2)}, u32[]{:S(2)}) collective-permute-start(bf16[2,64,256]{2,1,0:T(8,128)(2,1)S(1)} %get-tuple-element.97.refs_5_), channel_id=1, source_target_pairs={{0,24},{8,16},{16,8},{24,0},{1,25},{9,17},{17,9},{25,1},{2,26},{10... | collective-permute-start | bytes 196616 | tf_op jit(solution)/shard_map/ppermute | solution.py:296
  46.8 2.4 %collective-permute-done.16.refs_5_.refs_7_.refs_4_ = bf16[2,64,256]{2,1,0:T(8,128)(2,1)S(1)} collective-permute-done((bf16[2,64,256]{2,1,0:T(8,128)(2,1)S(1)}, bf16[2,64,256]{2,1,0:T(8,128)(2,1)S(1)}, u32[]{:S(2)}, u32[]{:S(2)}) %collective-permute-start.16) | collective-permute-done | bytes 65568 | tf_op jit(solution)/shard_map/ppermute | solution.py:296
  49.3 1.8 %collective-permute-start.24 = (bf16[1040,128]{1,0:T(8,128)(2,1)S(1)}, bf16[1040,128]{1,0:T(8,128)(2,1)S(1)}, u32[]{:S(2)}, u32[]{:S(2)}) collective-permute-start(bf16[1040,128]{1,0:T(8,128)(2,1)S(1)} %shard_map.145.refs_9_.refs_0_), channel_id=1, source_target_pairs={{0,24},{8,16},{16,8},{24,0},{1,25},{9,17},{17,9},{25,1},{2,26},{10... | collective-permute-start | bytes 798728 | tf_op jit(solution)/shard_map/ppermute | solution.py:296
  53.5 1.3 %collective-permute-start.19 = (f32[2,256]{1,0:T(2,128)S(1)}, f32[2,256]{1,0:T(2,128)S(1)}, u32[]{:S(2)}, u32[]{:S(2)}) collective-permute-start(f32[2,256]{1,0:T(2,128)S(1)} %get-tuple-element.102.refs_6_.refs_0_), channel_id=1, source_target_pairs={{0,2},{2,0},{4,6},{6,4},{1,3},{3,1},{5,7},{7,5},{8,10},{10,8},{12,... | collective-permute-start | bytes 6152 | tf_op jit(solution)/shard_map/ppermute | solution.py:308
  54.8 1.8 %shard_map.147 = (f32[8,128]{1,0:T(8,128)S(1)}, bf16[256,1024]{1,0:T(8,128)(2,1)}) custom-call(f32[256,1024]{1,0:T(8,128)S(1)} %get-tuple-element.103.refs_0_, bf16[8,512,128]{2,1,0:T(8,128)(2,1)S(1)} %copy-done.3, bf16[2,64,256]{2,1,0:T(8,128)(2,1)S(1)} %get-tuple-element.94.refs_2_.refs_5_, ...), custom_call_target="tpu_custom_call" | custom-call | flops 2000000000 | bytes 7200000 | tf_op jit(solution)/shard_map/pallas_call | solution.py:662
  57.2 2.5 %collective-permute-start.20 = (f32[2,256]{1,0:T(2,128)S(1)}, f32[2,256]{1,0:T(2,128)S(1)}, u32[]{:S(2)}, u32[]{:S(2)}) collective-permute-start(f32[2,256]{1,0:T(2,128)S(1)} %shard_map.148.refs_7_), channel_id=1, source_target_pairs={{0,4},{2,6},{4,0},{6,2},{1,5},{3,7},{5,1},{7,3},{8,12},{10,14},{12... | collective-permute-start | bytes 6152 | tf_op jit(solution)/shard_map/ppermute | solution.py:308
  61.7 1.7 %shard_map.150 = (f32[8,128]{1,0:T(8,128)S(1)}, bf16[256,1024]{1,0:T(8,128)(2,1)}, bf16[256,1024]{1,0:T(8,128)(2,1)}) custom-call(bf16[256,1024]{1,0:T(8,128)(2,1)S(1)} %bitcast.15, bf16[256,1024]{1,0:T(8,128)(2,1)S(1)} %get-tuple-element.70.refs_1_, f32[256,1024]{1,0:T(8,128)S(1)} %get-tuple-element.86.refs_2_, f32[256,1024]{1,0:T(8,128)S(1)} %get-tuple-element.101.refs_3_, ...), custom_call_target="tpu_custom_call" | custom-call | flops 10000000 | bytes 36000 | tf_op jit(solution)/shard_map/pallas_call | solution.py:662
  63.5 1.5 %shard_map.152 = (f32[1,1024]{1,0:T(1,128)S(1)}, f32[8,512,128]{2,1,0:T(8,128)}, f32[8,512,128]{2,1,0:T(8,128)}) custom-call(bf16[1040,128]{1,0:T(8,128)(2,1)S(1)} %shard_map.145.refs_9_.refs_0_, bf16[3,1040,128]{2,1,0:T(8,128)(2,1)S(1)} %shard_map.151.refs_1_.refs_2_, f32[1,1024]{1,0:T(1,128)S(1)} %bitcast.27, ...), custom_call_target="tpu_custom_call", output_to_operand_aliasing={{1}: (4, {}), {2}: (5, {})} | custom-call | flops 1600000000 | bytes 5760000 | tf_op jit(solution)/shard_map/pallas_call | solution.py:892
  (65 shorter events, 18.6 us)
Async XLA Ops:
  2.8 9.6 %collective-permute-start.2 = (f32[2,256]{1,0:T(2,128)}, f32[2,256]{1,0:T(2,128)S(1)}, u32[]{:S(2)}, u32[]{:S(2)}) collective-permute-start(f32[2,256]{1,0:T(2,128)} %shard_map.135.refs_3_), channel_id=1, source_target_pairs={{0,6},{2,4},{4,2},{6,0},{1,7},{3,5},{5,3},{7,1},{8,14},{10,12},{12... | collective-permute-start | bytes 6152 | tf_op jit(solution)/shard_map/ppermute | solution.py:296
  8.0 4.9 %collective-permute-start.1 = (f32[2,256]{1,0:T(2,128)}, f32[2,256]{1,0:T(2,128)S(1)}, u32[]{:S(2)}, u32[]{:S(2)}) collective-permute-start(f32[2,256]{1,0:T(2,128)} %shard_map.135.refs_3_), channel_id=1, source_target_pairs={{0,4},{2,6},{4,0},{6,2},{1,5},{3,7},{5,1},{7,3},{8,12},{10,14},{12... | collective-permute-start | bytes 6152 | tf_op jit(solution)/shard_map/ppermute | solution.py:296
  8.0 4.9 %collective-permute-start = (f32[2,256]{1,0:T(2,128)}, f32[2,256]{1,0:T(2,128)S(1)}, u32[]{:S(2)}, u32[]{:S(2)}) collective-permute-start(f32[2,256]{1,0:T(2,128)} %shard_map.135.refs_3_), channel_id=1, source_target_pairs={{0,2},{2,0},{4,6},{6,4},{1,3},{3,1},{5,7},{7,5},{8,10},{10,8},{12,... | collective-permute-start | bytes 6152 | tf_op jit(solution)/shard_map/ppermute | solution.py:296
  9.2 7.8 %collective-permute-start.3 = (bf16[192,256]{1,0:T(8,128)(2,1)S(1)}, bf16[192,256]{1,0:T(8,128)(2,1)S(1)}, u32[]{:S(2)}, u32[]{:S(2)}) collective-permute-start(bf16[192,256]{1,0:T(8,128)(2,1)S(1)} %get-tuple-element.66), channel_id=1, source_target_pairs={{0,8},{8,0},{16,24},{24,16},{1,9},{9,1},{17,25},{25,17},{2,10},{10... | collective-permute-start | bytes 294920 | tf_op jit(solution)/shard_map/ppermute | solution.py:296
  10.9 6.4 %collective-permute-start.4 = (bf16[192,256]{1,0:T(8,128)(2,1)S(1)}, bf16[192,256]{1,0:T(8,128)(2,1)S(1)}, u32[]{:S(2)}, u32[]{:S(2)}) collective-permute-start(bf16[192,256]{1,0:T(8,128)(2,1)S(1)} %get-tuple-element.67), channel_id=1, source_target_pairs={{0,16},{8,24},{16,0},{24,8},{1,17},{9,25},{17,1},{25,9},{2,18},{10... | collective-permute-start | bytes 294920 | tf_op jit(solution)/shard_map/ppermute | solution.py:296
  12.5 5.8 %collective-permute-start.5 = (bf16[192,256]{1,0:T(8,128)(2,1)S(1)}, bf16[192,256]{1,0:T(8,128)(2,1)S(1)}, u32[]{:S(2)}, u32[]{:S(2)}) collective-permute-start(bf16[192,256]{1,0:T(8,128)(2,1)S(1)} %get-tuple-element.68), channel_id=1, source_target_pairs={{0,24},{8,16},{16,8},{24,0},{1,25},{9,17},{17,9},{25,1},{2,26},{10... | collective-permute-start | bytes 294920 | tf_op jit(solution)/shard_map/ppermute | solution.py:296
  13.8 8.6 %collective-permute-start.9 = (bf16[192,256]{1,0:T(8,128)(2,1)S(1)}, bf16[192,256]{1,0:T(8,128)(2,1)S(1)}, u32[]{:S(2)}, u32[]{:S(2)}) collective-permute-start(bf16[192,256]{1,0:T(8,128)(2,1)S(1)} %get-tuple-element.75), channel_id=1, source_target_pairs={{0,8},{8,0},{16,24},{24,16},{1,9},{9,1},{17,25},{25,17},{2,10},{10... | collective-permute-start | bytes 294920 | tf_op jit(solution)/shard_map/ppermute | solution.py:296
  15.5 8.1 %collective-permute-start.10 = (bf16[192,256]{1,0:T(8,128)(2,1)S(1)}, bf16[192,256]{1,0:T(8,128)(2,1)S(1)}, u32[]{:S(2)}, u32[]{:S(2)}) collective-permute-start(bf16[192,256]{1,0:T(8,128)(2,1)S(1)} %get-tuple-element.76), channel_id=1, source_target_pairs={{0,16},{8,24},{16,0},{24,8},{1,17},{9,25},{17,1},{25,9},{2,18},{10... | collective-permute-start | bytes 294920 | tf_op jit(solution)/shard_map/ppermute | solution.py:296
  17.0 6.6 %collective-permute-start.11 = (bf16[192,256]{1,0:T(8,128)(2,1)S(1)}, bf16[192,256]{1,0:T(8,128)(2,1)S(1)}, u32[]{:S(2)}, u32[]{:S(2)}) collective-permute-start(bf16[192,256]{1,0:T(8,128)(2,1)S(1)} %get-tuple-element.77), channel_id=1, source_target_pairs={{0,24},{8,16},{16,8},{24,0},{1,25},{9,17},{17,9},{25,1},{2,26},{10... | collective-permute-start | bytes 294920 | tf_op jit(solution)/shard_map/ppermute | solution.py:296
  20.1 9.3 %collective-permute-start.6 = (bf16[2,256,256]{2,1,0:T(8,128)(2,1)S(1)}, bf16[2,256,256]{2,1,0:T(8,128)(2,1)S(1)}, u32[]{:S(2)}, u32[]{:S(2)}) collective-permute-start(bf16[2,256,256]{2,1,0:T(8,128)(2,1)S(1)} %get-tuple-element.72), channel_id=1, source_target_pairs={{0,8},{8,0},{16,24},{24,16},{1,9},{9,1},{17,25},{25,17},{2,10},{10... | collective-permute-start | bytes 786440 | tf_op jit(solution)/shard_map/ppermute | solution.py:296
  21.4 14.8 %collective-permute-start.7 = (bf16[2,256,256]{2,1,0:T(8,128)(2,1)S(1)}, bf16[2,256,256]{2,1,0:T(8,128)(2,1)S(1)}, u32[]{:S(2)}, u32[]{:S(2)}) collective-permute-start(bf16[2,256,256]{2,1,0:T(8,128)(2,1)S(1)} %get-tuple-element.73), channel_id=1, source_target_pairs={{0,16},{8,24},{16,0},{24,8},{1,17},{9,25},{17,1},{25,9},{2,18},{10... | collective-permute-start | bytes 786440 | tf_op jit(solution)/shard_map/ppermute | solution.py:296
  22.4 13.8 %collective-permute-start.8 = (bf16[2,256,256]{2,1,0:T(8,128)(2,1)S(1)}, bf16[2,256,256]{2,1,0:T(8,128)(2,1)S(1)}, u32[]{:S(2)}, u32[]{:S(2)}) collective-permute-start(bf16[2,256,256]{2,1,0:T(8,128)(2,1)S(1)} %get-tuple-element.74), channel_id=1, source_target_pairs={{0,24},{8,16},{16,8},{24,0},{1,25},{9,17},{17,9},{25,1},{2,26},{10... | collective-permute-start | bytes 786440 | tf_op jit(solution)/shard_map/ppermute | solution.py:296
  25.7 13.3 %collective-permute-start.12 = (bf16[2,192,256]{2,1,0:T(8,128)(2,1)S(1)}, bf16[2,192,256]{2,1,0:T(8,128)(2,1)S(1)}, u32[]{:S(2)}, u32[]{:S(2)}) collective-permute-start(bf16[2,192,256]{2,1,0:T(8,128)(2,1)S(1)} %get-tuple-element.90), channel_id=1, source_target_pairs={{0,8},{8,0},{16,24},{24,16},{1,9},{9,1},{17,25},{25,17},{2,10},{10... | collective-permute-start | bytes 589832 | tf_op jit(solution)/shard_map/ppermute | solution.py:296
  27.1 14.5 %collective-permute-start.13 = (bf16[2,192,256]{2,1,0:T(8,128)(2,1)S(1)}, bf16[2,192,256]{2,1,0:T(8,128)(2,1)S(1)}, u32[]{:S(2)}, u32[]{:S(2)}) collective-permute-start(bf16[2,192,256]{2,1,0:T(8,128)(2,1)S(1)} %get-tuple-element.91), channel_id=1, source_target_pairs={{0,16},{8,24},{16,0},{24,8},{1,17},{9,25},{17,1},{25,9},{2,18},{10... | collective-permute-start | bytes 589832 | tf_op jit(solution)/shard_map/ppermute | solution.py:296
  29.4 12.2 %collective-permute-start.14 = (bf16[2,192,256]{2,1,0:T(8,128)(2,1)S(1)}, bf16[2,192,256]{2,1,0:T(8,128)(2,1)S(1)}, u32[]{:S(2)}, u32[]{:S(2)}) collective-permute-start(bf16[2,192,256]{2,1,0:T(8,128)(2,1)S(1)} %get-tuple-element.92), channel_id=1, source_target_pairs={{0,24},{8,16},{16,8},{24,0},{1,25},{9,17},{17,9},{25,1},{2,26},{10... | collective-permute-start | bytes 589832 | tf_op jit(solution)/shard_map/ppermute | solution.py:296
  42.2 7.0 %collective-permute-start.18 = (bf16[1024,128]{1,0:T(8,128)(2,1)S(1)}, bf16[1024,128]{1,0:T(8,128)(2,1)S(1)}, u32[]{:S(2)}, u32[]{:S(2)}) collective-permute-start(bf16[1024,128]{1,0:T(8,128)(2,1)S(1)} %get-tuple-element.99), channel_id=1, source_target_pairs={{0,1},{1,0},{2,3},{3,2},{4,5},{5,4},{6,7},{7,6},{8,9},{9,8},{10,11... | collective-permute-start | bytes 786440 | tf_op jit(solution)/shard_map/ppermute | solution.py:313
  42.3 4.5 %collective-permute-start.15 = (bf16[2,64,256]{2,1,0:T(8,128)(2,1)S(1)}, bf16[2,64,256]{2,1,0:T(8,128)(2,1)S(1)}, u32[]{:S(2)}, u32[]{:S(2)}) collective-permute-start(bf16[2,64,256]{2,1,0:T(8,128)(2,1)S(1)} %get-tuple-element.95.refs_3_), channel_id=1, source_target_pairs={{0,8},{8,0},{16,24},{24,16},{1,9},{9,1},{17,25},{25,17},{2,10},{10... | collective-permute-start | bytes 196616 | tf_op jit(solution)/shard_map/ppermute | solution.py:296
  43.6 5.7 %collective-permute-start.16 = (bf16[2,64,256]{2,1,0:T(8,128)(2,1)S(1)}, bf16[2,64,256]{2,1,0:T(8,128)(2,1)S(1)}, u32[]{:S(2)}, u32[]{:S(2)}) collective-permute-start(bf16[2,64,256]{2,1,0:T(8,128)(2,1)S(1)} %get-tuple-element.96.refs_4_), channel_id=1, source_target_pairs={{0,16},{8,24},{16,0},{24,8},{1,17},{9,25},{17,1},{25,9},{2,18},{10... | collective-permute-start | bytes 196616 | tf_op jit(solution)/shard_map/ppermute | solution.py:296
  43.9 5.3 %collective-permute-start.17 = (bf16[2,64,256]{2,1,0:T(8,128)(2,1)S(1)}, bf16[2,64,256]{2,1,0:T(8,128)(2,1)S(1)}, u32[]{:S(2)}, u32[]{:S(2)}) collective-permute-start(bf16[2,64,256]{2,1,0:T(8,128)(2,1)S(1)} %get-tuple-element.97.refs_5_), channel_id=1, source_target_pairs={{0,24},{8,16},{16,8},{24,0},{1,25},{9,17},{17,9},{25,1},{2,26},{10... | collective-permute-start | bytes 196616 | tf_op jit(solution)/shard_map/ppermute | solution.py:296
  49.3 14.0 %collective-permute-start.24 = (bf16[1040,128]{1,0:T(8,128)(2,1)S(1)}, bf16[1040,128]{1,0:T(8,128)(2,1)S(1)}, u32[]{:S(2)}, u32[]{:S(2)}) collective-permute-start(bf16[1040,128]{1,0:T(8,128)(2,1)S(1)} %shard_map.145.refs_9_.refs_0_), channel_id=1, source_target_pairs={{0,24},{8,16},{16,8},{24,0},{1,25},{9,17},{17,9},{25,1},{2,26},{10... | collective-permute-start | bytes 798728 | tf_op jit(solution)/shard_map/ppermute | solution.py:296
  51.2 12.2 %collective-permute-start.23 = (bf16[1040,128]{1,0:T(8,128)(2,1)S(1)}, bf16[1040,128]{1,0:T(8,128)(2,1)S(1)}, u32[]{:S(2)}, u32[]{:S(2)}) collective-permute-start(bf16[1040,128]{1,0:T(8,128)(2,1)S(1)} %shard_map.145.refs_9_.refs_0_), channel_id=1, source_target_pairs={{0,16},{8,24},{16,0},{24,8},{1,17},{9,25},{17,1},{25,9},{2,18},{10... | collective-permute-start | bytes 798728 | tf_op jit(solution)/shard_map/ppermute | solution.py:296
  52.4 11.0 %collective-permute-start.22 = (bf16[1040,128]{1,0:T(8,128)(2,1)S(1)}, bf16[1040,128]{1,0:T(8,128)(2,1)S(1)}, u32[]{:S(2)}, u32[]{:S(2)}) collective-permute-start(bf16[1040,128]{1,0:T(8,128)(2,1)S(1)} %shard_map.145.refs_9_.refs_0_), channel_id=1, source_target_pairs={{0,8},{8,0},{16,24},{24,16},{1,9},{9,1},{17,25},{25,17},{2,10},{10... | collective-permute-start | bytes 798728 | tf_op jit(solution)/shard_map/ppermute | solution.py:296
  52.9 6.8 %collective-permute-start.21 = (bf16[1040,128]{1,0:T(8,128)(2,1)S(1)}, bf16[1040,128]{1,0:T(8,128)(2,1)S(1)}, u32[]{:S(2)}, u32[]{:S(2)}) collective-permute-start(bf16[1040,128]{1,0:T(8,128)(2,1)S(1)} %shard_map.145.refs_9_.refs_0_), channel_id=1, source_target_pairs={{0,1},{1,0},{2,3},{3,2},{4,5},{5,4},{6,7},{7,6},{8,9},{9,8},{10,11... | collective-permute-start | bytes 798728 | tf_op jit(solution)/shard_map/ppermute | solution.py:313
  57.2 4.5 %collective-permute-start.20 = (f32[2,256]{1,0:T(2,128)S(1)}, f32[2,256]{1,0:T(2,128)S(1)}, u32[]{:S(2)}, u32[]{:S(2)}) collective-permute-start(f32[2,256]{1,0:T(2,128)S(1)} %shard_map.148.refs_7_), channel_id=1, source_target_pairs={{0,4},{2,6},{4,0},{6,2},{1,5},{3,7},{5,1},{7,3},{8,12},{10,14},{12... | collective-permute-start | bytes 6152 | tf_op jit(solution)/shard_map/ppermute | solution.py:308
  (11 other events, 78.2 us)

commit v7 on v6

--- a/solution.py
+++ b/solution.py
@@ -644,7 +644,7 @@
         out_ref[span_rows:, :] = gains.astype(BF16)
 
     chunk_shape = sds((span_rows + 2 * heads, HD), BF16)
-    chunk = whole_call(chunk_body, chunk_shape, w_same, w_recv, gain_q, gain_k, micros=0.3, after=tuple(slots_recv))
+    chunk = whole_call(chunk_body, chunk_shape, w_same, w_recv, gain_q, gain_k, micros=0.3, after=(slots_recv[1],))
     chunks = to_peers("seq", [chunk] * (n_seq - 1))
     chunk_other = to_core(chunk)
 

time: 67.2 us -> 65.2 us (0.970)
  waiting for transfers between devices: 13.8 us -> 11.6 us
    ppermute x21, waiting for transfers between devices: 11.5 us -> 9.5 us  [to_peers(): lax.ppermute(a, axis, [(i, i ^ k) for i in range(n)])]
  transfers between devices with their start and end apart: 26 -> 26, of which waited for: 10 -> 10; matrix products, arithmetic and copies ran while one was open for 0% -> 0% of each run, Pallas kernels for 25% -> 26%
where the time goes in v7:
time: 65.2 us; the launch traced here: 65 us
  starting transfers between devices  31.6 us (48%)
  Pallas kernels  20.8 us (32%)
  waiting for transfers between devices  11.6 us (18%)
  between operations  0.86 us (1%)
    ppermute x21, starting transfers between devices, to_peers(): lax.ppermute(a, axis, [(i, i ^ k) for i in range(n)])  27.6 us
    pallas_call x14, Pallas kernels, whole_call(): pl.pallas_call(lambda *refs: body(*(ask() for ask in first), *refs[:len(i...  13.6 us
    ppermute x21, waiting for transfers between devices, to_peers(): lax.ppermute(a, axis, [(i, i ^ k) for i in range(n)])  9.5 us
    ppermute x2, starting transfers between devices, over_heads(): got = lax.ppermute(a, 'head', [(i, i ^ step) for i in range(n_head)])  3.92 us
    pallas_call x2, Pallas kernels, column_out(): pl.pallas_call(lambda *refs: body(*(ask() for ask in first), *refs[:len(i...  3.43 us
    pallas_call x1, Pallas kernels, on_device(): pl.pallas_call(lambda *refs: this_core_body(place(), *refs), out_shape=(g...  1.53 us
    ppermute x2, waiting for transfers between devices, over_heads(): got = lax.ppermute(a, 'head', [(i, i ^ step) for i in range(n_head)])  1.37 us
  transfers between devices with their start and end apart: 26, of which 10 were waited for; matrix products, arithmetic and copies ran while one was open for 0% of the time, Pallas kernels for 26%

profile of v7, /device:TPU:0, one launch (start us, length us, event | category | flops | bytes accessed | tf_op | source)
XLA Modules:
  0.0 65.0 jit_solution(909340166301968436)
XLA Ops:
  0.7 2.2 %shard_map.135.refs_3_ = f32[2,256]{1,0:T(2,128)} custom-call(bf16[256,1024]{1,0:T(8,128)(2,1)} %bitcast.11, bf16[256,1024]{1,0:T(8,128)(2,1)} %bitcast.30), custom_call_target="tpu_custom_call" | custom-call | flops 1500000000 | bytes 5400000 | tf_op jit(solution)/shard_map/pallas_call | solution.py:216
  2.8 5.1 %collective-permute-start.2 = (f32[2,256]{1,0:T(2,128)}, f32[2,256]{1,0:T(2,128)S(1)}, u32[]{:S(2)}, u32[]{:S(2)}) collective-permute-start(f32[2,256]{1,0:T(2,128)} %shard_map.135.refs_3_), channel_id=1, source_target_pairs={{0,6},{2,4},{4,2},{6,0},{1,7},{3,5},{5,3},{7,1},{8,14},{10,12},{12... | collective-permute-start | bytes 6152 | tf_op jit(solution)/shard_map/ppermute | solution.py:296
  9.2 1.7 %collective-permute-start.3 = (bf16[192,256]{1,0:T(8,128)(2,1)S(1)}, bf16[192,256]{1,0:T(8,128)(2,1)S(1)}, u32[]{:S(2)}, u32[]{:S(2)}) collective-permute-start(bf16[192,256]{1,0:T(8,128)(2,1)S(1)} %get-tuple-element.66), channel_id=1, source_target_pairs={{0,8},{8,0},{16,24},{24,16},{1,9},{9,1},{17,25},{25,17},{2,10},{10... | collective-permute-start | bytes 294920 | tf_op jit(solution)/shard_map/ppermute | solution.py:296
  10.9 1.5 %collective-permute-start.4 = (bf16[192,256]{1,0:T(8,128)(2,1)S(1)}, bf16[192,256]{1,0:T(8,128)(2,1)S(1)}, u32[]{:S(2)}, u32[]{:S(2)}) collective-permute-start(bf16[192,256]{1,0:T(8,128)(2,1)S(1)} %get-tuple-element.67), channel_id=1, source_target_pairs={{0,16},{8,24},{16,0},{24,8},{1,17},{9,25},{17,1},{25,9},{2,18},{10... | collective-permute-start | bytes 294920 | tf_op jit(solution)/shard_map/ppermute | solution.py:296
  13.8 1.7 %collective-permute-start.9 = (bf16[192,256]{1,0:T(8,128)(2,1)S(1)}, bf16[192,256]{1,0:T(8,128)(2,1)S(1)}, u32[]{:S(2)}, u32[]{:S(2)}) collective-permute-start(bf16[192,256]{1,0:T(8,128)(2,1)S(1)} %get-tuple-element.75), channel_id=1, source_target_pairs={{0,8},{8,0},{16,24},{24,16},{1,9},{9,1},{17,25},{25,17},{2,10},{10... | collective-permute-start | bytes 294920 | tf_op jit(solution)/shard_map/ppermute | solution.py:296
  15.5 1.5 %collective-permute-start.10 = (bf16[192,256]{1,0:T(8,128)(2,1)S(1)}, bf16[192,256]{1,0:T(8,128)(2,1)S(1)}, u32[]{:S(2)}, u32[]{:S(2)}) collective-permute-start(bf16[192,256]{1,0:T(8,128)(2,1)S(1)} %get-tuple-element.76), channel_id=1, source_target_pairs={{0,16},{8,24},{16,0},{24,8},{1,17},{9,25},{17,1},{25,9},{2,18},{10... | collective-permute-start | bytes 294920 | tf_op jit(solution)/shard_map/ppermute | solution.py:296
  18.3 1.4 %shard_map.138 = (bf16[256,1024]{1,0:T(8,128)(2,1)S(1)}, f32[8,8,256]{2,1,0:T(8,128)S(1)}) custom-call(bf16[256,1024]{1,0:T(8,128)(2,1)S(1)} %bitcast.12, f32[1,1024]{1,0:T(1,128)S(1)} %bitcast.20, f32[2,256]{1,0:T(2,128)S(1)} %get-tuple-element.65.refs_2_.refs_6_, bf16[256,1024]{1,0:T(8,128)(2,1)S(1)} %get-tuple-element.63.refs_3_.refs_0_, ...), custom_call_target="tpu_custom_call" | custom-call | flops 500000000 | bytes 1800000 | tf_op jit(solution)/shard_map/pallas_call | solution.py:216
  20.1 1.3 %collective-permute-start.6 = (bf16[2,256,256]{2,1,0:T(8,128)(2,1)S(1)}, bf16[2,256,256]{2,1,0:T(8,128)(2,1)S(1)}, u32[]{:S(2)}, u32[]{:S(2)}) collective-permute-start(bf16[2,256,256]{2,1,0:T(8,128)(2,1)S(1)} %get-tuple-element.72), channel_id=1, source_target_pairs={{0,8},{8,0},{16,24},{24,16},{1,9},{9,1},{17,25},{25,17},{2,10},{10... | collective-permute-start | bytes 786440 | tf_op jit(solution)/shard_map/ppermute | solution.py:296
  23.6 2.1 %shard_map.140 = (f32[6,8,256]{2,1,0:T(8,128)S(1)}, bf16[6,192,256]{2,1,0:T(8,128)(2,1)S(1)}, bf16[2,192,256]{2,1,0:T(8,128)(2,1)S(1)}, bf16[2,192,256]{2,1,0:T(8,128)(2,1)S(1)}, bf16[2,192,256]{2,1,0:T(8,128)(2,1)S(1)}) custom-call(bf16[256,1024]{1,0:T(8,128)(2,1)S(1)} %get-tuple-element.71.refs_0_.refs_2_, bf16[256,1024]{1,0:T(8,128)(2,1)S(1)} %bitcast.17, ...), custom_call_target="tpu_custom_call" | custom-call | flops 2000000000 | bytes 7200000 | tf_op jit(solution)/shard_map/pallas_call | solution.py:216
  25.7 1.3 %collective-permute-start.12 = (bf16[2,192,256]{2,1,0:T(8,128)(2,1)S(1)}, bf16[2,192,256]{2,1,0:T(8,128)(2,1)S(1)}, u32[]{:S(2)}, u32[]{:S(2)}) collective-permute-start(bf16[2,192,256]{2,1,0:T(8,128)(2,1)S(1)} %get-tuple-element.90), channel_id=1, source_target_pairs={{0,8},{8,0},{16,24},{24,16},{1,9},{9,1},{17,25},{25,17},{2,10},{10... | collective-permute-start | bytes 589832 | tf_op jit(solution)/shard_map/ppermute | solution.py:296
  28.1 1.3 %collective-permute-done.6.refs_11_.refs_6_ = bf16[2,256,256]{2,1,0:T(8,128)(2,1)S(1)} collective-permute-done((bf16[2,256,256]{2,1,0:T(8,128)(2,1)S(1)}, bf16[2,256,256]{2,1,0:T(8,128)(2,1)S(1)}, u32[]{:S(2)}, u32[]{:S(2)}) %collective-permute-start.6) | collective-permute-done | bytes 262176 | tf_op jit(solution)/shard_map/ppermute | solution.py:296
  29.4 1.7 %collective-permute-start.14 = (bf16[2,192,256]{2,1,0:T(8,128)(2,1)S(1)}, bf16[2,192,256]{2,1,0:T(8,128)(2,1)S(1)}, u32[]{:S(2)}, u32[]{:S(2)}) collective-permute-start(bf16[2,192,256]{2,1,0:T(8,128)(2,1)S(1)} %get-tuple-element.92), channel_id=1, source_target_pairs={{0,24},{8,16},{16,8},{24,0},{1,25},{9,17},{17,9},{25,1},{2,26},{10... | collective-permute-start | bytes 589832 | tf_op jit(solution)/shard_map/ppermute | solution.py:296
  31.1 2.7 %shard_map.141 = (f32[256,1024]{1,0:T(8,128)S(1)}, f32[256,1024]{1,0:T(8,128)S(1)}, f32[256,1024]{1,0:T(8,128)S(1)}, f32[8,128]{1,0:T(8,128)S(1)}, f32[8,128]{1,0:T(8,128)S(1)}, /*index=5*/f32[256,128]{1,0:T(8,128)S(1)}) custom-call(bf16[256,1024]{1,0:T(8,128)(2,1)S(1)} %bitcast.13, bf16[256,1024]{1,0:T(8,128)(2,1)S(1)} %get-tuple-element.70.refs_1_, ...), custom_call_target="tpu_custom_call" | custom-call | flops 500000000 | bytes 1800000 | tf_op jit(solution)/shard_map/pallas_call | solution.py:216
  33.7 2.5 %collective-permute-done.7.refs_12_.refs_7_ = bf16[2,256,256]{2,1,0:T(8,128)(2,1)S(1)} collective-permute-done((bf16[2,256,256]{2,1,0:T(8,128)(2,1)S(1)}, bf16[2,256,256]{2,1,0:T(8,128)(2,1)S(1)}, u32[]{:S(2)}, u32[]{:S(2)}) %collective-permute-start.7) | collective-permute-done | bytes 262176 | tf_op jit(solution)/shard_map/ppermute | solution.py:296
  36.2 2.0 %shard_map.142 = (f32[256,1024]{1,0:T(8,128)S(1)}, f32[256,1024]{1,0:T(8,128)S(1)}, f32[256,1024]{1,0:T(8,128)S(1)}, f32[8,128]{1,0:T(8,128)S(1)}, f32[8,128]{1,...) custom-call(bf16[256,1024]{1,0:T(8,128)(2,1)S(1)} %bitcast.14, ...), custom_call_target="tpu_custom_call", output_to_operand_aliasing={{0}: (14, {}), {1}: (15, {}), {2}: (16, {}), {3}: (17, {}),... | custom-call | flops 300000000 | bytes 1080000 | tf_op jit(solution)/shard_map/pallas_call | solution.py:216
  39.1 2.6 %collective-permute-done.13.refs_2_ = bf16[2,192,256]{2,1,0:T(8,128)(2,1)S(1)} collective-permute-done((bf16[2,192,256]{2,1,0:T(8,128)(2,1)S(1)}, bf16[2,192,256]{2,1,0:T(8,128)(2,1)S(1)}, u32[]{:S(2)}, u32[]{:S(2)}) %collective-permute-start.13) | collective-permute-done | bytes 196640 | tf_op jit(solution)/shard_map/ppermute | solution.py:296
  42.3 1.3 %collective-permute-start.16 = (bf16[2,64,256]{2,1,0:T(8,128)(2,1)S(1)}, bf16[2,64,256]{2,1,0:T(8,128)(2,1)S(1)}, u32[]{:S(2)}, u32[]{:S(2)}) collective-permute-start(bf16[2,64,256]{2,1,0:T(8,128)(2,1)S(1)} %get-tuple-element.96.refs_4_), channel_id=1, source_target_pairs={{0,16},{8,24},{16,0},{24,8},{1,17},{9,25},{17,1},{25,9},{2,18},{10... | collective-permute-start | bytes 196616 | tf_op jit(solution)/shard_map/ppermute | solution.py:296
  43.9 1.9 %collective-permute-start.17 = (bf16[2,64,256]{2,1,0:T(8,128)(2,1)S(1)}, bf16[2,64,256]{2,1,0:T(8,128)(2,1)S(1)}, u32[]{:S(2)}, u32[]{:S(2)}) collective-permute-start(bf16[2,64,256]{2,1,0:T(8,128)(2,1)S(1)} %get-tuple-element.97.refs_5_), channel_id=1, source_target_pairs={{0,24},{8,16},{16,8},{24,0},{1,25},{9,17},{17,9},{25,1},{2,26},{10... | collective-permute-start | bytes 196616 | tf_op jit(solution)/shard_map/ppermute | solution.py:296
  47.9 1.7 %collective-permute-start.23 = (bf16[1040,128]{1,0:T(8,128)(2,1)S(1)}, bf16[1040,128]{1,0:T(8,128)(2,1)S(1)}, u32[]{:S(2)}, u32[]{:S(2)}) collective-permute-start(bf16[1040,128]{1,0:T(8,128)(2,1)S(1)} %shard_map.145.refs_9_.refs_0_), channel_id=1, source_target_pairs={{0,16},{8,24},{16,0},{24,8},{1,17},{9,25},{17,1},{25,9},{2,18},{10... | collective-permute-start | bytes 798728 | tf_op jit(solution)/shard_map/ppermute | solution.py:296
  51.1 1.5 %collective-permute-start.19 = (f32[2,256]{1,0:T(2,128)S(1)}, f32[2,256]{1,0:T(2,128)S(1)}, u32[]{:S(2)}, u32[]{:S(2)}) collective-permute-start(f32[2,256]{1,0:T(2,128)S(1)} %get-tuple-element.102.refs_6_.refs_0_), channel_id=1, source_target_pairs={{0,2},{2,0},{4,6},{6,4},{1,3},{3,1},{5,7},{7,5},{8,10},{10,8},{12,... | collective-permute-start | bytes 6152 | tf_op jit(solution)/shard_map/ppermute | solution.py:308
  52.6 1.8 %shard_map.147 = (f32[8,128]{1,0:T(8,128)S(1)}, bf16[256,1024]{1,0:T(8,128)(2,1)}) custom-call(f32[256,1024]{1,0:T(8,128)S(1)} %get-tuple-element.103.refs_0_, bf16[8,512,128]{2,1,0:T(8,128)(2,1)S(1)} %copy-done.3, bf16[2,64,256]{2,1,0:T(8,128)(2,1)S(1)} %get-tuple-element.94.refs_2_.refs_5_, ...), custom_call_target="tpu_custom_call" | custom-call | flops 2000000000 | bytes 7200000 | tf_op jit(solution)/shard_map/pallas_call | solution.py:662
  54.8 2.5 %collective-permute-start.20 = (f32[2,256]{1,0:T(2,128)S(1)}, f32[2,256]{1,0:T(2,128)S(1)}, u32[]{:S(2)}, u32[]{:S(2)}) collective-permute-start(f32[2,256]{1,0:T(2,128)S(1)} %shard_map.148.refs_7_), channel_id=1, source_target_pairs={{0,4},{2,6},{4,0},{6,2},{1,5},{3,7},{5,1},{7,3},{8,12},{10,14},{12... | collective-permute-start | bytes 6152 | tf_op jit(solution)/shard_map/ppermute | solution.py:308
  59.3 1.7 %shard_map.150 = (f32[8,128]{1,0:T(8,128)S(1)}, bf16[256,1024]{1,0:T(8,128)(2,1)}, bf16[256,1024]{1,0:T(8,128)(2,1)}) custom-call(bf16[256,1024]{1,0:T(8,128)(2,1)S(1)} %bitcast.15, bf16[256,1024]{1,0:T(8,128)(2,1)S(1)} %get-tuple-element.70.refs_1_, f32[256,1024]{1,0:T(8,128)S(1)} %get-tuple-element.86.refs_2_, f32[256,1024]{1,0:T(8,128)S(1)} %get-tuple-element.101.refs_3_, ...), custom_call_target="tpu_custom_call" | custom-call | flops 10000000 | bytes 36000 | tf_op jit(solution)/shard_map/pallas_call | solution.py:662
  61.5 1.5 %shard_map.152 = (f32[1,1024]{1,0:T(1,128)S(1)}, f32[8,512,128]{2,1,0:T(8,128)}, f32[8,512,128]{2,1,0:T(8,128)}) custom-call(bf16[1040,128]{1,0:T(8,128)(2,1)S(1)} %shard_map.145.refs_9_.refs_0_, bf16[3,1040,128]{2,1,0:T(8,128)(2,1)S(1)} %shard_map.151.refs_1_.refs_2_, f32[1,1024]{1,0:T(1,128)S(1)} %bitcast.27, ...), custom_call_target="tpu_custom_call", output_to_operand_aliasing={{1}: (4, {}), {2}: (5, {})} | custom-call | flops 1600000000 | bytes 5760000 | tf_op jit(solution)/shard_map/pallas_call | solution.py:892
  (65 shorter events, 17.8 us)
Async XLA Ops:
  2.8 9.6 %collective-permute-start.2 = (f32[2,256]{1,0:T(2,128)}, f32[2,256]{1,0:T(2,128)S(1)}, u32[]{:S(2)}, u32[]{:S(2)}) collective-permute-start(f32[2,256]{1,0:T(2,128)} %shard_map.135.refs_3_), channel_id=1, source_target_pairs={{0,6},{2,4},{4,2},{6,0},{1,7},{3,5},{5,3},{7,1},{8,14},{10,12},{12... | collective-permute-start | bytes 6152 | tf_op jit(solution)/shard_map/ppermute | solution.py:296
  8.0 4.9 %collective-permute-start.1 = (f32[2,256]{1,0:T(2,128)}, f32[2,256]{1,0:T(2,128)S(1)}, u32[]{:S(2)}, u32[]{:S(2)}) collective-permute-start(f32[2,256]{1,0:T(2,128)} %shard_map.135.refs_3_), channel_id=1, source_target_pairs={{0,4},{2,6},{4,0},{6,2},{1,5},{3,7},{5,1},{7,3},{8,12},{10,14},{12... | collective-permute-start | bytes 6152 | tf_op jit(solution)/shard_map/ppermute | solution.py:296
  8.0 4.9 %collective-permute-start = (f32[2,256]{1,0:T(2,128)}, f32[2,256]{1,0:T(2,128)S(1)}, u32[]{:S(2)}, u32[]{:S(2)}) collective-permute-start(f32[2,256]{1,0:T(2,128)} %shard_map.135.refs_3_), channel_id=1, source_target_pairs={{0,2},{2,0},{4,6},{6,4},{1,3},{3,1},{5,7},{7,5},{8,10},{10,8},{12,... | collective-permute-start | bytes 6152 | tf_op jit(solution)/shard_map/ppermute | solution.py:296
  9.2 7.8 %collective-permute-start.3 = (bf16[192,256]{1,0:T(8,128)(2,1)S(1)}, bf16[192,256]{1,0:T(8,128)(2,1)S(1)}, u32[]{:S(2)}, u32[]{:S(2)}) collective-permute-start(bf16[192,256]{1,0:T(8,128)(2,1)S(1)} %get-tuple-element.66), channel_id=1, source_target_pairs={{0,8},{8,0},{16,24},{24,16},{1,9},{9,1},{17,25},{25,17},{2,10},{10... | collective-permute-start | bytes 294920 | tf_op jit(solution)/shard_map/ppermute | solution.py:296
  10.9 6.4 %collective-permute-start.4 = (bf16[192,256]{1,0:T(8,128)(2,1)S(1)}, bf16[192,256]{1,0:T(8,128)(2,1)S(1)}, u32[]{:S(2)}, u32[]{:S(2)}) collective-permute-start(bf16[192,256]{1,0:T(8,128)(2,1)S(1)} %get-tuple-element.67), channel_id=1, source_target_pairs={{0,16},{8,24},{16,0},{24,8},{1,17},{9,25},{17,1},{25,9},{2,18},{10... | collective-permute-start | bytes 294920 | tf_op jit(solution)/shard_map/ppermute | solution.py:296
  12.5 5.8 %collective-permute-start.5 = (bf16[192,256]{1,0:T(8,128)(2,1)S(1)}, bf16[192,256]{1,0:T(8,128)(2,1)S(1)}, u32[]{:S(2)}, u32[]{:S(2)}) collective-permute-start(bf16[192,256]{1,0:T(8,128)(2,1)S(1)} %get-tuple-element.68), channel_id=1, source_target_pairs={{0,24},{8,16},{16,8},{24,0},{1,25},{9,17},{17,9},{25,1},{2,26},{10... | collective-permute-start | bytes 294920 | tf_op jit(solution)/shard_map/ppermute | solution.py:296
  13.8 8.6 %collective-permute-start.9 = (bf16[192,256]{1,0:T(8,128)(2,1)S(1)}, bf16[192,256]{1,0:T(8,128)(2,1)S(1)}, u32[]{:S(2)}, u32[]{:S(2)}) collective-permute-start(bf16[192,256]{1,0:T(8,128)(2,1)S(1)} %get-tuple-element.75), channel_id=1, source_target_pairs={{0,8},{8,0},{16,24},{24,16},{1,9},{9,1},{17,25},{25,17},{2,10},{10... | collective-permute-start | bytes 294920 | tf_op jit(solution)/shard_map/ppermute | solution.py:296
  15.5 8.1 %collective-permute-start.10 = (bf16[192,256]{1,0:T(8,128)(2,1)S(1)}, bf16[192,256]{1,0:T(8,128)(2,1)S(1)}, u32[]{:S(2)}, u32[]{:S(2)}) collective-permute-start(bf16[192,256]{1,0:T(8,128)(2,1)S(1)} %get-tuple-element.76), channel_id=1, source_target_pairs={{0,16},{8,24},{16,0},{24,8},{1,17},{9,25},{17,1},{25,9},{2,18},{10... | collective-permute-start | bytes 294920 | tf_op jit(solution)/shard_map/ppermute | solution.py:296
  17.0 6.6 %collective-permute-start.11 = (bf16[192,256]{1,0:T(8,128)(2,1)S(1)}, bf16[192,256]{1,0:T(8,128)(2,1)S(1)}, u32[]{:S(2)}, u32[]{:S(2)}) collective-permute-start(bf16[192,256]{1,0:T(8,128)(2,1)S(1)} %get-tuple-element.77), channel_id=1, source_target_pairs={{0,24},{8,16},{16,8},{24,0},{1,25},{9,17},{17,9},{25,1},{2,26},{10... | collective-permute-start | bytes 294920 | tf_op jit(solution)/shard_map/ppermute | solution.py:296
  20.1 9.3 %collective-permute-start.6 = (bf16[2,256,256]{2,1,0:T(8,128)(2,1)S(1)}, bf16[2,256,256]{2,1,0:T(8,128)(2,1)S(1)}, u32[]{:S(2)}, u32[]{:S(2)}) collective-permute-start(bf16[2,256,256]{2,1,0:T(8,128)(2,1)S(1)} %get-tuple-element.72), channel_id=1, source_target_pairs={{0,8},{8,0},{16,24},{24,16},{1,9},{9,1},{17,25},{25,17},{2,10},{10... | collective-permute-start | bytes 786440 | tf_op jit(solution)/shard_map/ppermute | solution.py:296
  21.4 14.8 %collective-permute-start.7 = (bf16[2,256,256]{2,1,0:T(8,128)(2,1)S(1)}, bf16[2,256,256]{2,1,0:T(8,128)(2,1)S(1)}, u32[]{:S(2)}, u32[]{:S(2)}) collective-permute-start(bf16[2,256,256]{2,1,0:T(8,128)(2,1)S(1)} %get-tuple-element.73), channel_id=1, source_target_pairs={{0,16},{8,24},{16,0},{24,8},{1,17},{9,25},{17,1},{25,9},{2,18},{10... | collective-permute-start | bytes 786440 | tf_op jit(solution)/shard_map/ppermute | solution.py:296
  22.4 13.8 %collective-permute-start.8 = (bf16[2,256,256]{2,1,0:T(8,128)(2,1)S(1)}, bf16[2,256,256]{2,1,0:T(8,128)(2,1)S(1)}, u32[]{:S(2)}, u32[]{:S(2)}) collective-permute-start(bf16[2,256,256]{2,1,0:T(8,128)(2,1)S(1)} %get-tuple-element.74), channel_id=1, source_target_pairs={{0,24},{8,16},{16,8},{24,0},{1,25},{9,17},{17,9},{25,1},{2,26},{10... | collective-permute-start | bytes 786440 | tf_op jit(solution)/shard_map/ppermute | solution.py:296
  25.7 13.3 %collective-permute-start.12 = (bf16[2,192,256]{2,1,0:T(8,128)(2,1)S(1)}, bf16[2,192,256]{2,1,0:T(8,128)(2,1)S(1)}, u32[]{:S(2)}, u32[]{:S(2)}) collective-permute-start(bf16[2,192,256]{2,1,0:T(8,128)(2,1)S(1)} %get-tuple-element.90), channel_id=1, source_target_pairs={{0,8},{8,0},{16,24},{24,16},{1,9},{9,1},{17,25},{25,17},{2,10},{10... | collective-permute-start | bytes 589832 | tf_op jit(solution)/shard_map/ppermute | solution.py:296
  27.1 14.5 %collective-permute-start.13 = (bf16[2,192,256]{2,1,0:T(8,128)(2,1)S(1)}, bf16[2,192,256]{2,1,0:T(8,128)(2,1)S(1)}, u32[]{:S(2)}, u32[]{:S(2)}) collective-permute-start(bf16[2,192,256]{2,1,0:T(8,128)(2,1)S(1)} %get-tuple-element.91), channel_id=1, source_target_pairs={{0,16},{8,24},{16,0},{24,8},{1,17},{9,25},{17,1},{25,9},{2,18},{10... | collective-permute-start | bytes 589832 | tf_op jit(solution)/shard_map/ppermute | solution.py:296
  29.4 12.2 %collective-permute-start.14 = (bf16[2,192,256]{2,1,0:T(8,128)(2,1)S(1)}, bf16[2,192,256]{2,1,0:T(8,128)(2,1)S(1)}, u32[]{:S(2)}, u32[]{:S(2)}) collective-permute-start(bf16[2,192,256]{2,1,0:T(8,128)(2,1)S(1)} %get-tuple-element.92), channel_id=1, source_target_pairs={{0,24},{8,16},{16,8},{24,0},{1,25},{9,17},{17,9},{25,1},{2,26},{10... | collective-permute-start | bytes 589832 | tf_op jit(solution)/shard_map/ppermute | solution.py:296
  42.2 4.6 %collective-permute-start.18 = (bf16[1024,128]{1,0:T(8,128)(2,1)S(1)}, bf16[1024,128]{1,0:T(8,128)(2,1)S(1)}, u32[]{:S(2)}, u32[]{:S(2)}) collective-permute-start(bf16[1024,128]{1,0:T(8,128)(2,1)S(1)} %get-tuple-element.99), channel_id=1, source_target_pairs={{0,1},{1,0},{2,3},{3,2},{4,5},{5,4},{6,7},{7,6},{8,9},{9,8},{10,11... | collective-permute-start | bytes 786440 | tf_op jit(solution)/shard_map/ppermute | solution.py:313
  42.3 4.5 %collective-permute-start.16 = (bf16[2,64,256]{2,1,0:T(8,128)(2,1)S(1)}, bf16[2,64,256]{2,1,0:T(8,128)(2,1)S(1)}, u32[]{:S(2)}, u32[]{:S(2)}) collective-permute-start(bf16[2,64,256]{2,1,0:T(8,128)(2,1)S(1)} %get-tuple-element.96.refs_4_), channel_id=1, source_target_pairs={{0,16},{8,24},{16,0},{24,8},{1,17},{9,25},{17,1},{25,9},{2,18},{10... | collective-permute-start | bytes 196616 | tf_op jit(solution)/shard_map/ppermute | solution.py:296
  43.6 6.9 %collective-permute-start.15 = (bf16[2,64,256]{2,1,0:T(8,128)(2,1)S(1)}, bf16[2,64,256]{2,1,0:T(8,128)(2,1)S(1)}, u32[]{:S(2)}, u32[]{:S(2)}) collective-permute-start(bf16[2,64,256]{2,1,0:T(8,128)(2,1)S(1)} %get-tuple-element.95.refs_3_), channel_id=1, source_target_pairs={{0,8},{8,0},{16,24},{24,16},{1,9},{9,1},{17,25},{25,17},{2,10},{10... | collective-permute-start | bytes 196616 | tf_op jit(solution)/shard_map/ppermute | solution.py:296
  43.9 6.5 %collective-permute-start.17 = (bf16[2,64,256]{2,1,0:T(8,128)(2,1)S(1)}, bf16[2,64,256]{2,1,0:T(8,128)(2,1)S(1)}, u32[]{:S(2)}, u32[]{:S(2)}) collective-permute-start(bf16[2,64,256]{2,1,0:T(8,128)(2,1)S(1)} %get-tuple-element.97.refs_5_), channel_id=1, source_target_pairs={{0,24},{8,16},{16,8},{24,0},{1,25},{9,17},{17,9},{25,1},{2,26},{10... | collective-permute-start | bytes 196616 | tf_op jit(solution)/shard_map/ppermute | solution.py:296
  46.9 14.1 %collective-permute-start.24 = (bf16[1040,128]{1,0:T(8,128)(2,1)S(1)}, bf16[1040,128]{1,0:T(8,128)(2,1)S(1)}, u32[]{:S(2)}, u32[]{:S(2)}) collective-permute-start(bf16[1040,128]{1,0:T(8,128)(2,1)S(1)} %shard_map.145.refs_9_.refs_0_), channel_id=1, source_target_pairs={{0,24},{8,16},{16,8},{24,0},{1,25},{9,17},{17,9},{25,1},{2,26},{10... | collective-permute-start | bytes 798728 | tf_op jit(solution)/shard_map/ppermute | solution.py:296
  47.9 13.4 %collective-permute-start.23 = (bf16[1040,128]{1,0:T(8,128)(2,1)S(1)}, bf16[1040,128]{1,0:T(8,128)(2,1)S(1)}, u32[]{:S(2)}, u32[]{:S(2)}) collective-permute-start(bf16[1040,128]{1,0:T(8,128)(2,1)S(1)} %shard_map.145.refs_9_.refs_0_), channel_id=1, source_target_pairs={{0,16},{8,24},{16,0},{24,8},{1,17},{9,25},{17,1},{25,9},{2,18},{10... | collective-permute-start | bytes 798728 | tf_op jit(solution)/shard_map/ppermute | solution.py:296
  49.6 11.7 %collective-permute-start.22 = (bf16[1040,128]{1,0:T(8,128)(2,1)S(1)}, bf16[1040,128]{1,0:T(8,128)(2,1)S(1)}, u32[]{:S(2)}, u32[]{:S(2)}) collective-permute-start(bf16[1040,128]{1,0:T(8,128)(2,1)S(1)} %shard_map.145.refs_9_.refs_0_), channel_id=1, source_target_pairs={{0,8},{8,0},{16,24},{24,16},{1,9},{9,1},{17,25},{25,17},{2,10},{10... | collective-permute-start | bytes 798728 | tf_op jit(solution)/shard_map/ppermute | solution.py:296
  50.4 6.8 %collective-permute-start.21 = (bf16[1040,128]{1,0:T(8,128)(2,1)S(1)}, bf16[1040,128]{1,0:T(8,128)(2,1)S(1)}, u32[]{:S(2)}, u32[]{:S(2)}) collective-permute-start(bf16[1040,128]{1,0:T(8,128)(2,1)S(1)} %shard_map.145.refs_9_.refs_0_), channel_id=1, source_target_pairs={{0,1},{1,0},{2,3},{3,2},{4,5},{5,4},{6,7},{7,6},{8,9},{9,8},{10,11... | collective-permute-start | bytes 798728 | tf_op jit(solution)/shard_map/ppermute | solution.py:313
  54.8 4.5 %collective-permute-start.20 = (f32[2,256]{1,0:T(2,128)S(1)}, f32[2,256]{1,0:T(2,128)S(1)}, u32[]{:S(2)}, u32[]{:S(2)}) collective-permute-start(f32[2,256]{1,0:T(2,128)S(1)} %shard_map.148.refs_7_), channel_id=1, source_target_pairs={{0,4},{2,6},{4,0},{6,2},{1,5},{3,7},{5,1},{7,3},{8,12},{10,14},{12... | collective-permute-start | bytes 6152 | tf_op jit(solution)/shard_map/ppermute | solution.py:308
  (11 other events, 78.2 us)

commit v8 on v7

--- a/solution.py
+++ b/solution.py
@@ -377,6 +377,24 @@
             total = total + other[...]
         natural = as_columns(lax.rsqrt(total / full_width + epsilon))
         order = row_order(rows)
+        inv_ref[...] = natural.T[:2]
+        normed = (k_ref[...].astype(F32) * natural[:, 1:2] * kg_ref[...]).astype(BF16)
+        kn_ref[...] = dot(order, normed).astype(BF16)
+        compress(kn_ref, w_ref, mem_ref)
+        pack_slots(ids_ref[0], mem_ref, sends)
+
+    scales, kn, *mk_sends = whole_call(
+        keys_body,
+        (two_rows, rows_shape) + (slots_packet,) * (n_seq - 1),
+        place, k, kg, key_squeeze, *ss_parts,
+        scratch=mem_scratch,
+        micros=20.0,
+    )
+    mk_recv = to_peers("seq", mk_sends)
+
+    def local_body(q_ref, qg_ref, scale_ref, kn_ref, vp_ref, do_ref, inv_ref, qn_ref, st_ref):
+        natural = as_columns(scale_ref[...])
+        order = row_order(rows)
         high = natural.astype(BF16)
         rest_1 = natural - high.astype(F32)
         middle = rest_1.astype(BF16)
@@ -384,23 +402,8 @@
         ordered = dot(order, high) + dot(order, middle) + dot(order, low)
         inv_c = jnp.concatenate([natural[:, 0:1], ordered[:, 1:2], natural[:, 2:]], axis=1)
         inv_ref[...] = inv_c.T[:2]
-        normed = (k_ref[...].astype(F32) * natural[:, 1:2] * kg_ref[...]).astype(BF16)
-        kn_ref[...] = dot(order, normed).astype(BF16)
-        compress(kn_ref, w_ref, mem_ref)
-        pack_slots(ids_ref[0], mem_ref, sends)
-
-    inv, kn, *mk_sends = whole_call(
-        keys_body,
-        (two_rows, rows_shape) + (slots_packet,) * (n_seq - 1),
-        place, k, kg, key_squeeze, *ss_parts,
-        scratch=mem_scratch,
-        micros=20.0,
-    )
-    mk_recv = to_peers("seq", mk_sends)
-
-    def local_body(q_ref, qg_ref, inv_ref, kn_ref, vp_ref, do_ref, qn_ref, st_ref):
         allowed = causal_t(rows)
-        inv_c = as_columns(inv_ref[...])[:, 0:1]
+        inv_c = inv_c[:, 0:1]
         for h in range(heads):
             at = slice(h * HD, (h + 1) * HD)
             qn_h = (q_ref[:, at].astype(F32) * inv_c * qg_ref[:, at]).astype(BF16)
@@ -414,8 +417,8 @@
             st_ref[h, 2:3, :] = jnp.sum(p * g, axis=0, keepdims=True)
 
     stat_shape = sds((heads, 8, rows), F32)
-    qn, stats = whole_call(
-        local_body, (rows_shape, stat_shape), q, qg, inv, kn, vp, do,
+    inv, qn, stats = whole_call(
+        local_body, (two_rows, rows_shape, stat_shape), q, qg, scales, kn, vp, do,
         micros=0.5,
         after=tuple(mv_recv),
     )

time: 65.2 us -> 65.5 us (level)
  transfers between devices with their start and end apart: 26 -> 26, of which waited for: 10 -> 11; matrix products, arithmetic and copies ran while one was open for 0% -> 0% of each run, Pallas kernels for 26% -> 26%
where the time goes in v8:
time: 65.5 us; the launch traced here: 65.3 us
  starting transfers between devices  31.8 us (49%)
  Pallas kernels  21.2 us (32%)
  waiting for transfers between devices  11.2 us (17%)
  between operations  1.02 us (2%)
    ppermute x21, starting transfers between devices, to_peers(): lax.ppermute(a, axis, [(i, i ^ k) for i in range(n)])  27.5 us
    pallas_call x14, Pallas kernels, whole_call(): pl.pallas_call(lambda *refs: body(*(ask() for ask in first), *refs[:len(i...  13.8 us
    ppermute x21, waiting for transfers between devices, to_peers(): lax.ppermute(a, axis, [(i, i ^ k) for i in range(n)])  9.51 us
    ppermute x2, starting transfers between devices, over_heads(): got = lax.ppermute(a, 'head', [(i, i ^ step) for i in range(n_head)])  4.15 us
    pallas_call x2, Pallas kernels, column_out(): pl.pallas_call(lambda *refs: body(*(ask() for ask in first), *refs[:len(i...  3.61 us
    pallas_call x1, Pallas kernels, on_device(): pl.pallas_call(lambda *refs: this_core_body(place(), *refs), out_shape=(g...  1.53 us
  transfers between devices with their start and end apart: 26, of which 11 were waited for; matrix products, arithmetic and copies ran while one was open for 0% of the time, Pallas kernels for 26%

profile of v8, /device:TPU:0, one launch (start us, length us, event | category | flops | bytes accessed | tf_op | source)
XLA Modules:
  0.0 65.3 jit_solution(1764110749618905019)
XLA Ops:
  0.7 2.2 %shard_map.135.refs_3_ = f32[2,256]{1,0:T(2,128)} custom-call(bf16[256,1024]{1,0:T(8,128)(2,1)} %bitcast.11, bf16[256,1024]{1,0:T(8,128)(2,1)} %bitcast.30), custom_call_target="tpu_custom_call" | custom-call | flops 1500000000 | bytes 5400000 | tf_op jit(solution)/shard_map/pallas_call | solution.py:216
  2.8 5.1 %collective-permute-start.2 = (f32[2,256]{1,0:T(2,128)}, f32[2,256]{1,0:T(2,128)S(1)}, u32[]{:S(2)}, u32[]{:S(2)}) collective-permute-start(f32[2,256]{1,0:T(2,128)} %shard_map.135.refs_3_), channel_id=1, source_target_pairs={{0,6},{2,4},{4,2},{6,0},{1,7},{3,5},{5,3},{7,1},{8,14},{10,12},{12... | collective-permute-start | bytes 6152 | tf_op jit(solution)/shard_map/ppermute | solution.py:296
  9.2 1.7 %collective-permute-start.3 = (bf16[192,256]{1,0:T(8,128)(2,1)S(1)}, bf16[192,256]{1,0:T(8,128)(2,1)S(1)}, u32[]{:S(2)}, u32[]{:S(2)}) collective-permute-start(bf16[192,256]{1,0:T(8,128)(2,1)S(1)} %get-tuple-element.67), channel_id=1, source_target_pairs={{0,8},{8,0},{16,24},{24,16},{1,9},{9,1},{17,25},{25,17},{2,10},{10... | collective-permute-start | bytes 294920 | tf_op jit(solution)/shard_map/ppermute | solution.py:296
  10.9 1.5 %collective-permute-start.4 = (bf16[192,256]{1,0:T(8,128)(2,1)S(1)}, bf16[192,256]{1,0:T(8,128)(2,1)S(1)}, u32[]{:S(2)}, u32[]{:S(2)}) collective-permute-start(bf16[192,256]{1,0:T(8,128)(2,1)S(1)} %get-tuple-element.68), channel_id=1, source_target_pairs={{0,16},{8,24},{16,0},{24,8},{1,17},{9,25},{17,1},{25,9},{2,18},{10... | collective-permute-start | bytes 294920 | tf_op jit(solution)/shard_map/ppermute | solution.py:296
  13.8 1.7 %collective-permute-start.9 = (bf16[192,256]{1,0:T(8,128)(2,1)S(1)}, bf16[192,256]{1,0:T(8,128)(2,1)S(1)}, u32[]{:S(2)}, u32[]{:S(2)}) collective-permute-start(bf16[192,256]{1,0:T(8,128)(2,1)S(1)} %get-tuple-element.77), channel_id=1, source_target_pairs={{0,8},{8,0},{16,24},{24,16},{1,9},{9,1},{17,25},{25,17},{2,10},{10... | collective-permute-start | bytes 294920 | tf_op jit(solution)/shard_map/ppermute | solution.py:296
  15.5 1.5 %collective-permute-start.10 = (bf16[192,256]{1,0:T(8,128)(2,1)S(1)}, bf16[192,256]{1,0:T(8,128)(2,1)S(1)}, u32[]{:S(2)}, u32[]{:S(2)}) collective-permute-start(bf16[192,256]{1,0:T(8,128)(2,1)S(1)} %get-tuple-element.78), channel_id=1, source_target_pairs={{0,16},{8,24},{16,0},{24,8},{1,17},{9,25},{17,1},{25,9},{2,18},{10... | collective-permute-start | bytes 294920 | tf_op jit(solution)/shard_map/ppermute | solution.py:296
  18.3 1.7 %shard_map.138 = (f32[2,256]{1,0:T(2,128)S(1)}, bf16[256,1024]{1,0:T(8,128)(2,1)S(1)}, f32[8,8,256]{2,1,0:T(8,128)S(1)}) custom-call(bf16[256,1024]{1,0:T(8,128)(2,1)S(1)} %bitcast.12, f32[1,1024]{1,0:T(1,128)S(1)} %bitcast.20, f32[2,256]{1,0:T(2,128)S(1)} %get-tuple-element.66.refs_2_, bf16[256,1024]{1,0:T(8,128)(2,1)S(1)} %get-tuple-element.64.refs_3_.refs_0_, ...), custom_call_target="tpu_custom_call" | custom-call | flops 500000000 | bytes 1800000 | tf_op jit(solution)/shard_map/pallas_call | solution.py:216
  20.3 1.4 %collective-permute-start.6 = (bf16[2,256,256]{2,1,0:T(8,128)(2,1)S(1)}, bf16[2,256,256]{2,1,0:T(8,128)(2,1)S(1)}, u32[]{:S(2)}, u32[]{:S(2)}) collective-permute-start(bf16[2,256,256]{2,1,0:T(8,128)(2,1)S(1)} %get-tuple-element.74), channel_id=1, source_target_pairs={{0,8},{8,0},{16,24},{24,16},{1,9},{9,1},{17,25},{25,17},{2,10},{10... | collective-permute-start | bytes 786440 | tf_op jit(solution)/shard_map/ppermute | solution.py:296
  23.9 2.1 %shard_map.140 = (f32[6,8,256]{2,1,0:T(8,128)S(1)}, bf16[6,192,256]{2,1,0:T(8,128)(2,1)S(1)}, bf16[2,192,256]{2,1,0:T(8,128)(2,1)S(1)}, bf16[2,192,256]{2,1,0:T(8,128)(2,1)S(1)}, bf16[2,192,256]{2,1,0:T(8,128)(2,1)S(1)}) custom-call(bf16[256,1024]{1,0:T(8,128)(2,1)S(1)} %get-tuple-element.72.refs_0_.refs_2_, bf16[256,1024]{1,0:T(8,128)(2,1)S(1)} %bitcast.17, ...), custom_call_target="tpu_custom_call" | custom-call | flops 2000000000 | bytes 7200000 | tf_op jit(solution)/shard_map/pallas_call | solution.py:216
  26.0 1.4 %collective-permute-start.12 = (bf16[2,192,256]{2,1,0:T(8,128)(2,1)S(1)}, bf16[2,192,256]{2,1,0:T(8,128)(2,1)S(1)}, u32[]{:S(2)}, u32[]{:S(2)}) collective-permute-start(bf16[2,192,256]{2,1,0:T(8,128)(2,1)S(1)} %get-tuple-element.92), channel_id=1, source_target_pairs={{0,8},{8,0},{16,24},{24,16},{1,9},{9,1},{17,25},{25,17},{2,10},{10... | collective-permute-start | bytes 589832 | tf_op jit(solution)/shard_map/ppermute | solution.py:296
  28.3 1.3 %collective-permute-done.6.refs_11_.refs_6_ = bf16[2,256,256]{2,1,0:T(8,128)(2,1)S(1)} collective-permute-done((bf16[2,256,256]{2,1,0:T(8,128)(2,1)S(1)}, bf16[2,256,256]{2,1,0:T(8,128)(2,1)S(1)}, u32[]{:S(2)}, u32[]{:S(2)}) %collective-permute-start.6) | collective-permute-done | bytes 262176 | tf_op jit(solution)/shard_map/ppermute | solution.py:296
  29.6 1.7 %collective-permute-start.14 = (bf16[2,192,256]{2,1,0:T(8,128)(2,1)S(1)}, bf16[2,192,256]{2,1,0:T(8,128)(2,1)S(1)}, u32[]{:S(2)}, u32[]{:S(2)}) collective-permute-start(bf16[2,192,256]{2,1,0:T(8,128)(2,1)S(1)} %get-tuple-element.94), channel_id=1, source_target_pairs={{0,24},{8,16},{16,8},{24,0},{1,25},{9,17},{17,9},{25,1},{2,26},{10... | collective-permute-start | bytes 589832 | tf_op jit(solution)/shard_map/ppermute | solution.py:296
  31.3 2.7 %shard_map.141 = (f32[256,1024]{1,0:T(8,128)S(1)}, f32[256,1024]{1,0:T(8,128)S(1)}, f32[256,1024]{1,0:T(8,128)S(1)}, f32[8,128]{1,0:T(8,128)S(1)}, f32[8,128]{1,0:T(8,128)S(1)}, /*index=5*/f32[256,128]{1,0:T(8,128)S(1)}) custom-call(bf16[256,1024]{1,0:T(8,128)(2,1)S(1)} %bitcast.13, bf16[256,1024]{1,0:T(8,128)(2,1)S(1)} %get-tuple-element.71.refs_1_, ...), custom_call_target="tpu_custom_call" | custom-call | flops 500000000 | bytes 1800000 | tf_op jit(solution)/shard_map/pallas_call | solution.py:216
  33.9 2.5 %collective-permute-done.7.refs_12_.refs_7_ = bf16[2,256,256]{2,1,0:T(8,128)(2,1)S(1)} collective-permute-done((bf16[2,256,256]{2,1,0:T(8,128)(2,1)S(1)}, bf16[2,256,256]{2,1,0:T(8,128)(2,1)S(1)}, u32[]{:S(2)}, u32[]{:S(2)}) %collective-permute-start.7) | collective-permute-done | bytes 262176 | tf_op jit(solution)/shard_map/ppermute | solution.py:296
  36.5 2.0 %shard_map.142 = (f32[256,1024]{1,0:T(8,128)S(1)}, f32[256,1024]{1,0:T(8,128)S(1)}, f32[256,1024]{1,0:T(8,128)S(1)}, f32[8,128]{1,0:T(8,128)S(1)}, f32[8,128]{1,...) custom-call(bf16[256,1024]{1,0:T(8,128)(2,1)S(1)} %bitcast.14, ...), custom_call_target="tpu_custom_call", output_to_operand_aliasing={{0}: (14, {}), {1}: (15, {}), {2}: (16, {}), {3}: (17, {}),... | custom-call | flops 300000000 | bytes 1080000 | tf_op jit(solution)/shard_map/pallas_call | solution.py:216
  39.1 2.7 %collective-permute-done.13.refs_2_ = bf16[2,192,256]{2,1,0:T(8,128)(2,1)S(1)} collective-permute-done((bf16[2,192,256]{2,1,0:T(8,128)(2,1)S(1)}, bf16[2,192,256]{2,1,0:T(8,128)(2,1)S(1)}, u32[]{:S(2)}, u32[]{:S(2)}) %collective-permute-start.13) | collective-permute-done | bytes 196640 | tf_op jit(solution)/shard_map/ppermute | solution.py:296
  42.5 1.3 %collective-permute-start.16 = (bf16[2,64,256]{2,1,0:T(8,128)(2,1)S(1)}, bf16[2,64,256]{2,1,0:T(8,128)(2,1)S(1)}, u32[]{:S(2)}, u32[]{:S(2)}) collective-permute-start(bf16[2,64,256]{2,1,0:T(8,128)(2,1)S(1)} %get-tuple-element.98.refs_4_), channel_id=1, source_target_pairs={{0,16},{8,24},{16,0},{24,8},{1,17},{9,25},{17,1},{25,9},{2,18},{10... | collective-permute-start | bytes 196616 | tf_op jit(solution)/shard_map/ppermute | solution.py:296
  43.9 2.2 %collective-permute-start.17 = (bf16[2,64,256]{2,1,0:T(8,128)(2,1)S(1)}, bf16[2,64,256]{2,1,0:T(8,128)(2,1)S(1)}, u32[]{:S(2)}, u32[]{:S(2)}) collective-permute-start(bf16[2,64,256]{2,1,0:T(8,128)(2,1)S(1)} %get-tuple-element.99.refs_5_), channel_id=1, source_target_pairs={{0,24},{8,16},{16,8},{24,0},{1,25},{9,17},{17,9},{25,1},{2,26},{10... | collective-permute-start | bytes 196616 | tf_op jit(solution)/shard_map/ppermute | solution.py:296
  47.9 1.7 %collective-permute-start.23 = (bf16[1040,128]{1,0:T(8,128)(2,1)S(1)}, bf16[1040,128]{1,0:T(8,128)(2,1)S(1)}, u32[]{:S(2)}, u32[]{:S(2)}) collective-permute-start(bf16[1040,128]{1,0:T(8,128)(2,1)S(1)} %shard_map.145.refs_9_.refs_0_), channel_id=1, source_target_pairs={{0,16},{8,24},{16,0},{24,8},{1,17},{9,25},{17,1},{25,9},{2,18},{10... | collective-permute-start | bytes 798728 | tf_op jit(solution)/shard_map/ppermute | solution.py:296
  51.3 1.5 %collective-permute-start.19 = (f32[2,256]{1,0:T(2,128)S(1)}, f32[2,256]{1,0:T(2,128)S(1)}, u32[]{:S(2)}, u32[]{:S(2)}) collective-permute-start(f32[2,256]{1,0:T(2,128)S(1)} %get-tuple-element.104.refs_6_.refs_0_), channel_id=1, source_target_pairs={{0,2},{2,0},{4,6},{6,4},{1,3},{3,1},{5,7},{7,5},{8,10},{10,8},{12,... | collective-permute-start | bytes 6152 | tf_op jit(solution)/shard_map/ppermute | solution.py:308
  52.8 2.0 %shard_map.147 = (f32[8,128]{1,0:T(8,128)S(1)}, bf16[256,1024]{1,0:T(8,128)(2,1)}) custom-call(f32[256,1024]{1,0:T(8,128)S(1)} %get-tuple-element.105.refs_0_, bf16[8,512,128]{2,1,0:T(8,128)(2,1)S(1)} %copy-done.3, bf16[2,64,256]{2,1,0:T(8,128)(2,1)S(1)} %get-tuple-element.96.refs_2_.refs_5_, ...), custom_call_target="tpu_custom_call" | custom-call | flops 2000000000 | bytes 7200000 | tf_op jit(solution)/shard_map/pallas_call | solution.py:665
  55.0 2.7 %collective-permute-start.20 = (f32[2,256]{1,0:T(2,128)S(1)}, f32[2,256]{1,0:T(2,128)S(1)}, u32[]{:S(2)}, u32[]{:S(2)}) collective-permute-start(f32[2,256]{1,0:T(2,128)S(1)} %shard_map.148.refs_7_), channel_id=1, source_target_pairs={{0,4},{2,6},{4,0},{6,2},{1,5},{3,7},{5,1},{7,3},{8,12},{10,14},{12... | collective-permute-start | bytes 6152 | tf_op jit(solution)/shard_map/ppermute | solution.py:308
  59.5 1.7 %shard_map.150 = (f32[8,128]{1,0:T(8,128)S(1)}, bf16[256,1024]{1,0:T(8,128)(2,1)}, bf16[256,1024]{1,0:T(8,128)(2,1)}) custom-call(bf16[256,1024]{1,0:T(8,128)(2,1)S(1)} %bitcast.15, bf16[256,1024]{1,0:T(8,128)(2,1)S(1)} %get-tuple-element.71.refs_1_, f32[256,1024]{1,0:T(8,128)S(1)} %get-tuple-element.88.refs_2_, f32[256,1024]{1,0:T(8,128)S(1)} %get-tuple-element.103.refs_3_, ...), custom_call_target="tpu_custom_call" | custom-call | flops 10000000 | bytes 36000 | tf_op jit(solution)/shard_map/pallas_call | solution.py:665
  61.6 1.5 %shard_map.152 = (f32[1,1024]{1,0:T(1,128)S(1)}, f32[8,512,128]{2,1,0:T(8,128)}, f32[8,512,128]{2,1,0:T(8,128)}) custom-call(bf16[1040,128]{1,0:T(8,128)(2,1)S(1)} %shard_map.145.refs_9_.refs_0_, bf16[3,1040,128]{2,1,0:T(8,128)(2,1)S(1)} %shard_map.151.refs_1_.refs_2_, f32[1,1024]{1,0:T(1,128)S(1)} %bitcast.27, ...), custom_call_target="tpu_custom_call", output_to_operand_aliasing={{1}: (4, {}), {2}: (5, {})} | custom-call | flops 1600000000 | bytes 5760000 | tf_op jit(solution)/shard_map/pallas_call | solution.py:895
  (65 shorter events, 16.8 us)
Async XLA Ops:
  2.8 9.6 %collective-permute-start.2 = (f32[2,256]{1,0:T(2,128)}, f32[2,256]{1,0:T(2,128)S(1)}, u32[]{:S(2)}, u32[]{:S(2)}) collective-permute-start(f32[2,256]{1,0:T(2,128)} %shard_map.135.refs_3_), channel_id=1, source_target_pairs={{0,6},{2,4},{4,2},{6,0},{1,7},{3,5},{5,3},{7,1},{8,14},{10,12},{12... | collective-permute-start | bytes 6152 | tf_op jit(solution)/shard_map/ppermute | solution.py:296
  8.0 4.9 %collective-permute-start.1 = (f32[2,256]{1,0:T(2,128)}, f32[2,256]{1,0:T(2,128)S(1)}, u32[]{:S(2)}, u32[]{:S(2)}) collective-permute-start(f32[2,256]{1,0:T(2,128)} %shard_map.135.refs_3_), channel_id=1, source_target_pairs={{0,4},{2,6},{4,0},{6,2},{1,5},{3,7},{5,1},{7,3},{8,12},{10,14},{12... | collective-permute-start | bytes 6152 | tf_op jit(solution)/shard_map/ppermute | solution.py:296
  8.0 4.9 %collective-permute-start = (f32[2,256]{1,0:T(2,128)}, f32[2,256]{1,0:T(2,128)S(1)}, u32[]{:S(2)}, u32[]{:S(2)}) collective-permute-start(f32[2,256]{1,0:T(2,128)} %shard_map.135.refs_3_), channel_id=1, source_target_pairs={{0,2},{2,0},{4,6},{6,4},{1,3},{3,1},{5,7},{7,5},{8,10},{10,8},{12,... | collective-permute-start | bytes 6152 | tf_op jit(solution)/shard_map/ppermute | solution.py:296
  9.2 7.8 %collective-permute-start.3 = (bf16[192,256]{1,0:T(8,128)(2,1)S(1)}, bf16[192,256]{1,0:T(8,128)(2,1)S(1)}, u32[]{:S(2)}, u32[]{:S(2)}) collective-permute-start(bf16[192,256]{1,0:T(8,128)(2,1)S(1)} %get-tuple-element.67), channel_id=1, source_target_pairs={{0,8},{8,0},{16,24},{24,16},{1,9},{9,1},{17,25},{25,17},{2,10},{10... | collective-permute-start | bytes 294920 | tf_op jit(solution)/shard_map/ppermute | solution.py:296
  10.9 6.4 %collective-permute-start.4 = (bf16[192,256]{1,0:T(8,128)(2,1)S(1)}, bf16[192,256]{1,0:T(8,128)(2,1)S(1)}, u32[]{:S(2)}, u32[]{:S(2)}) collective-permute-start(bf16[192,256]{1,0:T(8,128)(2,1)S(1)} %get-tuple-element.68), channel_id=1, source_target_pairs={{0,16},{8,24},{16,0},{24,8},{1,17},{9,25},{17,1},{25,9},{2,18},{10... | collective-permute-start | bytes 294920 | tf_op jit(solution)/shard_map/ppermute | solution.py:296
  12.5 5.8 %collective-permute-start.5 = (bf16[192,256]{1,0:T(8,128)(2,1)S(1)}, bf16[192,256]{1,0:T(8,128)(2,1)S(1)}, u32[]{:S(2)}, u32[]{:S(2)}) collective-permute-start(bf16[192,256]{1,0:T(8,128)(2,1)S(1)} %get-tuple-element.69), channel_id=1, source_target_pairs={{0,24},{8,16},{16,8},{24,0},{1,25},{9,17},{17,9},{25,1},{2,26},{10... | collective-permute-start | bytes 294920 | tf_op jit(solution)/shard_map/ppermute | solution.py:296
  13.8 8.8 %collective-permute-start.9 = (bf16[192,256]{1,0:T(8,128)(2,1)S(1)}, bf16[192,256]{1,0:T(8,128)(2,1)S(1)}, u32[]{:S(2)}, u32[]{:S(2)}) collective-permute-start(bf16[192,256]{1,0:T(8,128)(2,1)S(1)} %get-tuple-element.77), channel_id=1, source_target_pairs={{0,8},{8,0},{16,24},{24,16},{1,9},{9,1},{17,25},{25,17},{2,10},{10... | collective-permute-start | bytes 294920 | tf_op jit(solution)/shard_map/ppermute | solution.py:296
  15.5 8.4 %collective-permute-start.10 = (bf16[192,256]{1,0:T(8,128)(2,1)S(1)}, bf16[192,256]{1,0:T(8,128)(2,1)S(1)}, u32[]{:S(2)}, u32[]{:S(2)}) collective-permute-start(bf16[192,256]{1,0:T(8,128)(2,1)S(1)} %get-tuple-element.78), channel_id=1, source_target_pairs={{0,16},{8,24},{16,0},{24,8},{1,17},{9,25},{17,1},{25,9},{2,18},{10... | collective-permute-start | bytes 294920 | tf_op jit(solution)/shard_map/ppermute | solution.py:296
  17.0 6.8 %collective-permute-start.11 = (bf16[192,256]{1,0:T(8,128)(2,1)S(1)}, bf16[192,256]{1,0:T(8,128)(2,1)S(1)}, u32[]{:S(2)}, u32[]{:S(2)}) collective-permute-start(bf16[192,256]{1,0:T(8,128)(2,1)S(1)} %get-tuple-element.79), channel_id=1, source_target_pairs={{0,24},{8,16},{16,8},{24,0},{1,25},{9,17},{17,9},{25,1},{2,26},{10... | collective-permute-start | bytes 294920 | tf_op jit(solution)/shard_map/ppermute | solution.py:296
  20.3 9.3 %collective-permute-start.6 = (bf16[2,256,256]{2,1,0:T(8,128)(2,1)S(1)}, bf16[2,256,256]{2,1,0:T(8,128)(2,1)S(1)}, u32[]{:S(2)}, u32[]{:S(2)}) collective-permute-start(bf16[2,256,256]{2,1,0:T(8,128)(2,1)S(1)} %get-tuple-element.74), channel_id=1, source_target_pairs={{0,8},{8,0},{16,24},{24,16},{1,9},{9,1},{17,25},{25,17},{2,10},{10... | collective-permute-start | bytes 786440 | tf_op jit(solution)/shard_map/ppermute | solution.py:296
  21.7 14.8 %collective-permute-start.7 = (bf16[2,256,256]{2,1,0:T(8,128)(2,1)S(1)}, bf16[2,256,256]{2,1,0:T(8,128)(2,1)S(1)}, u32[]{:S(2)}, u32[]{:S(2)}) collective-permute-start(bf16[2,256,256]{2,1,0:T(8,128)(2,1)S(1)} %get-tuple-element.75), channel_id=1, source_target_pairs={{0,16},{8,24},{16,0},{24,8},{1,17},{9,25},{17,1},{25,9},{2,18},{10... | collective-permute-start | bytes 786440 | tf_op jit(solution)/shard_map/ppermute | solution.py:296
  22.6 13.8 %collective-permute-start.8 = (bf16[2,256,256]{2,1,0:T(8,128)(2,1)S(1)}, bf16[2,256,256]{2,1,0:T(8,128)(2,1)S(1)}, u32[]{:S(2)}, u32[]{:S(2)}) collective-permute-start(bf16[2,256,256]{2,1,0:T(8,128)(2,1)S(1)} %get-tuple-element.76), channel_id=1, source_target_pairs={{0,24},{8,16},{16,8},{24,0},{1,25},{9,17},{17,9},{25,1},{2,26},{10... | collective-permute-start | bytes 786440 | tf_op jit(solution)/shard_map/ppermute | solution.py:296
  26.0 13.2 %collective-permute-start.12 = (bf16[2,192,256]{2,1,0:T(8,128)(2,1)S(1)}, bf16[2,192,256]{2,1,0:T(8,128)(2,1)S(1)}, u32[]{:S(2)}, u32[]{:S(2)}) collective-permute-start(bf16[2,192,256]{2,1,0:T(8,128)(2,1)S(1)} %get-tuple-element.92), channel_id=1, source_target_pairs={{0,8},{8,0},{16,24},{24,16},{1,9},{9,1},{17,25},{25,17},{2,10},{10... | collective-permute-start | bytes 589832 | tf_op jit(solution)/shard_map/ppermute | solution.py:296
  27.3 14.5 %collective-permute-start.13 = (bf16[2,192,256]{2,1,0:T(8,128)(2,1)S(1)}, bf16[2,192,256]{2,1,0:T(8,128)(2,1)S(1)}, u32[]{:S(2)}, u32[]{:S(2)}) collective-permute-start(bf16[2,192,256]{2,1,0:T(8,128)(2,1)S(1)} %get-tuple-element.93), channel_id=1, source_target_pairs={{0,16},{8,24},{16,0},{24,8},{1,17},{9,25},{17,1},{25,9},{2,18},{10... | collective-permute-start | bytes 589832 | tf_op jit(solution)/shard_map/ppermute | solution.py:296
  29.6 12.2 %collective-permute-start.14 = (bf16[2,192,256]{2,1,0:T(8,128)(2,1)S(1)}, bf16[2,192,256]{2,1,0:T(8,128)(2,1)S(1)}, u32[]{:S(2)}, u32[]{:S(2)}) collective-permute-start(bf16[2,192,256]{2,1,0:T(8,128)(2,1)S(1)} %get-tuple-element.94), channel_id=1, source_target_pairs={{0,24},{8,16},{16,8},{24,0},{1,25},{9,17},{17,9},{25,1},{2,26},{10... | collective-permute-start | bytes 589832 | tf_op jit(solution)/shard_map/ppermute | solution.py:296
  42.4 4.6 %collective-permute-start.18 = (bf16[1024,128]{1,0:T(8,128)(2,1)S(1)}, bf16[1024,128]{1,0:T(8,128)(2,1)S(1)}, u32[]{:S(2)}, u32[]{:S(2)}) collective-permute-start(bf16[1024,128]{1,0:T(8,128)(2,1)S(1)} %get-tuple-element.101), channel_id=1, source_target_pairs={{0,1},{1,0},{2,3},{3,2},{4,5},{5,4},{6,7},{7,6},{8,9},{9,8},{10,11... | collective-permute-start | bytes 786440 | tf_op jit(solution)/shard_map/ppermute | solution.py:313
  42.5 4.5 %collective-permute-start.16 = (bf16[2,64,256]{2,1,0:T(8,128)(2,1)S(1)}, bf16[2,64,256]{2,1,0:T(8,128)(2,1)S(1)}, u32[]{:S(2)}, u32[]{:S(2)}) collective-permute-start(bf16[2,64,256]{2,1,0:T(8,128)(2,1)S(1)} %get-tuple-element.98.refs_4_), channel_id=1, source_target_pairs={{0,16},{8,24},{16,0},{24,8},{1,17},{9,25},{17,1},{25,9},{2,18},{10... | collective-permute-start | bytes 196616 | tf_op jit(solution)/shard_map/ppermute | solution.py:296
  43.8 6.9 %collective-permute-start.15 = (bf16[2,64,256]{2,1,0:T(8,128)(2,1)S(1)}, bf16[2,64,256]{2,1,0:T(8,128)(2,1)S(1)}, u32[]{:S(2)}, u32[]{:S(2)}) collective-permute-start(bf16[2,64,256]{2,1,0:T(8,128)(2,1)S(1)} %get-tuple-element.97.refs_3_), channel_id=1, source_target_pairs={{0,8},{8,0},{16,24},{24,16},{1,9},{9,1},{17,25},{25,17},{2,10},{10... | collective-permute-start | bytes 196616 | tf_op jit(solution)/shard_map/ppermute | solution.py:296
  43.9 6.7 %collective-permute-start.17 = (bf16[2,64,256]{2,1,0:T(8,128)(2,1)S(1)}, bf16[2,64,256]{2,1,0:T(8,128)(2,1)S(1)}, u32[]{:S(2)}, u32[]{:S(2)}) collective-permute-start(bf16[2,64,256]{2,1,0:T(8,128)(2,1)S(1)} %get-tuple-element.99.refs_5_), channel_id=1, source_target_pairs={{0,24},{8,16},{16,8},{24,0},{1,25},{9,17},{17,9},{25,1},{2,26},{10... | collective-permute-start | bytes 196616 | tf_op jit(solution)/shard_map/ppermute | solution.py:296
  47.1 14.1 %collective-permute-start.24 = (bf16[1040,128]{1,0:T(8,128)(2,1)S(1)}, bf16[1040,128]{1,0:T(8,128)(2,1)S(1)}, u32[]{:S(2)}, u32[]{:S(2)}) collective-permute-start(bf16[1040,128]{1,0:T(8,128)(2,1)S(1)} %shard_map.145.refs_9_.refs_0_), channel_id=1, source_target_pairs={{0,24},{8,16},{16,8},{24,0},{1,25},{9,17},{17,9},{25,1},{2,26},{10... | collective-permute-start | bytes 798728 | tf_op jit(solution)/shard_map/ppermute | solution.py:296
  47.9 13.4 %collective-permute-start.23 = (bf16[1040,128]{1,0:T(8,128)(2,1)S(1)}, bf16[1040,128]{1,0:T(8,128)(2,1)S(1)}, u32[]{:S(2)}, u32[]{:S(2)}) collective-permute-start(bf16[1040,128]{1,0:T(8,128)(2,1)S(1)} %shard_map.145.refs_9_.refs_0_), channel_id=1, source_target_pairs={{0,16},{8,24},{16,0},{24,8},{1,17},{9,25},{17,1},{25,9},{2,18},{10... | collective-permute-start | bytes 798728 | tf_op jit(solution)/shard_map/ppermute | solution.py:296
  49.7 11.8 %collective-permute-start.22 = (bf16[1040,128]{1,0:T(8,128)(2,1)S(1)}, bf16[1040,128]{1,0:T(8,128)(2,1)S(1)}, u32[]{:S(2)}, u32[]{:S(2)}) collective-permute-start(bf16[1040,128]{1,0:T(8,128)(2,1)S(1)} %shard_map.145.refs_9_.refs_0_), channel_id=1, source_target_pairs={{0,8},{8,0},{16,24},{24,16},{1,9},{9,1},{17,25},{25,17},{2,10},{10... | collective-permute-start | bytes 798728 | tf_op jit(solution)/shard_map/ppermute | solution.py:296
  50.6 7.0 %collective-permute-start.21 = (bf16[1040,128]{1,0:T(8,128)(2,1)S(1)}, bf16[1040,128]{1,0:T(8,128)(2,1)S(1)}, u32[]{:S(2)}, u32[]{:S(2)}) collective-permute-start(bf16[1040,128]{1,0:T(8,128)(2,1)S(1)} %shard_map.145.refs_9_.refs_0_), channel_id=1, source_target_pairs={{0,1},{1,0},{2,3},{3,2},{4,5},{5,4},{6,7},{7,6},{8,9},{9,8},{10,11... | collective-permute-start | bytes 798728 | tf_op jit(solution)/shard_map/ppermute | solution.py:313
  55.0 4.5 %collective-permute-start.20 = (f32[2,256]{1,0:T(2,128)S(1)}, f32[2,256]{1,0:T(2,128)S(1)}, u32[]{:S(2)}, u32[]{:S(2)}) collective-permute-start(f32[2,256]{1,0:T(2,128)S(1)} %shard_map.148.refs_7_), channel_id=1, source_target_pairs={{0,4},{2,6},{4,0},{6,2},{1,5},{3,7},{5,1},{7,3},{8,12},{10,14},{12... | collective-permute-start | bytes 6152 | tf_op jit(solution)/shard_map/ppermute | solution.py:308
  (11 other events, 78.2 us)
